TPU v7x, 32 devices: a whole 2x2x4 slice. The times are simulated.
32 devices in a mesh: groups: 2 (over x), blk: 16 (over z, y, core).
Axes of the slice: x: 2, y: 2, z: 4, core: 2. Of those that a mesh axis runs over, the one named last changes fastest.
Arguments:
- tokens: bfloat16 [4096, 8192], P(('groups', 'blk')), parts along dimension 0, may hold values from -6 to 6
- cotangent: bfloat16 [4096, 8192], P(('groups', 'blk')), parts along dimension 0, may hold values from -6 to 6
- tenant: int32 [4096, 1], P(('groups', 'blk')), parts along dimension 0, may hold values from 0 to 15; in each aligned block of 128 rows (0 to 127, 128 to 255, ...) at most 16 rows name the same one
- owner: int32 [32], P('groups'), parts along dimension 0, may hold values from 0 to 15, each once
- down_factor_table: bfloat16 [32, 64, 8192], P(('groups', 'blk')), parts along dimension 0, may hold values from -0.0625 to 0.0625
- up_factor_table: bfloat16 [32, 64, 8192], P(('groups', 'blk')), parts along dimension 0, may hold values from -0.0625 to 0.0625
Outputs:
- input_grad: bfloat16 [4096, 8192], P(('groups', 'blk')), parts along dimension 0
- grad_a: bfloat16 [32, 64, 8192], P(('groups', 'blk')), parts along dimension 0
- grad_b: bfloat16 [32, 64, 8192], P(('groups', 'blk')), parts along dimension 0
There are 2 independent parts, one for each index of `groups`. A program takes and returns all parts, laid end to end along the dimension named above; each array names one. Nothing has to cross between parts.
Inputs may be any that keep to these rules, and one draw needn't show every extreme that they name: No tenant is named by more than 16 rows of one device; some tenant reaches 16 rows of some device; every tenant is named by some row. `owner`: each storage index appears once.
All inputs are finite; a program needn't handle non-finite values.
Results may differ from a plain program's by a relative error of at most 0.0049.
Values may be sent and summed in bfloat16 or wider, within the bound.
No kernel may reach another device: no remote copies, remote signals or barrier semaphores. Data moves between devices by JAX's collectives and lax.ppermute only.
A program may use at most 128 MiB of HBM per device.

v0:
```python
import jax
import jax.numpy as jnp
from jax import lax
from jax.sharding import PartitionSpec as P

SCALE = 2.0
DAMPING = 1.0
EPS = 1e-06


def project(grad, left, right):
    top = jnp.dot(left, grad, precision=lax.Precision.HIGHEST)
    inner = grad - left[:, None] * top[None, :] / (DAMPING + jnp.sum(left * left))
    side = jnp.dot(inner, right, precision=lax.Precision.HIGHEST)
    return inner - side[:, None] * right[None, :] / (DAMPING + jnp.sum(right * right))


def down_part(rows_x, down_weight):
    dims = (((1,), (1,)), ((), ()))
    hidden = lax.dot_general(rows_x, down_weight, dims, preferred_element_type=jnp.float32).astype(
        jnp.bfloat16
    )
    return hidden


def per_device(tokens, cotangent, tenant, owner, down_factor_table, up_factor_table):
    rows, width = tokens.shape
    count_blk = lax.axis_size("blk")
    adapters = owner.shape[0]
    rank_position = down_factor_table.shape[1]
    cap = 2 * rows // adapters
    slots = count_blk * cap
    tenant_ids = tenant[:, 0]
    match = tenant_ids[:, None] == jnp.arange(adapters, dtype=jnp.int32)[None, :]
    target_dev = jnp.sum(jnp.where(match, owner[None, :], 0), axis=1)
    earlier = (
        jnp.arange(rows, dtype=jnp.int32)[None, :] < jnp.arange(rows, dtype=jnp.int32)[:, None]
    )
    same_before = (tenant_ids[:, None] == tenant_ids[None, :]) & earlier
    position = jnp.sum(same_before.astype(jnp.int32), axis=1)
    target = target_dev * cap + position
    placing = (jnp.arange(slots, dtype=jnp.int32)[:, None] == target[None, :]).astype(jnp.bfloat16)
    send_x = (
        jnp.dot(placing, tokens, preferred_element_type=jnp.float32)
        .astype(jnp.bfloat16)
        .reshape(count_blk, cap, width)
    )
    send_dy = (
        jnp.dot(placing, cotangent, preferred_element_type=jnp.float32)
        .astype(jnp.bfloat16)
        .reshape(count_blk, cap, width)
    )
    live_flag = (
        jnp.sum(placing, axis=1, dtype=jnp.float32).astype(jnp.bfloat16).reshape(count_blk, cap)
    )
    down_weight = down_factor_table[0]
    up_weight = up_factor_table[0]
    got_x, got_live = (
        lax.all_to_all(send_x, "blk", split_axis=0, concat_axis=0, tiled=True),
        lax.all_to_all(live_flag, "blk", split_axis=0, concat_axis=0, tiled=True),
    )
    rows_x = got_x.reshape(slots, width)
    hidden = down_part(rows_x, down_weight)
    got_dy = lax.all_to_all(send_dy, "blk", split_axis=0, concat_axis=0, tiled=True)
    rows_dy = got_dy.reshape(slots, width)
    dims = (((1,), (1,)), ((), ()))
    rows_dims = (((0,), (0,)), ((), ()))
    grad_hidden = (
        SCALE * lax.dot_general(rows_dy, up_weight, dims, preferred_element_type=jnp.float32)
    ).astype(jnp.bfloat16)
    back = jnp.dot(grad_hidden, down_weight, preferred_element_type=jnp.float32).astype(
        jnp.bfloat16
    )
    returned = lax.all_to_all(
        back.reshape(count_blk, cap, width), "blk", split_axis=0, concat_axis=0, tiled=True
    ).reshape(slots, width)
    input_grad = lax.dot_general(
        placing, returned, rows_dims, preferred_element_type=jnp.float32
    ).astype(jnp.bfloat16)
    raw_a = lax.dot_general(grad_hidden, rows_x, rows_dims, preferred_element_type=jnp.float32)
    raw_b = SCALE * lax.dot_general(hidden, rows_dy, rows_dims, preferred_element_type=jnp.float32)
    amount = jnp.sum(got_live, dtype=jnp.float32)
    xbar = jnp.sum(rows_x, axis=0, dtype=jnp.float32) / amount
    ybar = jnp.sum(rows_dy, axis=0, dtype=jnp.float32) / amount
    hbar = jnp.sum(hidden, axis=0, dtype=jnp.float32) / amount
    gbar = jnp.sum(grad_hidden, axis=0, dtype=jnp.float32) / amount
    proj_a = project(raw_a, gbar, xbar)
    proj_b = project(raw_b, hbar, ybar)
    local_sq = jnp.sum(proj_a * proj_a) + jnp.sum(proj_b * proj_b)
    total = lax.psum(local_sq, "blk")
    mean_sq = total / (2.0 * adapters * rank_position * width)
    factor = jnp.minimum(1.0, 1.0 / jnp.sqrt(mean_sq + EPS))
    grad_a = (factor * proj_a).astype(jnp.bfloat16)[None]
    grad_b = (factor * proj_b).astype(jnp.bfloat16)[None]
    return (input_grad, grad_a, grad_b)


def solution(mesh):
    in_specs = (
        P(("groups", "blk"), None),
        P(("groups", "blk"), None),
        P(("groups", "blk"), None),
        P("groups"),
        P(("groups", "blk"), None, None),
        P(("groups", "blk"), None, None),
    )
    out_specs = (
        P(("groups", "blk"), None),
        P(("groups", "blk"), None, None),
        P(("groups", "blk"), None, None),
    )
    return jax.shard_map(
        per_device, mesh=mesh, in_specs=in_specs, out_specs=out_specs, check_vma=False
    )
```

profile of v0, /device:TPU:16, one launch (start us, length us, event | category | flops | bytes accessed | tf_op | source)
XLA Modules:
  0.0 342.5 jit_solution(16604896405414872012)
XLA Ops:
  0.6 0.0 copy-start
  0.6 1.0 convert_reduce_fusion.4
  1.6 0.8 select_reduce_fusion
  2.4 0.1 fusion.7
  2.5 0.7 all_to_all.20
  3.2 6.2 %all-to-all-start.3 = ((bf16[16,1,16]{2,1,0:T(2,128)(2,1)}), bf16[16,1,16]{2,1,0:T(2,128)(2,1)S(1)}, u32[]{:S(2)}, u32[]{:S(2)}) async-start(bf16[16,1,16]{2,1,0:T(2,128)(2,1)} %all_to_all.20), calls=%async_computation.3 | async-start | bytes 16384 | tf_op jit(solution)/shard_map/all_to_all | solution.py:60
  9.4 0.0 copy-done
  9.4 3.2 convolution_convert_fusion
  12.6 0.8 all-to-all-done.3
  13.4 6.7 %all-to-all-start.2 = ((bf16[16,16,8192]{2,1,0:T(8,128)(2,1)}), bf16[16,16,8192]{2,1,0:T(8,128)(2,1)}, u32[]{:S(2)}, u32[]{:S(2)}) async-start(bf16[16,16,8192]{2,1,0:T(8,128)(2,1)} %bitcast.53), calls=%async_computation.2 | async-start | bytes 8388608 | tf_op jit(solution)/shard_map/all_to_all | solution.py:59
  20.1 4.8 %convolution_convert_fusion.2 = bf16[256,8192]{1,0:T(8,128)(2,1)} fusion(bf16[128,8192]{1,0:T(8,128)(2,1)} %param.7, s32[128]{0:T(128)S(1)} %multiply_add_fusion), kind=kOutput, calls=%fused_computation.2 | convolution fusion | flops 539000832 | bytes 6291968 | tf_op jit(solution)/shard_map/dot_general | solution.py:49
  24.9 87.9 %all-to-all-done.2 = bf16[16,16,8192]{2,1,0:T(8,128)(2,1)} async-done(((bf16[16,16,8192]{2,1,0:T(8,128)(2,1)}), bf16[16,16,8192]{2,1,0:T(8,128)(2,1)}, u32[]{:S(2)}, u32[]{:S(2)}) %all-to-all-start.2) | async-done | bytes 4194336 | tf_op jit(solution)/shard_map/all_to_all | solution.py:59
  112.8 0.0 copy-start.2
  112.8 4.8 %all-to-all-start = ((bf16[16,16,8192]{2,1,0:T(8,128)(2,1)}), bf16[16,16,8192]{2,1,0:T(8,128)(2,1)}, u32[]{:S(2)}, u32[]{:S(2)}) async-start(bf16[16,16,8192]{2,1,0:T(8,128)(2,1)} %bitcast.52), calls=%async_computation | async-start | bytes 8388608 | tf_op jit(solution)/shard_map/all_to_all | solution.py:64
  117.6 0.6 convert_reduce_fusion.5
  118.3 0.0 copy-done.2
  118.3 3.7 %convert_reduce_fusion.2 = (f32[64]{0:T(128)S(1)}, bf16[256,64]{0,1:T(8,128)(2,1)S(1)}) fusion(bf16[256,8192]{1,0:T(8,128)(2,1)} %bitcast.8, bf16[1,64,8192]{2,1,0:T(8,128)(2,1)S(1)} %copy-done.2), kind=kOutput, calls=%fused_computation.28 | convolution fusion | flops 268484544 | bytes 5275904 | tf_op jit(solution)/shard_map/dot_general | solution.py:20
  121.9 88.4 %all-to-all-done = bf16[16,16,8192]{2,1,0:T(8,128)(2,1)} async-done(((bf16[16,16,8192]{2,1,0:T(8,128)(2,1)}), bf16[16,16,8192]{2,1,0:T(8,128)(2,1)}, u32[]{:S(2)}, u32[]{:S(2)}) %all-to-all-start) | async-done | bytes 4194336 | tf_op jit(solution)/shard_map/all_to_all | solution.py:64
  210.3 4.0 %convert_reduce_fusion.3 = (f32[64]{0:T(128)S(1)}, bf16[256,64]{0,1:T(8,128)(2,1)S(1)}) fusion(bf16[256,8192]{1,0:T(8,128)(2,1)} %bitcast.2, bf16[1,64,8192]{2,1,0:T(8,128)(2,1)} %param.11), kind=kOutput, calls=%fused_computation.29 | convolution fusion | flops 268500928 | bytes 5275904 | tf_op jit(solution)/shard_map/dot_general | solution.py:69
  214.3 3.3 convolution_convert_fusion.1
  217.6 4.7 %all-to-all-start.1 = ((bf16[16,16,8192]{2,1,0:T(8,128)(2,1)}), bf16[16,16,8192]{2,1,0:T(8,128)(2,1)}, u32[]{:S(2)}, u32[]{:S(2)}) async-start(bf16[16,16,8192]{2,1,0:T(8,128)(2,1)} %bitcast.51), calls=%async_computation.1 | async-start | bytes 8388608 | tf_op jit(solution)/shard_map/all_to_all | solution.py:74
  222.3 2.9 convert_reduce_fusion
  225.2 1.3 multiply_reduce_fusion.4
  227.1 2.9 convert_reduce_fusion.1
  229.9 1.3 multiply_reduce_fusion.2
  231.9 1.3 multiply_reduce_fusion.5
  234.4 3.0 convolution_multiply_fusion
  237.4 1.1 fusion.12
  238.5 3.0 fusion.16
  241.6 1.1 fusion.14
  242.7 1.9 convolution_bitcast_fusion
  244.6 1.9 convolution_bitcast_fusion.1
  246.5 2.6 multiply_reduce_fusion
  249.0 2.5 multiply_reduce_fusion.1
  252.9 80.7 %psum.7 = f32[]{:T(128)} all-reduce(f32[]{:T(128)S(6)} %add.32), channel_id=1, replica_groups=mesh['groups'=2,'blk'=16] {'blk'}, use_global_device_ids=true, to_apply=%region_14.15 | all-reduce | flops 1 | bytes 8 | tf_op jit(solution)/shard_map/psum | solution.py:90
  334.2 0.0 copy-start.1
  334.3 2.8 fusion.2
  337.1 0.0 copy-done.1
  337.1 1.1 fusion.1
  338.2 0.0 all-to-all-done.1
  338.2 4.3 %convolution_convert_fusion.3 = bf16[128,8192]{1,0:T(8,128)(2,1)} fusion(bf16[256,8192]{1,0:T(8,128)(2,1)} %bitcast.6, s32[128]{0:T(128)S(1)} %multiply_add_fusion), kind=kOutput, calls=%fused_computation.3 | convolution fusion | flops 537952256 | bytes 6291968 | tf_op jit(solution)/shard_map/dot_general | solution.py:77
  (1 shorter events, 0.0 us)
Async XLA Ops:
  0.6 8.8 %copy-start = (bf16[128,8192]{1,0:T(8,128)(2,1)S(1)}, bf16[128,8192]{1,0:T(8,128)(2,1)}, u32[]{:S(2)}) copy-start(bf16[128,8192]{1,0:T(8,128)(2,1)} %param.6) | copy-start | bytes 6291460
  3.2 10.2 %all-to-all-start.3 = ((bf16[16,1,16]{2,1,0:T(2,128)(2,1)}), bf16[16,1,16]{2,1,0:T(2,128)(2,1)S(1)}, u32[]{:S(2)}, u32[]{:S(2)}) async-start(bf16[16,1,16]{2,1,0:T(2,128)(2,1)} %all_to_all.20), calls=%async_computation.3 | async-start | bytes 16384 | tf_op jit(solution)/shard_map/all_to_all | solution.py:60
  13.4 99.4 %all-to-all-start.2 = ((bf16[16,16,8192]{2,1,0:T(8,128)(2,1)}), bf16[16,16,8192]{2,1,0:T(8,128)(2,1)}, u32[]{:S(2)}, u32[]{:S(2)}) async-start(bf16[16,16,8192]{2,1,0:T(8,128)(2,1)} %bitcast.53), calls=%async_computation.2 | async-start | bytes 8388608 | tf_op jit(solution)/shard_map/all_to_all | solution.py:59
  112.8 5.4 %copy-start.2 = (bf16[1,64,8192]{2,1,0:T(8,128)(2,1)S(1)}, bf16[1,64,8192]{2,1,0:T(8,128)(2,1)}, u32[]{:S(2)}) copy-start(bf16[1,64,8192]{2,1,0:T(8,128)(2,1)} %param.10) | copy-start | bytes 3145732
  112.8 97.5 %all-to-all-start = ((bf16[16,16,8192]{2,1,0:T(8,128)(2,1)}), bf16[16,16,8192]{2,1,0:T(8,128)(2,1)}, u32[]{:S(2)}, u32[]{:S(2)}) async-start(bf16[16,16,8192]{2,1,0:T(8,128)(2,1)} %bitcast.52), calls=%async_computation | async-start | bytes 8388608 | tf_op jit(solution)/shard_map/all_to_all | solution.py:64
  217.6 120.6 %all-to-all-start.1 = ((bf16[16,16,8192]{2,1,0:T(8,128)(2,1)}), bf16[16,16,8192]{2,1,0:T(8,128)(2,1)}, u32[]{:S(2)}, u32[]{:S(2)}) async-start(bf16[16,16,8192]{2,1,0:T(8,128)(2,1)} %bitcast.51), calls=%async_computation.1 | async-start | bytes 8388608 | tf_op jit(solution)/shard_map/all_to_all | solution.py:74
  334.2 2.8 copy-start.1
where the time goes:
time: 343 us; the launch traced here: 342 us
  waiting for transfers between devices  177 us (52%)
  blocking collectives  80.7 us (24%)
  matrix products  35.3 us (10%)
  starting transfers between devices  22.4 us (7%)
  other arithmetic  21 us (6%)
  between operations  5.3 us (2%)
    all_to_all x1, waiting for transfers between devices, per_device(): lax.all_to_all(send_dy, 'blk', split_axis=0, concat_axis=0, tiled=True)  88.4 us
    all_to_all x1, waiting for transfers between devices, per_device(): lax.all_to_all(send_x, 'blk', split_axis=0, concat_axis=0, tiled=True)  87.9 us
    psum x1, blocking collectives, per_device(): total = lax.psum(local_sq, 'blk')  80.7 us
  transfers between devices with their start and end apart: 4, of which 3 were waited for; matrix products, arithmetic and copies ran while one was open for 13% of the time, Pallas kernels for 0%

commit v1 on v0

v1 whole, which is shorter than its diff:
```python
import jax
import jax.numpy as jnp
from jax import lax
from jax.experimental import pallas as pl
from jax.experimental.pallas import tpu as pltpu
from jax.sharding import PartitionSpec as P

SCALE = 2.0
DAMPING = 1.0
EPS = 1e-06
VMEM_LIMIT = 48 * 1024 * 1024
LAST = (((1,), (1,)), ((), ()))
FIRST = (((0,), (0,)), ((), ()))


def total_over_blk(value):
    size = lax.axis_size("blk")
    if size & (size - 1):
        return lax.psum(value, "blk")
    step = 1
    while step < size:
        value = value + lax.ppermute(value, "blk", [(i, i ^ step) for i in range(size)])
        step *= 2
    return value


def rows_kernel(scale, rows_ref, weight_ref, low_ref, gram_ref, low_total):
    step = pl.program_id(0)

    @pl.when(step == 0)
    def _():
        low_total[...] = jnp.zeros_like(low_total)
        gram_ref[...] = jnp.zeros_like(gram_ref)

    rows = rows_ref[...]
    low_total[...] += lax.dot_general(rows, weight_ref[...], LAST, preferred_element_type=jnp.float32)
    gram_ref[...] += lax.dot_general(rows, rows, LAST, preferred_element_type=jnp.float32)

    @pl.when(step == pl.num_programs(0) - 1)
    def _():
        low_ref[...] = (scale * low_total[...]).astype(low_ref.dtype)


def rows_products(rows, weight, scale):
    slots, width = rows.shape
    rank = weight.shape[0]
    chunk = min(width, 2048)
    return pl.pallas_call(
        lambda *refs: rows_kernel(scale, *refs),
        grid=(width // chunk,),
        in_specs=[
            pl.BlockSpec((slots, chunk), lambda i: (0, i)),
            pl.BlockSpec((rank, chunk), lambda i: (0, i)),
        ],
        out_specs=[
            pl.BlockSpec((slots, rank), lambda i: (0, 0)),
            pl.BlockSpec((slots, slots), lambda i: (0, 0)),
        ],
        out_shape=[
            jax.ShapeDtypeStruct((slots, rank), jnp.bfloat16),
            jax.ShapeDtypeStruct((slots, slots), jnp.float32),
        ],
        scratch_shapes=[pltpu.VMEM((slots, rank), jnp.float32)],
        compiler_params=pltpu.CompilerParams(vmem_limit_bytes=VMEM_LIMIT),
        cost_estimate=pl.CostEstimate(
            flops=2 * slots * width * (slots + rank),
            bytes_accessed=2 * width * (slots + rank),
            transcendentals=0,
        ),
    )(rows, weight)


def fold_one(low, gram, scale, amount):
    high = lax.Precision.HIGHEST
    low = low.astype(jnp.float32)
    slots = low.shape[0]
    left = jnp.sum(low, axis=0, keepdims=True) / amount
    raw = scale * low
    along = jnp.sum(raw * left, axis=1, keepdims=True)
    inner = raw - along * left / (DAMPING + jnp.sum(left * left))
    cross = jnp.sum(gram, axis=1, keepdims=True) / amount
    right_sq = jnp.sum(cross) / amount
    side = jnp.sum(inner * cross, axis=0, keepdims=True)
    factor = inner - side / (amount * (DAMPING + right_sq))
    spread = jnp.dot(gram, factor, precision=high, preferred_element_type=jnp.float32)
    return factor, jnp.sum(spread * factor)


def split3(value):
    first = value.astype(jnp.bfloat16)
    rest = value - first.astype(jnp.float32)
    second = rest.astype(jnp.bfloat16)
    third = (rest - second.astype(jnp.float32)).astype(jnp.bfloat16)
    return first, second, third


def fold_kernel(amount_ref, gh_ref, gram_x_ref, hidden_ref, gram_dy_ref, left_a_ref, left_b_ref, sq_ref):
    amount = amount_ref[0, 0]
    rank = gh_ref.shape[1]
    factor_a, sq_a = fold_one(gh_ref[...], gram_x_ref[...], 1.0, amount)
    factor_b, sq_b = fold_one(hidden_ref[...], gram_dy_ref[...], SCALE, amount)
    for out_ref, factor in ((left_a_ref, factor_a), (left_b_ref, factor_b)):
        for at, part in enumerate(split3(factor)):
            out_ref[:, at * rank : (at + 1) * rank] = part
    sq_ref[...] = jnp.zeros_like(sq_ref) + (sq_a + sq_b)


def fold(amount, grad_hidden, gram_x, hidden, gram_dy):
    slots, rank = hidden.shape
    whole = lambda shape: pl.BlockSpec(shape, lambda: (0, 0))
    return pl.pallas_call(
        fold_kernel,
        in_specs=[pl.BlockSpec(memory_space=pltpu.SMEM)]
        + [whole((slots, rank)), whole((slots, slots))] * 2,
        out_specs=[whole((slots, 3 * rank))] * 2 + [whole((8, 128))],
        out_shape=[jax.ShapeDtypeStruct((slots, 3 * rank), jnp.bfloat16)] * 2
        + [jax.ShapeDtypeStruct((8, 128), jnp.float32)],
        compiler_params=pltpu.CompilerParams(vmem_limit_bytes=VMEM_LIMIT),
        cost_estimate=pl.CostEstimate(
            flops=24 * slots * slots * rank, bytes_accessed=12 * slots * slots, transcendentals=0
        ),
    )(amount, grad_hidden, gram_x, hidden, gram_dy)


def grads_kernel(factor_ref, left_a_ref, left_b_ref, rows_x_ref, rows_dy_ref, grad_a_ref, grad_b_ref):
    factor = factor_ref[0, 0]
    rank = grad_a_ref.shape[0]
    for left_ref, rows_ref, out_ref in (
        (left_a_ref, rows_x_ref, grad_a_ref),
        (left_b_ref, rows_dy_ref, grad_b_ref),
    ):
        parts = lax.dot_general(left_ref[...], rows_ref[...], FIRST, preferred_element_type=jnp.float32)
        proj = (parts[2 * rank :] + parts[rank : 2 * rank]) + parts[:rank]
        out_ref[...] = (factor * proj).astype(out_ref.dtype)


def grads(factor, left_a, left_b, rows_x, rows_dy):
    slots, width = rows_x.shape
    rank = left_a.shape[1] // 3
    chunk = min(width, 2048)
    left_spec = pl.BlockSpec((slots, 3 * rank), lambda i: (0, 0))
    rows_spec = pl.BlockSpec((slots, chunk), lambda i: (0, i))
    out_spec = pl.BlockSpec((rank, chunk), lambda i: (0, i))
    return pl.pallas_call(
        grads_kernel,
        grid=(width // chunk,),
        in_specs=[pl.BlockSpec(memory_space=pltpu.SMEM), left_spec, left_spec, rows_spec, rows_spec],
        out_specs=[out_spec, out_spec],
        out_shape=[jax.ShapeDtypeStruct((rank, width), jnp.bfloat16)] * 2,
        compiler_params=pltpu.CompilerParams(vmem_limit_bytes=VMEM_LIMIT),
        cost_estimate=pl.CostEstimate(
            flops=12 * slots * width * rank, bytes_accessed=4 * width * (slots + rank), transcendentals=0
        ),
    )(factor, left_a, left_b, rows_x, rows_dy)


def per_device(tokens, cotangent, tenant, owner, down_factor_table, up_factor_table):
    rows, width = tokens.shape
    count_blk = lax.axis_size("blk")
    adapters = owner.shape[0]
    rank = down_factor_table.shape[1]
    cap = 2 * rows // adapters
    slots = count_blk * cap
    down_weight = down_factor_table[0]
    up_weight = up_factor_table[0]

    with jax.named_scope("targets"):
        tenant_ids = tenant[:, 0]
        match = tenant_ids[:, None] == jnp.arange(adapters, dtype=jnp.int32)[None, :]
        target_dev = jnp.sum(jnp.where(match, owner[None, :], 0), axis=1)
        row_ids = jnp.arange(rows, dtype=jnp.int32)
        same_before = (tenant_ids[:, None] == tenant_ids[None, :]) & (row_ids[None, :] < row_ids[:, None])
        position = jnp.sum(same_before.astype(jnp.int32), axis=1)
        target = target_dev * cap + position
        placing = (jnp.arange(slots, dtype=jnp.int32)[:, None] == target[None, :]).astype(jnp.bfloat16)

    def exchange(value):
        value = value.reshape(count_blk, cap, width)
        return lax.all_to_all(value, "blk", split_axis=0, concat_axis=0, tiled=True).reshape(slots, width)

    def place(value):
        return jnp.dot(placing, value, preferred_element_type=jnp.float32).astype(jnp.bfloat16)

    with jax.named_scope("send_cotangent"):
        rows_dy = exchange(place(cotangent))
    with jax.named_scope("send_tokens"):
        rows_x = exchange(place(tokens))
    with jax.named_scope("row_counts"):
        devices = jnp.arange(count_blk, dtype=jnp.int32)
        sent = jnp.sum((target_dev[:, None] == devices[None, :]).astype(jnp.float32), axis=0, keepdims=True)
        counts = total_over_blk(sent)
        amount = jnp.sum(jnp.where(devices == lax.axis_index("blk"), counts[0], 0.0)).reshape(1, 1)
    with jax.named_scope("grad_hidden"):
        grad_hidden, gram_dy = rows_products(rows_dy, up_weight, SCALE)
    with jax.named_scope("back"):
        back = jnp.dot(grad_hidden, down_weight, preferred_element_type=jnp.float32).astype(jnp.bfloat16)
        returned = exchange(back)
    with jax.named_scope("hidden"):
        hidden, gram_x = rows_products(rows_x, down_weight, 1.0)
    with jax.named_scope("fold"):
        left_a, left_b, local_sq = fold(amount, grad_hidden, gram_x, hidden, gram_dy)
    with jax.named_scope("clip"):
        total = total_over_blk(local_sq[:1, :1])
        mean_sq = total / (2.0 * adapters * rank * width)
        factor = jnp.minimum(1.0, 1.0 / jnp.sqrt(mean_sq + EPS))
    with jax.named_scope("grads"):
        grad_a, grad_b = grads(factor, left_a, left_b, rows_x, rows_dy)
    with jax.named_scope("input_grad"):
        input_grad = lax.dot_general(placing, returned, FIRST, preferred_element_type=jnp.float32).astype(
            jnp.bfloat16
        )
    return (input_grad, grad_a[None], grad_b[None])


def solution(mesh):
    split = ("groups", "blk")
    in_specs = (P(split, None), P(split, None), P(split, None), P("groups"), P(split, None, None), P(split, None, None))
    out_specs = (P(split, None), P(split, None, None), P(split, None, None))
    return jax.shard_map(per_device, mesh=mesh, in_specs=in_specs, out_specs=out_specs, check_vma=False)
```

time: 343 us -> 338 us (0.985); the launches traced: 342 us -> 333 us
  blocking collectives: 80.7 us -> 0 us
  waiting for transfers between devices: 177 us -> 256 us
  matrix products: 35.3 us -> 15.4 us
  other arithmetic: 21 us -> 2.48 us
  Pallas kernels: 0 us -> 17.9 us
  starting transfers between devices: 22.4 us -> 35.4 us
    ppermute x0 -> x8, waiting for transfers between devices: none -> 84.6 us  [total_over_blk(): lax.ppermute(value, 'blk', [(i, i ^ step) for i in range(size)])]
    psum x1 -> x0, blocking collectives: 80.7 us -> none  [per_device(): total = lax.psum(local_sq, 'blk')]
    ppermute x0 -> x8, starting transfers between devices: none -> 19.9 us  [total_over_blk(): lax.ppermute(value, 'blk', [(i, i ^ step) for i in range(size)])]
    dot_general x11 -> x3, matrix products: 32 us -> 12.2 us  [the longest x2 7.97 us: place(): jnp.dot(placing, value, preferred_element_type=jnp.float32)]
    pallas_call x0 -> x4, Pallas kernels: none -> 17.9 us  [the longest x2 9.43 us: rows_products(): pl.pallas_call(lambda *refs: rows_kernel(scale, *refs), grid=(width // ch...]
    reduce_sum x9 -> x2, other arithmetic: 15.4 us -> 0.71 us  [the longest x1 0.6 us: per_device(): jnp.sum(jnp.where(devices == lax.axis_index('blk'), counts[0], 0.0))]
    all_to_all x4 -> x3, starting transfers between devices: 22.4 us -> 15.5 us  [exchange(): lax.all_to_all(value, 'blk', split_axis=0, concat_axis=0, tiled=True)]
    all_to_all x4 -> x3, waiting for transfers between devices: 177 us -> 171 us  [exchange(): lax.all_to_all(value, 'blk', split_axis=0, concat_axis=0, tiled=True)]
  transfers between devices with their start and end apart: 4 -> 11, of which waited for: 3 -> 10; matrix products, arithmetic and copies ran while one was open for 13% -> 3% of each run, Pallas kernels for 0% -> 5%
where the time goes in v1:
time: 338 us; the launch traced here: 333 us
  waiting for transfers between devices  256 us (76%)
  starting transfers between devices  35.4 us (10%)
  Pallas kernels  17.9 us (5%)
  matrix products  15.4 us (5%)
  between operations  3.91 us (1%)
    all_to_all x3, waiting for transfers between devices, exchange(): lax.all_to_all(value, 'blk', split_axis=0, concat_axis=0, tiled=True)  171 us
    ppermute x8, waiting for transfers between devices, total_over_blk(): lax.ppermute(value, 'blk', [(i, i ^ step) for i in range(size)])  84.6 us
    ppermute x8, starting transfers between devices, total_over_blk(): lax.ppermute(value, 'blk', [(i, i ^ step) for i in range(size)])  19.9 us
    all_to_all x3, starting transfers between devices, exchange(): lax.all_to_all(value, 'blk', split_axis=0, concat_axis=0, tiled=True)  15.5 us
    pallas_call x2, Pallas kernels, rows_products(): pl.pallas_call(lambda *refs: rows_kernel(scale, *refs), grid=(width // ch...  9.43 us
    dot_general x2, matrix products, place(): jnp.dot(placing, value, preferred_element_type=jnp.float32)  7.97 us
  transfers between devices with their start and end apart: 11, of which 10 were waited for; matrix products, arithmetic and copies ran while one was open for 3% of the time, Pallas kernels for 5%

profile of v1, /device:TPU:16, one launch (start us, length us, event | category | flops | bytes accessed | tf_op | source)
XLA Modules:
  0.0 333.0 jit_solution(4523012395392180856)
XLA Ops:
  0.6 0.0 copy-start
  0.6 1.0 convert_reduce_fusion
  1.6 0.8 select_reduce_fusion
  2.4 0.0 copy-done
  2.4 3.2 convolution_convert_fusion.2
  5.6 6.2 %all-to-all-start = ((bf16[16,16,8192]{2,1,0:T(8,128)(2,1)}), bf16[16,16,8192]{2,1,0:T(8,128)(2,1)}, u32[]{:S(2)}, u32[]{:S(2)}) async-start(bf16[16,16,8192]{2,1,0:T(8,128)(2,1)} %bitcast.26), calls=%async_computation | async-start | bytes 8388608 | tf_op jit(solution)/shard_map/send_cotangent/all_to_all | solution.py:179
  11.8 4.8 %convolution_convert_fusion = bf16[256,8192]{1,0:T(8,128)(2,1)} fusion(bf16[128,8192]{1,0:T(8,128)(2,1)} %param.6, s32[128]{0:T(128)S(1)} %multiply_add_fusion), kind=kOutput, calls=%fused_computation | convolution fusion | flops 539000832 | bytes 6291968 | tf_op jit(solution)/shard_map/send_tokens/dot_general | solution.py:182
  16.6 87.9 %all-to-all-done = bf16[16,16,8192]{2,1,0:T(8,128)(2,1)} async-done(((bf16[16,16,8192]{2,1,0:T(8,128)(2,1)}), bf16[16,16,8192]{2,1,0:T(8,128)(2,1)}, u32[]{:S(2)}, u32[]{:S(2)}) %all-to-all-start) | async-done | bytes 4194336 | tf_op jit(solution)/shard_map/send_cotangent/all_to_all | solution.py:179
  104.5 4.7 %all-to-all-start.2 = ((bf16[16,16,8192]{2,1,0:T(8,128)(2,1)}), bf16[16,16,8192]{2,1,0:T(8,128)(2,1)}, u32[]{:S(2)}, u32[]{:S(2)}) async-start(bf16[16,16,8192]{2,1,0:T(8,128)(2,1)} %bitcast.25), calls=%async_computation.2 | async-start | bytes 8388608 | tf_op jit(solution)/shard_map/send_tokens/all_to_all | solution.py:179
  109.2 0.0 copy-start.1
  109.2 0.0 copy-start.2
  109.2 1.3 copy-done.2
  110.5 4.7 %grad_hidden.1 = (bf16[256,64]{1,0:T(8,128)(2,1)S(1)}, f32[256,256]{1,0:T(8,128)S(1)}) custom-call(bf16[256,8192]{1,0:T(8,128)(2,1)} %bitcast.2.refs_0_.rows_dy_ref, bf16[64,8192]{1,0:T(8,128)(2,1)S(1)} %bitcast.23), custom_call_target="tpu_custom_call" | custom-call | flops 1342177280 | bytes 5242880 | tf_op jit(solution)/shard_map/grad_hidden/pallas_call | solution.py:48
  115.2 0.0 copy-done.1
  115.2 3.2 convolution_convert_fusion.1
  118.5 83.4 %all-to-all-done.2 = bf16[16,16,8192]{2,1,0:T(8,128)(2,1)} async-done(((bf16[16,16,8192]{2,1,0:T(8,128)(2,1)}), bf16[16,16,8192]{2,1,0:T(8,128)(2,1)}, u32[]{:S(2)}, u32[]{:S(2)}) %all-to-all-start.2) | async-done | bytes 4194336 | tf_op jit(solution)/shard_map/send_tokens/all_to_all | solution.py:179
  201.9 4.7 %all-to-all-start.1 = ((bf16[16,16,8192]{2,1,0:T(8,128)(2,1)}), bf16[16,16,8192]{2,1,0:T(8,128)(2,1)}, u32[]{:S(2)}, u32[]{:S(2)}) async-start(bf16[16,16,8192]{2,1,0:T(8,128)(2,1)} %bitcast.24), calls=%async_computation.1 | async-start | bytes 8388608 | tf_op jit(solution)/shard_map/back/all_to_all | solution.py:179
  206.6 0.1 convert_reduce_fusion.1
  206.7 0.2 collective-permute-start
  206.9 1.0 collective-permute-done
  207.9 1.5 collective-permute-start.1
  209.3 16.7 %collective-permute-done.1 = f32[1,16]{1,0:T(1,128)S(1)} collective-permute-done((f32[1,16]{1,0:T(1,128)S(1)}, f32[1,16]{1,0:T(1,128)S(1)}, u32[]{:S(2)}, u32[]{:S(2)}) %collective-permute-start.1) | collective-permute-done | bytes 96 | tf_op jit(solution)/shard_map/row_counts/ppermute | solution.py:22
  226.1 7.4 %collective-permute-start.2 = (f32[1,16]{1,0:T(1,128)S(1)}, f32[1,16]{1,0:T(1,128)S(1)}, u32[]{:S(2)}, u32[]{:S(2)}) collective-permute-start(f32[1,16]{1,0:T(1,128)S(1)} %add.36), channel_id=1, source_target_pairs={{0,4},{1,5},{2,6},{3,7},{4,0},{5,1},{6,2},{7,3},{8,12},{9,13},{10,... | collective-permute-start | bytes 200 | tf_op jit(solution)/shard_map/row_counts/ppermute | solution.py:22
  233.4 43.4 %collective-permute-done.2 = f32[1,16]{1,0:T(1,128)S(1)} collective-permute-done((f32[1,16]{1,0:T(1,128)S(1)}, f32[1,16]{1,0:T(1,128)S(1)}, u32[]{:S(2)}, u32[]{:S(2)}) %collective-permute-start.2) | collective-permute-done | bytes 96 | tf_op jit(solution)/shard_map/row_counts/ppermute | solution.py:22
  276.8 0.0 collective-permute-start.3
  276.8 20.6 %collective-permute-done.3 = f32[1,16]{1,0:T(1,128)S(1)} collective-permute-done((f32[1,16]{1,0:T(1,128)S(1)}, f32[1,16]{1,0:T(1,128)S(1)}, u32[]{:S(2)}, u32[]{:S(2)}) %collective-permute-start.3) | collective-permute-done | bytes 96 | tf_op jit(solution)/shard_map/row_counts/ppermute | solution.py:22
  297.5 0.6 fusion.4
  298.1 4.7 %hidden.1 = (bf16[256,64]{1,0:T(8,128)(2,1)S(1)}, f32[256,256]{1,0:T(8,128)S(1)}) custom-call(bf16[256,8192]{1,0:T(8,128)(2,1)} %bitcast.11.refs_0_.rows_x_ref, bf16[64,8192]{1,0:T(8,128)(2,1)S(1)} %bitcast.22), custom_call_target="tpu_custom_call" | custom-call | flops 1342177280 | bytes 5242880 | tf_op jit(solution)/shard_map/hidden/pallas_call | solution.py:48
  302.8 2.4 fold.1
  305.2 0.5 slice.3
  305.7 0.0 collective-permute-start.4
  305.7 1.4 collective-permute-done.4
  308.3 2.8 collective-permute-start.5
  311.2 0.9 collective-permute-done.5
  312.7 3.7 %collective-permute-start.6 = (f32[1,1]{1,0:T(1,128)}, f32[1,1]{1,0:T(1,128)}, u32[]{:S(2)}, u32[]{:S(2)}) collective-permute-start(f32[1,1]{1,0:T(1,128)} %add.40), channel_id=1, source_target_pairs={{0,4},{1,5},{2,6},{3,7},{4,0},{5,1},{6,2},{7,3},{8,12},{9,13},{10,... | collective-permute-start | bytes 20 | tf_op jit(solution)/shard_map/clip/ppermute | solution.py:22
  316.3 0.3 collective-permute-done.6
  317.3 4.3 %collective-permute-start.7 = (f32[1,1]{1,0:T(1,128)}, f32[1,1]{1,0:T(1,128)}, u32[]{:S(2)}, u32[]{:S(2)}) collective-permute-start(f32[1,1]{1,0:T(1,128)} %add.41), channel_id=1, source_target_pairs={{0,8},{1,9},{2,10},{3,11},{4,12},{5,13},{6,14},{7,15},{8,0},{9,1},... | collective-permute-start | bytes 20 | tf_op jit(solution)/shard_map/clip/ppermute | solution.py:22
  321.6 0.3 collective-permute-done.7
  322.6 6.0 %grads.1 = (bf16[64,8192]{1,0:T(8,128)(2,1)}, bf16[64,8192]{1,0:T(8,128)(2,1)}) custom-call(f32[1,1]{1,0:T(1,128)S(6)} %min.3.factor_ref, bf16[256,192]{1,0:T(8,128)(2,1)S(1)} %get-tuple-element.17.left_a_ref, bf16[256,192]{1,0:T(8,128)(2,1)S(1)} %get-tuple-element.18.left_b_ref, bf16[256,8192]{1,0:T(8,128)(2,1)} %bitcast.11.refs_0_.rows_x_ref, ...), custom_call_target="tpu_custom_call" | custom-call | flops 1610612736 | bytes 10485760 | tf_op jit(solution)/shard_map/grads/pallas_call | solution.py:144
  328.7 0.0 all-to-all-done.1
  328.7 4.3 %convolution_convert_fusion.3 = bf16[128,8192]{1,0:T(8,128)(2,1)} fusion(bf16[256,8192]{1,0:T(8,128)(2,1)} %bitcast.6, s32[128]{0:T(128)S(1)} %multiply_add_fusion), kind=kOutput, calls=%fused_computation.3 | convolution fusion | flops 537952256 | bytes 6291968 | tf_op jit(solution)/shard_map/input_grad/dot_general | solution.py:209
  (4 shorter events, 0.0 us)
Async XLA Ops:
  0.6 1.8 copy-start
  5.6 98.9 %all-to-all-start = ((bf16[16,16,8192]{2,1,0:T(8,128)(2,1)}), bf16[16,16,8192]{2,1,0:T(8,128)(2,1)}, u32[]{:S(2)}, u32[]{:S(2)}) async-start(bf16[16,16,8192]{2,1,0:T(8,128)(2,1)} %bitcast.26), calls=%async_computation | async-start | bytes 8388608 | tf_op jit(solution)/shard_map/send_cotangent/all_to_all | solution.py:179
  104.5 97.4 %all-to-all-start.2 = ((bf16[16,16,8192]{2,1,0:T(8,128)(2,1)}), bf16[16,16,8192]{2,1,0:T(8,128)(2,1)}, u32[]{:S(2)}, u32[]{:S(2)}) async-start(bf16[16,16,8192]{2,1,0:T(8,128)(2,1)} %bitcast.25), calls=%async_computation.2 | async-start | bytes 8388608 | tf_op jit(solution)/shard_map/send_tokens/all_to_all | solution.py:179
  109.2 6.0 %copy-start.1 = (bf16[1,64,8192]{2,1,0:T(8,128)(2,1)S(1)}, bf16[1,64,8192]{2,1,0:T(8,128)(2,1)}, u32[]{:S(2)}) copy-start(bf16[1,64,8192]{2,1,0:T(8,128)(2,1)} %param.10) | copy-start | bytes 3145732
  109.2 1.3 copy-start.2
  201.9 126.8 %all-to-all-start.1 = ((bf16[16,16,8192]{2,1,0:T(8,128)(2,1)}), bf16[16,16,8192]{2,1,0:T(8,128)(2,1)}, u32[]{:S(2)}, u32[]{:S(2)}) async-start(bf16[16,16,8192]{2,1,0:T(8,128)(2,1)} %bitcast.24), calls=%async_computation.1 | async-start | bytes 8388608 | tf_op jit(solution)/shard_map/back/all_to_all | solution.py:179
  206.7 1.2 collective-permute-start
  207.9 18.2 %collective-permute-start.1 = (f32[1,16]{1,0:T(1,128)S(1)}, f32[1,16]{1,0:T(1,128)S(1)}, u32[]{:S(2)}, u32[]{:S(2)}) collective-permute-start(f32[1,16]{1,0:T(1,128)S(1)} %bitcast_add_fusion), channel_id=1, source_target_pairs={{0,2},{1,3},{2,0},{3,1},{4,6},{5,7},{6,4},{7,5},{8,10},{9,11},{10,... | collective-permute-start | bytes 200 | tf_op jit(solution)/shard_map/row_counts/ppermute | solution.py:22
  226.1 50.7 %collective-permute-start.2 = (f32[1,16]{1,0:T(1,128)S(1)}, f32[1,16]{1,0:T(1,128)S(1)}, u32[]{:S(2)}, u32[]{:S(2)}) collective-permute-start(f32[1,16]{1,0:T(1,128)S(1)} %add.36), channel_id=1, source_target_pairs={{0,4},{1,5},{2,6},{3,7},{4,0},{5,1},{6,2},{7,3},{8,12},{9,13},{10,... | collective-permute-start | bytes 200 | tf_op jit(solution)/shard_map/row_counts/ppermute | solution.py:22
  276.8 20.6 %collective-permute-start.3 = (f32[1,16]{1,0:T(1,128)S(1)}, f32[1,16]{1,0:T(1,128)S(1)}, u32[]{:S(2)}, u32[]{:S(2)}) collective-permute-start(f32[1,16]{1,0:T(1,128)S(1)} %add.37), channel_id=1, source_target_pairs={{0,8},{1,9},{2,10},{3,11},{4,12},{5,13},{6,14},{7,15},{8,0},{9,1},... | collective-permute-start | bytes 200 | tf_op jit(solution)/shard_map/row_counts/ppermute | solution.py:22
  305.7 1.4 collective-permute-start.4
  308.3 3.7 %collective-permute-start.5 = (f32[1,1]{1,0:T(1,128)}, f32[1,1]{1,0:T(1,128)}, u32[]{:S(2)}, u32[]{:S(2)}) collective-permute-start(f32[1,1]{1,0:T(1,128)} %add.39), channel_id=1, source_target_pairs={{0,2},{1,3},{2,0},{3,1},{4,6},{5,7},{6,4},{7,5},{8,10},{9,11},{10,... | collective-permute-start | bytes 20 | tf_op jit(solution)/shard_map/clip/ppermute | solution.py:22
  312.7 4.0 %collective-permute-start.6 = (f32[1,1]{1,0:T(1,128)}, f32[1,1]{1,0:T(1,128)}, u32[]{:S(2)}, u32[]{:S(2)}) collective-permute-start(f32[1,1]{1,0:T(1,128)} %add.40), channel_id=1, source_target_pairs={{0,4},{1,5},{2,6},{3,7},{4,0},{5,1},{6,2},{7,3},{8,12},{9,13},{10,... | collective-permute-start | bytes 20 | tf_op jit(solution)/shard_map/clip/ppermute | solution.py:22
  317.3 4.7 %collective-permute-start.7 = (f32[1,1]{1,0:T(1,128)}, f32[1,1]{1,0:T(1,128)}, u32[]{:S(2)}, u32[]{:S(2)}) collective-permute-start(f32[1,1]{1,0:T(1,128)} %add.41), channel_id=1, source_target_pairs={{0,8},{1,9},{2,10},{3,11},{4,12},{5,13},{6,14},{7,15},{8,0},{9,1},... | collective-permute-start | bytes 20 | tf_op jit(solution)/shard_map/clip/ppermute | solution.py:22

commit v2 on v1

--- a/solution.py
+++ b/solution.py
@@ -9,6 +9,7 @@
 DAMPING = 1.0
 EPS = 1e-06
 VMEM_LIMIT = 48 * 1024 * 1024
+LANES = 128
 LAST = (((1,), (1,)), ((), ()))
 FIRST = (((0,), (0,)), ((), ()))
 
@@ -24,15 +25,20 @@
     return value
 
 
-def rows_kernel(scale, rows_ref, weight_ref, low_ref, gram_ref, low_total):
+def rows_kernel(scale, count, with_extra, *refs):
+    blocks, extras = refs[:count], refs[count : 2 * count if with_extra else count]
+    weight_ref, low_ref, gram_ref, *rest = refs[count + len(extras) :]
+    low_total = rest[-1]
     step = pl.program_id(0)
 
     @pl.when(step == 0)
     def _():
         low_total[...] = jnp.zeros_like(low_total)
         gram_ref[...] = jnp.zeros_like(gram_ref)
-
-    rows = rows_ref[...]
+        if with_extra:
+            rest[0][...] = jnp.concatenate([ref[...] for ref in extras], axis=0)
+
+    rows = jnp.concatenate([ref[...] for ref in blocks], axis=0)
     low_total[...] += lax.dot_general(rows, weight_ref[...], LAST, preferred_element_type=jnp.float32)
     gram_ref[...] += lax.dot_general(rows, rows, LAST, preferred_element_type=jnp.float32)
 
@@ -41,25 +47,28 @@
         low_ref[...] = (scale * low_total[...]).astype(low_ref.dtype)
 
 
-def rows_products(rows, weight, scale):
-    slots, width = rows.shape
-    rank = weight.shape[0]
+def rows_products(blocks, weight, scale, with_extra=False):
+    slots = sum(block.shape[0] for block in blocks)
+    rank, width = weight.shape
     chunk = min(width, 2048)
-    return pl.pallas_call(
-        lambda *refs: rows_kernel(scale, *refs),
+    in_specs = [pl.BlockSpec((block.shape[0], chunk), lambda i: (0, i)) for block in blocks]
+    out_specs = [pl.BlockSpec((slots, rank), lambda i: (0, 0)), pl.BlockSpec((slots, slots), lambda i: (0, 0))]
+    out_shape = [
+        jax.ShapeDtypeStruct((slots, rank), jnp.bfloat16),
+        jax.ShapeDtypeStruct((slots, slots), jnp.float32),
+    ]
+    operands = list(blocks)
+    if with_extra:
+        in_specs += [pl.BlockSpec((block.shape[0], LANES), lambda i: (0, width // LANES)) for block in blocks]
+        operands += list(blocks)
+        out_specs.append(pl.BlockSpec((slots, LANES), lambda i: (0, 0)))
+        out_shape.append(jax.ShapeDtypeStruct((slots, LANES), jnp.bfloat16))
+    return pl.pallas_call(
+        lambda *refs: rows_kernel(scale, len(blocks), with_extra, *refs),
         grid=(width // chunk,),
-        in_specs=[
-            pl.BlockSpec((slots, chunk), lambda i: (0, i)),
-            pl.BlockSpec((rank, chunk), lambda i: (0, i)),
-        ],
-        out_specs=[
-            pl.BlockSpec((slots, rank), lambda i: (0, 0)),
-            pl.BlockSpec((slots, slots), lambda i: (0, 0)),
-        ],
-        out_shape=[
-            jax.ShapeDtypeStruct((slots, rank), jnp.bfloat16),
-            jax.ShapeDtypeStruct((slots, slots), jnp.float32),
-        ],
+        in_specs=in_specs + [pl.BlockSpec((rank, chunk), lambda i: (0, i))],
+        out_specs=out_specs,
+        out_shape=out_shape,
         scratch_shapes=[pltpu.VMEM((slots, rank), jnp.float32)],
         compiler_params=pltpu.CompilerParams(vmem_limit_bytes=VMEM_LIMIT),
         cost_estimate=pl.CostEstimate(
@@ -67,7 +76,168 @@
             bytes_accessed=2 * width * (slots + rank),
             transcendentals=0,
         ),
-    )(rows, weight)
+    )(*operands, weight)
+
+
+def low_kernel(scale, count, *refs):
+    blocks, weight_ref, low_ref, total = refs[:count], *refs[count:]
+    step = pl.program_id(0)
+
+    @pl.when(step == 0)
+    def _():
+        total[...] = jnp.zeros_like(total)
+
+    rows = jnp.concatenate([ref[...] for ref in blocks], axis=0)
+    total[...] += lax.dot_general(rows, weight_ref[...], LAST, preferred_element_type=jnp.float32)
+
+    @pl.when(step == pl.num_programs(0) - 1)
+    def _():
+        low_ref[...] = (scale * total[...]).astype(low_ref.dtype)
+
+
+def low_products(blocks, weight, scale):
+    slots = sum(block.shape[0] for block in blocks)
+    rank, width = weight.shape
+    chunk = min(width, 2048)
+    return pl.pallas_call(
+        lambda *refs: low_kernel(scale, len(blocks), *refs),
+        grid=(width // chunk,),
+        in_specs=[pl.BlockSpec((block.shape[0], chunk), lambda i: (0, i)) for block in blocks]
+        + [pl.BlockSpec((rank, chunk), lambda i: (0, i))],
+        out_specs=pl.BlockSpec((slots, rank), lambda i: (0, 0)),
+        out_shape=jax.ShapeDtypeStruct((slots, rank), jnp.bfloat16),
+        scratch_shapes=[pltpu.VMEM((slots, rank), jnp.float32)],
+        compiler_params=pltpu.CompilerParams(vmem_limit_bytes=VMEM_LIMIT),
+        cost_estimate=pl.CostEstimate(
+            flops=2 * slots * width * rank, bytes_accessed=2 * width * (slots + rank), transcendentals=0
+        ),
+    )(*blocks, weight)
+
+
+def slot_targets(cap, me, owner_ref, column_ref, row_ref):
+    column, row = column_ref[...], row_ref[...]
+    rows, adapters = row.shape[1], owner_ref.shape[0]
+    adapter = lax.broadcasted_iota(jnp.int32, (adapters, rows), 0)
+    device = jnp.sum(jnp.where(adapter == row, owner_ref[...], 0), axis=0, keepdims=True)
+    earlier = lax.broadcasted_iota(jnp.int32, (rows, rows), 0) < lax.broadcasted_iota(jnp.int32, (rows, rows), 1)
+    position = jnp.sum(jnp.where((column == row) & earlier, 1, 0), axis=0, keepdims=True)
+    partner = device ^ me
+    return partner, partner * cap + position
+
+
+def place_kernel(partners, cap, with_extra, me_ref, owner_ref, column_ref, row_ref, values_ref, *refs):
+    placing = refs[-1]
+    outs = refs[1:-1] if with_extra else refs[:-1]
+    step = pl.program_id(0)
+    rows = row_ref.shape[1]
+
+    @pl.when(step == 0)
+    def _():
+        _, target = slot_targets(cap, me_ref[0, 0], owner_ref, column_ref, row_ref)
+        slot = lax.broadcasted_iota(jnp.int32, (cap, rows), 0)
+        for at, partner in enumerate(partners):
+            placing[at * cap : (at + 1) * cap, :] = jnp.where(slot + partner * cap == target, 1.0, 0.0).astype(
+                placing.dtype
+            )
+
+    placed = jnp.dot(placing[...], values_ref[...], preferred_element_type=jnp.float32).astype(jnp.bfloat16)
+    for at, out in enumerate(outs):
+        out[...] = placed[at * cap : (at + 1) * cap]
+
+    if with_extra:
+
+        @pl.when(step == pl.num_programs(0) - 1)
+        def _():
+            live = jnp.sum(placing[...].astype(jnp.float32), axis=1, keepdims=True)
+            low = refs[0][...].astype(jnp.float32)
+            extra = jnp.concatenate(
+                [low, jnp.broadcast_to(live, (live.shape[0], LANES - low.shape[1]))], axis=1
+            ).astype(jnp.bfloat16)
+            for at, out in enumerate(outs):
+                out[:, out.shape[1] - LANES :] = extra[at * cap : (at + 1) * cap]
+
+
+def place(partners, cap, me, owner, tenant, values, low=None):
+    rows, width = values.shape
+    adapters = owner.shape[0]
+    with_extra = low is not None
+    full = width + LANES if with_extra else width
+    chunk = full // 5 if with_extra and full % (5 * LANES) == 0 else 2048
+    still = lambda shape: pl.BlockSpec(shape, lambda i: (0, 0))
+    in_specs = [
+        pl.BlockSpec(memory_space=pltpu.SMEM),
+        still((adapters, 1)),
+        still((rows, 1)),
+        still((1, rows)),
+        pl.BlockSpec((rows, chunk), lambda i: (0, i)),
+    ]
+    operands = [me.reshape(1, 1), owner.reshape(adapters, 1), tenant, tenant.reshape(1, rows), values]
+    if with_extra:
+        in_specs.append(still(low.shape))
+        operands.append(low)
+    return pl.pallas_call(
+        lambda *refs: place_kernel(partners, cap, with_extra, *refs),
+        grid=(full // chunk,),
+        in_specs=in_specs,
+        out_specs=[pl.BlockSpec((cap, chunk), lambda i: (0, i))] * len(partners),
+        out_shape=[jax.ShapeDtypeStruct((cap, full), jnp.bfloat16)] * len(partners),
+        scratch_shapes=[pltpu.VMEM((len(partners) * cap, rows), jnp.bfloat16)],
+        compiler_params=pltpu.CompilerParams(vmem_limit_bytes=VMEM_LIMIT),
+        cost_estimate=pl.CostEstimate(
+            flops=2 * len(partners) * cap * rows * width,
+            bytes_accessed=2 * width * (rows + len(partners) * cap),
+            transcendentals=0,
+        ),
+    )(*operands)
+
+
+def input_grad_kernel(cap, count, me_ref, owner_ref, column_ref, row_ref, partner_ref, extra_ref, *refs):
+    pieces, out_ref, left = refs[:count], refs[count], refs[count + 1]
+    step = pl.program_id(0)
+    rows, slots = row_ref.shape[1], extra_ref.shape[0]
+    rank = pieces[0].shape[0]
+
+    @pl.when(step == 0)
+    def _():
+        partner, target = slot_targets(cap, me_ref[0, 0], owner_ref, column_ref, row_ref)
+        slot = lax.broadcasted_iota(jnp.int32, (slots, rows), 0)
+        for at in range(count):
+            picked = jnp.where((slot == target) & (partner == partner_ref[at]), 1.0, 0.0).astype(jnp.bfloat16)
+            low = lax.dot_general(picked, extra_ref[:, :rank], FIRST, preferred_element_type=jnp.float32)
+            left[:, at * rank : (at + 1) * rank] = low.astype(left.dtype)
+
+    stacked = jnp.concatenate([ref[...] for ref in pieces], axis=0)
+    out_ref[...] = jnp.dot(left[...], stacked, preferred_element_type=jnp.float32).astype(out_ref.dtype)
+
+
+def input_grad_of(cap, me, owner, tenant, partners, extra, pieces):
+    rows, adapters, slots = tenant.shape[0], owner.shape[0], extra.shape[0]
+    rank, width = pieces[0].shape
+    count = len(pieces)
+    chunk = min(width, 1024)
+    still = lambda shape: pl.BlockSpec(shape, lambda i: (0, 0))
+    return pl.pallas_call(
+        lambda *refs: input_grad_kernel(cap, count, *refs),
+        grid=(width // chunk,),
+        in_specs=[
+            pl.BlockSpec(memory_space=pltpu.SMEM),
+            still((adapters, 1)),
+            still((rows, 1)),
+            still((1, rows)),
+            pl.BlockSpec(memory_space=pltpu.SMEM),
+            still((slots, LANES)),
+        ]
+        + [pl.BlockSpec((rank, chunk), lambda i: (0, i))] * count,
+        out_specs=pl.BlockSpec((rows, chunk), lambda i: (0, i)),
+        out_shape=jax.ShapeDtypeStruct((rows, width), jnp.bfloat16),
+        scratch_shapes=[pltpu.VMEM((rows, count * rank), jnp.bfloat16)],
+        compiler_params=pltpu.CompilerParams(vmem_limit_bytes=VMEM_LIMIT),
+        cost_estimate=pl.CostEstimate(
+            flops=2 * rows * count * rank * width,
+            bytes_accessed=2 * width * (rows + count * rank),
+            transcendentals=0,
+        ),
+    )(me.reshape(1, 1), owner.reshape(adapters, 1), tenant, tenant.reshape(1, rows), partners, extra, *pieces)
 
 
 def fold_one(low, gram, scale, amount):
@@ -122,36 +292,116 @@
     )(amount, grad_hidden, gram_x, hidden, gram_dy)
 
 
-def grads_kernel(factor_ref, left_a_ref, left_b_ref, rows_x_ref, rows_dy_ref, grad_a_ref, grad_b_ref):
+def grads_kernel(count, factor_ref, left_a_ref, left_b_ref, *refs):
+    blocks_x, blocks_dy = refs[:count], refs[count : 2 * count]
+    grad_a_ref, grad_b_ref = refs[2 * count :]
     factor = factor_ref[0, 0]
     rank = grad_a_ref.shape[0]
-    for left_ref, rows_ref, out_ref in (
-        (left_a_ref, rows_x_ref, grad_a_ref),
-        (left_b_ref, rows_dy_ref, grad_b_ref),
-    ):
-        parts = lax.dot_general(left_ref[...], rows_ref[...], FIRST, preferred_element_type=jnp.float32)
+    for left_ref, blocks, out_ref in ((left_a_ref, blocks_x, grad_a_ref), (left_b_ref, blocks_dy, grad_b_ref)):
+        rows = jnp.concatenate([ref[...] for ref in blocks], axis=0)
+        parts = lax.dot_general(left_ref[...], rows, FIRST, preferred_element_type=jnp.float32)
         proj = (parts[2 * rank :] + parts[rank : 2 * rank]) + parts[:rank]
         out_ref[...] = (factor * proj).astype(out_ref.dtype)
 
 
-def grads(factor, left_a, left_b, rows_x, rows_dy):
-    slots, width = rows_x.shape
+def grads(factor, left_a, left_b, blocks_x, blocks_dy, width):
+    slots = left_a.shape[0]
     rank = left_a.shape[1] // 3
     chunk = min(width, 2048)
     left_spec = pl.BlockSpec((slots, 3 * rank), lambda i: (0, 0))
-    rows_spec = pl.BlockSpec((slots, chunk), lambda i: (0, i))
+    rows_specs = [pl.BlockSpec((block.shape[0], chunk), lambda i: (0, i)) for block in blocks_x]
     out_spec = pl.BlockSpec((rank, chunk), lambda i: (0, i))
     return pl.pallas_call(
-        grads_kernel,
+        lambda *refs: grads_kernel(len(blocks_x), *refs),
         grid=(width // chunk,),
-        in_specs=[pl.BlockSpec(memory_space=pltpu.SMEM), left_spec, left_spec, rows_spec, rows_spec],
+        in_specs=[pl.BlockSpec(memory_space=pltpu.SMEM), left_spec, left_spec] + rows_specs * 2,
         out_specs=[out_spec, out_spec],
         out_shape=[jax.ShapeDtypeStruct((rank, width), jnp.bfloat16)] * 2,
         compiler_params=pltpu.CompilerParams(vmem_limit_bytes=VMEM_LIMIT),
         cost_estimate=pl.CostEstimate(
             flops=12 * slots * width * rank, bytes_accessed=4 * width * (slots + rank), transcendentals=0
         ),
-    )(factor, left_a, left_b, rows_x, rows_dy)
+    )(factor, left_a, left_b, *blocks_x, *blocks_dy)
+
+
+def clip_factor(local_sq, adapters, rank, width):
+    total = total_over_blk(local_sq[:1, :1])
+    mean_sq = total / (2.0 * adapters * rank * width)
+    return jnp.minimum(1.0, 1.0 / jnp.sqrt(mean_sq + EPS))
+
+
+def permute(value, pairs):
+    return lax.ppermute(value, "blk", pairs)
+
+
+def gathered(weight, me):
+    lines = [(z, rest) for z in range(4) for rest in range(4)]
+    hop = lambda ends: [(z * 4 + rest, ends[z] * 4 + rest) for z, rest in lines if z in ends]
+    near = permute(weight, hop({0: 1, 1: 0, 2: 3, 3: 2}))
+    across = permute(weight, hop({1: 2, 2: 1}))
+    across_near = permute(near, hop({1: 2, 2: 1}))
+    outward = permute(across, hop({1: 0, 2: 3}))
+    outward_near = permute(across_near, hop({1: 0, 2: 3}))
+    plane = me // 4
+    inner = (plane == 1) | (plane == 2)
+    second = jnp.where(inner, across, outward)
+    third = jnp.where(inner, across_near, outward_near)
+    pieces = [weight, near, second, third]
+    partners = [0, 4, jnp.where(inner, 12, 8), jnp.where(inner, 8, 12)]
+    for bit in (2, 1):
+        pieces += [permute(piece, [(i, i ^ bit) for i in range(16)]) for piece in pieces]
+        partners += [partner + bit for partner in partners]
+    return pieces, jnp.stack([jnp.asarray(partner, jnp.int32) for partner in partners])
+
+
+def per_device_blocks(tokens, cotangent, tenant, owner, down_factor_table, up_factor_table):
+    rows, width = tokens.shape
+    count_blk = lax.axis_size("blk")
+    adapters = owner.shape[0]
+    rank = down_factor_table.shape[1]
+    cap = 2 * rows // adapters
+    down_weight = down_factor_table[0]
+    up_weight = up_factor_table[0]
+    me = lax.axis_index("blk").astype(jnp.int32)
+    order = [8, 1, 9, 2, 10, 3, 11, 4, 12, 5, 13, 6, 14, 7, 15]
+    first, second = order[:8], order[8:]
+
+    def swap(value, partner):
+        return permute(value, [(i, i ^ partner) for i in range(count_blk)])
+
+    with jax.named_scope("down_factors"):
+        pieces, partners = gathered(down_weight, me)
+    with jax.named_scope("send_cotangent"):
+        own_dy, *sent_dy = place([0] + order, cap, me, owner, tenant, cotangent)
+        got_dy = [swap(block, partner) for block, partner in zip(sent_dy, order)]
+    with jax.named_scope("grad_hidden_first"):
+        low_first = low_products(got_dy[:8], up_weight, SCALE)
+    with jax.named_scope("send_tokens_first"):
+        sent_first = place(first, cap, me, owner, tenant, tokens, low_first)
+        got_x = [swap(block, partner) for block, partner in zip(sent_first, first)]
+    with jax.named_scope("grad_hidden"):
+        blocks_dy = got_dy + [own_dy]
+        grad_hidden, gram_dy = rows_products(blocks_dy, up_weight, SCALE)
+    with jax.named_scope("send_tokens_second"):
+        *sent_second, own_x = place(second + [0], cap, me, owner, tenant, tokens, grad_hidden[8 * cap :])
+        got_x += [swap(block, partner) for block, partner in zip(sent_second, second)]
+    with jax.named_scope("hidden"):
+        blocks_x = got_x + [own_x]
+        hidden, gram_x, extra = rows_products(blocks_x, down_weight, 1.0, with_extra=True)
+    with jax.named_scope("fold"):
+        amount = jnp.sum(extra[:, rank], dtype=jnp.float32).reshape(1, 1)
+        left_a, left_b, local_sq = fold(amount, grad_hidden, gram_x, hidden, gram_dy)
+    with jax.named_scope("clip"):
+        factor = clip_factor(local_sq, adapters, rank, width)
+    with jax.named_scope("grads"):
+        grad_a, grad_b = grads(factor, left_a, left_b, blocks_x, blocks_dy, width)
+    with jax.named_scope("input_grad"):
+        by_partner = dict(zip(order + [0], range(count_blk)))
+        extra = jnp.concatenate(
+            [extra[by_partner[s] * cap : (by_partner[s] + 1) * cap] for s in range(count_blk)], axis=0
+        )
+        input_grad = input_grad_of(cap, me, owner, tenant, partners, extra, pieces)
+    return (input_grad, grad_a[None], grad_b[None])
 
 
 def per_device(tokens, cotangent, tenant, owner, down_factor_table, up_factor_table):
@@ -191,20 +441,18 @@
         counts = total_over_blk(sent)
         amount = jnp.sum(jnp.where(devices == lax.axis_index("blk"), counts[0], 0.0)).reshape(1, 1)
     with jax.named_scope("grad_hidden"):
-        grad_hidden, gram_dy = rows_products(rows_dy, up_weight, SCALE)
+        grad_hidden, gram_dy = rows_products([rows_dy], up_weight, SCALE)
     with jax.named_scope("back"):
         back = jnp.dot(grad_hidden, down_weight, preferred_element_type=jnp.float32).astype(jnp.bfloat16)
         returned = exchange(back)
     with jax.named_scope("hidden"):
-        hidden, gram_x = rows_products(rows_x, down_weight, 1.0)
+        hidden, gram_x = rows_products([rows_x], down_weight, 1.0)
     with jax.named_scope("fold"):
         left_a, left_b, local_sq = fold(amount, grad_hidden, gram_x, hidden, gram_dy)
     with jax.named_scope("clip"):
-        total = total_over_blk(local_sq[:1, :1])
-        mean_sq = total / (2.0 * adapters * rank * width)
-        factor = jnp.minimum(1.0, 1.0 / jnp.sqrt(mean_sq + EPS))
+        factor = clip_factor(local_sq, adapters, rank, width)
     with jax.named_scope("grads"):
-        grad_a, grad_b = grads(factor, left_a, left_b, rows_x, rows_dy)
+        grad_a, grad_b = grads(factor, left_a, left_b, [rows_x], [rows_dy], width)
     with jax.named_scope("input_grad"):
         input_grad = lax.dot_general(placing, returned, FIRST, preferred_element_type=jnp.float32).astype(
             jnp.bfloat16
@@ -213,7 +461,8 @@
 
 
 def solution(mesh):
+    body = per_device_blocks if mesh.shape["blk"] == 16 else per_device
     split = ("groups", "blk")
     in_specs = (P(split, None), P(split, None), P(split, None), P("groups"), P(split, None, None), P(split, None, None))
     out_specs = (P(split, None), P(split, None, None), P(split, None, None))
-    return jax.shard_map(per_device, mesh=mesh, in_specs=in_specs, out_specs=out_specs, check_vma=False)
+    return jax.shard_map(body, mesh=mesh, in_specs=in_specs, out_specs=out_specs, check_vma=False)

time: 338 us -> 371 us (1.098)
  starting transfers between devices: 35.4 us -> 98 us
  waiting for transfers between devices: 256 us -> 209 us
  Pallas kernels: 17.9 us -> 39.9 us
  matrix products: 15.4 us -> 0 us
  local copies, waits for them, and re-layouts: 1.83 us -> 12.1 us
    ppermute x0 -> x47, waiting for transfers between devices: none -> 207 us  [permute(): return lax.ppermute(value, 'blk', pairs)]
    all_to_all x3 -> x0, waiting for transfers between devices: 171 us -> none  [exchange(): lax.all_to_all(value, 'blk', split_axis=0, concat_axis=0, tiled=True)]
    ppermute x8 -> x4, waiting for transfers between devices: 84.6 us -> 1.7 us  [total_over_blk(): lax.ppermute(value, 'blk', [(i, i ^ step) for i in range(size)])]
    ppermute x0 -> x47, starting transfers between devices: none -> 76.4 us  [permute(): return lax.ppermute(value, 'blk', pairs)]
    pallas_call x3 -> x8, Pallas kernels: 15.5 us -> 37.5 us  [the longest x2 10.5 us: rows_products(): pl.pallas_call(lambda *refs: rows_kernel(scale, len(blocks), with_extra,...]
    all_to_all x3 -> x0, starting transfers between devices: 15.5 us -> none  [exchange(): lax.all_to_all(value, 'blk', split_axis=0, concat_axis=0, tiled=True)]
    dot_general x4 -> x0, matrix products: 15.4 us -> none  [the longest x2 7.97 us: place(): jnp.dot(placing, value, preferred_element_type=jnp.float32)]
    unnamed x6 -> x140, local copies, waits for them, and re-layouts: 1.32 us -> 10.7 us
  transfers between devices with their start and end apart: 11 -> 51, of which waited for: 10 -> 22; matrix products, arithmetic and copies ran while one was open for 3% -> 1% of each run, Pallas kernels for 5% -> 5%
where the time goes in v2:
time: 371 us; the launch traced here: 366 us
  waiting for transfers between devices  209 us (56%)
  starting transfers between devices  98 us (26%)
  Pallas kernels  39.9 us (11%)
  local copies, waits for them, and re-layouts  12.1 us (3%)
  between operations  5.11 us (1%)
    ppermute x47, waiting for transfers between devices, permute(): return lax.ppermute(value, 'blk', pairs)  207 us
    ppermute x47, starting transfers between devices, permute(): return lax.ppermute(value, 'blk', pairs)  76.4 us
    ppermute x4, starting transfers between devices, total_over_blk(): lax.ppermute(value, 'blk', [(i, i ^ step) for i in range(size)])  21.6 us
    unnamed x140, local copies, waits for them, and re-layouts  10.7 us
    pallas_call x2, Pallas kernels, rows_products(): pl.pallas_call(lambda *refs: rows_kernel(scale, len(blocks), with_extra,...  10.5 us
    pallas_call x1, Pallas kernels, input_grad_of(): pl.pallas_call(lambda *refs: input_grad_kernel(cap, count, *refs), grid=(...  10.1 us
    pallas_call x3, Pallas kernels, place(): pl.pallas_call(lambda *refs: place_kernel(partners, cap, with_extra, *ref...  9.34 us
  transfers between devices with their start and end apart: 51, of which 22 were waited for; matrix products, arithmetic and copies ran while one was open for 1% of the time, Pallas kernels for 5%

profile of v2, /device:TPU:16, one launch (start us, length us, event | category | flops | bytes accessed | tf_op | source)
XLA Modules:
  0.0 365.9 jit_solution(17621229477989882933)
XLA Ops:
  0.6 0.8 copy.16.refs_2_
  1.5 0.7 copy.15.refs_1_
  2.9 3.9 %send_cotangent.1 = (bf16[16,8192]{1,0:T(8,128)(2,1)S(1)}, bf16[16,8192]{1,0:T(8,128)(2,1)S(1)}, bf16[16,8192]{1,0:T(8,128)(2,1)S(1)}, bf16[16,8192]{1,0:T(8,128...) custom-call(s32[1,1]{1,0:T(1,128)} %bitcast.refs_0_, ...), custom_call_target="tpu_custom_call" | custom-call | flops 536870912 | bytes 6291456 | tf_op jit(solution)/shard_map/send_cotangent/pallas_call | solution.py:178
  7.0 2.9 collective-permute-start.2
  9.9 1.5 collective-permute-start.3
  11.5 18.9 %collective-permute-done.refs_0_.refs_19_ = bf16[16,8192]{1,0:T(8,128)(2,1)S(1)} collective-permute-done((bf16[16,8192]{1,0:T(8,128)(2,1)S(1)}, bf16[16,8192]{1,0:T(8,128)(2,1)S(1)}, u32[]{:S(2)}, u32[]{:S(2)}) %collective-permute-start) | collective-permute-done | bytes 262176 | tf_op jit(solution)/shard_map/send_cotangent/ppermute | solution.py:334
  30.4 4.6 %collective-permute-start.6 = (bf16[16,8192]{1,0:T(8,128)(2,1)S(1)}, bf16[16,8192]{1,0:T(8,128)(2,1)S(1)}, u32[]{:S(2)}, u32[]{:S(2)}) collective-permute-start(bf16[16,8192]{1,0:T(8,128)(2,1)S(1)} %get-tuple-element.51), channel_id=1, source_target_pairs={{0,11},{1,10},{2,9},{3,8},{4,15},{5,14},{6,13},{7,12},{8,3},{9,2},... | collective-permute-start | bytes 786440 | tf_op jit(solution)/shard_map/send_cotangent/ppermute | solution.py:334
  35.0 0.9 collective-permute-done.2.refs_2_.refs_21_
  35.9 9.4 %collective-permute-start.7 = (bf16[16,8192]{1,0:T(8,128)(2,1)S(1)}, bf16[16,8192]{1,0:T(8,128)(2,1)S(1)}, u32[]{:S(2)}, u32[]{:S(2)}) collective-permute-start(bf16[16,8192]{1,0:T(8,128)(2,1)S(1)} %get-tuple-element.52), channel_id=1, source_target_pairs={{0,4},{1,5},{2,6},{3,7},{4,0},{5,1},{6,2},{7,3},{8,12},{9,13},{10,... | collective-permute-start | bytes 786440 | tf_op jit(solution)/shard_map/send_cotangent/ppermute | solution.py:334
  45.3 2.0 collective-permute-done.4.refs_4_.refs_23_
  47.3 4.3 %collective-permute-start.17 = (bf16[16,8192]{1,0:T(8,128)(2,1)S(1)}, bf16[16,8192]{1,0:T(8,128)(2,1)S(1)}, u32[]{:S(2)}, u32[]{:S(2)}) collective-permute-start(bf16[16,8192]{1,0:T(8,128)(2,1)S(1)} %get-tuple-element.62), channel_id=1, source_target_pairs={{0,5},{1,4},{2,7},{3,6},{4,1},{5,0},{6,3},{7,2},{8,13},{9,12},{10,... | collective-permute-start | bytes 786440 | tf_op jit(solution)/shard_map/send_cotangent/ppermute | solution.py:334
  51.6 0.7 collective-permute-start.18
  52.4 6.2 %collective-permute-done.6.refs_6_.refs_25_ = bf16[16,8192]{1,0:T(8,128)(2,1)S(1)} collective-permute-done((bf16[16,8192]{1,0:T(8,128)(2,1)S(1)}, bf16[16,8192]{1,0:T(8,128)(2,1)S(1)}, u32[]{:S(2)}, u32[]{:S(2)}) %collective-permute-start.6) | collective-permute-done | bytes 262176 | tf_op jit(solution)/shard_map/send_cotangent/ppermute | solution.py:334
  58.6 4.6 %collective-permute-start.19 = (bf16[16,8192]{1,0:T(8,128)(2,1)S(1)}, bf16[16,8192]{1,0:T(8,128)(2,1)S(1)}, u32[]{:S(2)}, u32[]{:S(2)}) collective-permute-start(bf16[16,8192]{1,0:T(8,128)(2,1)S(1)} %get-tuple-element.64), channel_id=1, source_target_pairs={{0,6},{1,7},{2,4},{3,5},{4,2},{5,3},{6,0},{7,1},{8,14},{9,15},{10,... | collective-permute-start | bytes 786440 | tf_op jit(solution)/shard_map/send_cotangent/ppermute | solution.py:334
  63.2 7.9 %collective-permute-done.7.refs_7_.refs_26_ = bf16[16,8192]{1,0:T(8,128)(2,1)S(1)} collective-permute-done((bf16[16,8192]{1,0:T(8,128)(2,1)S(1)}, bf16[16,8192]{1,0:T(8,128)(2,1)S(1)}, u32[]{:S(2)}, u32[]{:S(2)}) %collective-permute-start.7) | collective-permute-done | bytes 262176 | tf_op jit(solution)/shard_map/send_cotangent/ppermute | solution.py:334
  71.2 1.0 collective-permute-done.16.refs_8_.refs_27_
  72.2 2.0 collective-permute-start.21
  74.2 2.5 collective-permute-done.17.refs_9_.refs_28_
  76.7 5.7 %collective-permute-start.22 = (bf16[16,8192]{1,0:T(8,128)(2,1)S(1)}, bf16[16,8192]{1,0:T(8,128)(2,1)S(1)}, u32[]{:S(2)}, u32[]{:S(2)}) collective-permute-start(bf16[16,8192]{1,0:T(8,128)(2,1)S(1)} %get-tuple-element.67), channel_id=1, source_target_pairs={{0,15},{1,14},{2,13},{3,12},{4,11},{5,10},{6,9},{7,8},{8,7},{9,6},... | collective-permute-start | bytes 786440 | tf_op jit(solution)/shard_map/send_cotangent/ppermute | solution.py:334
  82.4 5.5 %collective-permute-done.19.refs_11_.refs_30_ = bf16[16,8192]{1,0:T(8,128)(2,1)S(1)} collective-permute-done((bf16[16,8192]{1,0:T(8,128)(2,1)S(1)}, bf16[16,8192]{1,0:T(8,128)(2,1)S(1)}, u32[]{:S(2)}, u32[]{:S(2)}) %collective-permute-start.19) | collective-permute-done | bytes 262176 | tf_op jit(solution)/shard_map/send_cotangent/ppermute | solution.py:334
  87.9 10.1 %collective-permute-done.20.refs_12_.refs_31_ = bf16[16,8192]{1,0:T(8,128)(2,1)S(1)} collective-permute-done((bf16[16,8192]{1,0:T(8,128)(2,1)S(1)}, bf16[16,8192]{1,0:T(8,128)(2,1)S(1)}, u32[]{:S(2)}, u32[]{:S(2)}) %collective-permute-start.20) | collective-permute-done | bytes 262176 | tf_op jit(solution)/shard_map/send_cotangent/ppermute | solution.py:334
  98.1 1.0 collective-permute-done.21.refs_13_.refs_32_
  99.1 4.4 %collective-permute-done.22.refs_14_.refs_33_ = bf16[16,8192]{1,0:T(8,128)(2,1)S(1)} collective-permute-done((bf16[16,8192]{1,0:T(8,128)(2,1)S(1)}, bf16[16,8192]{1,0:T(8,128)(2,1)S(1)}, u32[]{:S(2)}, u32[]{:S(2)}) %collective-permute-start.22) | collective-permute-done | bytes 262176 | tf_op jit(solution)/shard_map/send_cotangent/ppermute | solution.py:334
  103.5 3.6 grad_hidden.1
  107.9 2.2 send_tokens_second.1
  110.3 1.6 collective-permute-start.25
  111.9 3.7 %collective-permute-start.26 = (bf16[16,8320]{1,0:T(8,128)(2,1)S(1)}, bf16[16,8320]{1,0:T(8,128)(2,1)S(1)}, u32[]{:S(2)}, u32[]{:S(2)}) collective-permute-start(bf16[16,8320]{1,0:T(8,128)(2,1)S(1)} %get-tuple-element.73), channel_id=1, source_target_pairs={{0,6},{1,7},{2,4},{3,5},{4,2},{5,3},{6,0},{7,1},{8,14},{9,15},{10,... | collective-permute-start | bytes 798728 | tf_op jit(solution)/shard_map/send_tokens_second/ppermute | solution.py:334
  115.9 8.7 %collective-permute-done.23.refs_8_.refs_24_.refs_11_ = bf16[16,8320]{1,0:T(8,128)(2,1)S(1)} collective-permute-done((bf16[16,8320]{1,0:T(8,128)(2,1)S(1)}, bf16[16,8320]{1,0:T(8,128)(2,1)S(1)}, u32[]{:S(2)}, u32[]{:S(2)}) %collective-permute-start.23) | collective-permute-done | bytes 266272 | tf_op jit(solution)/shard_map/send_tokens_second/ppermute | solution.py:334
  124.8 1.5 grad_hidden_first.1.refs_5_
  126.3 3.2 send_tokens_first.1
  129.5 6.1 %collective-permute-done.25.refs_10_.refs_26_.refs_13_ = bf16[16,8320]{1,0:T(8,128)(2,1)S(1)} collective-permute-done((bf16[16,8320]{1,0:T(8,128)(2,1)S(1)}, bf16[16,8320]{1,0:T(8,128)(2,1)S(1)}, u32[]{:S(2)}, u32[]{:S(2)}) %collective-permute-start.25) | collective-permute-done | bytes 266272 | tf_op jit(solution)/shard_map/send_tokens_second/ppermute | solution.py:334
  136.2 14.6 %collective-permute-done.27.refs_12_.refs_28_.refs_15_ = bf16[16,8320]{1,0:T(8,128)(2,1)S(1)} collective-permute-done((bf16[16,8320]{1,0:T(8,128)(2,1)S(1)}, bf16[16,8320]{1,0:T(8,128)(2,1)S(1)}, u32[]{:S(2)}, u32[]{:S(2)}) %collective-permute-start.27) | collective-permute-done | bytes 266272 | tf_op jit(solution)/shard_map/send_tokens_second/ppermute | solution.py:334
  151.5 0.7 copy-done.10
  152.2 0.9 collective-permute-start.13
  153.1 19.6 %collective-permute-done.29.refs_14_.refs_30_.refs_17_ = bf16[16,8320]{1,0:T(8,128)(2,1)S(1)} collective-permute-done((bf16[16,8320]{1,0:T(8,128)(2,1)S(1)}, bf16[16,8320]{1,0:T(8,128)(2,1)S(1)}, u32[]{:S(2)}, u32[]{:S(2)}) %collective-permute-start.29) | collective-permute-done | bytes 266272 | tf_op jit(solution)/shard_map/send_tokens_second/ppermute | solution.py:334
  172.7 0.7 copy-done.12
  173.4 1.0 collective-permute-done.10.refs_2_.refs_18_.refs_5_
  174.4 11.0 %collective-permute-start.30 = (bf16[64,8192]{1,0:T(8,128)(2,1)S(1)}, bf16[64,8192]{1,0:T(8,128)(2,1)}, u32[]{:S(2)}, u32[]{:S(2)}) collective-permute-start(bf16[64,8192]{1,0:T(8,128)(2,1)S(1)} %bitcast.18), channel_id=1, source_target_pairs={{0,4},{1,5},{2,6},{3,7},{4,0},{5,1},{6,2},{7,3},{8,12},{9,13},{10,... | collective-permute-start | bytes 3145736 | tf_op jit(solution)/shard_map/down_factors/ppermute | solution.py:334
  185.5 1.9 collective-permute-start.31
  187.4 4.1 %collective-permute-start.15 = (bf16[16,8320]{1,0:T(8,128)(2,1)}, bf16[16,8320]{1,0:T(8,128)(2,1)}, u32[]{:S(2)}, u32[]{:S(2)}) collective-permute-start(bf16[16,8320]{1,0:T(8,128)(2,1)} %get-tuple-element.60), channel_id=1, source_target_pairs={{0,4},{1,5},{2,6},{3,7},{4,0},{5,1},{6,2},{7,3},{8,12},{9,13},{10,... | collective-permute-start | bytes 798728 | tf_op jit(solution)/shard_map/send_tokens_first/ppermute | solution.py:334
  193.0 30.0 %collective-permute-done.15.refs_7_.refs_23_.refs_10_ = bf16[16,8320]{1,0:T(8,128)(2,1)} collective-permute-done((bf16[16,8320]{1,0:T(8,128)(2,1)}, bf16[16,8320]{1,0:T(8,128)(2,1)}, u32[]{:S(2)}, u32[]{:S(2)}) %collective-permute-start.15) | collective-permute-done | bytes 266272 | tf_op jit(solution)/shard_map/send_tokens_first/ppermute | solution.py:334
  223.6 1.9 collective-permute-done.8.refs_0_.refs_16_.refs_3_
  225.6 0.9 copy-done.9
  226.6 0.9 copy-done.11
  227.5 0.9 copy-done.13
  228.5 0.9 copy-done.15
  229.4 0.9 copy-done.17
  230.4 6.9 %hidden.1 = (bf16[256,64]{1,0:T(8,128)(2,1)S(1)}, f32[256,256]{1,0:T(8,128)S(1)}, bf16[256,128]{1,0:T(8,128)(2,1)S(1)}) custom-call(bf16[16,8320]{1,0:T(8,128)(2,1)} %collective-permute-done.8.refs_0_.refs_16_.refs_3_, bf16[16,8320]{1,0:T(8,128)(2,1)} %collective-permute-done.9.refs_1_.refs_17_.refs_4_, ...), custom_call_target="tpu_custom_call" | custom-call | flops 1342177280 | bytes 5242880 | tf_op jit(solution)/shard_map/hidden/pallas_call | solution.py:66
  237.3 0.7 convert_reduce_fusion
  238.0 2.4 fold.1
  241.4 5.6 %collective-permute-start.33 = (bf16[64,8192]{1,0:T(8,128)(2,1)}, bf16[64,8192]{1,0:T(8,128)(2,1)S(1)}, u32[]{:S(2)}, u32[]{:S(2)}) collective-permute-start(bf16[64,8192]{1,0:T(8,128)(2,1)} %collective-permute-done.30.refs_7_), channel_id=1, source_target_pairs={{4,8},{5,9},{6,10},{7,11},{8,4},{9,5},{10,6},{11,7},{20,24},{21,25... | collective-permute-start | bytes 3145736 | tf_op jit(solution)/shard_map/down_factors/ppermute | solution.py:334
  247.0 2.7 collective-permute-start.32
  251.1 1.9 collective-permute-start.48
  253.0 1.7 collective-permute-done.48
  255.4 17.2 %collective-permute-start.49 = (f32[1,1]{1,0:T(1,128)}, f32[1,1]{1,0:T(1,128)}, u32[]{:S(2)}, u32[]{:S(2)}) collective-permute-start(f32[1,1]{1,0:T(1,128)} %add.45), channel_id=1, source_target_pairs={{0,4},{1,5},{2,6},{3,7},{4,0},{5,1},{6,2},{7,3},{8,12},{9,13},{10,... | collective-permute-start | bytes 20 | tf_op jit(solution)/shard_map/clip/ppermute | solution.py:23
  273.2 2.1 collective-permute-start.50
  275.9 3.8 %collective-permute-start.34 = (bf16[64,8192]{1,0:T(8,128)(2,1)S(1)}, bf16[64,8192]{1,0:T(8,128)(2,1)S(1)}, u32[]{:S(2)}, u32[]{:S(2)}) collective-permute-start(bf16[64,8192]{1,0:T(8,128)(2,1)S(1)} %collective-permute-done.33), channel_id=1, source_target_pairs={{4,0},{5,1},{6,2},{7,3},{8,12},{9,13},{10,14},{11,15},{20,16},{21,... | collective-permute-start | bytes 3145736 | tf_op jit(solution)/shard_map/down_factors/ppermute | solution.py:334
  279.7 1.4 broadcast_select_fusion.1.refs_8_
  281.4 19.0 %collective-permute-done.34 = bf16[64,8192]{1,0:T(8,128)(2,1)S(1)} collective-permute-done((bf16[64,8192]{1,0:T(8,128)(2,1)S(1)}, bf16[64,8192]{1,0:T(8,128)(2,1)S(1)}, u32[]{:S(2)}, u32[]{:S(2)}) %collective-permute-start.34) | collective-permute-done | bytes 1048608 | tf_op jit(solution)/shard_map/down_factors/ppermute | solution.py:334
  300.4 1.6 collective-permute-start.37
  303.3 23.2 %collective-permute-done.37.refs_12_ = bf16[64,8192]{1,0:T(8,128)(2,1)S(1)} collective-permute-done((bf16[64,8192]{1,0:T(8,128)(2,1)S(1)}, bf16[64,8192]{1,0:T(8,128)(2,1)S(1)}, u32[]{:S(2)}, u32[]{:S(2)}) %collective-permute-start.37) | collective-permute-done | bytes 1048608 | tf_op jit(solution)/shard_map/down_factors/ppermute | solution.py:334
  326.5 22.1 %collective-permute-done.38.refs_13_ = bf16[64,8192]{1,0:T(8,128)(2,1)S(1)} collective-permute-done((bf16[64,8192]{1,0:T(8,128)(2,1)S(1)}, bf16[64,8192]{1,0:T(8,128)(2,1)S(1)}, u32[]{:S(2)}, u32[]{:S(2)}) %collective-permute-start.38) | collective-permute-done | bytes 1048608 | tf_op jit(solution)/shard_map/down_factors/ppermute | solution.py:334
  349.5 6.0 %grads.1 = (bf16[64,8192]{1,0:T(8,128)(2,1)}, bf16[64,8192]{1,0:T(8,128)(2,1)}) custom-call(f32[1,1]{1,0:T(1,128)S(6)} %min.3.refs_0_, bf16[256,192]{1,0:T(8,128)(2,1)S(1)} %get-tuple-element.83.refs_1_, bf16[256,192]{1,0:T(8,128)(2,1)S(1)} %get-tuple-element.84.refs_2_, bf16[16,8320]{1,0:T(8,128)(2,1)} %collective-permute-done.8.refs_0_.refs_16_.refs_3_, ...), custom_call_target="tpu_custom_call" | custom-call | flops 1610612736 | bytes 10485760 | tf_op jit(solution)/shard_map/grads/pallas_call | solution.py:314
  355.6 10.1 %input_grad.1 = bf16[128,8192]{1,0:T(8,128)(2,1)} custom-call(s32[1,1]{1,0:T(1,128)} %bitcast.refs_0_, s32[16,1]{1,0:T(8,128)S(1)} %copy.15.refs_1_, s32[128,1]{1,0:T(8,128)S(1)} %copy.16.refs_2_, s32[1,128]{1,0:T(1,128)S(1)} %bitcast.27, s32[16]{0:T(128)S(1)} %stack.35.refs_4_, bf16[256,128]{1,0:T(8,128)(2,1)S(1)} %constant_dynamic-update-slice_fusion.refs_5_, ...), custom_call_target="tpu_custom_call" | custom-call | flops 2147483648 | bytes 18874368 | tf_op jit(solution)/shard_map/input_grad/pallas_call | solution.py:219
  (195 shorter events, 8.8 us)
Async XLA Ops:
  0.6 102.8 %copy-start.1 = (bf16[1,64,8192]{2,1,0:T(8,128)(2,1)S(1)}, bf16[1,64,8192]{2,1,0:T(8,128)(2,1)}, u32[]{:S(2)}) copy-start(bf16[1,64,8192]{2,1,0:T(8,128)(2,1)} %param.11) | copy-start | bytes 3145732
  6.8 100.3 %copy-start.34 = (bf16[16,8192]{1,0:T(8,128)(2,1)}, bf16[16,8192]{1,0:T(8,128)(2,1)S(1)}, u32[]{:S(2)}) copy-start(bf16[16,8192]{1,0:T(8,128)(2,1)S(1)} %get-tuple-element.68.refs_15_.refs_34_) | copy-start | bytes 786436
  6.8 23.6 %collective-permute-start = (bf16[16,8192]{1,0:T(8,128)(2,1)S(1)}, bf16[16,8192]{1,0:T(8,128)(2,1)S(1)}, u32[]{:S(2)}, u32[]{:S(2)}) collective-permute-start(bf16[16,8192]{1,0:T(8,128)(2,1)S(1)} %get-tuple-element.45), channel_id=1, source_target_pairs={{0,8},{1,9},{2,10},{3,11},{4,12},{5,13},{6,14},{7,15},{8,0},{9,1},... | collective-permute-start | bytes 786440 | tf_op jit(solution)/shard_map/send_cotangent/ppermute | solution.py:334
  6.9 23.5 %collective-permute-start.1 = (bf16[16,8192]{1,0:T(8,128)(2,1)S(1)}, bf16[16,8192]{1,0:T(8,128)(2,1)S(1)}, u32[]{:S(2)}, u32[]{:S(2)}) collective-permute-start(bf16[16,8192]{1,0:T(8,128)(2,1)S(1)} %get-tuple-element.46), channel_id=1, source_target_pairs={{0,1},{1,0},{2,3},{3,2},{4,5},{5,4},{6,7},{7,6},{8,9},{9,8},{10,11... | collective-permute-start | bytes 786440 | tf_op jit(solution)/shard_map/send_cotangent/ppermute | solution.py:334
  7.0 28.9 %collective-permute-start.2 = (bf16[16,8192]{1,0:T(8,128)(2,1)S(1)}, bf16[16,8192]{1,0:T(8,128)(2,1)S(1)}, u32[]{:S(2)}, u32[]{:S(2)}) collective-permute-start(bf16[16,8192]{1,0:T(8,128)(2,1)S(1)} %get-tuple-element.47), channel_id=1, source_target_pairs={{0,9},{1,8},{2,11},{3,10},{4,13},{5,12},{6,15},{7,14},{8,1},{9,0},... | collective-permute-start | bytes 786440 | tf_op jit(solution)/shard_map/send_cotangent/ppermute | solution.py:334
  9.9 35.4 %collective-permute-start.3 = (bf16[16,8192]{1,0:T(8,128)(2,1)S(1)}, bf16[16,8192]{1,0:T(8,128)(2,1)S(1)}, u32[]{:S(2)}, u32[]{:S(2)}) collective-permute-start(bf16[16,8192]{1,0:T(8,128)(2,1)S(1)} %get-tuple-element.48), channel_id=1, source_target_pairs={{0,2},{1,3},{2,0},{3,1},{4,6},{5,7},{6,4},{7,5},{8,10},{9,11},{10,... | collective-permute-start | bytes 786440 | tf_op jit(solution)/shard_map/send_cotangent/ppermute | solution.py:334
  11.5 35.9 %collective-permute-start.4 = (bf16[16,8192]{1,0:T(8,128)(2,1)S(1)}, bf16[16,8192]{1,0:T(8,128)(2,1)S(1)}, u32[]{:S(2)}, u32[]{:S(2)}) collective-permute-start(bf16[16,8192]{1,0:T(8,128)(2,1)S(1)} %get-tuple-element.49), channel_id=1, source_target_pairs={{0,10},{1,11},{2,8},{3,9},{4,14},{5,15},{6,12},{7,13},{8,2},{9,3},... | collective-permute-start | bytes 786440 | tf_op jit(solution)/shard_map/send_cotangent/ppermute | solution.py:334
  30.4 94.3 %copy-start.18 = (bf16[16,8192]{1,0:T(8,128)(2,1)}, bf16[16,8192]{1,0:T(8,128)(2,1)S(1)}, u32[]{:S(2)}) copy-start(bf16[16,8192]{1,0:T(8,128)(2,1)S(1)} %collective-permute-done.refs_0_.refs_19_) | copy-start | bytes 786436
  30.4 21.2 %collective-permute-start.5 = (bf16[16,8192]{1,0:T(8,128)(2,1)S(1)}, bf16[16,8192]{1,0:T(8,128)(2,1)S(1)}, u32[]{:S(2)}, u32[]{:S(2)}) collective-permute-start(bf16[16,8192]{1,0:T(8,128)(2,1)S(1)} %get-tuple-element.50), channel_id=1, source_target_pairs={{0,3},{1,2},{2,1},{3,0},{4,7},{5,6},{6,5},{7,4},{8,11},{9,10},{10,... | collective-permute-start | bytes 786440 | tf_op jit(solution)/shard_map/send_cotangent/ppermute | solution.py:334
  30.4 94.3 %copy-start.20 = (bf16[16,8192]{1,0:T(8,128)(2,1)}, bf16[16,8192]{1,0:T(8,128)(2,1)S(1)}, u32[]{:S(2)}) copy-start(bf16[16,8192]{1,0:T(8,128)(2,1)S(1)} %collective-permute-done.1.refs_1_.refs_20_) | copy-start | bytes 786436
  30.4 28.1 %collective-permute-start.6 = (bf16[16,8192]{1,0:T(8,128)(2,1)S(1)}, bf16[16,8192]{1,0:T(8,128)(2,1)S(1)}, u32[]{:S(2)}, u32[]{:S(2)}) collective-permute-start(bf16[16,8192]{1,0:T(8,128)(2,1)S(1)} %get-tuple-element.51), channel_id=1, source_target_pairs={{0,11},{1,10},{2,9},{3,8},{4,15},{5,14},{6,13},{7,12},{8,3},{9,2},... | collective-permute-start | bytes 786440 | tf_op jit(solution)/shard_map/send_cotangent/ppermute | solution.py:334
  35.9 88.8 %copy-start.22 = (bf16[16,8192]{1,0:T(8,128)(2,1)}, bf16[16,8192]{1,0:T(8,128)(2,1)S(1)}, u32[]{:S(2)}) copy-start(bf16[16,8192]{1,0:T(8,128)(2,1)S(1)} %collective-permute-done.2.refs_2_.refs_21_) | copy-start | bytes 786436
  35.9 35.1 %collective-permute-start.7 = (bf16[16,8192]{1,0:T(8,128)(2,1)S(1)}, bf16[16,8192]{1,0:T(8,128)(2,1)S(1)}, u32[]{:S(2)}, u32[]{:S(2)}) collective-permute-start(bf16[16,8192]{1,0:T(8,128)(2,1)S(1)} %get-tuple-element.52), channel_id=1, source_target_pairs={{0,4},{1,5},{2,6},{3,7},{4,0},{5,1},{6,2},{7,3},{8,12},{9,13},{10,... | collective-permute-start | bytes 786440 | tf_op jit(solution)/shard_map/send_cotangent/ppermute | solution.py:334
  45.3 79.5 %copy-start.24 = (bf16[16,8192]{1,0:T(8,128)(2,1)}, bf16[16,8192]{1,0:T(8,128)(2,1)S(1)}, u32[]{:S(2)}) copy-start(bf16[16,8192]{1,0:T(8,128)(2,1)S(1)} %collective-permute-done.3.refs_3_.refs_22_) | copy-start | bytes 786436
  45.3 26.9 %collective-permute-start.16 = (bf16[16,8192]{1,0:T(8,128)(2,1)S(1)}, bf16[16,8192]{1,0:T(8,128)(2,1)S(1)}, u32[]{:S(2)}, u32[]{:S(2)}) collective-permute-start(bf16[16,8192]{1,0:T(8,128)(2,1)S(1)} %get-tuple-element.61), channel_id=1, source_target_pairs={{0,12},{1,13},{2,14},{3,15},{4,8},{5,9},{6,10},{7,11},{8,4},{9,5},... | collective-permute-start | bytes 786440 | tf_op jit(solution)/shard_map/send_cotangent/ppermute | solution.py:334
  47.3 77.4 %copy-start.26 = (bf16[16,8192]{1,0:T(8,128)(2,1)}, bf16[16,8192]{1,0:T(8,128)(2,1)S(1)}, u32[]{:S(2)}) copy-start(bf16[16,8192]{1,0:T(8,128)(2,1)S(1)} %collective-permute-done.4.refs_4_.refs_23_) | copy-start | bytes 786436
  47.3 29.3 %collective-permute-start.17 = (bf16[16,8192]{1,0:T(8,128)(2,1)S(1)}, bf16[16,8192]{1,0:T(8,128)(2,1)S(1)}, u32[]{:S(2)}, u32[]{:S(2)}) collective-permute-start(bf16[16,8192]{1,0:T(8,128)(2,1)S(1)} %get-tuple-element.62), channel_id=1, source_target_pairs={{0,5},{1,4},{2,7},{3,6},{4,1},{5,0},{6,3},{7,2},{8,13},{9,12},{10,... | collective-permute-start | bytes 786440 | tf_op jit(solution)/shard_map/send_cotangent/ppermute | solution.py:334
  51.6 73.1 %copy-start.28 = (bf16[16,8192]{1,0:T(8,128)(2,1)}, bf16[16,8192]{1,0:T(8,128)(2,1)S(1)}, u32[]{:S(2)}) copy-start(bf16[16,8192]{1,0:T(8,128)(2,1)S(1)} %collective-permute-done.5.refs_5_.refs_24_) | copy-start | bytes 786436
  51.6 30.8 %collective-permute-start.18 = (bf16[16,8192]{1,0:T(8,128)(2,1)S(1)}, bf16[16,8192]{1,0:T(8,128)(2,1)S(1)}, u32[]{:S(2)}, u32[]{:S(2)}) collective-permute-start(bf16[16,8192]{1,0:T(8,128)(2,1)S(1)} %get-tuple-element.63), channel_id=1, source_target_pairs={{0,13},{1,12},{2,15},{3,14},{4,9},{5,8},{6,11},{7,10},{8,5},{9,4},... | collective-permute-start | bytes 786440 | tf_op jit(solution)/shard_map/send_cotangent/ppermute | solution.py:334
  58.6 29.4 %collective-permute-start.19 = (bf16[16,8192]{1,0:T(8,128)(2,1)S(1)}, bf16[16,8192]{1,0:T(8,128)(2,1)S(1)}, u32[]{:S(2)}, u32[]{:S(2)}) collective-permute-start(bf16[16,8192]{1,0:T(8,128)(2,1)S(1)} %get-tuple-element.64), channel_id=1, source_target_pairs={{0,6},{1,7},{2,4},{3,5},{4,2},{5,3},{6,0},{7,1},{8,14},{9,15},{10,... | collective-permute-start | bytes 786440 | tf_op jit(solution)/shard_map/send_cotangent/ppermute | solution.py:334
  71.1 27.0 %collective-permute-start.20 = (bf16[16,8192]{1,0:T(8,128)(2,1)S(1)}, bf16[16,8192]{1,0:T(8,128)(2,1)S(1)}, u32[]{:S(2)}, u32[]{:S(2)}) collective-permute-start(bf16[16,8192]{1,0:T(8,128)(2,1)S(1)} %get-tuple-element.65), channel_id=1, source_target_pairs={{0,14},{1,15},{2,12},{3,13},{4,10},{5,11},{6,8},{7,9},{8,6},{9,7},... | collective-permute-start | bytes 786440 | tf_op jit(solution)/shard_map/send_cotangent/ppermute | solution.py:334
  72.2 26.9 %collective-permute-start.21 = (bf16[16,8192]{1,0:T(8,128)(2,1)S(1)}, bf16[16,8192]{1,0:T(8,128)(2,1)S(1)}, u32[]{:S(2)}, u32[]{:S(2)}) collective-permute-start(bf16[16,8192]{1,0:T(8,128)(2,1)S(1)} %get-tuple-element.66), channel_id=1, source_target_pairs={{0,7},{1,6},{2,5},{3,4},{4,3},{5,2},{6,1},{7,0},{8,15},{9,14},{10,... | collective-permute-start | bytes 786440 | tf_op jit(solution)/shard_map/send_cotangent/ppermute | solution.py:334
  76.7 26.8 %collective-permute-start.22 = (bf16[16,8192]{1,0:T(8,128)(2,1)S(1)}, bf16[16,8192]{1,0:T(8,128)(2,1)S(1)}, u32[]{:S(2)}, u32[]{:S(2)}) collective-permute-start(bf16[16,8192]{1,0:T(8,128)(2,1)S(1)} %get-tuple-element.67), channel_id=1, source_target_pairs={{0,15},{1,14},{2,13},{3,12},{4,11},{5,10},{6,9},{7,8},{8,7},{9,6},... | collective-permute-start | bytes 786440 | tf_op jit(solution)/shard_map/send_cotangent/ppermute | solution.py:334
  110.1 115.5 %copy-start.3 = (bf16[16,8320]{1,0:T(8,128)(2,1)}, bf16[16,8320]{1,0:T(8,128)(2,1)S(1)}, u32[]{:S(2)}) copy-start(bf16[16,8320]{1,0:T(8,128)(2,1)S(1)} %get-tuple-element.77.refs_15_.refs_31_.refs_18_) | copy-start | bytes 798724
  110.1 14.5 %collective-permute-start.23 = (bf16[16,8320]{1,0:T(8,128)(2,1)S(1)}, bf16[16,8320]{1,0:T(8,128)(2,1)S(1)}, u32[]{:S(2)}, u32[]{:S(2)}) collective-permute-start(bf16[16,8320]{1,0:T(8,128)(2,1)S(1)} %get-tuple-element.70), channel_id=1, source_target_pairs={{0,12},{1,13},{2,14},{3,15},{4,8},{5,9},{6,10},{7,11},{8,4},{9,5},... | collective-permute-start | bytes 798728 | tf_op jit(solution)/shard_map/send_tokens_second/ppermute | solution.py:334
  110.2 14.4 %collective-permute-start.24 = (bf16[16,8320]{1,0:T(8,128)(2,1)S(1)}, bf16[16,8320]{1,0:T(8,128)(2,1)S(1)}, u32[]{:S(2)}, u32[]{:S(2)}) collective-permute-start(bf16[16,8320]{1,0:T(8,128)(2,1)S(1)} %get-tuple-element.71), channel_id=1, source_target_pairs={{0,5},{1,4},{2,7},{3,6},{4,1},{5,0},{6,3},{7,2},{8,13},{9,12},{10,... | collective-permute-start | bytes 798728 | tf_op jit(solution)/shard_map/send_tokens_second/ppermute | solution.py:334
  110.3 25.3 %collective-permute-start.25 = (bf16[16,8320]{1,0:T(8,128)(2,1)S(1)}, bf16[16,8320]{1,0:T(8,128)(2,1)S(1)}, u32[]{:S(2)}, u32[]{:S(2)}) collective-permute-start(bf16[16,8320]{1,0:T(8,128)(2,1)S(1)} %get-tuple-element.72), channel_id=1, source_target_pairs={{0,13},{1,12},{2,15},{3,14},{4,9},{5,8},{6,11},{7,10},{8,5},{9,4},... | collective-permute-start | bytes 798728 | tf_op jit(solution)/shard_map/send_tokens_second/ppermute | solution.py:334
  111.9 23.8 %collective-permute-start.26 = (bf16[16,8320]{1,0:T(8,128)(2,1)S(1)}, bf16[16,8320]{1,0:T(8,128)(2,1)S(1)}, u32[]{:S(2)}, u32[]{:S(2)}) collective-permute-start(bf16[16,8320]{1,0:T(8,128)(2,1)S(1)} %get-tuple-element.73), channel_id=1, source_target_pairs={{0,6},{1,7},{2,4},{3,5},{4,2},{5,3},{6,0},{7,1},{8,14},{9,15},{10,... | collective-permute-start | bytes 798728 | tf_op jit(solution)/shard_map/send_tokens_second/ppermute | solution.py:334
  115.5 35.3 %collective-permute-start.27 = (bf16[16,8320]{1,0:T(8,128)(2,1)S(1)}, bf16[16,8320]{1,0:T(8,128)(2,1)S(1)}, u32[]{:S(2)}, u32[]{:S(2)}) collective-permute-start(bf16[16,8320]{1,0:T(8,128)(2,1)S(1)} %get-tuple-element.74), channel_id=1, source_target_pairs={{0,14},{1,15},{2,12},{3,13},{4,10},{5,11},{6,8},{7,9},{8,6},{9,7},... | collective-permute-start | bytes 798728 | tf_op jit(solution)/shard_map/send_tokens_second/ppermute | solution.py:334
  124.6 101.0 %copy-start.4 = (bf16[16,8320]{1,0:T(8,128)(2,1)}, bf16[16,8320]{1,0:T(8,128)(2,1)S(1)}, u32[]{:S(2)}) copy-start(bf16[16,8320]{1,0:T(8,128)(2,1)S(1)} %collective-permute-done.23.refs_8_.refs_24_.refs_11_) | copy-start | bytes 798724
  124.6 26.9 %collective-permute-start.28 = (bf16[16,8320]{1,0:T(8,128)(2,1)S(1)}, bf16[16,8320]{1,0:T(8,128)(2,1)S(1)}, u32[]{:S(2)}, u32[]{:S(2)}) collective-permute-start(bf16[16,8320]{1,0:T(8,128)(2,1)S(1)} %get-tuple-element.75), channel_id=1, source_target_pairs={{0,7},{1,6},{2,5},{3,4},{4,3},{5,2},{6,1},{7,0},{8,15},{9,14},{10,... | collective-permute-start | bytes 798728 | tf_op jit(solution)/shard_map/send_tokens_second/ppermute | solution.py:334
  124.6 101.0 %copy-start.5 = (bf16[16,8320]{1,0:T(8,128)(2,1)}, bf16[16,8320]{1,0:T(8,128)(2,1)S(1)}, u32[]{:S(2)}) copy-start(bf16[16,8320]{1,0:T(8,128)(2,1)S(1)} %collective-permute-done.24.refs_9_.refs_25_.refs_12_) | copy-start | bytes 798724
  124.6 48.1 %collective-permute-start.29 = (bf16[16,8320]{1,0:T(8,128)(2,1)S(1)}, bf16[16,8320]{1,0:T(8,128)(2,1)S(1)}, u32[]{:S(2)}, u32[]{:S(2)}) collective-permute-start(bf16[16,8320]{1,0:T(8,128)(2,1)S(1)} %get-tuple-element.76), channel_id=1, source_target_pairs={{0,15},{1,14},{2,13},{3,12},{4,11},{5,10},{6,9},{7,8},{8,7},{9,6},... | collective-permute-start | bytes 798728 | tf_op jit(solution)/shard_map/send_tokens_second/ppermute | solution.py:334
  135.6 101.7 %copy-start.6 = (bf16[16,8320]{1,0:T(8,128)(2,1)}, bf16[16,8320]{1,0:T(8,128)(2,1)S(1)}, u32[]{:S(2)}) copy-start(bf16[16,8320]{1,0:T(8,128)(2,1)S(1)} %collective-permute-done.25.refs_10_.refs_26_.refs_13_) | copy-start | bytes 798724
  135.6 38.8 %collective-permute-start.10 = (bf16[16,8320]{1,0:T(8,128)(2,1)S(1)}, bf16[16,8320]{1,0:T(8,128)(2,1)S(1)}, u32[]{:S(2)}, u32[]{:S(2)}) collective-permute-start(bf16[16,8320]{1,0:T(8,128)(2,1)S(1)} %get-tuple-element.55), channel_id=1, source_target_pairs={{0,9},{1,8},{2,11},{3,10},{4,13},{5,12},{6,15},{7,14},{8,1},{9,0},... | collective-permute-start | bytes 798728 | tf_op jit(solution)/shard_map/send_tokens_first/ppermute | solution.py:334
  135.6 101.7 %copy-start.7 = (bf16[16,8320]{1,0:T(8,128)(2,1)}, bf16[16,8320]{1,0:T(8,128)(2,1)S(1)}, u32[]{:S(2)}) copy-start(bf16[16,8320]{1,0:T(8,128)(2,1)S(1)} %collective-permute-done.26.refs_11_.refs_27_.refs_14_) | copy-start | bytes 798724
  135.6 49.9 %collective-permute-start.11 = (bf16[16,8320]{1,0:T(8,128)(2,1)S(1)}, bf16[16,8320]{1,0:T(8,128)(2,1)S(1)}, u32[]{:S(2)}, u32[]{:S(2)}) collective-permute-start(bf16[16,8320]{1,0:T(8,128)(2,1)S(1)} %get-tuple-element.56), channel_id=1, source_target_pairs={{0,2},{1,3},{2,0},{3,1},{4,6},{5,7},{6,4},{7,5},{8,10},{9,11},{10,... | collective-permute-start | bytes 798728 | tf_op jit(solution)/shard_map/send_tokens_first/ppermute | solution.py:334
  151.5 35.9 %collective-permute-start.12 = (bf16[16,8320]{1,0:T(8,128)(2,1)S(1)}, bf16[16,8320]{1,0:T(8,128)(2,1)S(1)}, u32[]{:S(2)}, u32[]{:S(2)}) collective-permute-start(bf16[16,8320]{1,0:T(8,128)(2,1)S(1)} %get-tuple-element.57), channel_id=1, source_target_pairs={{0,10},{1,11},{2,8},{3,9},{4,14},{5,15},{6,12},{7,13},{8,2},{9,3},... | collective-permute-start | bytes 798728 | tf_op jit(solution)/shard_map/send_tokens_first/ppermute | solution.py:334
  152.2 39.3 %collective-permute-start.13 = (bf16[16,8320]{1,0:T(8,128)(2,1)S(1)}, bf16[16,8320]{1,0:T(8,128)(2,1)S(1)}, u32[]{:S(2)}, u32[]{:S(2)}) collective-permute-start(bf16[16,8320]{1,0:T(8,128)(2,1)S(1)} %get-tuple-element.58), channel_id=1, source_target_pairs={{0,3},{1,2},{2,1},{3,0},{4,7},{5,6},{6,5},{7,4},{8,11},{9,10},{10,... | collective-permute-start | bytes 798728 | tf_op jit(solution)/shard_map/send_tokens_first/ppermute | solution.py:334
  173.4 18.8 %collective-permute-start.14 = (bf16[16,8320]{1,0:T(8,128)(2,1)S(1)}, bf16[16,8320]{1,0:T(8,128)(2,1)S(1)}, u32[]{:S(2)}, u32[]{:S(2)}) collective-permute-start(bf16[16,8320]{1,0:T(8,128)(2,1)S(1)} %get-tuple-element.59), channel_id=1, source_target_pairs={{0,11},{1,10},{2,9},{3,8},{4,15},{5,14},{6,13},{7,12},{8,3},{9,2},... | collective-permute-start | bytes 798728 | tf_op jit(solution)/shard_map/send_tokens_first/ppermute | solution.py:334
  174.4 66.9 %collective-permute-start.30 = (bf16[64,8192]{1,0:T(8,128)(2,1)S(1)}, bf16[64,8192]{1,0:T(8,128)(2,1)}, u32[]{:S(2)}, u32[]{:S(2)}) collective-permute-start(bf16[64,8192]{1,0:T(8,128)(2,1)S(1)} %bitcast.18), channel_id=1, source_target_pairs={{0,4},{1,5},{2,6},{3,7},{4,0},{5,1},{6,2},{7,3},{8,12},{9,13},{10,... | collective-permute-start | bytes 3145736 | tf_op jit(solution)/shard_map/down_factors/ppermute | solution.py:334
  185.5 61.5 %collective-permute-start.31 = (bf16[64,8192]{1,0:T(8,128)(2,1)S(1)}, bf16[64,8192]{1,0:T(8,128)(2,1)}, u32[]{:S(2)}, u32[]{:S(2)}) collective-permute-start(bf16[64,8192]{1,0:T(8,128)(2,1)S(1)} %bitcast.19), channel_id=1, source_target_pairs={{4,8},{5,9},{6,10},{7,11},{8,4},{9,5},{10,6},{11,7},{20,24},{21,25... | collective-permute-start | bytes 3145736 | tf_op jit(solution)/shard_map/down_factors/ppermute | solution.py:334
  187.4 35.7 %collective-permute-start.15 = (bf16[16,8320]{1,0:T(8,128)(2,1)}, bf16[16,8320]{1,0:T(8,128)(2,1)}, u32[]{:S(2)}, u32[]{:S(2)}) collective-permute-start(bf16[16,8320]{1,0:T(8,128)(2,1)} %get-tuple-element.60), channel_id=1, source_target_pairs={{0,4},{1,5},{2,6},{3,7},{4,0},{5,1},{6,2},{7,3},{8,12},{9,13},{10,... | collective-permute-start | bytes 798728 | tf_op jit(solution)/shard_map/send_tokens_first/ppermute | solution.py:334
  192.2 33.3 %collective-permute-start.8 = (bf16[16,8320]{1,0:T(8,128)(2,1)}, bf16[16,8320]{1,0:T(8,128)(2,1)}, u32[]{:S(2)}, u32[]{:S(2)}) collective-permute-start(bf16[16,8320]{1,0:T(8,128)(2,1)} %get-tuple-element.53), channel_id=1, source_target_pairs={{0,8},{1,9},{2,10},{3,11},{4,12},{5,13},{6,14},{7,15},{8,0},{9,1},... | collective-permute-start | bytes 798728 | tf_op jit(solution)/shard_map/send_tokens_first/ppermute | solution.py:334
  193.0 32.7 %collective-permute-start.9 = (bf16[16,8320]{1,0:T(8,128)(2,1)}, bf16[16,8320]{1,0:T(8,128)(2,1)}, u32[]{:S(2)}, u32[]{:S(2)}) collective-permute-start(bf16[16,8320]{1,0:T(8,128)(2,1)} %get-tuple-element.54), channel_id=1, source_target_pairs={{0,1},{1,0},{2,3},{3,2},{4,5},{5,4},{6,7},{7,6},{8,9},{9,8},{10,11... | collective-permute-start | bytes 798728 | tf_op jit(solution)/shard_map/send_tokens_first/ppermute | solution.py:334
  223.1 58.2 %collective-permute-start.35 = (bf16[64,8192]{1,0:T(8,128)(2,1)S(1)}, bf16[64,8192]{1,0:T(8,128)(2,1)S(1)}, u32[]{:S(2)}, u32[]{:S(2)}) collective-permute-start(bf16[64,8192]{1,0:T(8,128)(2,1)S(1)} %bitcast.20), channel_id=1, source_target_pairs={{0,2},{1,3},{2,0},{3,1},{4,6},{5,7},{6,4},{7,5},{8,10},{9,11},{10,... | collective-permute-start | bytes 3145736 | tf_op jit(solution)/shard_map/down_factors/ppermute | solution.py:334
  225.5 76.5 %collective-permute-start.39 = (bf16[64,8192]{1,0:T(8,128)(2,1)S(1)}, bf16[64,8192]{1,0:T(8,128)(2,1)S(1)}, u32[]{:S(2)}, u32[]{:S(2)}) collective-permute-start(bf16[64,8192]{1,0:T(8,128)(2,1)S(1)} %bitcast.21), channel_id=1, source_target_pairs={{0,1},{1,0},{2,3},{3,2},{4,5},{5,4},{6,7},{7,6},{8,9},{9,8},{10,11... | collective-permute-start | bytes 3145736 | tf_op jit(solution)/shard_map/down_factors/ppermute | solution.py:334
  240.9 8.9 %collective-permute-start.47 = (f32[1,1]{1,0:T(1,128)}, f32[1,1]{1,0:T(1,128)}, u32[]{:S(2)}, u32[]{:S(2)}) collective-permute-start(f32[1,1]{1,0:T(1,128)} %slice.75), channel_id=1, source_target_pairs={{0,1},{1,0},{2,3},{3,2},{4,5},{5,4},{6,7},{7,6},{8,9},{9,8},{10,11... | collective-permute-start | bytes 20 | tf_op jit(solution)/shard_map/clip/ppermute | solution.py:23
  241.4 34.0 %collective-permute-start.33 = (bf16[64,8192]{1,0:T(8,128)(2,1)}, bf16[64,8192]{1,0:T(8,128)(2,1)S(1)}, u32[]{:S(2)}, u32[]{:S(2)}) collective-permute-start(bf16[64,8192]{1,0:T(8,128)(2,1)} %collective-permute-done.30.refs_7_), channel_id=1, source_target_pairs={{4,8},{5,9},{6,10},{7,11},{8,4},{9,5},{10,6},{11,7},{20,24},{21,25... | collective-permute-start | bytes 3145736 | tf_op jit(solution)/shard_map/down_factors/ppermute | solution.py:334
  247.0 28.9 %collective-permute-start.32 = (bf16[64,8192]{1,0:T(8,128)(2,1)}, bf16[64,8192]{1,0:T(8,128)(2,1)S(1)}, u32[]{:S(2)}, u32[]{:S(2)}) collective-permute-start(bf16[64,8192]{1,0:T(8,128)(2,1)} %collective-permute-done.31), channel_id=1, source_target_pairs={{4,0},{5,1},{6,2},{7,3},{8,12},{9,13},{10,14},{11,15},{20,16},{21,... | collective-permute-start | bytes 3145736 | tf_op jit(solution)/shard_map/down_factors/ppermute | solution.py:334
  251.1 3.6 collective-permute-start.48
  255.4 17.2 %collective-permute-start.49 = (f32[1,1]{1,0:T(1,128)}, f32[1,1]{1,0:T(1,128)}, u32[]{:S(2)}, u32[]{:S(2)}) collective-permute-start(f32[1,1]{1,0:T(1,128)} %add.45), channel_id=1, source_target_pairs={{0,4},{1,5},{2,6},{3,7},{4,0},{5,1},{6,2},{7,3},{8,12},{9,13},{10,... | collective-permute-start | bytes 20 | tf_op jit(solution)/shard_map/clip/ppermute | solution.py:23
  273.2 27.2 %collective-permute-start.50 = (f32[1,1]{1,0:T(1,128)}, f32[1,1]{1,0:T(1,128)}, u32[]{:S(2)}, u32[]{:S(2)}) collective-permute-start(f32[1,1]{1,0:T(1,128)} %add.46), channel_id=1, source_target_pairs={{0,8},{1,9},{2,10},{3,11},{4,12},{5,13},{6,14},{7,15},{8,0},{9,1},... | collective-permute-start | bytes 20 | tf_op jit(solution)/shard_map/clip/ppermute | solution.py:23
  275.4 27.2 %collective-permute-start.36 = (bf16[64,8192]{1,0:T(8,128)(2,1)}, bf16[64,8192]{1,0:T(8,128)(2,1)S(1)}, u32[]{:S(2)}, u32[]{:S(2)}) collective-permute-start(bf16[64,8192]{1,0:T(8,128)(2,1)} %collective-permute-done.30.refs_7_), channel_id=1, source_target_pairs={{0,2},{1,3},{2,0},{3,1},{4,6},{5,7},{6,4},{7,5},{8,10},{9,11},{10,... | collective-permute-start | bytes 3145736 | tf_op jit(solution)/shard_map/down_factors/ppermute | solution.py:334
  275.9 24.4 %collective-permute-start.34 = (bf16[64,8192]{1,0:T(8,128)(2,1)S(1)}, bf16[64,8192]{1,0:T(8,128)(2,1)S(1)}, u32[]{:S(2)}, u32[]{:S(2)}) collective-permute-start(bf16[64,8192]{1,0:T(8,128)(2,1)S(1)} %collective-permute-done.33), channel_id=1, source_target_pairs={{4,0},{5,1},{6,2},{7,3},{8,12},{9,13},{10,14},{11,15},{20,16},{21,... | collective-permute-start | bytes 3145736 | tf_op jit(solution)/shard_map/down_factors/ppermute | solution.py:334
  281.3 21.4 %collective-permute-start.40 = (bf16[64,8192]{1,0:T(8,128)(2,1)}, bf16[64,8192]{1,0:T(8,128)(2,1)S(1)}, u32[]{:S(2)}, u32[]{:S(2)}) collective-permute-start(bf16[64,8192]{1,0:T(8,128)(2,1)} %collective-permute-done.30.refs_7_), channel_id=1, source_target_pairs={{0,1},{1,0},{2,3},{3,2},{4,5},{5,4},{6,7},{7,6},{8,9},{9,8},{10,11... | collective-permute-start | bytes 3145736 | tf_op jit(solution)/shard_map/down_factors/ppermute | solution.py:334
  300.3 2.9 collective-permute-start.43
  300.4 26.0 %collective-permute-start.37 = (bf16[64,8192]{1,0:T(8,128)(2,1)S(1)}, bf16[64,8192]{1,0:T(8,128)(2,1)S(1)}, u32[]{:S(2)}, u32[]{:S(2)}) collective-permute-start(bf16[64,8192]{1,0:T(8,128)(2,1)S(1)} %broadcast_select_fusion.1.refs_8_), channel_id=1, source_target_pairs={{0,2},{1,3},{2,0},{3,1},{4,6},{5,7},{6,4},{7,5},{8,10},{9,11},{10,... | collective-permute-start | bytes 3145736 | tf_op jit(solution)/shard_map/down_factors/ppermute | solution.py:334
  302.0 46.5 %collective-permute-start.38 = (bf16[64,8192]{1,0:T(8,128)(2,1)S(1)}, bf16[64,8192]{1,0:T(8,128)(2,1)S(1)}, u32[]{:S(2)}, u32[]{:S(2)}) collective-permute-start(bf16[64,8192]{1,0:T(8,128)(2,1)S(1)} %broadcast_select_fusion.refs_9_), channel_id=1, source_target_pairs={{0,2},{1,3},{2,0},{3,1},{4,6},{5,7},{6,4},{7,5},{8,10},{9,11},{10,... | collective-permute-start | bytes 3145736 | tf_op jit(solution)/shard_map/down_factors/ppermute | solution.py:334
  302.6 53.0 %collective-permute-start.41 = (bf16[64,8192]{1,0:T(8,128)(2,1)S(1)}, bf16[64,8192]{1,0:T(8,128)(2,1)}, u32[]{:S(2)}, u32[]{:S(2)}) collective-permute-start(bf16[64,8192]{1,0:T(8,128)(2,1)S(1)} %broadcast_select_fusion.1.refs_8_), channel_id=1, source_target_pairs={{0,1},{1,0},{2,3},{3,2},{4,5},{5,4},{6,7},{7,6},{8,9},{9,8},{10,11... | collective-permute-start | bytes 3145736 | tf_op jit(solution)/shard_map/down_factors/ppermute | solution.py:334
  302.7 52.9 %collective-permute-start.44 = (bf16[64,8192]{1,0:T(8,128)(2,1)S(1)}, bf16[64,8192]{1,0:T(8,128)(2,1)}, u32[]{:S(2)}, u32[]{:S(2)}) collective-permute-start(bf16[64,8192]{1,0:T(8,128)(2,1)S(1)} %collective-permute-done.36.refs_11_), channel_id=1, source_target_pairs={{0,1},{1,0},{2,3},{3,2},{4,5},{5,4},{6,7},{7,6},{8,9},{9,8},{10,11... | collective-permute-start | bytes 3145736 | tf_op jit(solution)/shard_map/down_factors/ppermute | solution.py:334
  303.2 52.4 %collective-permute-start.42 = (bf16[64,8192]{1,0:T(8,128)(2,1)S(1)}, bf16[64,8192]{1,0:T(8,128)(2,1)}, u32[]{:S(2)}, u32[]{:S(2)}) collective-permute-start(bf16[64,8192]{1,0:T(8,128)(2,1)S(1)} %broadcast_select_fusion.refs_9_), channel_id=1, source_target_pairs={{0,1},{1,0},{2,3},{3,2},{4,5},{5,4},{6,7},{7,6},{8,9},{9,8},{10,11... | collective-permute-start | bytes 3145736 | tf_op jit(solution)/shard_map/down_factors/ppermute | solution.py:334
  326.5 29.1 %collective-permute-start.45 = (bf16[64,8192]{1,0:T(8,128)(2,1)S(1)}, bf16[64,8192]{1,0:T(8,128)(2,1)}, u32[]{:S(2)}, u32[]{:S(2)}) collective-permute-start(bf16[64,8192]{1,0:T(8,128)(2,1)S(1)} %collective-permute-done.37.refs_12_), channel_id=1, source_target_pairs={{0,1},{1,0},{2,3},{3,2},{4,5},{5,4},{6,7},{7,6},{8,9},{9,8},{10,11... | collective-permute-start | bytes 3145736 | tf_op jit(solution)/shard_map/down_factors/ppermute | solution.py:334
  348.5 7.1 %collective-permute-start.46 = (bf16[64,8192]{1,0:T(8,128)(2,1)S(1)}, bf16[64,8192]{1,0:T(8,128)(2,1)}, u32[]{:S(2)}, u32[]{:S(2)}) collective-permute-start(bf16[64,8192]{1,0:T(8,128)(2,1)S(1)} %collective-permute-done.38.refs_13_), channel_id=1, source_target_pairs={{0,1},{1,0},{2,3},{3,2},{4,5},{5,4},{6,7},{7,6},{8,9},{9,8},{10,11... | collective-permute-start | bytes 3145736 | tf_op jit(solution)/shard_map/down_factors/ppermute | solution.py:334
  (49 other events, 1685.1 us)

commit v3 on v2

--- a/solution.py
+++ b/solution.py
@@ -10,6 +10,7 @@
 EPS = 1e-06
 VMEM_LIMIT = 48 * 1024 * 1024
 LANES = 128
+WINDOW = 5
 LAST = (((1,), (1,)), ((), ()))
 FIRST = (((0,), (0,)), ((), ()))
 
@@ -59,7 +60,9 @@
     ]
     operands = list(blocks)
     if with_extra:
-        in_specs += [pl.BlockSpec((block.shape[0], LANES), lambda i: (0, width // LANES)) for block in blocks]
+        in_specs += [
+            pl.BlockSpec((block.shape[0], LANES), lambda i, at=block.shape[1] // LANES - 1: (0, at)) for block in blocks
+        ]
         operands += list(blocks)
         out_specs.append(pl.BlockSpec((slots, LANES), lambda i: (0, 0)))
         out_shape.append(jax.ShapeDtypeStruct((slots, LANES), jnp.bfloat16))
@@ -77,41 +80,6 @@
             transcendentals=0,
         ),
     )(*operands, weight)
-
-
-def low_kernel(scale, count, *refs):
-    blocks, weight_ref, low_ref, total = refs[:count], *refs[count:]
-    step = pl.program_id(0)
-
-    @pl.when(step == 0)
-    def _():
-        total[...] = jnp.zeros_like(total)
-
-    rows = jnp.concatenate([ref[...] for ref in blocks], axis=0)
-    total[...] += lax.dot_general(rows, weight_ref[...], LAST, preferred_element_type=jnp.float32)
-
-    @pl.when(step == pl.num_programs(0) - 1)
-    def _():
-        low_ref[...] = (scale * total[...]).astype(low_ref.dtype)
-
-
-def low_products(blocks, weight, scale):
-    slots = sum(block.shape[0] for block in blocks)
-    rank, width = weight.shape
-    chunk = min(width, 2048)
-    return pl.pallas_call(
-        lambda *refs: low_kernel(scale, len(blocks), *refs),
-        grid=(width // chunk,),
-        in_specs=[pl.BlockSpec((block.shape[0], chunk), lambda i: (0, i)) for block in blocks]
-        + [pl.BlockSpec((rank, chunk), lambda i: (0, i))],
-        out_specs=pl.BlockSpec((slots, rank), lambda i: (0, 0)),
-        out_shape=jax.ShapeDtypeStruct((slots, rank), jnp.bfloat16),
-        scratch_shapes=[pltpu.VMEM((slots, rank), jnp.float32)],
-        compiler_params=pltpu.CompilerParams(vmem_limit_bytes=VMEM_LIMIT),
-        cost_estimate=pl.CostEstimate(
-            flops=2 * slots * width * rank, bytes_accessed=2 * width * (slots + rank), transcendentals=0
-        ),
-    )(*blocks, weight)
 
 
 def slot_targets(cap, me, owner_ref, column_ref, row_ref):
@@ -125,11 +93,11 @@
     return partner, partner * cap + position
 
 
-def place_kernel(partners, cap, with_extra, me_ref, owner_ref, column_ref, row_ref, values_ref, *refs):
+def place_kernel(partners, cap, with_live, me_ref, owner_ref, column_ref, row_ref, values_ref, *refs):
     placing = refs[-1]
-    outs = refs[1:-1] if with_extra else refs[:-1]
+    low_refs, outs = refs[: len(refs) - 1 - len(partners)], refs[len(refs) - 1 - len(partners) : -1]
     step = pl.program_id(0)
-    rows = row_ref.shape[1]
+    rows, chunk = row_ref.shape[1], values_ref.shape[1]
 
     @pl.when(step == 0)
     def _():
@@ -142,27 +110,32 @@
 
     placed = jnp.dot(placing[...], values_ref[...], preferred_element_type=jnp.float32).astype(jnp.bfloat16)
     for at, out in enumerate(outs):
-        out[...] = placed[at * cap : (at + 1) * cap]
-
-    if with_extra:
+        if with_live:
+            out[:, pl.ds(pl.multiple_of(step * chunk, chunk), chunk)] = placed[at * cap : (at + 1) * cap]
+        else:
+            out[...] = placed[at * cap : (at + 1) * cap]
+
+    if with_live:
 
         @pl.when(step == pl.num_programs(0) - 1)
         def _():
-            live = jnp.sum(placing[...].astype(jnp.float32), axis=1, keepdims=True)
-            low = refs[0][...].astype(jnp.float32)
-            extra = jnp.concatenate(
-                [low, jnp.broadcast_to(live, (live.shape[0], LANES - low.shape[1]))], axis=1
-            ).astype(jnp.bfloat16)
+            live = jnp.sum(placing[...].astype(jnp.float32), axis=1, keepdims=True).astype(jnp.bfloat16)
             for at, out in enumerate(outs):
-                out[:, out.shape[1] - LANES :] = extra[at * cap : (at + 1) * cap]
-
-
-def place(partners, cap, me, owner, tenant, values, low=None):
+                full = out.shape[1]
+                out[:, full - LANES :] = jnp.broadcast_to(live[at * cap : (at + 1) * cap], (cap, LANES))
+                if low_refs:
+                    low = low_refs[0][...].astype(jnp.float32)
+                    lanes = [low[q * cap : (q + 1) * cap] for q in range(low.shape[0] // cap)]
+                    out[:, pl.num_programs(0) * chunk : full - LANES] = jnp.concatenate(lanes, axis=1).astype(
+                        jnp.bfloat16
+                    )
+
+
+def place(partners, cap, me, owner, tenant, values, with_live=False, low=None):
     rows, width = values.shape
     adapters = owner.shape[0]
-    with_extra = low is not None
-    full = width + LANES if with_extra else width
-    chunk = full // 5 if with_extra and full % (5 * LANES) == 0 else 2048
+    full = width + (LANES if with_live else 0) + (low.size // cap if low is not None else 0)
+    chunk = min(width, 2048)
     still = lambda shape: pl.BlockSpec(shape, lambda i: (0, 0))
     in_specs = [
         pl.BlockSpec(memory_space=pltpu.SMEM),
@@ -172,14 +145,15 @@
         pl.BlockSpec((rows, chunk), lambda i: (0, i)),
     ]
     operands = [me.reshape(1, 1), owner.reshape(adapters, 1), tenant, tenant.reshape(1, rows), values]
-    if with_extra:
+    if low is not None:
         in_specs.append(still(low.shape))
         operands.append(low)
-    return pl.pallas_call(
-        lambda *refs: place_kernel(partners, cap, with_extra, *refs),
-        grid=(full // chunk,),
+    out_spec = still((cap, full)) if with_live else pl.BlockSpec((cap, chunk), lambda i: (0, i))
+    return pl.pallas_call(
+        lambda *refs: place_kernel(partners, cap, with_live, *refs),
+        grid=(width // chunk,),
         in_specs=in_specs,
-        out_specs=[pl.BlockSpec((cap, chunk), lambda i: (0, i))] * len(partners),
+        out_specs=[out_spec] * len(partners),
         out_shape=[jax.ShapeDtypeStruct((cap, full), jnp.bfloat16)] * len(partners),
         scratch_shapes=[pltpu.VMEM((len(partners) * cap, rows), jnp.bfloat16)],
         compiler_params=pltpu.CompilerParams(vmem_limit_bytes=VMEM_LIMIT),
@@ -191,30 +165,56 @@
     )(*operands)
 
 
-def input_grad_kernel(cap, count, me_ref, owner_ref, column_ref, row_ref, partner_ref, extra_ref, *refs):
-    pieces, out_ref, left = refs[:count], refs[count], refs[count + 1]
+def back_kernel(count, stacked, low_ref, weight_ref, *outs):
+    cap = outs[0].shape[0]
+    rank = weight_ref.shape[0]
+    if stacked:
+        low = low_ref[...].astype(jnp.float32)
+        low = jnp.concatenate([low[:, at * rank : (at + 1) * rank] for at in range(count)], axis=0)
+        low = low.astype(jnp.bfloat16)
+    else:
+        low = low_ref[...]
+    rows = jnp.dot(low, weight_ref[...], preferred_element_type=jnp.float32).astype(jnp.bfloat16)
+    for at, out in enumerate(outs):
+        out[...] = rows[at * cap : (at + 1) * cap]
+
+
+def back_rows(count, cap, low, weight, low_spec, stacked):
+    rank, width = weight.shape
+    chunk = min(width, 2048)
+    return pl.pallas_call(
+        lambda *refs: back_kernel(count, stacked, *refs),
+        grid=(width // chunk,),
+        in_specs=[low_spec, pl.BlockSpec((rank, chunk), lambda i: (0, i))],
+        out_specs=[pl.BlockSpec((cap, chunk), lambda i: (0, i))] * count,
+        out_shape=[jax.ShapeDtypeStruct((cap, width), jnp.bfloat16)] * count,
+        compiler_params=pltpu.CompilerParams(vmem_limit_bytes=VMEM_LIMIT),
+        cost_estimate=pl.CostEstimate(
+            flops=2 * count * cap * rank * width, bytes_accessed=2 * width * (rank + count * cap), transcendentals=0
+        ),
+    )(low, weight)
+
+
+def input_grad_kernel(cap, count, me_ref, owner_ref, column_ref, row_ref, *refs):
+    blocks, out_ref, placing = refs[:count], refs[count], refs[count + 1]
     step = pl.program_id(0)
-    rows, slots = row_ref.shape[1], extra_ref.shape[0]
-    rank = pieces[0].shape[0]
 
     @pl.when(step == 0)
     def _():
-        partner, target = slot_targets(cap, me_ref[0, 0], owner_ref, column_ref, row_ref)
-        slot = lax.broadcasted_iota(jnp.int32, (slots, rows), 0)
-        for at in range(count):
-            picked = jnp.where((slot == target) & (partner == partner_ref[at]), 1.0, 0.0).astype(jnp.bfloat16)
-            low = lax.dot_general(picked, extra_ref[:, :rank], FIRST, preferred_element_type=jnp.float32)
-            left[:, at * rank : (at + 1) * rank] = low.astype(left.dtype)
-
-    stacked = jnp.concatenate([ref[...] for ref in pieces], axis=0)
-    out_ref[...] = jnp.dot(left[...], stacked, preferred_element_type=jnp.float32).astype(out_ref.dtype)
-
-
-def input_grad_of(cap, me, owner, tenant, partners, extra, pieces):
-    rows, adapters, slots = tenant.shape[0], owner.shape[0], extra.shape[0]
-    rank, width = pieces[0].shape
-    count = len(pieces)
-    chunk = min(width, 1024)
+        _, target = slot_targets(cap, me_ref[0, 0], owner_ref, column_ref, row_ref)
+        slot = lax.broadcasted_iota(jnp.int32, placing.shape, 0)
+        placing[...] = jnp.where(slot == target, 1.0, 0.0).astype(placing.dtype)
+
+    returned = jnp.concatenate([ref[...] for ref in blocks], axis=0)
+    out_ref[...] = lax.dot_general(placing[...], returned, FIRST, preferred_element_type=jnp.float32).astype(
+        out_ref.dtype
+    )
+
+
+def input_grad_of(cap, me, owner, tenant, blocks):
+    rows, adapters, count = tenant.shape[0], owner.shape[0], len(blocks)
+    width = blocks[0].shape[1]
+    chunk = min(width, 2048)
     still = lambda shape: pl.BlockSpec(shape, lambda i: (0, 0))
     return pl.pallas_call(
         lambda *refs: input_grad_kernel(cap, count, *refs),
@@ -224,20 +224,18 @@
             still((adapters, 1)),
             still((rows, 1)),
             still((1, rows)),
-            pl.BlockSpec(memory_space=pltpu.SMEM),
-            still((slots, LANES)),
         ]
-        + [pl.BlockSpec((rank, chunk), lambda i: (0, i))] * count,
+        + [pl.BlockSpec((cap, chunk), lambda i: (0, i))] * count,
         out_specs=pl.BlockSpec((rows, chunk), lambda i: (0, i)),
         out_shape=jax.ShapeDtypeStruct((rows, width), jnp.bfloat16),
-        scratch_shapes=[pltpu.VMEM((rows, count * rank), jnp.bfloat16)],
-        compiler_params=pltpu.CompilerParams(vmem_limit_bytes=VMEM_LIMIT),
-        cost_estimate=pl.CostEstimate(
-            flops=2 * rows * count * rank * width,
-            bytes_accessed=2 * width * (rows + count * rank),
+        scratch_shapes=[pltpu.VMEM((count * cap, rows), jnp.bfloat16)],
+        compiler_params=pltpu.CompilerParams(vmem_limit_bytes=VMEM_LIMIT),
+        cost_estimate=pl.CostEstimate(
+            flops=2 * rows * count * cap * width,
+            bytes_accessed=2 * width * (rows + count * cap),
             transcendentals=0,
         ),
-    )(me.reshape(1, 1), owner.reshape(adapters, 1), tenant, tenant.reshape(1, rows), partners, extra, *pieces)
+    )(me.reshape(1, 1), owner.reshape(adapters, 1), tenant, tenant.reshape(1, rows), *blocks)
 
 
 def fold_one(low, gram, scale, amount):
@@ -330,77 +328,81 @@
     return jnp.minimum(1.0, 1.0 / jnp.sqrt(mean_sq + EPS))
 
 
-def permute(value, pairs):
-    return lax.ppermute(value, "blk", pairs)
-
-
-def gathered(weight, me):
-    lines = [(z, rest) for z in range(4) for rest in range(4)]
-    hop = lambda ends: [(z * 4 + rest, ends[z] * 4 + rest) for z, rest in lines if z in ends]
-    near = permute(weight, hop({0: 1, 1: 0, 2: 3, 3: 2}))
-    across = permute(weight, hop({1: 2, 2: 1}))
-    across_near = permute(near, hop({1: 2, 2: 1}))
-    outward = permute(across, hop({1: 0, 2: 3}))
-    outward_near = permute(across_near, hop({1: 0, 2: 3}))
-    plane = me // 4
-    inner = (plane == 1) | (plane == 2)
-    second = jnp.where(inner, across, outward)
-    third = jnp.where(inner, across_near, outward_near)
-    pieces = [weight, near, second, third]
-    partners = [0, 4, jnp.where(inner, 12, 8), jnp.where(inner, 8, 12)]
-    for bit in (2, 1):
-        pieces += [permute(piece, [(i, i ^ bit) for i in range(16)]) for piece in pieces]
-        partners += [partner + bit for partner in partners]
-    return pieces, jnp.stack([jnp.asarray(partner, jnp.int32) for partner in partners])
+class Line:
+    def __init__(self, window):
+        self.window = window
+        self.results = []
+
+    def swap(self, value, partner):
+        if len(self.results) >= self.window:
+            value, _ = lax.optimization_barrier((value, self.results[-self.window]))
+        size = lax.axis_size("blk")
+        result = lax.ppermute(value, "blk", [(i, i ^ partner) for i in range(size)])
+        self.results.append(result)
+        return result
 
 
 def per_device_blocks(tokens, cotangent, tenant, owner, down_factor_table, up_factor_table):
     rows, width = tokens.shape
     count_blk = lax.axis_size("blk")
+    half = count_blk // 2
     adapters = owner.shape[0]
     rank = down_factor_table.shape[1]
     cap = 2 * rows // adapters
     down_weight = down_factor_table[0]
     up_weight = up_factor_table[0]
     me = lax.axis_index("blk").astype(jnp.int32)
-    order = [8, 1, 9, 2, 10, 3, 11, 4, 12, 5, 13, 6, 14, 7, 15]
-    first, second = order[:8], order[8:]
-
-    def swap(value, partner):
-        return permute(value, [(i, i ^ partner) for i in range(count_blk)])
-
-    with jax.named_scope("down_factors"):
-        pieces, partners = gathered(down_weight, me)
-    with jax.named_scope("send_cotangent"):
-        own_dy, *sent_dy = place([0] + order, cap, me, owner, tenant, cotangent)
-        got_dy = [swap(block, partner) for block, partner in zip(sent_dy, order)]
-    with jax.named_scope("grad_hidden_first"):
-        low_first = low_products(got_dy[:8], up_weight, SCALE)
-    with jax.named_scope("send_tokens_first"):
-        sent_first = place(first, cap, me, owner, tenant, tokens, low_first)
-        got_x = [swap(block, partner) for block, partner in zip(sent_first, first)]
-    with jax.named_scope("grad_hidden"):
-        blocks_dy = got_dy + [own_dy]
-        grad_hidden, gram_dy = rows_products(blocks_dy, up_weight, SCALE)
-    with jax.named_scope("send_tokens_second"):
-        *sent_second, own_x = place(second + [0], cap, me, owner, tenant, tokens, grad_hidden[8 * cap :])
-        got_x += [swap(block, partner) for block, partner in zip(sent_second, second)]
-    with jax.named_scope("hidden"):
-        blocks_x = got_x + [own_x]
-        hidden, gram_x, extra = rows_products(blocks_x, down_weight, 1.0, with_extra=True)
-    with jax.named_scope("fold"):
-        amount = jnp.sum(extra[:, rank], dtype=jnp.float32).reshape(1, 1)
-        left_a, left_b, local_sq = fold(amount, grad_hidden, gram_x, hidden, gram_dy)
-    with jax.named_scope("clip"):
-        factor = clip_factor(local_sq, adapters, rank, width)
-    with jax.named_scope("grads"):
-        grad_a, grad_b = grads(factor, left_a, left_b, blocks_x, blocks_dy, width)
-    with jax.named_scope("input_grad"):
-        by_partner = dict(zip(order + [0], range(count_blk)))
-        extra = jnp.concatenate(
-            [extra[by_partner[s] * cap : (by_partner[s] + 1) * cap] for s in range(count_blk)], axis=0
-        )
-        input_grad = input_grad_of(cap, me, owner, tenant, partners, extra, pieces)
+    line = Line(WINDOW)
+    low_of = lambda low, first, count: low[first * cap : (first + count) * cap]
+
+    order = [half]
+    for s in range(1, half):
+        order += [s, half + s]
+    sent_dy = place(list(range(count_blk)), cap, me, owner, tenant, cotangent)
+    got_dy = {0: sent_dy[0]}
+    for s in order:
+        got_dy[s] = line.swap(sent_dy[s], s)
+
+    others = [s for s in range(count_blk) if s != half]
+    sent_x = dict(zip(others, place(others, cap, me, owner, tenant, tokens, with_live=True)))
+    got_x = {0: sent_x[0]}
+    parts = 4
+    mirror_parts = []
+    for part in range(parts):
+        columns = slice(part * width // parts, (part + 1) * width // parts)
+        mirror_parts.append(line.swap(down_weight[:, columns], half))
+        got_x[part + 1] = line.swap(sent_x[part + 1], part + 1)
+
+    blocks_dy = [got_dy[s] for s in range(count_blk)]
+    grad_hidden, gram_dy = rows_products(blocks_dy, up_weight, SCALE)
+    (sent_mirror,) = place(
+        [half], cap, me, owner, tenant, tokens, with_live=True, low=low_of(grad_hidden, half, half)
+    )
+    got_x[half] = line.swap(sent_mirror, half)
+    still = pl.BlockSpec((half * cap, rank), lambda i: (0, 0))
+    own_back = back_rows(half, cap, low_of(grad_hidden, 0, half), down_weight, still, False)
+    back = {0: own_back[0]}
+    rest = [s for s in order if s > parts and s != half]
+    for at, s in enumerate(rest):
+        got_x[s] = line.swap(sent_x[s], s)
+        if at % 2 == 1 and len(back) < half:
+            back[len(back)] = line.swap(own_back[len(back)], len(back))
+    while len(back) < half:
+        back[len(back)] = line.swap(own_back[len(back)], len(back))
+    mirror_low = pl.BlockSpec((cap, half * rank), lambda i: (0, width // (half * rank)))
+    mirror_weight = jnp.concatenate(mirror_parts, axis=1)
+    mirror_back = back_rows(half, cap, got_x[half], mirror_weight, mirror_low, True)
+    back[half] = mirror_back[0]
+    for s in range(1, half):
+        back[half + s] = line.swap(mirror_back[s], s)
+
+    blocks_x = [got_x[s] for s in range(count_blk)]
+    hidden, gram_x, live = rows_products(blocks_x, down_weight, 1.0, with_extra=True)
+    amount = jnp.sum(live[:, 0], dtype=jnp.float32).reshape(1, 1)
+    left_a, left_b, local_sq = fold(amount, grad_hidden, gram_x, hidden, gram_dy)
+    factor = clip_factor(local_sq, adapters, rank, width)
+    grad_a, grad_b = grads(factor, left_a, left_b, blocks_x, blocks_dy, width)
+    input_grad = input_grad_of(cap, me, owner, tenant, [back[s] for s in range(count_blk)])
     return (input_grad, grad_a[None], grad_b[None])
 
 

time: 371 us -> 323 us (0.87)
  starting transfers between devices: 98 us -> 62.3 us
  local copies, waits for them, and re-layouts: 12.1 us -> 4.37 us
  Pallas kernels: 39.9 us -> 36 us
    ppermute x47 -> x48, starting transfers between devices: 76.4 us -> 54.9 us  [swap(): result = lax.ppermute(value, 'blk', [(i, i ^ partner) for i in range(size)])]
    ppermute x4, starting transfers between devices: 21.6 us -> 7.42 us  [total_over_blk(): lax.ppermute(value, 'blk', [(i, i ^ step) for i in range(size)])]
    unnamed x140 -> x35, local copies, waits for them, and re-layouts: 10.7 us -> 2.33 us
    pallas_call x1, Pallas kernels: 10.1 us -> 3.21 us  [input_grad_of(): pl.pallas_call(lambda *refs: input_grad_kernel(cap, count, *refs), grid=(...]
    pallas_call x4 -> x5, Pallas kernels: 10.8 us -> 12.7 us  [the longest x3 7.88 us: place(): pl.pallas_call(lambda *refs: place_kernel(partners, cap, with_live, *refs...]
    ppermute x47 -> x48, waiting for transfers between devices: 207 us -> 208 us  [swap(): result = lax.ppermute(value, 'blk', [(i, i ^ partner) for i in range(size)])]
  transfers between devices with their start and end apart: 51 -> 52, of which waited for: 22 -> 25; matrix products, arithmetic and copies ran while one was open for 1% -> 1% of each run, Pallas kernels for 5% -> 9%
where the time goes in v3:
time: 323 us; the launch traced here: 319 us
  waiting for transfers between devices  212 us (66%)
  starting transfers between devices  62.3 us (19%)
  Pallas kernels  36 us (11%)
  local copies, waits for them, and re-layouts  4.37 us (1%)
  between operations  4.19 us (1%)
    ppermute x48, waiting for transfers between devices, swap(): result = lax.ppermute(value, 'blk', [(i, i ^ partner) for i in range(size)])  208 us
    ppermute x48, starting transfers between devices, swap(): result = lax.ppermute(value, 'blk', [(i, i ^ partner) for i in range(size)])  54.9 us
    pallas_call x2, Pallas kernels, rows_products(): pl.pallas_call(lambda *refs: rows_kernel(scale, len(blocks), with_extra,...  11.3 us
    pallas_call x3, Pallas kernels, place(): pl.pallas_call(lambda *refs: place_kernel(partners, cap, with_live, *refs...  7.88 us
    ppermute x4, starting transfers between devices, total_over_blk(): lax.ppermute(value, 'blk', [(i, i ^ step) for i in range(size)])  7.42 us
  transfers between devices with their start and end apart: 52, of which 25 were waited for; matrix products, arithmetic and copies ran while one was open for 1% of the time, Pallas kernels for 9%

profile of v3, /device:TPU:16, one launch (start us, length us, event | category | flops | bytes accessed | tf_op | source)
XLA Modules:
  0.0 319.2 jit_solution(6266891382950937143)
XLA Ops:
  0.6 0.9 copy.16.refs_2_
  1.6 0.7 copy.15.refs_1_
  2.3 0.7 copy-done.13
  2.9 4.0 %shard_map.85 = (bf16[16,8192]{1,0:T(8,128)(2,1)S(1)}, bf16[16,8192]{1,0:T(8,128)(2,1)S(1)}, bf16[16,8192]{1,0:T(8,128)(2,1)S(1)}, bf16[16,8192]{1,0:T(8,128)(2,...) custom-call(s32[1,1]{1,0:T(1,128)} %bitcast.refs_0_, ...), custom_call_target="tpu_custom_call" | custom-call | flops 536870912 | bytes 6291456 | tf_op jit(solution)/shard_map/pallas_call | solution.py:152
  7.1 1.4 collective-permute-start.6
  8.4 2.4 collective-permute-start.4
  11.1 2.2 collective-permute-start.8
  13.3 1.5 collective-permute-start.1
  14.8 22.7 %collective-permute-done.6.refs_10_.refs_29_ = bf16[16,8192]{1,0:T(8,128)(2,1)S(1)} collective-permute-done((bf16[16,8192]{1,0:T(8,128)(2,1)S(1)}, bf16[16,8192]{1,0:T(8,128)(2,1)S(1)}, u32[]{:S(2)}, u32[]{:S(2)}) %collective-permute-start.6) | collective-permute-done | bytes 262176 | tf_op jit(solution)/shard_map/ppermute | solution.py:340
  37.5 3.7 %collective-permute-start.7 = (bf16[16,8192]{1,0:T(8,128)(2,1)S(1)}, bf16[16,8192]{1,0:T(8,128)(2,1)S(1)}, u32[]{:S(2)}, u32[]{:S(2)}) collective-permute-start(bf16[16,8192]{1,0:T(8,128)(2,1)S(1)} %get-tuple-element.114), channel_id=1, source_target_pairs={{0,5},{1,4},{2,7},{3,6},{4,1},{5,0},{6,3},{7,2},{8,13},{9,12},{10,... | collective-permute-start | bytes 786440 | tf_op jit(solution)/shard_map/ppermute | solution.py:340
  41.2 2.0 collective-permute-done.4.refs_9_.refs_28_
  43.2 4.1 %collective-permute-start.5 = (bf16[16,8192]{1,0:T(8,128)(2,1)S(1)}, bf16[16,8192]{1,0:T(8,128)(2,1)S(1)}, u32[]{:S(2)}, u32[]{:S(2)}) collective-permute-start(bf16[16,8192]{1,0:T(8,128)(2,1)S(1)} %get-tuple-element.111), channel_id=1, source_target_pairs={{0,4},{1,5},{2,6},{3,7},{4,0},{5,1},{6,2},{7,3},{8,12},{9,13},{10,... | collective-permute-start | bytes 786440 | tf_op jit(solution)/shard_map/ppermute | solution.py:340
  47.2 1.6 collective-permute-done.2.refs_8_.refs_27_
  48.8 5.2 %collective-permute-done.8.refs_11_.refs_30_ = bf16[16,8192]{1,0:T(8,128)(2,1)S(1)} collective-permute-done((bf16[16,8192]{1,0:T(8,128)(2,1)S(1)}, bf16[16,8192]{1,0:T(8,128)(2,1)S(1)}, u32[]{:S(2)}, u32[]{:S(2)}) %collective-permute-start.8) | collective-permute-done | bytes 262176 | tf_op jit(solution)/shard_map/ppermute | solution.py:340
  54.0 5.5 %collective-permute-start.9 = (bf16[16,8192]{1,0:T(8,128)(2,1)S(1)}, bf16[16,8192]{1,0:T(8,128)(2,1)S(1)}, u32[]{:S(2)}, u32[]{:S(2)}) collective-permute-start(bf16[16,8192]{1,0:T(8,128)(2,1)S(1)} %get-tuple-element.118), channel_id=1, source_target_pairs={{0,6},{1,7},{2,4},{3,5},{4,2},{5,3},{6,0},{7,1},{8,14},{9,15},{10,... | collective-permute-start | bytes 786440 | tf_op jit(solution)/shard_map/ppermute | solution.py:340
  59.5 2.8 shard_map.88
  62.3 1.0 collective-permute-start.14
  63.3 15.1 %collective-permute-done.5.refs_4_.refs_23_ = bf16[16,8192]{1,0:T(8,128)(2,1)S(1)} collective-permute-done((bf16[16,8192]{1,0:T(8,128)(2,1)S(1)}, bf16[16,8192]{1,0:T(8,128)(2,1)S(1)}, u32[]{:S(2)}, u32[]{:S(2)}) %collective-permute-start.5) | collective-permute-done | bytes 262176 | tf_op jit(solution)/shard_map/ppermute | solution.py:340
  78.4 1.4 collective-permute-start.12
  79.8 15.5 %collective-permute-done.9.refs_6_.refs_25_ = bf16[16,8192]{1,0:T(8,128)(2,1)S(1)} collective-permute-done((bf16[16,8192]{1,0:T(8,128)(2,1)S(1)}, bf16[16,8192]{1,0:T(8,128)(2,1)S(1)}, u32[]{:S(2)}, u32[]{:S(2)}) %collective-permute-start.9) | collective-permute-done | bytes 262176 | tf_op jit(solution)/shard_map/ppermute | solution.py:340
  95.4 0.8 fusion
  96.2 3.4 %collective-permute-start.11 = (bf16[16,8192]{1,0:T(8,128)(2,1)S(1)}, bf16[16,8192]{1,0:T(8,128)(2,1)S(1)}, u32[]{:S(2)}, u32[]{:S(2)}) collective-permute-start(bf16[16,8192]{1,0:T(8,128)(2,1)S(1)} %get-tuple-element.122), channel_id=1, source_target_pairs={{0,7},{1,6},{2,5},{3,4},{4,3},{5,2},{6,1},{7,0},{8,15},{9,14},{10,... | collective-permute-start | bytes 786440 | tf_op jit(solution)/shard_map/ppermute | solution.py:340
  99.6 7.3 %collective-permute-done.13.refs_14_.refs_33_ = bf16[16,8192]{1,0:T(8,128)(2,1)S(1)} collective-permute-done((bf16[16,8192]{1,0:T(8,128)(2,1)S(1)}, bf16[16,8192]{1,0:T(8,128)(2,1)S(1)}, u32[]{:S(2)}, u32[]{:S(2)}) %collective-permute-start.13) | collective-permute-done | bytes 262176 | tf_op jit(solution)/shard_map/ppermute | solution.py:340
  106.9 2.9 collective-permute-start.18
  109.8 13.4 %collective-permute-done.12.refs_13_.refs_32_ = bf16[16,8192]{1,0:T(8,128)(2,1)S(1)} collective-permute-done((bf16[16,8192]{1,0:T(8,128)(2,1)S(1)}, bf16[16,8192]{1,0:T(8,128)(2,1)S(1)}, u32[]{:S(2)}, u32[]{:S(2)}) %collective-permute-start.12) | collective-permute-done | bytes 262176 | tf_op jit(solution)/shard_map/ppermute | solution.py:340
  123.3 11.2 %collective-permute-done.21 = bf16[64,2048]{1,0:T(8,128)(2,1)S(1)} collective-permute-done((bf16[64,2048]{1,0:T(8,128)(2,1)S(1)}, bf16[64,2048]{1,0:T(8,128)(2,1)S(1)}, u32[]{:S(2)}, u32[]{:S(2)}) %collective-permute-start.21) | collective-permute-done | bytes 262176 | tf_op jit(solution)/shard_map/ppermute | solution.py:340
  134.5 1.4 collective-permute-start.22
  135.9 4.2 %collective-permute-done.18 = bf16[64,2048]{1,0:T(8,128)(2,1)S(1)} collective-permute-done((bf16[64,2048]{1,0:T(8,128)(2,1)S(1)}, bf16[64,2048]{1,0:T(8,128)(2,1)S(1)}, u32[]{:S(2)}, u32[]{:S(2)}) %collective-permute-start.18) | collective-permute-done | bytes 262176 | tf_op jit(solution)/shard_map/ppermute | solution.py:340
  140.1 1.3 collective-permute-start.19
  141.5 10.0 %collective-permute-done.25 = bf16[64,2048]{1,0:T(8,128)(2,1)S(1)} collective-permute-done((bf16[64,2048]{1,0:T(8,128)(2,1)S(1)}, bf16[64,2048]{1,0:T(8,128)(2,1)S(1)}, u32[]{:S(2)}, u32[]{:S(2)}) %collective-permute-start.25) | collective-permute-done | bytes 262176 | tf_op jit(solution)/shard_map/ppermute | solution.py:340
  151.5 3.4 %collective-permute-start.16 = (bf16[64,2048]{1,0:T(8,128)(2,1)}, bf16[64,2048]{1,0:T(8,128)(2,1)S(1)}, u32[]{:S(2)}, u32[]{:S(2)}) collective-permute-start(bf16[64,2048]{1,0:T(8,128)(2,1)} %get-tuple-element.134), channel_id=1, source_target_pairs={{0,8},{1,9},{2,10},{3,11},{4,12},{5,13},{6,14},{7,15},{8,0},{9,1},... | collective-permute-start | bytes 786440 | tf_op jit(solution)/shard_map/ppermute | solution.py:340
  154.9 3.6 %shard_map.86 = (bf16[256,64]{1,0:T(8,128)(2,1)S(1)}, f32[256,256]{1,0:T(8,128)S(1)}) custom-call(bf16[16,8192]{1,0:T(8,128)(2,1)S(1)} %get-tuple-element.103.refs_0_.refs_19_, bf16[16,8192]{1,0:T(8,128)(2,1)S(1)} %collective-permute-done.refs_1_.refs_20_, bf16[16,8192]{1,0:T(8,128)(2,1)S(1)} %collective-permute-done.1.refs_2_.refs_21_, ...), custom_call_target="tpu_custom_call" | custom-call | flops 1342177280 | bytes 5242880 | tf_op jit(solution)/shard_map/pallas_call | solution.py:69
  158.5 1.0 shard_map.89
  159.7 2.3 collective-permute-start.27
  161.9 2.2 shard_map.87
  164.2 16.1 %collective-permute-done.16 = bf16[64,2048]{1,0:T(8,128)(2,1)S(1)} collective-permute-done((bf16[64,2048]{1,0:T(8,128)(2,1)}, bf16[64,2048]{1,0:T(8,128)(2,1)S(1)}, u32[]{:S(2)}, u32[]{:S(2)}) %collective-permute-start.16) | collective-permute-done | bytes 262176 | tf_op jit(solution)/shard_map/ppermute | solution.py:340
  180.9 4.2 %collective-permute-start.20 = (bf16[16,8192]{1,0:T(8,128)(2,1)S(1)}, bf16[16,8192]{1,0:T(8,128)(2,1)S(1)}, u32[]{:S(2)}, u32[]{:S(2)}) collective-permute-start(bf16[16,8192]{1,0:T(8,128)(2,1)S(1)} %get-tuple-element.140), channel_id=1, source_target_pairs={{0,2},{1,3},{2,0},{3,1},{4,6},{5,7},{6,4},{7,5},{8,10},{9,11},{10,... | collective-permute-start | bytes 786440 | tf_op jit(solution)/shard_map/ppermute | solution.py:340
  185.1 6.8 %collective-permute-done.31.refs_0_.refs_8_.refs_24_.refs_11_ = bf16[16,8832]{1,0:T(8,128)(2,1)S(1)} collective-permute-done((bf16[16,8832]{1,0:T(8,128)(2,1)S(1)}, bf16[16,8832]{1,0:T(8,128)(2,1)S(1)}, u32[]{:S(2)}, u32[]{:S(2)}) %collective-permute-start.31) | collective-permute-done | bytes 282656 | tf_op jit(solution)/shard_map/ppermute | solution.py:340
  192.0 4.5 %collective-permute-done.20.refs_6_ = bf16[16,8192]{1,0:T(8,128)(2,1)S(1)} collective-permute-done((bf16[16,8192]{1,0:T(8,128)(2,1)S(1)}, bf16[16,8192]{1,0:T(8,128)(2,1)S(1)}, u32[]{:S(2)}, u32[]{:S(2)}) %collective-permute-start.20) | collective-permute-done | bytes 262176 | tf_op jit(solution)/shard_map/ppermute | solution.py:340
  196.7 18.0 %collective-permute-done.27.refs_10_.refs_26_.refs_13_ = bf16[16,8320]{1,0:T(8,128)(2,1)S(1)} collective-permute-done((bf16[16,8320]{1,0:T(8,128)(2,1)S(1)}, bf16[16,8320]{1,0:T(8,128)(2,1)S(1)}, u32[]{:S(2)}, u32[]{:S(2)}) %collective-permute-start.27) | collective-permute-done | bytes 266272 | tf_op jit(solution)/shard_map/ppermute | solution.py:340
  214.8 5.7 %collective-permute-done.23.refs_11_.refs_27_.refs_14_ = bf16[16,8320]{1,0:T(8,128)(2,1)S(1)} collective-permute-done((bf16[16,8320]{1,0:T(8,128)(2,1)S(1)}, bf16[16,8320]{1,0:T(8,128)(2,1)S(1)}, u32[]{:S(2)}, u32[]{:S(2)}) %collective-permute-start.23) | collective-permute-done | bytes 266272 | tf_op jit(solution)/shard_map/ppermute | solution.py:340
  220.5 5.7 %collective-permute-done.32.refs_12_.refs_28_.refs_15_ = bf16[16,8320]{1,0:T(8,128)(2,1)S(1)} collective-permute-done((bf16[16,8320]{1,0:T(8,128)(2,1)S(1)}, bf16[16,8320]{1,0:T(8,128)(2,1)S(1)}, u32[]{:S(2)}, u32[]{:S(2)}) %collective-permute-start.32) | collective-permute-done | bytes 266272 | tf_op jit(solution)/shard_map/ppermute | solution.py:340
  226.2 5.7 %collective-permute-done.38.refs_13_.refs_29_.refs_16_ = bf16[16,8320]{1,0:T(8,128)(2,1)S(1)} collective-permute-done((bf16[16,8320]{1,0:T(8,128)(2,1)S(1)}, bf16[16,8320]{1,0:T(8,128)(2,1)S(1)}, u32[]{:S(2)}, u32[]{:S(2)}) %collective-permute-start.38) | collective-permute-done | bytes 266272 | tf_op jit(solution)/shard_map/ppermute | solution.py:340
  232.0 11.0 %collective-permute-done.35.refs_14_.refs_30_.refs_17_ = bf16[16,8320]{1,0:T(8,128)(2,1)S(1)} collective-permute-done((bf16[16,8320]{1,0:T(8,128)(2,1)S(1)}, bf16[16,8320]{1,0:T(8,128)(2,1)S(1)}, u32[]{:S(2)}, u32[]{:S(2)}) %collective-permute-start.35) | collective-permute-done | bytes 266272 | tf_op jit(solution)/shard_map/ppermute | solution.py:340
  243.5 2.8 collective-permute-start.29
  246.4 2.6 shard_map.90
  249.0 0.7 copy-done.15
  249.7 16.6 %collective-permute-done.29.refs_8_ = bf16[16,8192]{1,0:T(8,128)(2,1)S(1)} collective-permute-done((bf16[16,8192]{1,0:T(8,128)(2,1)S(1)}, bf16[16,8192]{1,0:T(8,128)(2,1)S(1)}, u32[]{:S(2)}, u32[]{:S(2)}) %collective-permute-start.29) | collective-permute-done | bytes 262176 | tf_op jit(solution)/shard_map/ppermute | solution.py:340
  266.4 2.0 collective-permute-start.42
  268.4 7.7 %shard_map.92 = (bf16[256,64]{1,0:T(8,128)(2,1)S(1)}, f32[256,256]{1,0:T(8,128)S(1)}, bf16[256,128]{1,0:T(8,128)(2,1)S(1)}) custom-call(bf16[16,8320]{1,0:T(8,128)(2,1)S(1)} %get-tuple-element.193.refs_0_.refs_16_.refs_3_, bf16[16,8320]{1,0:T(8,128)(2,1)S(1)} %collective-permute-done.15.refs_1_.refs_17_.refs_4_, ...), custom_call_target="tpu_custom_call" | custom-call | flops 1342177280 | bytes 5242880 | tf_op jit(solution)/shard_map/pallas_call | solution.py:69
  276.7 2.4 shard_map.93
  280.0 1.1 collective-permute-done.48
  282.4 1.9 collective-permute-start.49
  284.3 1.8 collective-permute-done.49
  286.8 2.7 collective-permute-start.50
  289.5 1.0 collective-permute-done.50
  290.5 1.4 collective-permute-start.44
  292.5 2.4 collective-permute-start.51
  294.9 2.8 collective-permute-start.45
  298.0 1.5 collective-permute-start.46
  300.1 6.4 %shard_map.94 = (bf16[64,8192]{1,0:T(8,128)(2,1)}, bf16[64,8192]{1,0:T(8,128)(2,1)}) custom-call(f32[1,1]{1,0:T(1,128)S(6)} %min.3.refs_0_, bf16[256,192]{1,0:T(8,128)(2,1)S(1)} %get-tuple-element.199.refs_1_, bf16[256,192]{1,0:T(8,128)(2,1)S(1)} %get-tuple-element.200.refs_2_, bf16[16,8320]{1,0:T(8,128)(2,1)S(1)} %get-tuple-element.193.refs_0_.refs_16_.refs_3_, ...), custom_call_target="tpu_custom_call" | custom-call | flops 1610612736 | bytes 10485760 | tf_op jit(solution)/shard_map/pallas_call | solution.py:312
  306.5 3.5 %collective-permute-done.47.refs_19_ = bf16[16,8192]{1,0:T(8,128)(2,1)S(1)} collective-permute-done((bf16[16,8192]{1,0:T(8,128)(2,1)S(1)}, bf16[16,8192]{1,0:T(8,128)(2,1)S(1)}, u32[]{:S(2)}, u32[]{:S(2)}) %collective-permute-start.47) | collective-permute-done | bytes 262176 | tf_op jit(solution)/shard_map/ppermute | solution.py:340
  310.0 6.0 %collective-permute-done.46.refs_18_ = bf16[16,8192]{1,0:T(8,128)(2,1)S(1)} collective-permute-done((bf16[16,8192]{1,0:T(8,128)(2,1)S(1)}, bf16[16,8192]{1,0:T(8,128)(2,1)S(1)}, u32[]{:S(2)}, u32[]{:S(2)}) %collective-permute-start.46) | collective-permute-done | bytes 262176 | tf_op jit(solution)/shard_map/ppermute | solution.py:340
  316.0 3.2 %shard_map.91 = bf16[128,8192]{1,0:T(8,128)(2,1)} custom-call(s32[1,1]{1,0:T(1,128)} %bitcast.refs_0_, s32[16,1]{1,0:T(8,128)S(1)} %copy.15.refs_1_, s32[128,1]{1,0:T(8,128)S(1)} %copy.16.refs_2_, s32[1,128]{1,0:T(1,128)S(1)} %bitcast.15, bf16[16,8192]{1,0:T(8,128)(2,1)S(1)} %get-tuple-element.130.refs_4_, ...), custom_call_target="tpu_custom_call" | custom-call | flops 536870912 | bytes 6291456 | tf_op jit(solution)/shard_map/pallas_call | solution.py:219
  (91 shorter events, 4.2 us)
Async XLA Ops:
  0.6 58.8 %copy-start.1 = (bf16[128,8192]{1,0:T(8,128)(2,1)S(1)}, bf16[128,8192]{1,0:T(8,128)(2,1)}, u32[]{:S(2)}) copy-start(bf16[128,8192]{1,0:T(8,128)(2,1)} %refs_4_.5) | copy-start | bytes 6291460
  2.9 92.4 %copy-start = (bf16[1,64,8192]{2,1,0:T(8,128)(2,1)S(1)}, bf16[1,64,8192]{2,1,0:T(8,128)(2,1)}, u32[]{:S(2)}) copy-start(bf16[1,64,8192]{2,1,0:T(8,128)(2,1)} %param.10) | copy-start | bytes 3145732
  7.0 4.1 %collective-permute-start = (bf16[16,8192]{1,0:T(8,128)(2,1)S(1)}, bf16[16,8192]{1,0:T(8,128)(2,1)S(1)}, u32[]{:S(2)}, u32[]{:S(2)}) collective-permute-start(bf16[16,8192]{1,0:T(8,128)(2,1)S(1)} %get-tuple-element.104), channel_id=1, source_target_pairs={{0,1},{1,0},{2,3},{3,2},{4,5},{5,4},{6,7},{7,6},{8,9},{9,8},{10,11... | collective-permute-start | bytes 786440 | tf_op jit(solution)/shard_map/ppermute | solution.py:340
  7.1 30.4 %collective-permute-start.6 = (bf16[16,8192]{1,0:T(8,128)(2,1)S(1)}, bf16[16,8192]{1,0:T(8,128)(2,1)S(1)}, u32[]{:S(2)}, u32[]{:S(2)}) collective-permute-start(bf16[16,8192]{1,0:T(8,128)(2,1)S(1)} %get-tuple-element.113), channel_id=1, source_target_pairs={{0,10},{1,11},{2,8},{3,9},{4,14},{5,15},{6,12},{7,13},{8,2},{9,3},... | collective-permute-start | bytes 786440 | tf_op jit(solution)/shard_map/ppermute | solution.py:340
  8.4 34.8 %collective-permute-start.4 = (bf16[16,8192]{1,0:T(8,128)(2,1)S(1)}, bf16[16,8192]{1,0:T(8,128)(2,1)S(1)}, u32[]{:S(2)}, u32[]{:S(2)}) collective-permute-start(bf16[16,8192]{1,0:T(8,128)(2,1)S(1)} %get-tuple-element.110), channel_id=1, source_target_pairs={{0,9},{1,8},{2,11},{3,10},{4,13},{5,12},{6,15},{7,14},{8,1},{9,0},... | collective-permute-start | bytes 786440 | tf_op jit(solution)/shard_map/ppermute | solution.py:340
  10.8 38.0 %collective-permute-start.2 = (bf16[16,8192]{1,0:T(8,128)(2,1)S(1)}, bf16[16,8192]{1,0:T(8,128)(2,1)S(1)}, u32[]{:S(2)}, u32[]{:S(2)}) collective-permute-start(bf16[16,8192]{1,0:T(8,128)(2,1)S(1)} %get-tuple-element.107), channel_id=1, source_target_pairs={{0,8},{1,9},{2,10},{3,11},{4,12},{5,13},{6,14},{7,15},{8,0},{9,1},... | collective-permute-start | bytes 786440 | tf_op jit(solution)/shard_map/ppermute | solution.py:340
  11.1 42.9 %collective-permute-start.8 = (bf16[16,8192]{1,0:T(8,128)(2,1)S(1)}, bf16[16,8192]{1,0:T(8,128)(2,1)S(1)}, u32[]{:S(2)}, u32[]{:S(2)}) collective-permute-start(bf16[16,8192]{1,0:T(8,128)(2,1)S(1)} %get-tuple-element.117), channel_id=1, source_target_pairs={{0,11},{1,10},{2,9},{3,8},{4,15},{5,14},{6,13},{7,12},{8,3},{9,2},... | collective-permute-start | bytes 786440 | tf_op jit(solution)/shard_map/ppermute | solution.py:340
  13.3 49.0 %collective-permute-start.1 = (bf16[16,8192]{1,0:T(8,128)(2,1)S(1)}, bf16[16,8192]{1,0:T(8,128)(2,1)S(1)}, u32[]{:S(2)}, u32[]{:S(2)}) collective-permute-start(bf16[16,8192]{1,0:T(8,128)(2,1)S(1)} %get-tuple-element.105), channel_id=1, source_target_pairs={{0,2},{1,3},{2,0},{3,1},{4,6},{5,7},{6,4},{7,5},{8,10},{9,11},{10,... | collective-permute-start | bytes 786440 | tf_op jit(solution)/shard_map/ppermute | solution.py:340
  37.5 24.8 %collective-permute-start.7 = (bf16[16,8192]{1,0:T(8,128)(2,1)S(1)}, bf16[16,8192]{1,0:T(8,128)(2,1)S(1)}, u32[]{:S(2)}, u32[]{:S(2)}) collective-permute-start(bf16[16,8192]{1,0:T(8,128)(2,1)S(1)} %get-tuple-element.114), channel_id=1, source_target_pairs={{0,5},{1,4},{2,7},{3,6},{4,1},{5,0},{6,3},{7,2},{8,13},{9,12},{10,... | collective-permute-start | bytes 786440 | tf_op jit(solution)/shard_map/ppermute | solution.py:340
  43.2 35.3 %collective-permute-start.5 = (bf16[16,8192]{1,0:T(8,128)(2,1)S(1)}, bf16[16,8192]{1,0:T(8,128)(2,1)S(1)}, u32[]{:S(2)}, u32[]{:S(2)}) collective-permute-start(bf16[16,8192]{1,0:T(8,128)(2,1)S(1)} %get-tuple-element.111), channel_id=1, source_target_pairs={{0,4},{1,5},{2,6},{3,7},{4,0},{5,1},{6,2},{7,3},{8,12},{9,13},{10,... | collective-permute-start | bytes 786440 | tf_op jit(solution)/shard_map/ppermute | solution.py:340
  48.8 29.6 %collective-permute-start.3 = (bf16[16,8192]{1,0:T(8,128)(2,1)S(1)}, bf16[16,8192]{1,0:T(8,128)(2,1)S(1)}, u32[]{:S(2)}, u32[]{:S(2)}) collective-permute-start(bf16[16,8192]{1,0:T(8,128)(2,1)S(1)} %get-tuple-element.108), channel_id=1, source_target_pairs={{0,3},{1,2},{2,1},{3,0},{4,7},{5,6},{6,5},{7,4},{8,11},{9,10},{10,... | collective-permute-start | bytes 786440 | tf_op jit(solution)/shard_map/ppermute | solution.py:340
  54.0 100.9 %copy-start.12 = (bf16[1,64,8192]{2,1,0:T(8,128)(2,1)S(1)}, bf16[1,64,8192]{2,1,0:T(8,128)(2,1)}, u32[]{:S(2)}) copy-start(bf16[1,64,8192]{2,1,0:T(8,128)(2,1)} %param.11) | copy-start | bytes 3145732
  54.0 41.3 %collective-permute-start.9 = (bf16[16,8192]{1,0:T(8,128)(2,1)S(1)}, bf16[16,8192]{1,0:T(8,128)(2,1)S(1)}, u32[]{:S(2)}, u32[]{:S(2)}) collective-permute-start(bf16[16,8192]{1,0:T(8,128)(2,1)S(1)} %get-tuple-element.118), channel_id=1, source_target_pairs={{0,6},{1,7},{2,4},{3,5},{4,2},{5,3},{6,0},{7,1},{8,14},{9,15},{10,... | collective-permute-start | bytes 786440 | tf_op jit(solution)/shard_map/ppermute | solution.py:340
  62.3 33.9 %collective-permute-start.10 = (bf16[16,8192]{1,0:T(8,128)(2,1)S(1)}, bf16[16,8192]{1,0:T(8,128)(2,1)S(1)}, u32[]{:S(2)}, u32[]{:S(2)}) collective-permute-start(bf16[16,8192]{1,0:T(8,128)(2,1)S(1)} %get-tuple-element.121), channel_id=1, source_target_pairs={{0,12},{1,13},{2,14},{3,15},{4,8},{5,9},{6,10},{7,11},{8,4},{9,5},... | collective-permute-start | bytes 786440 | tf_op jit(solution)/shard_map/ppermute | solution.py:340
  62.3 44.6 %collective-permute-start.14 = (bf16[16,8192]{1,0:T(8,128)(2,1)S(1)}, bf16[16,8192]{1,0:T(8,128)(2,1)S(1)}, u32[]{:S(2)}, u32[]{:S(2)}) collective-permute-start(bf16[16,8192]{1,0:T(8,128)(2,1)S(1)} %get-tuple-element.128), channel_id=1, source_target_pairs={{0,15},{1,14},{2,13},{3,12},{4,11},{5,10},{6,9},{7,8},{8,7},{9,6},... | collective-permute-start | bytes 786440 | tf_op jit(solution)/shard_map/ppermute | solution.py:340
  78.4 28.5 %collective-permute-start.13 = (bf16[16,8192]{1,0:T(8,128)(2,1)S(1)}, bf16[16,8192]{1,0:T(8,128)(2,1)S(1)}, u32[]{:S(2)}, u32[]{:S(2)}) collective-permute-start(bf16[16,8192]{1,0:T(8,128)(2,1)S(1)} %get-tuple-element.126), channel_id=1, source_target_pairs={{0,14},{1,15},{2,12},{3,13},{4,10},{5,11},{6,8},{7,9},{8,6},{9,7},... | collective-permute-start | bytes 786440 | tf_op jit(solution)/shard_map/ppermute | solution.py:340
  78.4 44.8 %collective-permute-start.12 = (bf16[16,8192]{1,0:T(8,128)(2,1)S(1)}, bf16[16,8192]{1,0:T(8,128)(2,1)S(1)}, u32[]{:S(2)}, u32[]{:S(2)}) collective-permute-start(bf16[16,8192]{1,0:T(8,128)(2,1)S(1)} %get-tuple-element.124), channel_id=1, source_target_pairs={{0,13},{1,12},{2,15},{3,14},{4,9},{5,8},{6,11},{7,10},{8,5},{9,4},... | collective-permute-start | bytes 786440 | tf_op jit(solution)/shard_map/ppermute | solution.py:340
  95.3 56.2 %collective-permute-start.15 = (bf16[16,8320]{1,0:T(8,128)(2,1)S(1)}, bf16[16,8320]{1,0:T(8,128)(2,1)S(1)}, u32[]{:S(2)}, u32[]{:S(2)}) collective-permute-start(bf16[16,8320]{1,0:T(8,128)(2,1)S(1)} %get-tuple-element.133), channel_id=1, source_target_pairs={{0,1},{1,0},{2,3},{3,2},{4,5},{5,4},{6,7},{7,6},{8,9},{9,8},{10,11... | collective-permute-start | bytes 798728 | tf_op jit(solution)/shard_map/ppermute | solution.py:340
  96.2 27.1 %collective-permute-start.11 = (bf16[16,8192]{1,0:T(8,128)(2,1)S(1)}, bf16[16,8192]{1,0:T(8,128)(2,1)S(1)}, u32[]{:S(2)}, u32[]{:S(2)}) collective-permute-start(bf16[16,8192]{1,0:T(8,128)(2,1)S(1)} %get-tuple-element.122), channel_id=1, source_target_pairs={{0,7},{1,6},{2,5},{3,4},{4,3},{5,2},{6,1},{7,0},{8,15},{9,14},{10,... | collective-permute-start | bytes 786440 | tf_op jit(solution)/shard_map/ppermute | solution.py:340
  106.9 27.6 %collective-permute-start.21 = (bf16[64,2048]{1,0:T(8,128)(2,1)S(1)}, bf16[64,2048]{1,0:T(8,128)(2,1)S(1)}, u32[]{:S(2)}, u32[]{:S(2)}) collective-permute-start(bf16[64,2048]{1,0:T(8,128)(2,1)S(1)} %get-tuple-element.144), channel_id=1, source_target_pairs={{0,8},{1,9},{2,10},{3,11},{4,12},{5,13},{6,14},{7,15},{8,0},{9,1},... | collective-permute-start | bytes 786440 | tf_op jit(solution)/shard_map/ppermute | solution.py:340
  106.9 33.2 %collective-permute-start.18 = (bf16[64,2048]{1,0:T(8,128)(2,1)S(1)}, bf16[64,2048]{1,0:T(8,128)(2,1)S(1)}, u32[]{:S(2)}, u32[]{:S(2)}) collective-permute-start(bf16[64,2048]{1,0:T(8,128)(2,1)S(1)} %get-tuple-element.138), channel_id=1, source_target_pairs={{0,8},{1,9},{2,10},{3,11},{4,12},{5,13},{6,14},{7,15},{8,0},{9,1},... | collective-permute-start | bytes 786440 | tf_op jit(solution)/shard_map/ppermute | solution.py:340
  123.2 28.2 %collective-permute-start.25 = (bf16[64,2048]{1,0:T(8,128)(2,1)S(1)}, bf16[64,2048]{1,0:T(8,128)(2,1)S(1)}, u32[]{:S(2)}, u32[]{:S(2)}) collective-permute-start(bf16[64,2048]{1,0:T(8,128)(2,1)S(1)} %get-tuple-element.152), channel_id=1, source_target_pairs={{0,8},{1,9},{2,10},{3,11},{4,12},{5,13},{6,14},{7,15},{8,0},{9,1},... | collective-permute-start | bytes 786440 | tf_op jit(solution)/shard_map/ppermute | solution.py:340
  123.3 36.3 %collective-permute-start.30 = (bf16[16,8320]{1,0:T(8,128)(2,1)S(1)}, bf16[16,8320]{1,0:T(8,128)(2,1)S(1)}, u32[]{:S(2)}, u32[]{:S(2)}) collective-permute-start(bf16[16,8320]{1,0:T(8,128)(2,1)S(1)} %get-tuple-element.161), channel_id=1, source_target_pairs={{0,2},{1,3},{2,0},{3,1},{4,6},{5,7},{6,4},{7,5},{8,10},{9,11},{10,... | collective-permute-start | bytes 798728 | tf_op jit(solution)/shard_map/ppermute | solution.py:340
  134.5 45.8 %collective-permute-start.22 = (bf16[16,8320]{1,0:T(8,128)(2,1)S(1)}, bf16[16,8320]{1,0:T(8,128)(2,1)S(1)}, u32[]{:S(2)}, u32[]{:S(2)}) collective-permute-start(bf16[16,8320]{1,0:T(8,128)(2,1)S(1)} %get-tuple-element.145), channel_id=1, source_target_pairs={{0,4},{1,5},{2,6},{3,7},{4,0},{5,1},{6,2},{7,3},{8,12},{9,13},{10,... | collective-permute-start | bytes 798728 | tf_op jit(solution)/shard_map/ppermute | solution.py:340
  140.1 40.8 %collective-permute-start.19 = (bf16[16,8320]{1,0:T(8,128)(2,1)S(1)}, bf16[16,8320]{1,0:T(8,128)(2,1)S(1)}, u32[]{:S(2)}, u32[]{:S(2)}) collective-permute-start(bf16[16,8320]{1,0:T(8,128)(2,1)S(1)} %get-tuple-element.139), channel_id=1, source_target_pairs={{0,9},{1,8},{2,11},{3,10},{4,13},{5,12},{6,15},{7,14},{8,1},{9,0},... | collective-permute-start | bytes 798728 | tf_op jit(solution)/shard_map/ppermute | solution.py:340
  151.5 8.2 %collective-permute-start.26 = (bf16[16,8320]{1,0:T(8,128)(2,1)S(1)}, bf16[16,8320]{1,0:T(8,128)(2,1)S(1)}, u32[]{:S(2)}, u32[]{:S(2)}) collective-permute-start(bf16[16,8320]{1,0:T(8,128)(2,1)S(1)} %get-tuple-element.153), channel_id=1, source_target_pairs={{0,3},{1,2},{2,1},{3,0},{4,7},{5,6},{6,5},{7,4},{8,11},{9,10},{10,... | collective-permute-start | bytes 798728 | tf_op jit(solution)/shard_map/ppermute | solution.py:340
  151.5 28.8 %collective-permute-start.16 = (bf16[64,2048]{1,0:T(8,128)(2,1)}, bf16[64,2048]{1,0:T(8,128)(2,1)S(1)}, u32[]{:S(2)}, u32[]{:S(2)}) collective-permute-start(bf16[64,2048]{1,0:T(8,128)(2,1)} %get-tuple-element.134), channel_id=1, source_target_pairs={{0,8},{1,9},{2,10},{3,11},{4,12},{5,13},{6,14},{7,15},{8,0},{9,1},... | collective-permute-start | bytes 786440 | tf_op jit(solution)/shard_map/ppermute | solution.py:340
  159.5 32.4 %collective-permute-start.31 = (bf16[16,8832]{1,0:T(8,128)(2,1)S(1)}, bf16[16,8832]{1,0:T(8,128)(2,1)S(1)}, u32[]{:S(2)}, u32[]{:S(2)}) collective-permute-start(bf16[16,8832]{1,0:T(8,128)(2,1)S(1)} %shard_map.89), channel_id=1, source_target_pairs={{0,8},{1,9},{2,10},{3,11},{4,12},{5,13},{6,14},{7,15},{8,0},{9,1},... | collective-permute-start | bytes 847880 | tf_op jit(solution)/shard_map/ppermute | solution.py:340
  159.7 55.1 %collective-permute-start.27 = (bf16[16,8320]{1,0:T(8,128)(2,1)S(1)}, bf16[16,8320]{1,0:T(8,128)(2,1)S(1)}, u32[]{:S(2)}, u32[]{:S(2)}) collective-permute-start(bf16[16,8320]{1,0:T(8,128)(2,1)S(1)} %get-tuple-element.154), channel_id=1, source_target_pairs={{0,10},{1,11},{2,8},{3,9},{4,14},{5,15},{6,12},{7,13},{8,2},{9,3},... | collective-permute-start | bytes 798728 | tf_op jit(solution)/shard_map/ppermute | solution.py:340
  180.3 11.7 %collective-permute-start.17 = (bf16[16,8192]{1,0:T(8,128)(2,1)S(1)}, bf16[16,8192]{1,0:T(8,128)(2,1)S(1)}, u32[]{:S(2)}, u32[]{:S(2)}) collective-permute-start(bf16[16,8192]{1,0:T(8,128)(2,1)S(1)} %get-tuple-element.135), channel_id=1, source_target_pairs={{0,1},{1,0},{2,3},{3,2},{4,5},{5,4},{6,7},{7,6},{8,9},{9,8},{10,11... | collective-permute-start | bytes 786440 | tf_op jit(solution)/shard_map/ppermute | solution.py:340
  180.3 40.2 %collective-permute-start.23 = (bf16[16,8320]{1,0:T(8,128)(2,1)S(1)}, bf16[16,8320]{1,0:T(8,128)(2,1)S(1)}, u32[]{:S(2)}, u32[]{:S(2)}) collective-permute-start(bf16[16,8320]{1,0:T(8,128)(2,1)S(1)} %get-tuple-element.146), channel_id=1, source_target_pairs={{0,11},{1,10},{2,9},{3,8},{4,15},{5,14},{6,13},{7,12},{8,3},{9,2},... | collective-permute-start | bytes 798728 | tf_op jit(solution)/shard_map/ppermute | solution.py:340
  180.9 95.1 %copy-start.3 = (bf16[16,8320]{1,0:T(8,128)(2,1)}, bf16[16,8320]{1,0:T(8,128)(2,1)S(1)}, u32[]{:S(2)}) copy-start(bf16[16,8320]{1,0:T(8,128)(2,1)S(1)} %collective-permute-done.19.refs_9_.refs_25_.refs_12_) | copy-start | bytes 798724
  180.9 15.6 %collective-permute-start.20 = (bf16[16,8192]{1,0:T(8,128)(2,1)S(1)}, bf16[16,8192]{1,0:T(8,128)(2,1)S(1)}, u32[]{:S(2)}, u32[]{:S(2)}) collective-permute-start(bf16[16,8192]{1,0:T(8,128)(2,1)S(1)} %get-tuple-element.140), channel_id=1, source_target_pairs={{0,2},{1,3},{2,0},{3,1},{4,6},{5,7},{6,4},{7,5},{8,10},{9,11},{10,... | collective-permute-start | bytes 786440 | tf_op jit(solution)/shard_map/ppermute | solution.py:340
  191.9 84.1 %copy-start.2 = (bf16[16,8832]{1,0:T(8,128)(2,1)}, bf16[16,8832]{1,0:T(8,128)(2,1)S(1)}, u32[]{:S(2)}) copy-start(bf16[16,8832]{1,0:T(8,128)(2,1)S(1)} %collective-permute-done.31.refs_0_.refs_8_.refs_24_.refs_11_) | copy-start | bytes 847876
  191.9 34.3 %collective-permute-start.32 = (bf16[16,8320]{1,0:T(8,128)(2,1)S(1)}, bf16[16,8320]{1,0:T(8,128)(2,1)S(1)}, u32[]{:S(2)}, u32[]{:S(2)}) collective-permute-start(bf16[16,8320]{1,0:T(8,128)(2,1)S(1)} %get-tuple-element.163), channel_id=1, source_target_pairs={{0,12},{1,13},{2,14},{3,15},{4,8},{5,9},{6,10},{7,11},{8,4},{9,5},... | collective-permute-start | bytes 798728 | tf_op jit(solution)/shard_map/ppermute | solution.py:340
  191.9 40.0 %collective-permute-start.38 = (bf16[16,8320]{1,0:T(8,128)(2,1)S(1)}, bf16[16,8320]{1,0:T(8,128)(2,1)S(1)}, u32[]{:S(2)}, u32[]{:S(2)}) collective-permute-start(bf16[16,8320]{1,0:T(8,128)(2,1)S(1)} %get-tuple-element.176), channel_id=1, source_target_pairs={{0,13},{1,12},{2,15},{3,14},{4,9},{5,8},{6,11},{7,10},{8,5},{9,4},... | collective-permute-start | bytes 798728 | tf_op jit(solution)/shard_map/ppermute | solution.py:340
  196.5 46.5 %collective-permute-start.35 = (bf16[16,8320]{1,0:T(8,128)(2,1)S(1)}, bf16[16,8320]{1,0:T(8,128)(2,1)S(1)}, u32[]{:S(2)}, u32[]{:S(2)}) collective-permute-start(bf16[16,8320]{1,0:T(8,128)(2,1)S(1)} %get-tuple-element.168), channel_id=1, source_target_pairs={{0,14},{1,15},{2,12},{3,13},{4,10},{5,11},{6,8},{7,9},{8,6},{9,7},... | collective-permute-start | bytes 798728 | tf_op jit(solution)/shard_map/ppermute | solution.py:340
  214.8 61.3 %copy-start.4 = (bf16[16,8320]{1,0:T(8,128)(2,1)}, bf16[16,8320]{1,0:T(8,128)(2,1)S(1)}, u32[]{:S(2)}) copy-start(bf16[16,8320]{1,0:T(8,128)(2,1)S(1)} %collective-permute-done.27.refs_10_.refs_26_.refs_13_) | copy-start | bytes 798724
  214.8 28.7 %collective-permute-start.28 = (bf16[16,8320]{1,0:T(8,128)(2,1)S(1)}, bf16[16,8320]{1,0:T(8,128)(2,1)S(1)}, u32[]{:S(2)}, u32[]{:S(2)}) collective-permute-start(bf16[16,8320]{1,0:T(8,128)(2,1)S(1)} %get-tuple-element.155), channel_id=1, source_target_pairs={{0,5},{1,4},{2,7},{3,6},{4,1},{5,0},{6,3},{7,2},{8,13},{9,12},{10,... | collective-permute-start | bytes 798728 | tf_op jit(solution)/shard_map/ppermute | solution.py:340
  220.5 55.5 %copy-start.5 = (bf16[16,8320]{1,0:T(8,128)(2,1)}, bf16[16,8320]{1,0:T(8,128)(2,1)S(1)}, u32[]{:S(2)}) copy-start(bf16[16,8320]{1,0:T(8,128)(2,1)S(1)} %collective-permute-done.23.refs_11_.refs_27_.refs_14_) | copy-start | bytes 798724
  220.5 11.4 %collective-permute-start.24 = (bf16[16,8192]{1,0:T(8,128)(2,1)S(1)}, bf16[16,8192]{1,0:T(8,128)(2,1)S(1)}, u32[]{:S(2)}, u32[]{:S(2)}) collective-permute-start(bf16[16,8192]{1,0:T(8,128)(2,1)S(1)} %get-tuple-element.147), channel_id=1, source_target_pairs={{0,3},{1,2},{2,1},{3,0},{4,7},{5,6},{6,5},{7,4},{8,11},{9,10},{10,... | collective-permute-start | bytes 786440 | tf_op jit(solution)/shard_map/ppermute | solution.py:340
  226.2 49.8 %copy-start.6 = (bf16[16,8320]{1,0:T(8,128)(2,1)}, bf16[16,8320]{1,0:T(8,128)(2,1)S(1)}, u32[]{:S(2)}) copy-start(bf16[16,8320]{1,0:T(8,128)(2,1)S(1)} %collective-permute-done.32.refs_12_.refs_28_.refs_15_) | copy-start | bytes 798724
  226.2 23.5 %collective-permute-start.33 = (bf16[16,8320]{1,0:T(8,128)(2,1)}, bf16[16,8320]{1,0:T(8,128)(2,1)S(1)}, u32[]{:S(2)}, u32[]{:S(2)}) collective-permute-start(bf16[16,8320]{1,0:T(8,128)(2,1)} %get-tuple-element.164), channel_id=1, source_target_pairs={{0,6},{1,7},{2,4},{3,5},{4,2},{5,3},{6,0},{7,1},{8,14},{9,15},{10,... | collective-permute-start | bytes 798728 | tf_op jit(solution)/shard_map/ppermute | solution.py:340
  231.9 44.1 %copy-start.7 = (bf16[16,8320]{1,0:T(8,128)(2,1)}, bf16[16,8320]{1,0:T(8,128)(2,1)S(1)}, u32[]{:S(2)}) copy-start(bf16[16,8320]{1,0:T(8,128)(2,1)S(1)} %collective-permute-done.38.refs_13_.refs_29_.refs_16_) | copy-start | bytes 798724
  231.9 36.4 %collective-permute-start.39 = (bf16[16,8320]{1,0:T(8,128)(2,1)}, bf16[16,8320]{1,0:T(8,128)(2,1)S(1)}, u32[]{:S(2)}, u32[]{:S(2)}) collective-permute-start(bf16[16,8320]{1,0:T(8,128)(2,1)} %get-tuple-element.177), channel_id=1, source_target_pairs={{0,7},{1,6},{2,5},{3,4},{4,3},{5,2},{6,1},{7,0},{8,15},{9,14},{10,... | collective-permute-start | bytes 798728 | tf_op jit(solution)/shard_map/ppermute | solution.py:340
  231.9 34.4 %collective-permute-start.41 = (bf16[16,8320]{1,0:T(8,128)(2,1)S(1)}, bf16[16,8320]{1,0:T(8,128)(2,1)S(1)}, u32[]{:S(2)}, u32[]{:S(2)}) collective-permute-start(bf16[16,8320]{1,0:T(8,128)(2,1)S(1)} %get-tuple-element.181), channel_id=1, source_target_pairs={{0,15},{1,14},{2,13},{3,12},{4,11},{5,10},{6,9},{7,8},{8,7},{9,6},... | collective-permute-start | bytes 798728 | tf_op jit(solution)/shard_map/ppermute | solution.py:340
  243.0 33.1 %copy-start.8 = (bf16[16,8320]{1,0:T(8,128)(2,1)}, bf16[16,8320]{1,0:T(8,128)(2,1)S(1)}, u32[]{:S(2)}) copy-start(bf16[16,8320]{1,0:T(8,128)(2,1)S(1)} %collective-permute-done.35.refs_14_.refs_30_.refs_17_) | copy-start | bytes 798724
  243.0 25.4 %collective-permute-start.36 = (bf16[16,8192]{1,0:T(8,128)(2,1)}, bf16[16,8192]{1,0:T(8,128)(2,1)S(1)}, u32[]{:S(2)}, u32[]{:S(2)}) collective-permute-start(bf16[16,8192]{1,0:T(8,128)(2,1)} %get-tuple-element.169), channel_id=1, source_target_pairs={{0,6},{1,7},{2,4},{3,5},{4,2},{5,3},{6,0},{7,1},{8,14},{9,15},{10,... | collective-permute-start | bytes 786440 | tf_op jit(solution)/shard_map/ppermute | solution.py:340
  243.5 22.9 %collective-permute-start.29 = (bf16[16,8192]{1,0:T(8,128)(2,1)S(1)}, bf16[16,8192]{1,0:T(8,128)(2,1)S(1)}, u32[]{:S(2)}, u32[]{:S(2)}) collective-permute-start(bf16[16,8192]{1,0:T(8,128)(2,1)S(1)} %get-tuple-element.156), channel_id=1, source_target_pairs={{0,4},{1,5},{2,6},{3,7},{4,0},{5,1},{6,2},{7,3},{8,12},{9,13},{10,... | collective-permute-start | bytes 786440 | tf_op jit(solution)/shard_map/ppermute | solution.py:340
  249.7 26.4 %copy-start.9 = (bf16[16,8320]{1,0:T(8,128)(2,1)}, bf16[16,8320]{1,0:T(8,128)(2,1)S(1)}, u32[]{:S(2)}) copy-start(bf16[16,8320]{1,0:T(8,128)(2,1)S(1)} %collective-permute-done.33.refs_6_.refs_22_.refs_9_) | copy-start | bytes 798724
  249.7 42.8 %collective-permute-start.34 = (bf16[16,8192]{1,0:T(8,128)(2,1)S(1)}, bf16[16,8192]{1,0:T(8,128)(2,1)S(1)}, u32[]{:S(2)}, u32[]{:S(2)}) collective-permute-start(bf16[16,8192]{1,0:T(8,128)(2,1)S(1)} %get-tuple-element.165), channel_id=1, source_target_pairs={{0,5},{1,4},{2,7},{3,6},{4,1},{5,0},{6,3},{7,2},{8,13},{9,12},{10,... | collective-permute-start | bytes 786440 | tf_op jit(solution)/shard_map/ppermute | solution.py:340
  266.3 28.5 %collective-permute-start.37 = (bf16[16,8192]{1,0:T(8,128)(2,1)S(1)}, bf16[16,8192]{1,0:T(8,128)(2,1)S(1)}, u32[]{:S(2)}, u32[]{:S(2)}) collective-permute-start(bf16[16,8192]{1,0:T(8,128)(2,1)S(1)} %get-tuple-element.171), channel_id=1, source_target_pairs={{0,7},{1,6},{2,5},{3,4},{4,3},{5,2},{6,1},{7,0},{8,15},{9,14},{10,... | collective-permute-start | bytes 786440 | tf_op jit(solution)/shard_map/ppermute | solution.py:340
  266.4 28.5 %collective-permute-start.42 = (bf16[16,8192]{1,0:T(8,128)(2,1)}, bf16[16,8192]{1,0:T(8,128)(2,1)S(1)}, u32[]{:S(2)}, u32[]{:S(2)}) collective-permute-start(bf16[16,8192]{1,0:T(8,128)(2,1)} %get-tuple-element.182), channel_id=1, source_target_pairs={{0,2},{1,3},{2,0},{3,1},{4,6},{5,7},{6,4},{7,5},{8,10},{9,11},{10,... | collective-permute-start | bytes 786440 | tf_op jit(solution)/shard_map/ppermute | solution.py:340
  268.3 29.3 %collective-permute-start.40 = (bf16[16,8192]{1,0:T(8,128)(2,1)}, bf16[16,8192]{1,0:T(8,128)(2,1)S(1)}, u32[]{:S(2)}, u32[]{:S(2)}) collective-permute-start(bf16[16,8192]{1,0:T(8,128)(2,1)} %get-tuple-element.178), channel_id=1, source_target_pairs={{0,1},{1,0},{2,3},{3,2},{4,5},{5,4},{6,7},{7,6},{8,9},{9,8},{10,11... | collective-permute-start | bytes 786440 | tf_op jit(solution)/shard_map/ppermute | solution.py:340
  268.3 26.5 %copy-start.16 = (bf16[16,8192]{1,0:T(8,128)(2,1)S(1)}, bf16[16,8192]{1,0:T(8,128)(2,1)}, u32[]{:S(2)}) copy-start(bf16[16,8192]{1,0:T(8,128)(2,1)} %copy-done.15) | copy-start | bytes 786436
  279.6 1.5 collective-permute-start.48
  282.4 3.7 %collective-permute-start.49 = (f32[1,1]{1,0:T(1,128)}, f32[1,1]{1,0:T(1,128)}, u32[]{:S(2)}, u32[]{:S(2)}) collective-permute-start(f32[1,1]{1,0:T(1,128)} %add.15), channel_id=1, source_target_pairs={{0,2},{1,3},{2,0},{3,1},{4,6},{5,7},{6,4},{7,5},{8,10},{9,11},{10,... | collective-permute-start | bytes 20 | tf_op jit(solution)/shard_map/ppermute | solution.py:24
  286.8 3.7 %collective-permute-start.50 = (f32[1,1]{1,0:T(1,128)}, f32[1,1]{1,0:T(1,128)}, u32[]{:S(2)}, u32[]{:S(2)}) collective-permute-start(f32[1,1]{1,0:T(1,128)} %add.16), channel_id=1, source_target_pairs={{0,4},{1,5},{2,6},{3,7},{4,0},{5,1},{6,2},{7,3},{8,12},{9,13},{10,... | collective-permute-start | bytes 20 | tf_op jit(solution)/shard_map/ppermute | solution.py:24
  290.5 16.0 %collective-permute-start.44 = (bf16[16,8192]{1,0:T(8,128)(2,1)}, bf16[16,8192]{1,0:T(8,128)(2,1)S(1)}, u32[]{:S(2)}, u32[]{:S(2)}) collective-permute-start(bf16[16,8192]{1,0:T(8,128)(2,1)} %get-tuple-element.186), channel_id=1, source_target_pairs={{0,4},{1,5},{2,6},{3,7},{4,0},{5,1},{6,2},{7,3},{8,12},{9,13},{10,... | collective-permute-start | bytes 786440 | tf_op jit(solution)/shard_map/ppermute | solution.py:340
  292.5 5.5 %collective-permute-start.51 = (f32[1,1]{1,0:T(1,128)}, f32[1,1]{1,0:T(1,128)}, u32[]{:S(2)}, u32[]{:S(2)}) collective-permute-start(f32[1,1]{1,0:T(1,128)} %add.17), channel_id=1, source_target_pairs={{0,8},{1,9},{2,10},{3,11},{4,12},{5,13},{6,14},{7,15},{8,0},{9,1},... | collective-permute-start | bytes 20 | tf_op jit(solution)/shard_map/ppermute | solution.py:24
  294.9 11.6 %collective-permute-start.43 = (bf16[16,8192]{1,0:T(8,128)(2,1)}, bf16[16,8192]{1,0:T(8,128)(2,1)S(1)}, u32[]{:S(2)}, u32[]{:S(2)}) collective-permute-start(bf16[16,8192]{1,0:T(8,128)(2,1)} %get-tuple-element.184), channel_id=1, source_target_pairs={{0,3},{1,2},{2,1},{3,0},{4,7},{5,6},{6,5},{7,4},{8,11},{9,10},{10,... | collective-permute-start | bytes 786440 | tf_op jit(solution)/shard_map/ppermute | solution.py:340
  294.9 11.6 %collective-permute-start.45 = (bf16[16,8192]{1,0:T(8,128)(2,1)S(1)}, bf16[16,8192]{1,0:T(8,128)(2,1)S(1)}, u32[]{:S(2)}, u32[]{:S(2)}) collective-permute-start(bf16[16,8192]{1,0:T(8,128)(2,1)S(1)} %copy-done.16), channel_id=1, source_target_pairs={{0,5},{1,4},{2,7},{3,6},{4,1},{5,0},{6,3},{7,2},{8,13},{9,12},{10,... | collective-permute-start | bytes 786440 | tf_op jit(solution)/shard_map/ppermute | solution.py:340
  297.6 12.4 %collective-permute-start.47 = (bf16[16,8192]{1,0:T(8,128)(2,1)S(1)}, bf16[16,8192]{1,0:T(8,128)(2,1)S(1)}, u32[]{:S(2)}, u32[]{:S(2)}) collective-permute-start(bf16[16,8192]{1,0:T(8,128)(2,1)S(1)} %get-tuple-element.192), channel_id=1, source_target_pairs={{0,7},{1,6},{2,5},{3,4},{4,3},{5,2},{6,1},{7,0},{8,15},{9,14},{10,... | collective-permute-start | bytes 786440 | tf_op jit(solution)/shard_map/ppermute | solution.py:340
  298.0 18.0 %collective-permute-start.46 = (bf16[16,8192]{1,0:T(8,128)(2,1)S(1)}, bf16[16,8192]{1,0:T(8,128)(2,1)S(1)}, u32[]{:S(2)}, u32[]{:S(2)}) collective-permute-start(bf16[16,8192]{1,0:T(8,128)(2,1)S(1)} %get-tuple-element.190), channel_id=1, source_target_pairs={{0,6},{1,7},{2,4},{3,5},{4,2},{5,3},{6,0},{7,1},{8,14},{9,15},{10,... | collective-permute-start | bytes 786440 | tf_op jit(solution)/shard_map/ppermute | solution.py:340
  (5 other events, 22.5 us)

commit v4 on v3

--- a/solution.py
+++ b/solution.py
@@ -10,7 +10,8 @@
 EPS = 1e-06
 VMEM_LIMIT = 48 * 1024 * 1024
 LANES = 128
-WINDOW = 5
+FAR_WINDOW = 4
+NEAR_WINDOW = 4
 LAST = (((1,), (1,)), ((), ()))
 FIRST = (((0,), (0,)), ((), ()))
 
@@ -352,49 +353,55 @@
     down_weight = down_factor_table[0]
     up_weight = up_factor_table[0]
     me = lax.axis_index("blk").astype(jnp.int32)
-    line = Line(WINDOW)
+    far, near = Line(FAR_WINDOW), Line(NEAR_WINDOW)
     low_of = lambda low, first, count: low[first * cap : (first + count) * cap]
-
-    order = [half]
-    for s in range(1, half):
-        order += [s, half + s]
+    parts = rank // cap
+    mirror_parts = []
+
+    def send_weight(number):
+        for _ in range(number):
+            at = len(mirror_parts)
+            mirror_parts.append(far.swap(down_weight[at * cap : (at + 1) * cap], half))
+
+    send_weight(parts // 2)
     sent_dy = place(list(range(count_blk)), cap, me, owner, tenant, cotangent)
-    got_dy = {0: sent_dy[0]}
-    for s in order:
-        got_dy[s] = line.swap(sent_dy[s], s)
-
     others = [s for s in range(count_blk) if s != half]
     sent_x = dict(zip(others, place(others, cap, me, owner, tenant, tokens, with_live=True)))
-    got_x = {0: sent_x[0]}
-    parts = 4
-    mirror_parts = []
-    for part in range(parts):
-        columns = slice(part * width // parts, (part + 1) * width // parts)
-        mirror_parts.append(line.swap(down_weight[:, columns], half))
-        got_x[part + 1] = line.swap(sent_x[part + 1], part + 1)
+    got_dy, got_x = {0: sent_dy[0]}, {0: sent_x[0]}
+    near_queue = [(got_dy, sent_dy, s) for s in range(1, half)] + [(got_x, sent_x, s) for s in range(1, half)]
+    for s in range(half, count_blk):
+        got_dy[s] = far.swap(sent_dy[s], s)
+        for got, sent, partner in near_queue[:2]:
+            got[partner] = near.swap(sent[partner], partner)
+        del near_queue[:2]
+    send_weight(parts - len(mirror_parts))
 
     blocks_dy = [got_dy[s] for s in range(count_blk)]
     grad_hidden, gram_dy = rows_products(blocks_dy, up_weight, SCALE)
     (sent_mirror,) = place(
         [half], cap, me, owner, tenant, tokens, with_live=True, low=low_of(grad_hidden, half, half)
     )
-    got_x[half] = line.swap(sent_mirror, half)
     still = pl.BlockSpec((half * cap, rank), lambda i: (0, 0))
     own_back = back_rows(half, cap, low_of(grad_hidden, 0, half), down_weight, still, False)
     back = {0: own_back[0]}
-    rest = [s for s in order if s > parts and s != half]
-    for at, s in enumerate(rest):
-        got_x[s] = line.swap(sent_x[s], s)
-        if at % 2 == 1 and len(back) < half:
-            back[len(back)] = line.swap(own_back[len(back)], len(back))
-    while len(back) < half:
-        back[len(back)] = line.swap(own_back[len(back)], len(back))
+    got_x[half + 1] = far.swap(sent_x[half + 1], half + 1)
+    got_x[half] = far.swap(sent_mirror, half)
+    for s in range(1, half // 2):
+        got_x[half + 1 + s] = far.swap(sent_x[half + 1 + s], half + 1 + s)
+        for at in (2 * s - 1, 2 * s):
+            back[at] = near.swap(own_back[at], at)
+    back[half - 1] = near.swap(own_back[half - 1], half - 1)
     mirror_low = pl.BlockSpec((cap, half * rank), lambda i: (0, width // (half * rank)))
-    mirror_weight = jnp.concatenate(mirror_parts, axis=1)
+    mirror_weight = jnp.concatenate(mirror_parts, axis=0)
     mirror_back = back_rows(half, cap, got_x[half], mirror_weight, mirror_low, True)
     back[half] = mirror_back[0]
-    for s in range(1, half):
-        back[half + s] = line.swap(mirror_back[s], s)
+    for at, s in enumerate(range(half + 1 + half // 2, count_blk)):
+        got_x[s] = far.swap(sent_x[s], s)
+        for partner in (2 * at + 1, 2 * at + 2):
+            back[half + partner] = near.swap(mirror_back[partner], partner)
+    for partner in range(1, half):
+        if half + partner not in back:
+            back[half + partner] = near.swap(mirror_back[partner], partner)
 
     blocks_x = [got_x[s] for s in range(count_blk)]
     hidden, gram_x, live = rows_products(blocks_x, down_weight, 1.0, with_extra=True)

time: 323 us -> 289 us (0.89)
  waiting for transfers between devices: 212 us -> 137 us
  starting transfers between devices: 62.3 us -> 106 us
    ppermute x48, waiting for transfers between devices: 208 us -> 130 us  [swap(): result = lax.ppermute(value, 'blk', [(i, i ^ partner) for i in range(size)])]
    ppermute x48, starting transfers between devices: 54.9 us -> 93 us  [swap(): result = lax.ppermute(value, 'blk', [(i, i ^ partner) for i in range(size)])]
    ppermute x4, starting transfers between devices: 7.42 us -> 12.5 us  [total_over_blk(): lax.ppermute(value, 'blk', [(i, i ^ step) for i in range(size)])]
  transfers between devices with their start and end apart: 52 -> 52, of which waited for: 25 -> 26; matrix products, arithmetic and copies ran while one was open for 1% -> 1% of each run, Pallas kernels for 9% -> 11%
where the time goes in v4:
time: 289 us; the launch traced here: 286 us
  waiting for transfers between devices  137 us (47%)
  starting transfers between devices  106 us (37%)
  Pallas kernels  35.2 us (12%)
  between operations  4.42 us (2%)
  local copies, waits for them, and re-layouts  2.98 us (1%)
    ppermute x48, waiting for transfers between devices, swap(): result = lax.ppermute(value, 'blk', [(i, i ^ partner) for i in range(size)])  130 us
    ppermute x48, starting transfers between devices, swap(): result = lax.ppermute(value, 'blk', [(i, i ^ partner) for i in range(size)])  93 us
    ppermute x4, starting transfers between devices, total_over_blk(): lax.ppermute(value, 'blk', [(i, i ^ step) for i in range(size)])  12.5 us
    pallas_call x2, Pallas kernels, rows_products(): pl.pallas_call(lambda *refs: rows_kernel(scale, len(blocks), with_extra,...  11.2 us
    pallas_call x3, Pallas kernels, place(): pl.pallas_call(lambda *refs: place_kernel(partners, cap, with_live, *refs...  7.91 us
    ppermute x4, waiting for transfers between devices, total_over_blk(): lax.ppermute(value, 'blk', [(i, i ^ step) for i in range(size)])  6.69 us
    pallas_call x1, Pallas kernels, grads(): pl.pallas_call(lambda *refs: grads_kernel(len(blocks_x), *refs), grid=(wi...  6.38 us
  transfers between devices with their start and end apart: 52, of which 26 were waited for; matrix products, arithmetic and copies ran while one was open for 1% of the time, Pallas kernels for 11%

profile of v4, /device:TPU:16, one launch (start us, length us, event | category | flops | bytes accessed | tf_op | source)
XLA Modules:
  0.0 286.4 jit_solution(966646823775353015)
XLA Ops:
  0.7 2.2 slice_bitcast_fusion.1
  2.8 2.9 %collective-permute-start.11 = (bf16[16,8192]{1,0:T(8,128)(2,1)S(1)}, bf16[16,8192]{1,0:T(8,128)(2,1)}, u32[]{:S(2)}, u32[]{:S(2)}) collective-permute-start(bf16[16,8192]{1,0:T(8,128)(2,1)S(1)} %get-tuple-element.198), channel_id=1, source_target_pairs={{0,8},{1,9},{2,10},{3,11},{4,12},{5,13},{6,14},{7,15},{8,0},{9,1},... | collective-permute-start | bytes 786440 | tf_op jit(solution)/shard_map/ppermute | solution.py:341
  6.0 4.1 %shard_map.85 = (bf16[16,8192]{1,0:T(8,128)(2,1)S(1)}, bf16[16,8192]{1,0:T(8,128)(2,1)S(1)}, bf16[16,8192]{1,0:T(8,128)(2,1)S(1)}, bf16[16,8192]{1,0:T(8,128)(2,...) custom-call(s32[1,1]{1,0:T(1,128)} %bitcast.refs_0_, ...), custom_call_target="tpu_custom_call" | custom-call | flops 536870912 | bytes 6291456 | tf_op jit(solution)/shard_map/pallas_call | solution.py:153
  10.2 1.6 collective-permute-start.1
  11.8 14.5 %collective-permute-done.9 = bf16[16,8192]{1,0:T(8,128)(2,1)S(1)} collective-permute-done((bf16[16,8192]{1,0:T(8,128)(2,1)S(1)}, bf16[16,8192]{1,0:T(8,128)(2,1)S(1)}, u32[]{:S(2)}, u32[]{:S(2)}) %collective-permute-start.9) | collective-permute-done | bytes 262176 | tf_op jit(solution)/shard_map/ppermute | solution.py:341
  26.4 3.4 %collective-permute-start.7 = (bf16[16,8192]{1,0:T(8,128)(2,1)S(1)}, bf16[16,8192]{1,0:T(8,128)(2,1)S(1)}, u32[]{:S(2)}, u32[]{:S(2)}) collective-permute-start(bf16[16,8192]{1,0:T(8,128)(2,1)S(1)} %get-tuple-element.111), channel_id=1, source_target_pairs={{0,8},{1,9},{2,10},{3,11},{4,12},{5,13},{6,14},{7,15},{8,0},{9,1},... | collective-permute-start | bytes 786440 | tf_op jit(solution)/shard_map/ppermute | solution.py:341
  29.8 7.9 %collective-permute-done.11 = bf16[16,8192]{1,0:T(8,128)(2,1)} collective-permute-done((bf16[16,8192]{1,0:T(8,128)(2,1)S(1)}, bf16[16,8192]{1,0:T(8,128)(2,1)}, u32[]{:S(2)}, u32[]{:S(2)}) %collective-permute-start.11) | collective-permute-done | bytes 262176 | tf_op jit(solution)/shard_map/ppermute | solution.py:341
  37.6 5.0 %collective-permute-start.3 = (bf16[16,8192]{1,0:T(8,128)(2,1)S(1)}, bf16[16,8192]{1,0:T(8,128)(2,1)S(1)}, u32[]{:S(2)}, u32[]{:S(2)}) collective-permute-start(bf16[16,8192]{1,0:T(8,128)(2,1)S(1)} %get-tuple-element.104), channel_id=1, source_target_pairs={{0,4},{1,5},{2,6},{3,7},{4,0},{5,1},{6,2},{7,3},{8,12},{9,13},{10,... | collective-permute-start | bytes 786440 | tf_op jit(solution)/shard_map/ppermute | solution.py:341
  43.3 3.1 %collective-permute-start.10 = (bf16[16,8192]{1,0:T(8,128)(2,1)S(1)}, bf16[16,8192]{1,0:T(8,128)(2,1)S(1)}, u32[]{:S(2)}, u32[]{:S(2)}) collective-permute-start(bf16[16,8192]{1,0:T(8,128)(2,1)S(1)} %get-tuple-element.114), channel_id=1, source_target_pairs={{0,10},{1,11},{2,8},{3,9},{4,14},{5,15},{6,12},{7,13},{8,2},{9,3},... | collective-permute-start | bytes 786440 | tf_op jit(solution)/shard_map/ppermute | solution.py:341
  46.3 2.4 collective-permute-done.7.refs_8_.refs_27_
  48.7 12.8 %collective-permute-start.14 = (bf16[16,8192]{1,0:T(8,128)(2,1)S(1)}, bf16[16,8192]{1,0:T(8,128)(2,1)S(1)}, u32[]{:S(2)}, u32[]{:S(2)}) collective-permute-start(bf16[16,8192]{1,0:T(8,128)(2,1)S(1)} %get-tuple-element.120), channel_id=1, source_target_pairs={{0,13},{1,12},{2,15},{3,14},{4,9},{5,8},{6,11},{7,10},{8,5},{9,4},... | collective-permute-start | bytes 786440 | tf_op jit(solution)/shard_map/ppermute | solution.py:341
  62.1 5.2 %collective-permute-start.4 = (bf16[16,8192]{1,0:T(8,128)(2,1)S(1)}, bf16[16,8192]{1,0:T(8,128)(2,1)S(1)}, u32[]{:S(2)}, u32[]{:S(2)}) collective-permute-start(bf16[16,8192]{1,0:T(8,128)(2,1)S(1)} %get-tuple-element.106), channel_id=1, source_target_pairs={{0,5},{1,4},{2,7},{3,6},{4,1},{5,0},{6,3},{7,2},{8,13},{9,12},{10,... | collective-permute-start | bytes 786440 | tf_op jit(solution)/shard_map/ppermute | solution.py:341
  67.2 9.8 %collective-permute-done.12.refs_11_.refs_30_ = bf16[16,8192]{1,0:T(8,128)(2,1)S(1)} collective-permute-done((bf16[16,8192]{1,0:T(8,128)(2,1)S(1)}, bf16[16,8192]{1,0:T(8,128)(2,1)S(1)}, u32[]{:S(2)}, u32[]{:S(2)}) %collective-permute-start.12) | collective-permute-done | bytes 262176 | tf_op jit(solution)/shard_map/ppermute | solution.py:341
  77.0 4.6 %collective-permute-start.5 = (bf16[16,8192]{1,0:T(8,128)(2,1)S(1)}, bf16[16,8192]{1,0:T(8,128)(2,1)S(1)}, u32[]{:S(2)}, u32[]{:S(2)}) collective-permute-start(bf16[16,8192]{1,0:T(8,128)(2,1)S(1)} %get-tuple-element.108), channel_id=1, source_target_pairs={{0,6},{1,7},{2,4},{3,5},{4,2},{5,3},{6,0},{7,1},{8,14},{9,15},{10,... | collective-permute-start | bytes 786440 | tf_op jit(solution)/shard_map/ppermute | solution.py:341
  81.6 1.0 collective-permute-done.10.refs_10_.refs_29_
  82.6 4.3 %collective-permute-start.6 = (bf16[16,8192]{1,0:T(8,128)(2,1)S(1)}, bf16[16,8192]{1,0:T(8,128)(2,1)S(1)}, u32[]{:S(2)}, u32[]{:S(2)}) collective-permute-start(bf16[16,8192]{1,0:T(8,128)(2,1)S(1)} %get-tuple-element.110), channel_id=1, source_target_pairs={{0,7},{1,6},{2,5},{3,4},{4,3},{5,2},{6,1},{7,0},{8,15},{9,14},{10,... | collective-permute-start | bytes 786440 | tf_op jit(solution)/shard_map/ppermute | solution.py:341
  86.9 2.8 shard_map.88
  90.7 5.4 %collective-permute-done.13.refs_12_.refs_31_ = bf16[16,8192]{1,0:T(8,128)(2,1)S(1)} collective-permute-done((bf16[16,8192]{1,0:T(8,128)(2,1)S(1)}, bf16[16,8192]{1,0:T(8,128)(2,1)S(1)}, u32[]{:S(2)}, u32[]{:S(2)}) %collective-permute-start.13) | collective-permute-done | bytes 262176 | tf_op jit(solution)/shard_map/ppermute | solution.py:341
  96.3 2.4 collective-permute-start.15
  98.8 5.4 %collective-permute-done.6.refs_7_.refs_26_ = bf16[16,8192]{1,0:T(8,128)(2,1)S(1)} collective-permute-done((bf16[16,8192]{1,0:T(8,128)(2,1)S(1)}, bf16[16,8192]{1,0:T(8,128)(2,1)S(1)}, u32[]{:S(2)}, u32[]{:S(2)}) %collective-permute-start.6) | collective-permute-done | bytes 262176 | tf_op jit(solution)/shard_map/ppermute | solution.py:341
  105.0 19.9 %collective-permute-done.33 = bf16[16,8192]{1,0:T(8,128)(2,1)S(1)} collective-permute-done((bf16[16,8192]{1,0:T(8,128)(2,1)S(1)}, bf16[16,8192]{1,0:T(8,128)(2,1)S(1)}, u32[]{:S(2)}, u32[]{:S(2)}) %collective-permute-start.33) | collective-permute-done | bytes 262176 | tf_op jit(solution)/shard_map/ppermute | solution.py:341
  124.9 1.9 collective-permute-start.17
  126.8 3.9 %collective-permute-done.16.refs_15_.refs_34_ = bf16[16,8192]{1,0:T(8,128)(2,1)S(1)} collective-permute-done((bf16[16,8192]{1,0:T(8,128)(2,1)S(1)}, bf16[16,8192]{1,0:T(8,128)(2,1)S(1)}, u32[]{:S(2)}, u32[]{:S(2)}) %collective-permute-start.16) | collective-permute-done | bytes 262176 | tf_op jit(solution)/shard_map/ppermute | solution.py:341
  130.6 1.4 collective-permute-start.22
  132.0 5.5 %collective-permute-done.15.refs_14_.refs_33_ = bf16[16,8192]{1,0:T(8,128)(2,1)S(1)} collective-permute-done((bf16[16,8192]{1,0:T(8,128)(2,1)S(1)}, bf16[16,8192]{1,0:T(8,128)(2,1)S(1)}, u32[]{:S(2)}, u32[]{:S(2)}) %collective-permute-start.15) | collective-permute-done | bytes 262176 | tf_op jit(solution)/shard_map/ppermute | solution.py:341
  137.5 4.0 %collective-permute-done.32 = bf16[16,8192]{1,0:T(8,128)(2,1)} collective-permute-done((bf16[16,8192]{1,0:T(8,128)(2,1)S(1)}, bf16[16,8192]{1,0:T(8,128)(2,1)}, u32[]{:S(2)}, u32[]{:S(2)}) %collective-permute-start.32) | collective-permute-done | bytes 262176 | tf_op jit(solution)/shard_map/ppermute | solution.py:341
  141.6 3.9 %collective-permute-start.43 = (bf16[16,8320]{1,0:T(8,128)(2,1)S(1)}, bf16[16,8320]{1,0:T(8,128)(2,1)S(1)}, u32[]{:S(2)}, u32[]{:S(2)}) collective-permute-start(bf16[16,8320]{1,0:T(8,128)(2,1)S(1)} %get-tuple-element.179), channel_id=1, source_target_pairs={{0,11},{1,10},{2,9},{3,8},{4,15},{5,14},{6,13},{7,12},{8,3},{9,2},... | collective-permute-start | bytes 798728 | tf_op jit(solution)/shard_map/ppermute | solution.py:341
  145.5 3.6 %shard_map.86 = (bf16[256,64]{1,0:T(8,128)(2,1)S(1)}, f32[256,256]{1,0:T(8,128)S(1)}) custom-call(bf16[16,8192]{1,0:T(8,128)(2,1)S(1)} %get-tuple-element.100.refs_0_.refs_19_, bf16[16,8192]{1,0:T(8,128)(2,1)S(1)} %collective-permute-done.refs_1_.refs_20_, bf16[16,8192]{1,0:T(8,128)(2,1)S(1)} %collective-permute-done.1.refs_2_.refs_21_, ...), custom_call_target="tpu_custom_call" | custom-call | flops 1342177280 | bytes 5242880 | tf_op jit(solution)/shard_map/pallas_call | solution.py:70
  149.8 2.3 collective-permute-start.41
  152.2 2.4 shard_map.87
  154.6 2.6 collective-permute-start.23
  157.3 9.8 %collective-permute-done.43.refs_11_.refs_27_.refs_14_ = bf16[16,8320]{1,0:T(8,128)(2,1)S(1)} collective-permute-done((bf16[16,8320]{1,0:T(8,128)(2,1)S(1)}, bf16[16,8320]{1,0:T(8,128)(2,1)S(1)}, u32[]{:S(2)}, u32[]{:S(2)}) %collective-permute-start.43) | collective-permute-done | bytes 266272 | tf_op jit(solution)/shard_map/ppermute | solution.py:341
  167.2 1.0 shard_map.89
  168.3 4.6 %collective-permute-done.42.refs_10_.refs_26_.refs_13_ = bf16[16,8320]{1,0:T(8,128)(2,1)S(1)} collective-permute-done((bf16[16,8320]{1,0:T(8,128)(2,1)S(1)}, bf16[16,8320]{1,0:T(8,128)(2,1)S(1)}, u32[]{:S(2)}, u32[]{:S(2)}) %collective-permute-start.42) | collective-permute-done | bytes 266272 | tf_op jit(solution)/shard_map/ppermute | solution.py:341
  172.8 3.8 %collective-permute-start.31 = (bf16[16,8832]{1,0:T(8,128)(2,1)S(1)}, bf16[16,8832]{1,0:T(8,128)(2,1)S(1)}, u32[]{:S(2)}, u32[]{:S(2)}) collective-permute-start(bf16[16,8832]{1,0:T(8,128)(2,1)S(1)} %shard_map.89), channel_id=1, source_target_pairs={{0,8},{1,9},{2,10},{3,11},{4,12},{5,13},{6,14},{7,15},{8,0},{9,1},... | collective-permute-start | bytes 847880 | tf_op jit(solution)/shard_map/ppermute | solution.py:341
  176.6 8.0 %collective-permute-done.41.refs_9_.refs_25_.refs_12_ = bf16[16,8320]{1,0:T(8,128)(2,1)S(1)} collective-permute-done((bf16[16,8320]{1,0:T(8,128)(2,1)S(1)}, bf16[16,8320]{1,0:T(8,128)(2,1)S(1)}, u32[]{:S(2)}, u32[]{:S(2)}) %collective-permute-start.41) | collective-permute-done | bytes 266272 | tf_op jit(solution)/shard_map/ppermute | solution.py:341
  184.6 1.5 collective-permute-start.47
  186.1 1.1 collective-permute-start.46
  188.2 4.6 %collective-permute-start.28 = (bf16[16,8192]{1,0:T(8,128)(2,1)S(1)}, bf16[16,8192]{1,0:T(8,128)(2,1)S(1)}, u32[]{:S(2)}, u32[]{:S(2)}) collective-permute-start(bf16[16,8192]{1,0:T(8,128)(2,1)S(1)} %get-tuple-element.150), channel_id=1, source_target_pairs={{0,5},{1,4},{2,7},{3,6},{4,1},{5,0},{6,3},{7,2},{8,13},{9,12},{10,... | collective-permute-start | bytes 786440 | tf_op jit(solution)/shard_map/ppermute | solution.py:341
  192.8 2.8 collective-permute-done.21.refs_6_
  195.6 1.2 collective-permute-start.44
  196.8 5.1 %collective-permute-done.31.refs_0_.refs_8_.refs_24_.refs_11_ = bf16[16,8832]{1,0:T(8,128)(2,1)S(1)} collective-permute-done((bf16[16,8832]{1,0:T(8,128)(2,1)S(1)}, bf16[16,8832]{1,0:T(8,128)(2,1)S(1)}, u32[]{:S(2)}, u32[]{:S(2)}) %collective-permute-start.31) | collective-permute-done | bytes 282656 | tf_op jit(solution)/shard_map/ppermute | solution.py:341
  202.0 10.3 %collective-permute-start.27 = (bf16[16,8192]{1,0:T(8,128)(2,1)}, bf16[16,8192]{1,0:T(8,128)(2,1)S(1)}, u32[]{:S(2)}, u32[]{:S(2)}) collective-permute-start(bf16[16,8192]{1,0:T(8,128)(2,1)} %get-tuple-element.148), channel_id=1, source_target_pairs={{0,4},{1,5},{2,6},{3,7},{4,0},{5,1},{6,2},{7,3},{8,12},{9,13},{10,... | collective-permute-start | bytes 786440 | tf_op jit(solution)/shard_map/ppermute | solution.py:341
  212.3 0.9 collective-permute-start.29
  213.2 7.8 %collective-permute-done.46.refs_14_.refs_30_.refs_17_ = bf16[16,8320]{1,0:T(8,128)(2,1)S(1)} collective-permute-done((bf16[16,8320]{1,0:T(8,128)(2,1)S(1)}, bf16[16,8320]{1,0:T(8,128)(2,1)S(1)}, u32[]{:S(2)}, u32[]{:S(2)}) %collective-permute-start.46) | collective-permute-done | bytes 266272 | tf_op jit(solution)/shard_map/ppermute | solution.py:341
  221.8 1.1 pad_maximum_fusion.refs_1_
  222.9 1.7 shard_map.90
  226.3 5.1 %collective-permute-done.29.refs_10_ = bf16[16,8192]{1,0:T(8,128)(2,1)S(1)} collective-permute-done((bf16[16,8192]{1,0:T(8,128)(2,1)}, bf16[16,8192]{1,0:T(8,128)(2,1)S(1)}, u32[]{:S(2)}, u32[]{:S(2)}) %collective-permute-start.29) | collective-permute-done | bytes 262176 | tf_op jit(solution)/shard_map/ppermute | solution.py:341
  231.5 2.2 collective-permute-start.36
  233.7 4.6 %collective-permute-done.45.refs_13_.refs_29_.refs_16_ = bf16[16,8320]{1,0:T(8,128)(2,1)S(1)} collective-permute-done((bf16[16,8320]{1,0:T(8,128)(2,1)}, bf16[16,8320]{1,0:T(8,128)(2,1)S(1)}, u32[]{:S(2)}, u32[]{:S(2)}) %collective-permute-start.45) | collective-permute-done | bytes 266272 | tf_op jit(solution)/shard_map/ppermute | solution.py:341
  238.4 7.6 %shard_map.92 = (bf16[256,64]{1,0:T(8,128)(2,1)S(1)}, f32[256,256]{1,0:T(8,128)S(1)}, bf16[256,128]{1,0:T(8,128)(2,1)S(1)}) custom-call(bf16[16,8320]{1,0:T(8,128)(2,1)S(1)} %get-tuple-element.173.refs_0_.refs_16_.refs_3_, bf16[16,8320]{1,0:T(8,128)(2,1)S(1)} %collective-permute-done.19.refs_1_.refs_17_.refs_4_, ...), custom_call_target="tpu_custom_call" | custom-call | flops 1342177280 | bytes 5242880 | tf_op jit(solution)/shard_map/pallas_call | solution.py:70
  246.1 1.1 collective-permute-start.38
  247.2 0.9 collective-permute-start.37
  248.1 2.4 collective-permute-start.40
  251.1 2.4 shard_map.93
  254.0 1.2 collective-permute-done.48
  256.6 1.9 collective-permute-start.49
  258.5 1.7 collective-permute-done.49
  260.9 8.4 %collective-permute-start.50 = (f32[1,1]{1,0:T(1,128)}, f32[1,1]{1,0:T(1,128)}, u32[]{:S(2)}, u32[]{:S(2)}) collective-permute-start(f32[1,1]{1,0:T(1,128)} %add.16), channel_id=1, source_target_pairs={{0,4},{1,5},{2,6},{3,7},{4,0},{5,1},{6,2},{7,3},{8,12},{9,13},{10,... | collective-permute-start | bytes 20 | tf_op jit(solution)/shard_map/ppermute | solution.py:25
  269.2 1.6 collective-permute-done.50
  271.5 2.3 collective-permute-start.51
  273.9 2.1 collective-permute-done.51
  276.7 6.4 %shard_map.94 = (bf16[64,8192]{1,0:T(8,128)(2,1)}, bf16[64,8192]{1,0:T(8,128)(2,1)}) custom-call(f32[1,1]{1,0:T(1,128)S(6)} %min.3.refs_0_, bf16[256,192]{1,0:T(8,128)(2,1)S(1)} %get-tuple-element.193.refs_1_, bf16[256,192]{1,0:T(8,128)(2,1)S(1)} %get-tuple-element.194.refs_2_, bf16[16,8320]{1,0:T(8,128)(2,1)S(1)} %get-tuple-element.173.refs_0_.refs_16_.refs_3_, ...), custom_call_target="tpu_custom_call" | custom-call | flops 1610612736 | bytes 10485760 | tf_op jit(solution)/shard_map/pallas_call | solution.py:313
  283.2 3.2 %shard_map.91 = bf16[128,8192]{1,0:T(8,128)(2,1)} custom-call(s32[1,1]{1,0:T(1,128)} %bitcast.refs_0_, s32[16,1]{1,0:T(8,128)S(1)} %copy.15.refs_1_, s32[128,1]{1,0:T(8,128)S(1)} %copy.16.refs_2_, s32[1,128]{1,0:T(1,128)S(1)} %bitcast.22, bf16[16,8192]{1,0:T(8,128)(2,1)S(1)} %get-tuple-element.126.refs_4_, ...), custom_call_target="tpu_custom_call" | custom-call | flops 536870912 | bytes 6291456 | tf_op jit(solution)/shard_map/pallas_call | solution.py:220
  (99 shorter events, 9.4 us)
Async XLA Ops:
  0.7 86.2 %copy-start.1 = (bf16[128,8192]{1,0:T(8,128)(2,1)S(1)}, bf16[128,8192]{1,0:T(8,128)(2,1)}, u32[]{:S(2)}) copy-start(bf16[128,8192]{1,0:T(8,128)(2,1)} %refs_4_.5) | copy-start | bytes 6291460
  2.8 23.5 %collective-permute-start.9 = (bf16[16,8192]{1,0:T(8,128)(2,1)S(1)}, bf16[16,8192]{1,0:T(8,128)(2,1)S(1)}, u32[]{:S(2)}, u32[]{:S(2)}) collective-permute-start(bf16[16,8192]{1,0:T(8,128)(2,1)S(1)} %get-tuple-element.199), channel_id=1, source_target_pairs={{0,8},{1,9},{2,10},{3,11},{4,12},{5,13},{6,14},{7,15},{8,0},{9,1},... | collective-permute-start | bytes 786440 | tf_op jit(solution)/shard_map/ppermute | solution.py:341
  2.8 34.8 %collective-permute-start.11 = (bf16[16,8192]{1,0:T(8,128)(2,1)S(1)}, bf16[16,8192]{1,0:T(8,128)(2,1)}, u32[]{:S(2)}, u32[]{:S(2)}) collective-permute-start(bf16[16,8192]{1,0:T(8,128)(2,1)S(1)} %get-tuple-element.198), channel_id=1, source_target_pairs={{0,8},{1,9},{2,10},{3,11},{4,12},{5,13},{6,14},{7,15},{8,0},{9,1},... | collective-permute-start | bytes 786440 | tf_op jit(solution)/shard_map/ppermute | solution.py:341
  6.0 90.2 %copy-start.19 = (bf16[16,8192]{1,0:T(8,128)(2,1)S(1)}, bf16[16,8192]{1,0:T(8,128)(2,1)}, u32[]{:S(2)}) copy-start(bf16[16,8192]{1,0:T(8,128)(2,1)} %get-tuple-element.157) | copy-start | bytes 786436
  6.0 98.2 %copy-start.16 = (bf16[16,8192]{1,0:T(8,128)(2,1)S(1)}, bf16[16,8192]{1,0:T(8,128)(2,1)}, u32[]{:S(2)}) copy-start(bf16[16,8192]{1,0:T(8,128)(2,1)} %get-tuple-element.156) | copy-start | bytes 786436
  6.0 139.5 %copy-start.12 = (bf16[1,64,8192]{2,1,0:T(8,128)(2,1)S(1)}, bf16[1,64,8192]{2,1,0:T(8,128)(2,1)}, u32[]{:S(2)}) copy-start(bf16[1,64,8192]{2,1,0:T(8,128)(2,1)} %param.11) | copy-start | bytes 3145732
  10.1 27.5 %collective-permute-start = (bf16[16,8192]{1,0:T(8,128)(2,1)S(1)}, bf16[16,8192]{1,0:T(8,128)(2,1)S(1)}, u32[]{:S(2)}, u32[]{:S(2)}) collective-permute-start(bf16[16,8192]{1,0:T(8,128)(2,1)S(1)} %get-tuple-element.101), channel_id=1, source_target_pairs={{0,1},{1,0},{2,3},{3,2},{4,5},{5,4},{6,7},{7,6},{8,9},{9,8},{10,11... | collective-permute-start | bytes 786440 | tf_op jit(solution)/shard_map/ppermute | solution.py:341
  10.2 32.4 %collective-permute-start.1 = (bf16[16,8192]{1,0:T(8,128)(2,1)S(1)}, bf16[16,8192]{1,0:T(8,128)(2,1)S(1)}, u32[]{:S(2)}, u32[]{:S(2)}) collective-permute-start(bf16[16,8192]{1,0:T(8,128)(2,1)S(1)} %get-tuple-element.102), channel_id=1, source_target_pairs={{0,2},{1,3},{2,0},{3,1},{4,6},{5,7},{6,4},{7,5},{8,10},{9,11},{10,... | collective-permute-start | bytes 786440 | tf_op jit(solution)/shard_map/ppermute | solution.py:341
  11.7 31.5 %collective-permute-start.8 = (bf16[16,8192]{1,0:T(8,128)(2,1)S(1)}, bf16[16,8192]{1,0:T(8,128)(2,1)S(1)}, u32[]{:S(2)}, u32[]{:S(2)}) collective-permute-start(bf16[16,8192]{1,0:T(8,128)(2,1)S(1)} %get-tuple-element.112), channel_id=1, source_target_pairs={{0,9},{1,8},{2,11},{3,10},{4,13},{5,12},{6,15},{7,14},{8,1},{9,0},... | collective-permute-start | bytes 786440 | tf_op jit(solution)/shard_map/ppermute | solution.py:341
  26.4 22.4 %collective-permute-start.7 = (bf16[16,8192]{1,0:T(8,128)(2,1)S(1)}, bf16[16,8192]{1,0:T(8,128)(2,1)S(1)}, u32[]{:S(2)}, u32[]{:S(2)}) collective-permute-start(bf16[16,8192]{1,0:T(8,128)(2,1)S(1)} %get-tuple-element.111), channel_id=1, source_target_pairs={{0,8},{1,9},{2,10},{3,11},{4,12},{5,13},{6,14},{7,15},{8,0},{9,1},... | collective-permute-start | bytes 786440 | tf_op jit(solution)/shard_map/ppermute | solution.py:341
  37.6 24.0 %collective-permute-start.2 = (bf16[16,8192]{1,0:T(8,128)(2,1)S(1)}, bf16[16,8192]{1,0:T(8,128)(2,1)S(1)}, u32[]{:S(2)}, u32[]{:S(2)}) collective-permute-start(bf16[16,8192]{1,0:T(8,128)(2,1)S(1)} %get-tuple-element.103), channel_id=1, source_target_pairs={{0,3},{1,2},{2,1},{3,0},{4,7},{5,6},{6,5},{7,4},{8,11},{9,10},{10,... | collective-permute-start | bytes 786440 | tf_op jit(solution)/shard_map/ppermute | solution.py:341
  37.6 24.5 %collective-permute-start.3 = (bf16[16,8192]{1,0:T(8,128)(2,1)S(1)}, bf16[16,8192]{1,0:T(8,128)(2,1)S(1)}, u32[]{:S(2)}, u32[]{:S(2)}) collective-permute-start(bf16[16,8192]{1,0:T(8,128)(2,1)S(1)} %get-tuple-element.104), channel_id=1, source_target_pairs={{0,4},{1,5},{2,6},{3,7},{4,0},{5,1},{6,2},{7,3},{8,12},{9,13},{10,... | collective-permute-start | bytes 786440 | tf_op jit(solution)/shard_map/ppermute | solution.py:341
  42.6 34.4 %collective-permute-start.12 = (bf16[16,8192]{1,0:T(8,128)(2,1)S(1)}, bf16[16,8192]{1,0:T(8,128)(2,1)S(1)}, u32[]{:S(2)}, u32[]{:S(2)}) collective-permute-start(bf16[16,8192]{1,0:T(8,128)(2,1)S(1)} %get-tuple-element.116), channel_id=1, source_target_pairs={{0,11},{1,10},{2,9},{3,8},{4,15},{5,14},{6,13},{7,12},{8,3},{9,2},... | collective-permute-start | bytes 786440 | tf_op jit(solution)/shard_map/ppermute | solution.py:341
  43.3 39.4 %collective-permute-start.10 = (bf16[16,8192]{1,0:T(8,128)(2,1)S(1)}, bf16[16,8192]{1,0:T(8,128)(2,1)S(1)}, u32[]{:S(2)}, u32[]{:S(2)}) collective-permute-start(bf16[16,8192]{1,0:T(8,128)(2,1)S(1)} %get-tuple-element.114), channel_id=1, source_target_pairs={{0,10},{1,11},{2,8},{3,9},{4,14},{5,15},{6,12},{7,13},{8,2},{9,3},... | collective-permute-start | bytes 786440 | tf_op jit(solution)/shard_map/ppermute | solution.py:341
  48.7 41.7 %collective-permute-start.14 = (bf16[16,8192]{1,0:T(8,128)(2,1)S(1)}, bf16[16,8192]{1,0:T(8,128)(2,1)S(1)}, u32[]{:S(2)}, u32[]{:S(2)}) collective-permute-start(bf16[16,8192]{1,0:T(8,128)(2,1)S(1)} %get-tuple-element.120), channel_id=1, source_target_pairs={{0,13},{1,12},{2,15},{3,14},{4,9},{5,8},{6,11},{7,10},{8,5},{9,4},... | collective-permute-start | bytes 786440 | tf_op jit(solution)/shard_map/ppermute | solution.py:341
  61.6 34.6 %collective-permute-start.13 = (bf16[16,8192]{1,0:T(8,128)(2,1)S(1)}, bf16[16,8192]{1,0:T(8,128)(2,1)S(1)}, u32[]{:S(2)}, u32[]{:S(2)}) collective-permute-start(bf16[16,8192]{1,0:T(8,128)(2,1)S(1)} %get-tuple-element.118), channel_id=1, source_target_pairs={{0,12},{1,13},{2,14},{3,15},{4,8},{5,9},{6,10},{7,11},{8,4},{9,5},... | collective-permute-start | bytes 786440 | tf_op jit(solution)/shard_map/ppermute | solution.py:341
  62.1 34.1 %collective-permute-start.4 = (bf16[16,8192]{1,0:T(8,128)(2,1)S(1)}, bf16[16,8192]{1,0:T(8,128)(2,1)S(1)}, u32[]{:S(2)}, u32[]{:S(2)}) collective-permute-start(bf16[16,8192]{1,0:T(8,128)(2,1)S(1)} %get-tuple-element.106), channel_id=1, source_target_pairs={{0,5},{1,4},{2,7},{3,6},{4,1},{5,0},{6,3},{7,2},{8,13},{9,12},{10,... | collective-permute-start | bytes 786440 | tf_op jit(solution)/shard_map/ppermute | solution.py:341
  77.0 19.3 %collective-permute-start.5 = (bf16[16,8192]{1,0:T(8,128)(2,1)S(1)}, bf16[16,8192]{1,0:T(8,128)(2,1)S(1)}, u32[]{:S(2)}, u32[]{:S(2)}) collective-permute-start(bf16[16,8192]{1,0:T(8,128)(2,1)S(1)} %get-tuple-element.108), channel_id=1, source_target_pairs={{0,6},{1,7},{2,4},{3,5},{4,2},{5,3},{6,0},{7,1},{8,14},{9,15},{10,... | collective-permute-start | bytes 786440 | tf_op jit(solution)/shard_map/ppermute | solution.py:341
  82.6 21.5 %collective-permute-start.6 = (bf16[16,8192]{1,0:T(8,128)(2,1)S(1)}, bf16[16,8192]{1,0:T(8,128)(2,1)S(1)}, u32[]{:S(2)}, u32[]{:S(2)}) collective-permute-start(bf16[16,8192]{1,0:T(8,128)(2,1)S(1)} %get-tuple-element.110), channel_id=1, source_target_pairs={{0,7},{1,6},{2,5},{3,4},{4,3},{5,2},{6,1},{7,0},{8,15},{9,14},{10,... | collective-permute-start | bytes 786440 | tf_op jit(solution)/shard_map/ppermute | solution.py:341
  90.4 13.7 %collective-permute-start.19 = (bf16[16,8320]{1,0:T(8,128)(2,1)S(1)}, bf16[16,8320]{1,0:T(8,128)(2,1)S(1)}, u32[]{:S(2)}, u32[]{:S(2)}) collective-permute-start(bf16[16,8320]{1,0:T(8,128)(2,1)S(1)} %get-tuple-element.134), channel_id=1, source_target_pairs={{0,1},{1,0},{2,3},{3,2},{4,5},{5,4},{6,7},{7,6},{8,9},{9,8},{10,11... | collective-permute-start | bytes 798728 | tf_op jit(solution)/shard_map/ppermute | solution.py:341
  96.1 28.8 %collective-permute-start.33 = (bf16[16,8192]{1,0:T(8,128)(2,1)S(1)}, bf16[16,8192]{1,0:T(8,128)(2,1)S(1)}, u32[]{:S(2)}, u32[]{:S(2)}) collective-permute-start(bf16[16,8192]{1,0:T(8,128)(2,1)S(1)} %copy-done.19), channel_id=1, source_target_pairs={{0,8},{1,9},{2,10},{3,11},{4,12},{5,13},{6,14},{7,15},{8,0},{9,1},... | collective-permute-start | bytes 786440 | tf_op jit(solution)/shard_map/ppermute | solution.py:341
  96.1 34.5 %collective-permute-start.16 = (bf16[16,8192]{1,0:T(8,128)(2,1)S(1)}, bf16[16,8192]{1,0:T(8,128)(2,1)S(1)}, u32[]{:S(2)}, u32[]{:S(2)}) collective-permute-start(bf16[16,8192]{1,0:T(8,128)(2,1)S(1)} %get-tuple-element.124), channel_id=1, source_target_pairs={{0,15},{1,14},{2,13},{3,12},{4,11},{5,10},{6,9},{7,8},{8,7},{9,6},... | collective-permute-start | bytes 786440 | tf_op jit(solution)/shard_map/ppermute | solution.py:341
  96.3 41.2 %collective-permute-start.15 = (bf16[16,8192]{1,0:T(8,128)(2,1)S(1)}, bf16[16,8192]{1,0:T(8,128)(2,1)S(1)}, u32[]{:S(2)}, u32[]{:S(2)}) collective-permute-start(bf16[16,8192]{1,0:T(8,128)(2,1)S(1)} %get-tuple-element.122), channel_id=1, source_target_pairs={{0,14},{1,15},{2,12},{3,13},{4,10},{5,11},{6,8},{7,9},{8,6},{9,7},... | collective-permute-start | bytes 786440 | tf_op jit(solution)/shard_map/ppermute | solution.py:341
  104.1 37.4 %collective-permute-start.32 = (bf16[16,8192]{1,0:T(8,128)(2,1)S(1)}, bf16[16,8192]{1,0:T(8,128)(2,1)}, u32[]{:S(2)}, u32[]{:S(2)}) collective-permute-start(bf16[16,8192]{1,0:T(8,128)(2,1)S(1)} %copy-done.16), channel_id=1, source_target_pairs={{0,8},{1,9},{2,10},{3,11},{4,12},{5,13},{6,14},{7,15},{8,0},{9,1},... | collective-permute-start | bytes 786440 | tf_op jit(solution)/shard_map/ppermute | solution.py:341
  104.1 45.0 %collective-permute-start.25 = (bf16[16,8320]{1,0:T(8,128)(2,1)S(1)}, bf16[16,8320]{1,0:T(8,128)(2,1)S(1)}, u32[]{:S(2)}, u32[]{:S(2)}) collective-permute-start(bf16[16,8320]{1,0:T(8,128)(2,1)S(1)} %get-tuple-element.146), channel_id=1, source_target_pairs={{0,3},{1,2},{2,1},{3,0},{4,7},{5,6},{6,5},{7,4},{8,11},{9,10},{10,... | collective-permute-start | bytes 798728 | tf_op jit(solution)/shard_map/ppermute | solution.py:341
  124.9 24.9 %collective-permute-start.17 = (bf16[16,8320]{1,0:T(8,128)(2,1)S(1)}, bf16[16,8320]{1,0:T(8,128)(2,1)S(1)}, u32[]{:S(2)}, u32[]{:S(2)}) collective-permute-start(bf16[16,8320]{1,0:T(8,128)(2,1)S(1)} %get-tuple-element.129), channel_id=1, source_target_pairs={{0,4},{1,5},{2,6},{3,7},{4,0},{5,1},{6,2},{7,3},{8,12},{9,13},{10,... | collective-permute-start | bytes 798728 | tf_op jit(solution)/shard_map/ppermute | solution.py:341
  130.6 21.5 %collective-permute-start.22 = (bf16[16,8320]{1,0:T(8,128)(2,1)S(1)}, bf16[16,8320]{1,0:T(8,128)(2,1)S(1)}, u32[]{:S(2)}, u32[]{:S(2)}) collective-permute-start(bf16[16,8320]{1,0:T(8,128)(2,1)S(1)} %get-tuple-element.140), channel_id=1, source_target_pairs={{0,2},{1,3},{2,0},{3,1},{4,6},{5,7},{6,4},{7,5},{8,10},{9,11},{10,... | collective-permute-start | bytes 798728 | tf_op jit(solution)/shard_map/ppermute | solution.py:341
  137.5 17.1 %collective-permute-start.20 = (bf16[16,8320]{1,0:T(8,128)(2,1)S(1)}, bf16[16,8320]{1,0:T(8,128)(2,1)S(1)}, u32[]{:S(2)}, u32[]{:S(2)}) collective-permute-start(bf16[16,8320]{1,0:T(8,128)(2,1)S(1)} %get-tuple-element.135), channel_id=1, source_target_pairs={{0,5},{1,4},{2,7},{3,6},{4,1},{5,0},{6,3},{7,2},{8,13},{9,12},{10,... | collective-permute-start | bytes 798728 | tf_op jit(solution)/shard_map/ppermute | solution.py:341
  141.6 25.5 %collective-permute-start.43 = (bf16[16,8320]{1,0:T(8,128)(2,1)S(1)}, bf16[16,8320]{1,0:T(8,128)(2,1)S(1)}, u32[]{:S(2)}, u32[]{:S(2)}) collective-permute-start(bf16[16,8320]{1,0:T(8,128)(2,1)S(1)} %get-tuple-element.179), channel_id=1, source_target_pairs={{0,11},{1,10},{2,9},{3,8},{4,15},{5,14},{6,13},{7,12},{8,3},{9,2},... | collective-permute-start | bytes 798728 | tf_op jit(solution)/shard_map/ppermute | solution.py:341
  149.1 72.7 %copy-start.15 = (bf16[16,8192]{1,0:T(8,128)(2,1)S(1)}, bf16[16,8192]{1,0:T(8,128)(2,1)}, u32[]{:S(2)}) copy-start(bf16[16,8192]{1,0:T(8,128)(2,1)} %copy-done.14) | copy-start | bytes 786436
  149.1 23.7 %collective-permute-start.42 = (bf16[16,8320]{1,0:T(8,128)(2,1)S(1)}, bf16[16,8320]{1,0:T(8,128)(2,1)S(1)}, u32[]{:S(2)}, u32[]{:S(2)}) collective-permute-start(bf16[16,8320]{1,0:T(8,128)(2,1)S(1)} %get-tuple-element.177), channel_id=1, source_target_pairs={{0,10},{1,11},{2,8},{3,9},{4,14},{5,15},{6,12},{7,13},{8,2},{9,3},... | collective-permute-start | bytes 798728 | tf_op jit(solution)/shard_map/ppermute | solution.py:341
  149.8 34.7 %collective-permute-start.41 = (bf16[16,8320]{1,0:T(8,128)(2,1)S(1)}, bf16[16,8320]{1,0:T(8,128)(2,1)S(1)}, u32[]{:S(2)}, u32[]{:S(2)}) collective-permute-start(bf16[16,8320]{1,0:T(8,128)(2,1)S(1)} %get-tuple-element.175), channel_id=1, source_target_pairs={{0,9},{1,8},{2,11},{3,10},{4,13},{5,12},{6,15},{7,14},{8,1},{9,0},... | collective-permute-start | bytes 798728 | tf_op jit(solution)/shard_map/ppermute | solution.py:341
  152.2 35.1 %collective-permute-start.26 = (bf16[16,8320]{1,0:T(8,128)(2,1)S(1)}, bf16[16,8320]{1,0:T(8,128)(2,1)S(1)}, u32[]{:S(2)}, u32[]{:S(2)}) collective-permute-start(bf16[16,8320]{1,0:T(8,128)(2,1)S(1)} %get-tuple-element.147), channel_id=1, source_target_pairs={{0,7},{1,6},{2,5},{3,4},{4,3},{5,2},{6,1},{7,0},{8,15},{9,14},{10,... | collective-permute-start | bytes 798728 | tf_op jit(solution)/shard_map/ppermute | solution.py:341
  154.6 67.1 %copy-start.18 = (bf16[16,8192]{1,0:T(8,128)(2,1)S(1)}, bf16[16,8192]{1,0:T(8,128)(2,1)}, u32[]{:S(2)}) copy-start(bf16[16,8192]{1,0:T(8,128)(2,1)} %copy-done.17) | copy-start | bytes 786436
  154.6 33.5 %collective-permute-start.23 = (bf16[16,8320]{1,0:T(8,128)(2,1)S(1)}, bf16[16,8320]{1,0:T(8,128)(2,1)S(1)}, u32[]{:S(2)}, u32[]{:S(2)}) collective-permute-start(bf16[16,8320]{1,0:T(8,128)(2,1)S(1)} %get-tuple-element.141), channel_id=1, source_target_pairs={{0,6},{1,7},{2,4},{3,5},{4,2},{5,3},{6,0},{7,1},{8,14},{9,15},{10,... | collective-permute-start | bytes 798728 | tf_op jit(solution)/shard_map/ppermute | solution.py:341
  167.1 71.2 %copy-start.3 = (bf16[16,8320]{1,0:T(8,128)(2,1)}, bf16[16,8320]{1,0:T(8,128)(2,1)S(1)}, u32[]{:S(2)}) copy-start(bf16[16,8320]{1,0:T(8,128)(2,1)S(1)} %collective-permute-done.43.refs_11_.refs_27_.refs_14_) | copy-start | bytes 798724
  167.1 19.0 %collective-permute-start.18 = (bf16[16,8192]{1,0:T(8,128)(2,1)S(1)}, bf16[16,8192]{1,0:T(8,128)(2,1)S(1)}, u32[]{:S(2)}, u32[]{:S(2)}) collective-permute-start(bf16[16,8192]{1,0:T(8,128)(2,1)S(1)} %get-tuple-element.130), channel_id=1, source_target_pairs={{0,1},{1,0},{2,3},{3,2},{4,5},{5,4},{6,7},{7,6},{8,9},{9,8},{10,11... | collective-permute-start | bytes 786440 | tf_op jit(solution)/shard_map/ppermute | solution.py:341
  172.8 73.1 %copy-start.4 = (bf16[16,8320]{1,0:T(8,128)(2,1)}, bf16[16,8320]{1,0:T(8,128)(2,1)S(1)}, u32[]{:S(2)}) copy-start(bf16[16,8320]{1,0:T(8,128)(2,1)S(1)} %collective-permute-done.42.refs_10_.refs_26_.refs_13_) | copy-start | bytes 798724
  172.8 29.2 %collective-permute-start.31 = (bf16[16,8832]{1,0:T(8,128)(2,1)S(1)}, bf16[16,8832]{1,0:T(8,128)(2,1)S(1)}, u32[]{:S(2)}, u32[]{:S(2)}) collective-permute-start(bf16[16,8832]{1,0:T(8,128)(2,1)S(1)} %shard_map.89), channel_id=1, source_target_pairs={{0,8},{1,9},{2,10},{3,11},{4,12},{5,13},{6,14},{7,15},{8,0},{9,1},... | collective-permute-start | bytes 847880 | tf_op jit(solution)/shard_map/ppermute | solution.py:341
  184.6 61.4 %copy-start.5 = (bf16[16,8320]{1,0:T(8,128)(2,1)}, bf16[16,8320]{1,0:T(8,128)(2,1)S(1)}, u32[]{:S(2)}) copy-start(bf16[16,8320]{1,0:T(8,128)(2,1)S(1)} %collective-permute-done.41.refs_9_.refs_25_.refs_12_) | copy-start | bytes 798724
  184.6 27.7 %collective-permute-start.47 = (bf16[16,8320]{1,0:T(8,128)(2,1)S(1)}, bf16[16,8320]{1,0:T(8,128)(2,1)S(1)}, u32[]{:S(2)}, u32[]{:S(2)}) collective-permute-start(bf16[16,8320]{1,0:T(8,128)(2,1)S(1)} %get-tuple-element.187), channel_id=1, source_target_pairs={{0,15},{1,14},{2,13},{3,12},{4,11},{5,10},{6,9},{7,8},{8,7},{9,6},... | collective-permute-start | bytes 798728 | tf_op jit(solution)/shard_map/ppermute | solution.py:341
  186.1 34.8 %collective-permute-start.46 = (bf16[16,8320]{1,0:T(8,128)(2,1)S(1)}, bf16[16,8320]{1,0:T(8,128)(2,1)S(1)}, u32[]{:S(2)}, u32[]{:S(2)}) collective-permute-start(bf16[16,8320]{1,0:T(8,128)(2,1)S(1)} %get-tuple-element.185), channel_id=1, source_target_pairs={{0,14},{1,15},{2,12},{3,13},{4,10},{5,11},{6,8},{7,9},{8,6},{9,7},... | collective-permute-start | bytes 798728 | tf_op jit(solution)/shard_map/ppermute | solution.py:341
  187.3 58.7 %copy-start.6 = (bf16[16,8320]{1,0:T(8,128)(2,1)}, bf16[16,8320]{1,0:T(8,128)(2,1)S(1)}, u32[]{:S(2)}) copy-start(bf16[16,8320]{1,0:T(8,128)(2,1)S(1)} %collective-permute-done.26.refs_7_.refs_23_.refs_10_) | copy-start | bytes 798724
  187.3 8.3 %collective-permute-start.21 = (bf16[16,8192]{1,0:T(8,128)(2,1)S(1)}, bf16[16,8192]{1,0:T(8,128)(2,1)S(1)}, u32[]{:S(2)}, u32[]{:S(2)}) collective-permute-start(bf16[16,8192]{1,0:T(8,128)(2,1)S(1)} %get-tuple-element.136), channel_id=1, source_target_pairs={{0,2},{1,3},{2,0},{3,1},{4,6},{5,7},{6,4},{7,5},{8,10},{9,11},{10,... | collective-permute-start | bytes 786440 | tf_op jit(solution)/shard_map/ppermute | solution.py:341
  188.2 57.8 %copy-start.7 = (bf16[16,8320]{1,0:T(8,128)(2,1)}, bf16[16,8320]{1,0:T(8,128)(2,1)S(1)}, u32[]{:S(2)}) copy-start(bf16[16,8320]{1,0:T(8,128)(2,1)S(1)} %collective-permute-done.23.refs_6_.refs_22_.refs_9_) | copy-start | bytes 798724
  188.2 24.1 %collective-permute-start.28 = (bf16[16,8192]{1,0:T(8,128)(2,1)S(1)}, bf16[16,8192]{1,0:T(8,128)(2,1)S(1)}, u32[]{:S(2)}, u32[]{:S(2)}) collective-permute-start(bf16[16,8192]{1,0:T(8,128)(2,1)S(1)} %get-tuple-element.150), channel_id=1, source_target_pairs={{0,5},{1,4},{2,7},{3,6},{4,1},{5,0},{6,3},{7,2},{8,13},{9,12},{10,... | collective-permute-start | bytes 786440 | tf_op jit(solution)/shard_map/ppermute | solution.py:341
  195.6 35.9 %collective-permute-start.44 = (bf16[16,8320]{1,0:T(8,128)(2,1)}, bf16[16,8320]{1,0:T(8,128)(2,1)S(1)}, u32[]{:S(2)}, u32[]{:S(2)}) collective-permute-start(bf16[16,8320]{1,0:T(8,128)(2,1)} %get-tuple-element.181), channel_id=1, source_target_pairs={{0,12},{1,13},{2,14},{3,15},{4,8},{5,9},{6,10},{7,11},{8,4},{9,5},... | collective-permute-start | bytes 798728 | tf_op jit(solution)/shard_map/ppermute | solution.py:341
  202.0 44.0 %copy-start.2 = (bf16[16,8832]{1,0:T(8,128)(2,1)}, bf16[16,8832]{1,0:T(8,128)(2,1)S(1)}, u32[]{:S(2)}) copy-start(bf16[16,8832]{1,0:T(8,128)(2,1)S(1)} %collective-permute-done.31.refs_0_.refs_8_.refs_24_.refs_11_) | copy-start | bytes 847876
  202.0 23.4 %collective-permute-start.27 = (bf16[16,8192]{1,0:T(8,128)(2,1)}, bf16[16,8192]{1,0:T(8,128)(2,1)S(1)}, u32[]{:S(2)}, u32[]{:S(2)}) collective-permute-start(bf16[16,8192]{1,0:T(8,128)(2,1)} %get-tuple-element.148), channel_id=1, source_target_pairs={{0,4},{1,5},{2,6},{3,7},{4,0},{5,1},{6,2},{7,3},{8,12},{9,13},{10,... | collective-permute-start | bytes 786440 | tf_op jit(solution)/shard_map/ppermute | solution.py:341
  212.3 14.0 %collective-permute-start.24 = (bf16[16,8192]{1,0:T(8,128)(2,1)}, bf16[16,8192]{1,0:T(8,128)(2,1)S(1)}, u32[]{:S(2)}, u32[]{:S(2)}) collective-permute-start(bf16[16,8192]{1,0:T(8,128)(2,1)} %get-tuple-element.142), channel_id=1, source_target_pairs={{0,3},{1,2},{2,1},{3,0},{4,7},{5,6},{6,5},{7,4},{8,11},{9,10},{10,... | collective-permute-start | bytes 786440 | tf_op jit(solution)/shard_map/ppermute | solution.py:341
  212.3 19.1 %collective-permute-start.29 = (bf16[16,8192]{1,0:T(8,128)(2,1)}, bf16[16,8192]{1,0:T(8,128)(2,1)S(1)}, u32[]{:S(2)}, u32[]{:S(2)}) collective-permute-start(bf16[16,8192]{1,0:T(8,128)(2,1)} %get-tuple-element.152), channel_id=1, source_target_pairs={{0,6},{1,7},{2,4},{3,5},{4,2},{5,3},{6,0},{7,1},{8,14},{9,15},{10,... | collective-permute-start | bytes 786440 | tf_op jit(solution)/shard_map/ppermute | solution.py:341
  221.0 17.4 %collective-permute-start.45 = (bf16[16,8320]{1,0:T(8,128)(2,1)}, bf16[16,8320]{1,0:T(8,128)(2,1)S(1)}, u32[]{:S(2)}, u32[]{:S(2)}) collective-permute-start(bf16[16,8320]{1,0:T(8,128)(2,1)} %get-tuple-element.183), channel_id=1, source_target_pairs={{0,13},{1,12},{2,15},{3,14},{4,9},{5,8},{6,11},{7,10},{8,5},{9,4},... | collective-permute-start | bytes 798728 | tf_op jit(solution)/shard_map/ppermute | solution.py:341
  225.4 20.6 %collective-permute-start.35 = (bf16[16,8192]{1,0:T(8,128)(2,1)S(1)}, bf16[16,8192]{1,0:T(8,128)(2,1)S(1)}, u32[]{:S(2)}, u32[]{:S(2)}) collective-permute-start(bf16[16,8192]{1,0:T(8,128)(2,1)S(1)} %get-tuple-element.162), channel_id=1, source_target_pairs={{0,2},{1,3},{2,0},{3,1},{4,6},{5,7},{6,4},{7,5},{8,10},{9,11},{10,... | collective-permute-start | bytes 786440 | tf_op jit(solution)/shard_map/ppermute | solution.py:341
  226.3 19.8 %collective-permute-start.34 = (bf16[16,8192]{1,0:T(8,128)(2,1)S(1)}, bf16[16,8192]{1,0:T(8,128)(2,1)S(1)}, u32[]{:S(2)}, u32[]{:S(2)}) collective-permute-start(bf16[16,8192]{1,0:T(8,128)(2,1)S(1)} %get-tuple-element.160), channel_id=1, source_target_pairs={{0,1},{1,0},{2,3},{3,2},{4,5},{5,4},{6,7},{7,6},{8,9},{9,8},{10,11... | collective-permute-start | bytes 786440 | tf_op jit(solution)/shard_map/ppermute | solution.py:341
  231.4 15.8 %collective-permute-start.30 = (bf16[16,8192]{1,0:T(8,128)(2,1)}, bf16[16,8192]{1,0:T(8,128)(2,1)S(1)}, u32[]{:S(2)}, u32[]{:S(2)}) collective-permute-start(bf16[16,8192]{1,0:T(8,128)(2,1)} %get-tuple-element.154), channel_id=1, source_target_pairs={{0,7},{1,6},{2,5},{3,4},{4,3},{5,2},{6,1},{7,0},{8,15},{9,14},{10,... | collective-permute-start | bytes 786440 | tf_op jit(solution)/shard_map/ppermute | solution.py:341
  231.5 16.6 %collective-permute-start.36 = (bf16[16,8192]{1,0:T(8,128)(2,1)S(1)}, bf16[16,8192]{1,0:T(8,128)(2,1)S(1)}, u32[]{:S(2)}, u32[]{:S(2)}) collective-permute-start(bf16[16,8192]{1,0:T(8,128)(2,1)S(1)} %get-tuple-element.164), channel_id=1, source_target_pairs={{0,3},{1,2},{2,1},{3,0},{4,7},{5,6},{6,5},{7,4},{8,11},{9,10},{10,... | collective-permute-start | bytes 786440 | tf_op jit(solution)/shard_map/ppermute | solution.py:341
  246.0 37.1 %collective-permute-start.39 = (bf16[16,8192]{1,0:T(8,128)(2,1)S(1)}, bf16[16,8192]{1,0:T(8,128)(2,1)S(1)}, u32[]{:S(2)}, u32[]{:S(2)}) collective-permute-start(bf16[16,8192]{1,0:T(8,128)(2,1)S(1)} %get-tuple-element.170), channel_id=1, source_target_pairs={{0,6},{1,7},{2,4},{3,5},{4,2},{5,3},{6,0},{7,1},{8,14},{9,15},{10,... | collective-permute-start | bytes 786440 | tf_op jit(solution)/shard_map/ppermute | solution.py:341
  246.1 37.0 %collective-permute-start.38 = (bf16[16,8192]{1,0:T(8,128)(2,1)S(1)}, bf16[16,8192]{1,0:T(8,128)(2,1)S(1)}, u32[]{:S(2)}, u32[]{:S(2)}) collective-permute-start(bf16[16,8192]{1,0:T(8,128)(2,1)S(1)} %get-tuple-element.168), channel_id=1, source_target_pairs={{0,5},{1,4},{2,7},{3,6},{4,1},{5,0},{6,3},{7,2},{8,13},{9,12},{10,... | collective-permute-start | bytes 786440 | tf_op jit(solution)/shard_map/ppermute | solution.py:341
  247.2 35.9 %collective-permute-start.37 = (bf16[16,8192]{1,0:T(8,128)(2,1)S(1)}, bf16[16,8192]{1,0:T(8,128)(2,1)S(1)}, u32[]{:S(2)}, u32[]{:S(2)}) collective-permute-start(bf16[16,8192]{1,0:T(8,128)(2,1)S(1)} %get-tuple-element.166), channel_id=1, source_target_pairs={{0,4},{1,5},{2,6},{3,7},{4,0},{5,1},{6,2},{7,3},{8,12},{9,13},{10,... | collective-permute-start | bytes 786440 | tf_op jit(solution)/shard_map/ppermute | solution.py:341
  248.1 35.0 %collective-permute-start.40 = (bf16[16,8192]{1,0:T(8,128)(2,1)S(1)}, bf16[16,8192]{1,0:T(8,128)(2,1)S(1)}, u32[]{:S(2)}, u32[]{:S(2)}) collective-permute-start(bf16[16,8192]{1,0:T(8,128)(2,1)S(1)} %get-tuple-element.172), channel_id=1, source_target_pairs={{0,7},{1,6},{2,5},{3,4},{4,3},{5,2},{6,1},{7,0},{8,15},{9,14},{10,... | collective-permute-start | bytes 786440 | tf_op jit(solution)/shard_map/ppermute | solution.py:341
  254.0 1.2 collective-permute-start.48
  256.6 3.6 %collective-permute-start.49 = (f32[1,1]{1,0:T(1,128)}, f32[1,1]{1,0:T(1,128)}, u32[]{:S(2)}, u32[]{:S(2)}) collective-permute-start(f32[1,1]{1,0:T(1,128)} %add.15), channel_id=1, source_target_pairs={{0,2},{1,3},{2,0},{3,1},{4,6},{5,7},{6,4},{7,5},{8,10},{9,11},{10,... | collective-permute-start | bytes 20 | tf_op jit(solution)/shard_map/ppermute | solution.py:25
  260.9 10.0 %collective-permute-start.50 = (f32[1,1]{1,0:T(1,128)}, f32[1,1]{1,0:T(1,128)}, u32[]{:S(2)}, u32[]{:S(2)}) collective-permute-start(f32[1,1]{1,0:T(1,128)} %add.16), channel_id=1, source_target_pairs={{0,4},{1,5},{2,6},{3,7},{4,0},{5,1},{6,2},{7,3},{8,12},{9,13},{10,... | collective-permute-start | bytes 20 | tf_op jit(solution)/shard_map/ppermute | solution.py:25
  271.5 4.5 %collective-permute-start.51 = (f32[1,1]{1,0:T(1,128)}, f32[1,1]{1,0:T(1,128)}, u32[]{:S(2)}, u32[]{:S(2)}) collective-permute-start(f32[1,1]{1,0:T(1,128)} %add.17), channel_id=1, source_target_pairs={{0,8},{1,9},{2,10},{3,11},{4,12},{5,13},{6,14},{7,15},{8,0},{9,1},... | collective-permute-start | bytes 20 | tf_op jit(solution)/shard_map/ppermute | solution.py:25
  (9 other events, 154.2 us)

commit v5 on v4

--- a/solution.py
+++ b/solution.py
@@ -8,9 +8,11 @@
 SCALE = 2.0
 DAMPING = 1.0
 EPS = 1e-06
-VMEM_LIMIT = 48 * 1024 * 1024
+VMEM_LIMIT = 44 * 1024 * 1024
 LANES = 128
 FAR_WINDOW = 4
+CHUNK = 8192
+MIRROR_ORDER = [1, 2, 3, 4, 5, 6, 7]
 NEAR_WINDOW = 4
 LAST = (((1,), (1,)), ((), ()))
 FIRST = (((0,), (0,)), ((), ()))
@@ -28,19 +30,19 @@
 
 
 def rows_kernel(scale, count, with_extra, *refs):
-    blocks, extras = refs[:count], refs[count : 2 * count if with_extra else count]
-    weight_ref, low_ref, gram_ref, *rest = refs[count + len(extras) :]
+    blocks, (weight_ref, low_ref, gram_ref, *rest) = refs[:count], refs[count:]
     low_total = rest[-1]
     step = pl.program_id(0)
+    chunk = weight_ref.shape[1]
 
     @pl.when(step == 0)
     def _():
         low_total[...] = jnp.zeros_like(low_total)
         gram_ref[...] = jnp.zeros_like(gram_ref)
         if with_extra:
-            rest[0][...] = jnp.concatenate([ref[...] for ref in extras], axis=0)
-
-    rows = jnp.concatenate([ref[...] for ref in blocks], axis=0)
+            rest[0][...] = jnp.concatenate([ref[:, ref.shape[1] - LANES :] for ref in blocks], axis=0)
+
+    rows = jnp.concatenate([ref[:, :chunk] for ref in blocks], axis=0)
     low_total[...] += lax.dot_general(rows, weight_ref[...], LAST, preferred_element_type=jnp.float32)
     gram_ref[...] += lax.dot_general(rows, rows, LAST, preferred_element_type=jnp.float32)
 
@@ -52,19 +54,16 @@
 def rows_products(blocks, weight, scale, with_extra=False):
     slots = sum(block.shape[0] for block in blocks)
     rank, width = weight.shape
-    chunk = min(width, 2048)
-    in_specs = [pl.BlockSpec((block.shape[0], chunk), lambda i: (0, i)) for block in blocks]
+    chunk = width if with_extra else min(width, CHUNK)
+    in_specs = [
+        pl.BlockSpec((block.shape[0], block.shape[1] if with_extra else chunk), lambda i: (0, i)) for block in blocks
+    ]
     out_specs = [pl.BlockSpec((slots, rank), lambda i: (0, 0)), pl.BlockSpec((slots, slots), lambda i: (0, 0))]
     out_shape = [
         jax.ShapeDtypeStruct((slots, rank), jnp.bfloat16),
         jax.ShapeDtypeStruct((slots, slots), jnp.float32),
     ]
-    operands = list(blocks)
     if with_extra:
-        in_specs += [
-            pl.BlockSpec((block.shape[0], LANES), lambda i, at=block.shape[1] // LANES - 1: (0, at)) for block in blocks
-        ]
-        operands += list(blocks)
         out_specs.append(pl.BlockSpec((slots, LANES), lambda i: (0, 0)))
         out_shape.append(jax.ShapeDtypeStruct((slots, LANES), jnp.bfloat16))
     return pl.pallas_call(
@@ -80,7 +79,7 @@
             bytes_accessed=2 * width * (slots + rank),
             transcendentals=0,
         ),
-    )(*operands, weight)
+    )(*blocks, weight)
 
 
 def slot_targets(cap, me, owner_ref, column_ref, row_ref):
@@ -136,7 +135,7 @@
     rows, width = values.shape
     adapters = owner.shape[0]
     full = width + (LANES if with_live else 0) + (low.size // cap if low is not None else 0)
-    chunk = min(width, 2048)
+    chunk = min(width, CHUNK)
     still = lambda shape: pl.BlockSpec(shape, lambda i: (0, 0))
     in_specs = [
         pl.BlockSpec(memory_space=pltpu.SMEM),
@@ -182,7 +181,7 @@
 
 def back_rows(count, cap, low, weight, low_spec, stacked):
     rank, width = weight.shape
-    chunk = min(width, 2048)
+    chunk = min(width, CHUNK)
     return pl.pallas_call(
         lambda *refs: back_kernel(count, stacked, *refs),
         grid=(width // chunk,),
@@ -215,7 +214,7 @@
 def input_grad_of(cap, me, owner, tenant, blocks):
     rows, adapters, count = tenant.shape[0], owner.shape[0], len(blocks)
     width = blocks[0].shape[1]
-    chunk = min(width, 2048)
+    chunk = min(width, CHUNK)
     still = lambda shape: pl.BlockSpec(shape, lambda i: (0, 0))
     return pl.pallas_call(
         lambda *refs: input_grad_kernel(cap, count, *refs),
@@ -306,7 +305,7 @@
 def grads(factor, left_a, left_b, blocks_x, blocks_dy, width):
     slots = left_a.shape[0]
     rank = left_a.shape[1] // 3
-    chunk = min(width, 2048)
+    chunk = min(width, CHUNK)
     left_spec = pl.BlockSpec((slots, 3 * rank), lambda i: (0, 0))
     rows_specs = [pl.BlockSpec((block.shape[0], chunk), lambda i: (0, i)) for block in blocks_x]
     out_spec = pl.BlockSpec((rank, chunk), lambda i: (0, i))
@@ -397,11 +396,10 @@
     back[half] = mirror_back[0]
     for at, s in enumerate(range(half + 1 + half // 2, count_blk)):
         got_x[s] = far.swap(sent_x[s], s)
-        for partner in (2 * at + 1, 2 * at + 2):
+        for partner in MIRROR_ORDER[2 * at : 2 * at + 2]:
             back[half + partner] = near.swap(mirror_back[partner], partner)
-    for partner in range(1, half):
-        if half + partner not in back:
-            back[half + partner] = near.swap(mirror_back[partner], partner)
+    for partner in MIRROR_ORDER[6:]:
+        back[half + partner] = near.swap(mirror_back[partner], partner)
 
     blocks_x = [got_x[s] for s in range(count_blk)]
     hidden, gram_x, live = rows_products(blocks_x, down_weight, 1.0, with_extra=True)

time: 289 us -> 282 us (0.976)
  Pallas kernels: 35.2 us -> 16.8 us
  waiting for transfers between devices: 137 us -> 154 us
  starting transfers between devices: 106 us -> 100 us
    ppermute x48, waiting for transfers between devices: 130 us -> 148 us  [swap(): result = lax.ppermute(value, 'blk', [(i, i ^ partner) for i in range(size)])]
    pallas_call x2, Pallas kernels: 11.2 us -> 4.72 us  [rows_products(): pl.pallas_call(lambda *refs: rows_kernel(scale, len(blocks), with_extra,...]
    ppermute x4, starting transfers between devices: 12.5 us -> 6.84 us  [total_over_blk(): lax.ppermute(value, 'blk', [(i, i ^ step) for i in range(size)])]
    pallas_call x3, Pallas kernels: 7.91 us -> 3.03 us  [place(): pl.pallas_call(lambda *refs: place_kernel(partners, cap, with_live, *refs...]
    pallas_call x1, Pallas kernels: 6.38 us -> 3.03 us  [grads(): pl.pallas_call(lambda *refs: grads_kernel(len(blocks_x), *refs), grid=(wi...]
  transfers between devices with their start and end apart: 52 -> 52, of which waited for: 26 -> 27; matrix products, arithmetic and copies ran while one was open for 1% -> 1% of each run, Pallas kernels for 11% -> 5%
where the time goes in v5:
time: 282 us; the launch traced here: 280 us
  waiting for transfers between devices  154 us (55%)
  starting transfers between devices  100 us (35%)
  Pallas kernels  16.8 us (6%)
  local copies, waits for them, and re-layouts  4.43 us (2%)
  between operations  4.07 us (1%)
    ppermute x48, waiting for transfers between devices, swap(): result = lax.ppermute(value, 'blk', [(i, i ^ partner) for i in range(size)])  148 us
    ppermute x48, starting transfers between devices, swap(): result = lax.ppermute(value, 'blk', [(i, i ^ partner) for i in range(size)])  93.1 us
    ppermute x4, starting transfers between devices, total_over_blk(): lax.ppermute(value, 'blk', [(i, i ^ step) for i in range(size)])  6.84 us
    ppermute x4, waiting for transfers between devices, total_over_blk(): lax.ppermute(value, 'blk', [(i, i ^ step) for i in range(size)])  5.98 us
  transfers between devices with their start and end apart: 52, of which 27 were waited for; matrix products, arithmetic and copies ran while one was open for 1% of the time, Pallas kernels for 5%

profile of v5, /device:TPU:16, one launch (start us, length us, event | category | flops | bytes accessed | tf_op | source)
XLA Modules:
  0.0 279.6 jit_solution(261730661650425518)
XLA Ops:
  0.7 2.1 slice_bitcast_fusion.1
  2.8 2.9 %collective-permute-start.11 = (bf16[16,8192]{1,0:T(8,128)(2,1)S(1)}, bf16[16,8192]{1,0:T(8,128)(2,1)S(1)}, u32[]{:S(2)}, u32[]{:S(2)}) collective-permute-start(bf16[16,8192]{1,0:T(8,128)(2,1)S(1)} %get-tuple-element.198), channel_id=1, source_target_pairs={{0,8},{1,9},{2,10},{3,11},{4,12},{5,13},{6,14},{7,15},{8,0},{9,1},... | collective-permute-start | bytes 786440 | tf_op jit(solution)/shard_map/ppermute | solution.py:340
  5.9 1.6 copy-done.2
  7.5 1.3 shard_map.85
  8.9 1.6 collective-permute-start.1
  10.6 16.0 %collective-permute-done.9 = bf16[16,8192]{1,0:T(8,128)(2,1)S(1)} collective-permute-done((bf16[16,8192]{1,0:T(8,128)(2,1)}, bf16[16,8192]{1,0:T(8,128)(2,1)S(1)}, u32[]{:S(2)}, u32[]{:S(2)}) %collective-permute-start.9) | collective-permute-done | bytes 262176 | tf_op jit(solution)/shard_map/ppermute | solution.py:340
  26.6 3.3 %collective-permute-start.7 = (bf16[16,8192]{1,0:T(8,128)(2,1)S(1)}, bf16[16,8192]{1,0:T(8,128)(2,1)S(1)}, u32[]{:S(2)}, u32[]{:S(2)}) collective-permute-start(bf16[16,8192]{1,0:T(8,128)(2,1)S(1)} %get-tuple-element.111), channel_id=1, source_target_pairs={{0,8},{1,9},{2,10},{3,11},{4,12},{5,13},{6,14},{7,15},{8,0},{9,1},... | collective-permute-start | bytes 786440 | tf_op jit(solution)/shard_map/ppermute | solution.py:340
  29.9 7.9 %collective-permute-done.11 = bf16[16,8192]{1,0:T(8,128)(2,1)S(1)} collective-permute-done((bf16[16,8192]{1,0:T(8,128)(2,1)S(1)}, bf16[16,8192]{1,0:T(8,128)(2,1)S(1)}, u32[]{:S(2)}, u32[]{:S(2)}) %collective-permute-start.11) | collective-permute-done | bytes 262176 | tf_op jit(solution)/shard_map/ppermute | solution.py:340
  37.8 4.9 %collective-permute-start.3 = (bf16[16,8192]{1,0:T(8,128)(2,1)S(1)}, bf16[16,8192]{1,0:T(8,128)(2,1)S(1)}, u32[]{:S(2)}, u32[]{:S(2)}) collective-permute-start(bf16[16,8192]{1,0:T(8,128)(2,1)S(1)} %get-tuple-element.104), channel_id=1, source_target_pairs={{0,4},{1,5},{2,6},{3,7},{4,0},{5,1},{6,2},{7,3},{8,12},{9,13},{10,... | collective-permute-start | bytes 786440 | tf_op jit(solution)/shard_map/ppermute | solution.py:340
  43.4 3.0 %collective-permute-start.10 = (bf16[16,8192]{1,0:T(8,128)(2,1)S(1)}, bf16[16,8192]{1,0:T(8,128)(2,1)S(1)}, u32[]{:S(2)}, u32[]{:S(2)}) collective-permute-start(bf16[16,8192]{1,0:T(8,128)(2,1)S(1)} %get-tuple-element.114), channel_id=1, source_target_pairs={{0,10},{1,11},{2,8},{3,9},{4,14},{5,15},{6,12},{7,13},{8,2},{9,3},... | collective-permute-start | bytes 786440 | tf_op jit(solution)/shard_map/ppermute | solution.py:340
  46.4 2.6 collective-permute-done.7.refs_8_.refs_27_
  49.0 12.7 %collective-permute-start.14 = (bf16[16,8192]{1,0:T(8,128)(2,1)S(1)}, bf16[16,8192]{1,0:T(8,128)(2,1)S(1)}, u32[]{:S(2)}, u32[]{:S(2)}) collective-permute-start(bf16[16,8192]{1,0:T(8,128)(2,1)S(1)} %get-tuple-element.120), channel_id=1, source_target_pairs={{0,13},{1,12},{2,15},{3,14},{4,9},{5,8},{6,11},{7,10},{8,5},{9,4},... | collective-permute-start | bytes 786440 | tf_op jit(solution)/shard_map/ppermute | solution.py:340
  62.2 5.2 %collective-permute-start.4 = (bf16[16,8192]{1,0:T(8,128)(2,1)S(1)}, bf16[16,8192]{1,0:T(8,128)(2,1)S(1)}, u32[]{:S(2)}, u32[]{:S(2)}) collective-permute-start(bf16[16,8192]{1,0:T(8,128)(2,1)S(1)} %get-tuple-element.106), channel_id=1, source_target_pairs={{0,5},{1,4},{2,7},{3,6},{4,1},{5,0},{6,3},{7,2},{8,13},{9,12},{10,... | collective-permute-start | bytes 786440 | tf_op jit(solution)/shard_map/ppermute | solution.py:340
  67.4 9.8 %collective-permute-done.12.refs_11_.refs_30_ = bf16[16,8192]{1,0:T(8,128)(2,1)S(1)} collective-permute-done((bf16[16,8192]{1,0:T(8,128)(2,1)S(1)}, bf16[16,8192]{1,0:T(8,128)(2,1)S(1)}, u32[]{:S(2)}, u32[]{:S(2)}) %collective-permute-start.12) | collective-permute-done | bytes 262176 | tf_op jit(solution)/shard_map/ppermute | solution.py:340
  77.2 4.6 %collective-permute-start.5 = (bf16[16,8192]{1,0:T(8,128)(2,1)S(1)}, bf16[16,8192]{1,0:T(8,128)(2,1)S(1)}, u32[]{:S(2)}, u32[]{:S(2)}) collective-permute-start(bf16[16,8192]{1,0:T(8,128)(2,1)S(1)} %get-tuple-element.108), channel_id=1, source_target_pairs={{0,6},{1,7},{2,4},{3,5},{4,2},{5,3},{6,0},{7,1},{8,14},{9,15},{10,... | collective-permute-start | bytes 786440 | tf_op jit(solution)/shard_map/ppermute | solution.py:340
  81.7 1.0 collective-permute-done.10.refs_10_.refs_29_
  82.8 4.3 %collective-permute-start.6 = (bf16[16,8192]{1,0:T(8,128)(2,1)S(1)}, bf16[16,8192]{1,0:T(8,128)(2,1)S(1)}, u32[]{:S(2)}, u32[]{:S(2)}) collective-permute-start(bf16[16,8192]{1,0:T(8,128)(2,1)S(1)} %get-tuple-element.110), channel_id=1, source_target_pairs={{0,7},{1,6},{2,5},{3,4},{4,3},{5,2},{6,1},{7,0},{8,15},{9,14},{10,... | collective-permute-start | bytes 786440 | tf_op jit(solution)/shard_map/ppermute | solution.py:340
  87.0 1.3 shard_map.88
  88.3 2.3 collective-permute-done.14.refs_13_.refs_32_
  90.9 5.4 %collective-permute-done.13.refs_12_.refs_31_ = bf16[16,8192]{1,0:T(8,128)(2,1)S(1)} collective-permute-done((bf16[16,8192]{1,0:T(8,128)(2,1)S(1)}, bf16[16,8192]{1,0:T(8,128)(2,1)S(1)}, u32[]{:S(2)}, u32[]{:S(2)}) %collective-permute-start.13) | collective-permute-done | bytes 262176 | tf_op jit(solution)/shard_map/ppermute | solution.py:340
  96.4 2.4 collective-permute-start.15
  98.8 5.4 %collective-permute-done.6.refs_7_.refs_26_ = bf16[16,8192]{1,0:T(8,128)(2,1)S(1)} collective-permute-done((bf16[16,8192]{1,0:T(8,128)(2,1)S(1)}, bf16[16,8192]{1,0:T(8,128)(2,1)S(1)}, u32[]{:S(2)}, u32[]{:S(2)}) %collective-permute-start.6) | collective-permute-done | bytes 262176 | tf_op jit(solution)/shard_map/ppermute | solution.py:340
  105.1 20.0 %collective-permute-done.33 = bf16[16,8192]{1,0:T(8,128)(2,1)S(1)} collective-permute-done((bf16[16,8192]{1,0:T(8,128)(2,1)S(1)}, bf16[16,8192]{1,0:T(8,128)(2,1)S(1)}, u32[]{:S(2)}, u32[]{:S(2)}) %collective-permute-start.33) | collective-permute-done | bytes 262176 | tf_op jit(solution)/shard_map/ppermute | solution.py:340
  125.0 1.9 collective-permute-start.17
  126.9 3.9 %collective-permute-done.16.refs_15_.refs_34_ = bf16[16,8192]{1,0:T(8,128)(2,1)S(1)} collective-permute-done((bf16[16,8192]{1,0:T(8,128)(2,1)S(1)}, bf16[16,8192]{1,0:T(8,128)(2,1)S(1)}, u32[]{:S(2)}, u32[]{:S(2)}) %collective-permute-start.16) | collective-permute-done | bytes 262176 | tf_op jit(solution)/shard_map/ppermute | solution.py:340
  130.8 1.4 collective-permute-start.22
  132.2 5.5 %collective-permute-done.15.refs_14_.refs_33_ = bf16[16,8192]{1,0:T(8,128)(2,1)S(1)} collective-permute-done((bf16[16,8192]{1,0:T(8,128)(2,1)S(1)}, bf16[16,8192]{1,0:T(8,128)(2,1)S(1)}, u32[]{:S(2)}, u32[]{:S(2)}) %collective-permute-start.15) | collective-permute-done | bytes 262176 | tf_op jit(solution)/shard_map/ppermute | solution.py:340
  137.7 4.0 %collective-permute-done.32 = bf16[16,8192]{1,0:T(8,128)(2,1)S(1)} collective-permute-done((bf16[16,8192]{1,0:T(8,128)(2,1)S(1)}, bf16[16,8192]{1,0:T(8,128)(2,1)S(1)}, u32[]{:S(2)}, u32[]{:S(2)}) %collective-permute-start.32) | collective-permute-done | bytes 262176 | tf_op jit(solution)/shard_map/ppermute | solution.py:340
  141.7 3.8 %collective-permute-start.43 = (bf16[16,8320]{1,0:T(8,128)(2,1)S(1)}, bf16[16,8320]{1,0:T(8,128)(2,1)S(1)}, u32[]{:S(2)}, u32[]{:S(2)}) collective-permute-start(bf16[16,8320]{1,0:T(8,128)(2,1)S(1)} %get-tuple-element.179), channel_id=1, source_target_pairs={{0,11},{1,10},{2,9},{3,8},{4,15},{5,14},{6,13},{7,12},{8,3},{9,2},... | collective-permute-start | bytes 798728 | tf_op jit(solution)/shard_map/ppermute | solution.py:340
  145.5 2.4 shard_map.86
  148.6 2.4 collective-permute-start.41
  151.7 2.7 collective-permute-start.23
  154.3 13.0 %collective-permute-done.43.refs_11_.refs_14_ = bf16[16,8320]{1,0:T(8,128)(2,1)S(1)} collective-permute-done((bf16[16,8320]{1,0:T(8,128)(2,1)S(1)}, bf16[16,8320]{1,0:T(8,128)(2,1)S(1)}, u32[]{:S(2)}, u32[]{:S(2)}) %collective-permute-start.43) | collective-permute-done | bytes 266272 | tf_op jit(solution)/shard_map/ppermute | solution.py:340
  167.8 5.1 %collective-permute-done.42.refs_10_.refs_13_ = bf16[16,8320]{1,0:T(8,128)(2,1)S(1)} collective-permute-done((bf16[16,8320]{1,0:T(8,128)(2,1)S(1)}, bf16[16,8320]{1,0:T(8,128)(2,1)S(1)}, u32[]{:S(2)}, u32[]{:S(2)}) %collective-permute-start.42) | collective-permute-done | bytes 266272 | tf_op jit(solution)/shard_map/ppermute | solution.py:340
  173.0 3.8 %collective-permute-start.31 = (bf16[16,8832]{1,0:T(8,128)(2,1)S(1)}, bf16[16,8832]{1,0:T(8,128)(2,1)S(1)}, u32[]{:S(2)}, u32[]{:S(2)}) collective-permute-start(bf16[16,8832]{1,0:T(8,128)(2,1)S(1)} %shard_map.89), channel_id=1, source_target_pairs={{0,8},{1,9},{2,10},{3,11},{4,12},{5,13},{6,14},{7,15},{8,0},{9,1},... | collective-permute-start | bytes 847880 | tf_op jit(solution)/shard_map/ppermute | solution.py:340
  176.7 8.0 %collective-permute-done.41.refs_9_.refs_12_ = bf16[16,8320]{1,0:T(8,128)(2,1)S(1)} collective-permute-done((bf16[16,8320]{1,0:T(8,128)(2,1)S(1)}, bf16[16,8320]{1,0:T(8,128)(2,1)S(1)}, u32[]{:S(2)}, u32[]{:S(2)}) %collective-permute-start.41) | collective-permute-done | bytes 266272 | tf_op jit(solution)/shard_map/ppermute | solution.py:340
  184.7 1.4 collective-permute-start.47
  186.1 1.3 collective-permute-start.46
  188.3 4.5 %collective-permute-start.28 = (bf16[16,8192]{1,0:T(8,128)(2,1)S(1)}, bf16[16,8192]{1,0:T(8,128)(2,1)S(1)}, u32[]{:S(2)}, u32[]{:S(2)}) collective-permute-start(bf16[16,8192]{1,0:T(8,128)(2,1)S(1)} %get-tuple-element.150), channel_id=1, source_target_pairs={{0,5},{1,4},{2,7},{3,6},{4,1},{5,0},{6,3},{7,2},{8,13},{9,12},{10,... | collective-permute-start | bytes 786440 | tf_op jit(solution)/shard_map/ppermute | solution.py:340
  192.8 3.0 %collective-permute-done.21.refs_6_ = bf16[16,8192]{1,0:T(8,128)(2,1)S(1)} collective-permute-done((bf16[16,8192]{1,0:T(8,128)(2,1)S(1)}, bf16[16,8192]{1,0:T(8,128)(2,1)S(1)}, u32[]{:S(2)}, u32[]{:S(2)}) %collective-permute-start.21) | collective-permute-done | bytes 262176 | tf_op jit(solution)/shard_map/ppermute | solution.py:340
  195.8 1.1 collective-permute-start.44
  196.8 5.3 %collective-permute-done.31.refs_0_.refs_8_.refs_11_ = bf16[16,8832]{1,0:T(8,128)(2,1)S(1)} collective-permute-done((bf16[16,8832]{1,0:T(8,128)(2,1)S(1)}, bf16[16,8832]{1,0:T(8,128)(2,1)S(1)}, u32[]{:S(2)}, u32[]{:S(2)}) %collective-permute-start.31) | collective-permute-done | bytes 282656 | tf_op jit(solution)/shard_map/ppermute | solution.py:340
  202.1 10.3 %collective-permute-start.27 = (bf16[16,8192]{1,0:T(8,128)(2,1)S(1)}, bf16[16,8192]{1,0:T(8,128)(2,1)S(1)}, u32[]{:S(2)}, u32[]{:S(2)}) collective-permute-start(bf16[16,8192]{1,0:T(8,128)(2,1)S(1)} %get-tuple-element.148), channel_id=1, source_target_pairs={{0,4},{1,5},{2,6},{3,7},{4,0},{5,1},{6,2},{7,3},{8,12},{9,13},{10,... | collective-permute-start | bytes 786440 | tf_op jit(solution)/shard_map/ppermute | solution.py:340
  213.3 7.7 %collective-permute-done.46.refs_14_.refs_17_ = bf16[16,8320]{1,0:T(8,128)(2,1)S(1)} collective-permute-done((bf16[16,8320]{1,0:T(8,128)(2,1)S(1)}, bf16[16,8320]{1,0:T(8,128)(2,1)S(1)}, u32[]{:S(2)}, u32[]{:S(2)}) %collective-permute-start.46) | collective-permute-done | bytes 266272 | tf_op jit(solution)/shard_map/ppermute | solution.py:340
  221.0 0.9 collective-permute-start.45
  222.7 2.6 collective-permute-done.27.refs_8_
  226.2 5.1 %collective-permute-done.29.refs_10_ = bf16[16,8192]{1,0:T(8,128)(2,1)S(1)} collective-permute-done((bf16[16,8192]{1,0:T(8,128)(2,1)S(1)}, bf16[16,8192]{1,0:T(8,128)(2,1)S(1)}, u32[]{:S(2)}, u32[]{:S(2)}) %collective-permute-start.29) | collective-permute-done | bytes 262176 | tf_op jit(solution)/shard_map/ppermute | solution.py:340
  231.6 2.2 collective-permute-start.36
  233.8 4.5 %collective-permute-done.45.refs_13_.refs_16_ = bf16[16,8320]{1,0:T(8,128)(2,1)S(1)} collective-permute-done((bf16[16,8320]{1,0:T(8,128)(2,1)S(1)}, bf16[16,8320]{1,0:T(8,128)(2,1)S(1)}, u32[]{:S(2)}, u32[]{:S(2)}) %collective-permute-start.45) | collective-permute-done | bytes 266272 | tf_op jit(solution)/shard_map/ppermute | solution.py:340
  238.4 2.4 shard_map.92
  240.8 1.1 collective-permute-start.38
  241.9 2.0 collective-permute-start.37
  243.9 8.8 %collective-permute-done.36.refs_15_ = bf16[16,8192]{1,0:T(8,128)(2,1)S(1)} collective-permute-done((bf16[16,8192]{1,0:T(8,128)(2,1)S(1)}, bf16[16,8192]{1,0:T(8,128)(2,1)S(1)}, u32[]{:S(2)}, u32[]{:S(2)}) %collective-permute-start.36) | collective-permute-done | bytes 262176 | tf_op jit(solution)/shard_map/ppermute | solution.py:340
  252.7 2.1 collective-permute-start.40
  255.4 2.4 shard_map.93
  258.6 1.0 collective-permute-done.48
  260.9 2.2 collective-permute-start.49
  263.1 1.3 collective-permute-done.49
  265.1 1.7 collective-permute-start.50
  266.8 1.8 collective-permute-done.50
  269.2 2.6 collective-permute-start.51
  271.8 1.9 collective-permute-done.51
  274.4 3.0 %shard_map.94 = (bf16[64,8192]{1,0:T(8,128)(2,1)}, bf16[64,8192]{1,0:T(8,128)(2,1)}) custom-call(f32[1,1]{1,0:T(1,128)S(6)} %min.3.refs_0_, bf16[256,192]{1,0:T(8,128)(2,1)S(1)} %get-tuple-element.193.refs_1_, bf16[256,192]{1,0:T(8,128)(2,1)S(1)} %get-tuple-element.194.refs_2_, bf16[16,8320]{1,0:T(8,128)(2,1)S(1)} %get-tuple-element.173.refs_0_.refs_3_, ...), custom_call_target="tpu_custom_call" | custom-call | flops 1610612736 | bytes 10485760 | tf_op jit(solution)/shard_map/pallas_call | solution.py:312
  277.4 2.2 shard_map.91
  (69 shorter events, 10.2 us)
Async XLA Ops:
  0.6 5.1 %copy-start.5 = (s32[16]{0:T(128)S(1)}, s32[16]{0:T(128)}, u32[]{:S(2)}) copy-start(s32[16]{0:T(128)} %param.9) | copy-start | bytes 196
  0.6 5.1 %copy-start.4 = (s32[128,1]{0,1:T(1,128)S(1)}, s32[128,1]{0,1:T(1,128)}, u32[]{:S(2)}) copy-start(s32[128,1]{0,1:T(1,128)} %param.8) | copy-start | bytes 1540
  0.7 86.4 %copy-start.1 = (bf16[128,8192]{1,0:T(8,128)(2,1)S(1)}, bf16[128,8192]{1,0:T(8,128)(2,1)}, u32[]{:S(2)}) copy-start(bf16[128,8192]{1,0:T(8,128)(2,1)} %refs_4_.5) | copy-start | bytes 6291460
  2.8 23.8 %collective-permute-start.9 = (bf16[16,8192]{1,0:T(8,128)(2,1)}, bf16[16,8192]{1,0:T(8,128)(2,1)S(1)}, u32[]{:S(2)}, u32[]{:S(2)}) collective-permute-start(bf16[16,8192]{1,0:T(8,128)(2,1)} %get-tuple-element.199), channel_id=1, source_target_pairs={{0,8},{1,9},{2,10},{3,11},{4,12},{5,13},{6,14},{7,15},{8,0},{9,1},... | collective-permute-start | bytes 786440 | tf_op jit(solution)/shard_map/ppermute | solution.py:340
  2.8 35.0 %collective-permute-start.11 = (bf16[16,8192]{1,0:T(8,128)(2,1)S(1)}, bf16[16,8192]{1,0:T(8,128)(2,1)S(1)}, u32[]{:S(2)}, u32[]{:S(2)}) collective-permute-start(bf16[16,8192]{1,0:T(8,128)(2,1)S(1)} %get-tuple-element.198), channel_id=1, source_target_pairs={{0,8},{1,9},{2,10},{3,11},{4,12},{5,13},{6,14},{7,15},{8,0},{9,1},... | collective-permute-start | bytes 786440 | tf_op jit(solution)/shard_map/ppermute | solution.py:340
  5.9 1.6 copy-start.2
  7.5 138.0 %copy-start.3 = (bf16[1,64,8192]{2,1,0:T(8,128)(2,1)S(1)}, bf16[1,64,8192]{2,1,0:T(8,128)(2,1)}, u32[]{:S(2)}) copy-start(bf16[1,64,8192]{2,1,0:T(8,128)(2,1)} %param.11) | copy-start | bytes 3145732
  8.8 28.9 %collective-permute-start = (bf16[16,8192]{1,0:T(8,128)(2,1)S(1)}, bf16[16,8192]{1,0:T(8,128)(2,1)S(1)}, u32[]{:S(2)}, u32[]{:S(2)}) collective-permute-start(bf16[16,8192]{1,0:T(8,128)(2,1)S(1)} %get-tuple-element.101), channel_id=1, source_target_pairs={{0,1},{1,0},{2,3},{3,2},{4,5},{5,4},{6,7},{7,6},{8,9},{9,8},{10,11... | collective-permute-start | bytes 786440 | tf_op jit(solution)/shard_map/ppermute | solution.py:340
  8.9 33.7 %collective-permute-start.1 = (bf16[16,8192]{1,0:T(8,128)(2,1)S(1)}, bf16[16,8192]{1,0:T(8,128)(2,1)S(1)}, u32[]{:S(2)}, u32[]{:S(2)}) collective-permute-start(bf16[16,8192]{1,0:T(8,128)(2,1)S(1)} %get-tuple-element.102), channel_id=1, source_target_pairs={{0,2},{1,3},{2,0},{3,1},{4,6},{5,7},{6,4},{7,5},{8,10},{9,11},{10,... | collective-permute-start | bytes 786440 | tf_op jit(solution)/shard_map/ppermute | solution.py:340
  10.5 32.9 %collective-permute-start.8 = (bf16[16,8192]{1,0:T(8,128)(2,1)S(1)}, bf16[16,8192]{1,0:T(8,128)(2,1)S(1)}, u32[]{:S(2)}, u32[]{:S(2)}) collective-permute-start(bf16[16,8192]{1,0:T(8,128)(2,1)S(1)} %get-tuple-element.112), channel_id=1, source_target_pairs={{0,9},{1,8},{2,11},{3,10},{4,13},{5,12},{6,15},{7,14},{8,1},{9,0},... | collective-permute-start | bytes 786440 | tf_op jit(solution)/shard_map/ppermute | solution.py:340
  26.6 22.4 %collective-permute-start.7 = (bf16[16,8192]{1,0:T(8,128)(2,1)S(1)}, bf16[16,8192]{1,0:T(8,128)(2,1)S(1)}, u32[]{:S(2)}, u32[]{:S(2)}) collective-permute-start(bf16[16,8192]{1,0:T(8,128)(2,1)S(1)} %get-tuple-element.111), channel_id=1, source_target_pairs={{0,8},{1,9},{2,10},{3,11},{4,12},{5,13},{6,14},{7,15},{8,0},{9,1},... | collective-permute-start | bytes 786440 | tf_op jit(solution)/shard_map/ppermute | solution.py:340
  37.7 24.0 %collective-permute-start.2 = (bf16[16,8192]{1,0:T(8,128)(2,1)S(1)}, bf16[16,8192]{1,0:T(8,128)(2,1)S(1)}, u32[]{:S(2)}, u32[]{:S(2)}) collective-permute-start(bf16[16,8192]{1,0:T(8,128)(2,1)S(1)} %get-tuple-element.103), channel_id=1, source_target_pairs={{0,3},{1,2},{2,1},{3,0},{4,7},{5,6},{6,5},{7,4},{8,11},{9,10},{10,... | collective-permute-start | bytes 786440 | tf_op jit(solution)/shard_map/ppermute | solution.py:340
  37.8 24.5 %collective-permute-start.3 = (bf16[16,8192]{1,0:T(8,128)(2,1)S(1)}, bf16[16,8192]{1,0:T(8,128)(2,1)S(1)}, u32[]{:S(2)}, u32[]{:S(2)}) collective-permute-start(bf16[16,8192]{1,0:T(8,128)(2,1)S(1)} %get-tuple-element.104), channel_id=1, source_target_pairs={{0,4},{1,5},{2,6},{3,7},{4,0},{5,1},{6,2},{7,3},{8,12},{9,13},{10,... | collective-permute-start | bytes 786440 | tf_op jit(solution)/shard_map/ppermute | solution.py:340
  42.6 34.5 %collective-permute-start.12 = (bf16[16,8192]{1,0:T(8,128)(2,1)S(1)}, bf16[16,8192]{1,0:T(8,128)(2,1)S(1)}, u32[]{:S(2)}, u32[]{:S(2)}) collective-permute-start(bf16[16,8192]{1,0:T(8,128)(2,1)S(1)} %get-tuple-element.116), channel_id=1, source_target_pairs={{0,11},{1,10},{2,9},{3,8},{4,15},{5,14},{6,13},{7,12},{8,3},{9,2},... | collective-permute-start | bytes 786440 | tf_op jit(solution)/shard_map/ppermute | solution.py:340
  43.4 39.4 %collective-permute-start.10 = (bf16[16,8192]{1,0:T(8,128)(2,1)S(1)}, bf16[16,8192]{1,0:T(8,128)(2,1)S(1)}, u32[]{:S(2)}, u32[]{:S(2)}) collective-permute-start(bf16[16,8192]{1,0:T(8,128)(2,1)S(1)} %get-tuple-element.114), channel_id=1, source_target_pairs={{0,10},{1,11},{2,8},{3,9},{4,14},{5,15},{6,12},{7,13},{8,2},{9,3},... | collective-permute-start | bytes 786440 | tf_op jit(solution)/shard_map/ppermute | solution.py:340
  49.0 41.6 %collective-permute-start.14 = (bf16[16,8192]{1,0:T(8,128)(2,1)S(1)}, bf16[16,8192]{1,0:T(8,128)(2,1)S(1)}, u32[]{:S(2)}, u32[]{:S(2)}) collective-permute-start(bf16[16,8192]{1,0:T(8,128)(2,1)S(1)} %get-tuple-element.120), channel_id=1, source_target_pairs={{0,13},{1,12},{2,15},{3,14},{4,9},{5,8},{6,11},{7,10},{8,5},{9,4},... | collective-permute-start | bytes 786440 | tf_op jit(solution)/shard_map/ppermute | solution.py:340
  61.7 34.6 %collective-permute-start.13 = (bf16[16,8192]{1,0:T(8,128)(2,1)S(1)}, bf16[16,8192]{1,0:T(8,128)(2,1)S(1)}, u32[]{:S(2)}, u32[]{:S(2)}) collective-permute-start(bf16[16,8192]{1,0:T(8,128)(2,1)S(1)} %get-tuple-element.118), channel_id=1, source_target_pairs={{0,12},{1,13},{2,14},{3,15},{4,8},{5,9},{6,10},{7,11},{8,4},{9,5},... | collective-permute-start | bytes 786440 | tf_op jit(solution)/shard_map/ppermute | solution.py:340
  62.2 34.1 %collective-permute-start.4 = (bf16[16,8192]{1,0:T(8,128)(2,1)S(1)}, bf16[16,8192]{1,0:T(8,128)(2,1)S(1)}, u32[]{:S(2)}, u32[]{:S(2)}) collective-permute-start(bf16[16,8192]{1,0:T(8,128)(2,1)S(1)} %get-tuple-element.106), channel_id=1, source_target_pairs={{0,5},{1,4},{2,7},{3,6},{4,1},{5,0},{6,3},{7,2},{8,13},{9,12},{10,... | collective-permute-start | bytes 786440 | tf_op jit(solution)/shard_map/ppermute | solution.py:340
  77.2 19.3 %collective-permute-start.5 = (bf16[16,8192]{1,0:T(8,128)(2,1)S(1)}, bf16[16,8192]{1,0:T(8,128)(2,1)S(1)}, u32[]{:S(2)}, u32[]{:S(2)}) collective-permute-start(bf16[16,8192]{1,0:T(8,128)(2,1)S(1)} %get-tuple-element.108), channel_id=1, source_target_pairs={{0,6},{1,7},{2,4},{3,5},{4,2},{5,3},{6,0},{7,1},{8,14},{9,15},{10,... | collective-permute-start | bytes 786440 | tf_op jit(solution)/shard_map/ppermute | solution.py:340
  82.8 21.5 %collective-permute-start.6 = (bf16[16,8192]{1,0:T(8,128)(2,1)S(1)}, bf16[16,8192]{1,0:T(8,128)(2,1)S(1)}, u32[]{:S(2)}, u32[]{:S(2)}) collective-permute-start(bf16[16,8192]{1,0:T(8,128)(2,1)S(1)} %get-tuple-element.110), channel_id=1, source_target_pairs={{0,7},{1,6},{2,5},{3,4},{4,3},{5,2},{6,1},{7,0},{8,15},{9,14},{10,... | collective-permute-start | bytes 786440 | tf_op jit(solution)/shard_map/ppermute | solution.py:340
  90.6 13.7 %collective-permute-start.19 = (bf16[16,8320]{1,0:T(8,128)(2,1)S(1)}, bf16[16,8320]{1,0:T(8,128)(2,1)S(1)}, u32[]{:S(2)}, u32[]{:S(2)}) collective-permute-start(bf16[16,8320]{1,0:T(8,128)(2,1)S(1)} %get-tuple-element.134), channel_id=1, source_target_pairs={{0,1},{1,0},{2,3},{3,2},{4,5},{5,4},{6,7},{7,6},{8,9},{9,8},{10,11... | collective-permute-start | bytes 798728 | tf_op jit(solution)/shard_map/ppermute | solution.py:340
  96.3 28.8 %collective-permute-start.33 = (bf16[16,8192]{1,0:T(8,128)(2,1)S(1)}, bf16[16,8192]{1,0:T(8,128)(2,1)S(1)}, u32[]{:S(2)}, u32[]{:S(2)}) collective-permute-start(bf16[16,8192]{1,0:T(8,128)(2,1)S(1)} %get-tuple-element.157), channel_id=1, source_target_pairs={{0,8},{1,9},{2,10},{3,11},{4,12},{5,13},{6,14},{7,15},{8,0},{9,1},... | collective-permute-start | bytes 786440 | tf_op jit(solution)/shard_map/ppermute | solution.py:340
  96.3 34.5 %collective-permute-start.16 = (bf16[16,8192]{1,0:T(8,128)(2,1)S(1)}, bf16[16,8192]{1,0:T(8,128)(2,1)S(1)}, u32[]{:S(2)}, u32[]{:S(2)}) collective-permute-start(bf16[16,8192]{1,0:T(8,128)(2,1)S(1)} %get-tuple-element.124), channel_id=1, source_target_pairs={{0,15},{1,14},{2,13},{3,12},{4,11},{5,10},{6,9},{7,8},{8,7},{9,6},... | collective-permute-start | bytes 786440 | tf_op jit(solution)/shard_map/ppermute | solution.py:340
  96.4 41.3 %collective-permute-start.15 = (bf16[16,8192]{1,0:T(8,128)(2,1)S(1)}, bf16[16,8192]{1,0:T(8,128)(2,1)S(1)}, u32[]{:S(2)}, u32[]{:S(2)}) collective-permute-start(bf16[16,8192]{1,0:T(8,128)(2,1)S(1)} %get-tuple-element.122), channel_id=1, source_target_pairs={{0,14},{1,15},{2,12},{3,13},{4,10},{5,11},{6,8},{7,9},{8,6},{9,7},... | collective-permute-start | bytes 786440 | tf_op jit(solution)/shard_map/ppermute | solution.py:340
  104.3 37.4 %collective-permute-start.32 = (bf16[16,8192]{1,0:T(8,128)(2,1)S(1)}, bf16[16,8192]{1,0:T(8,128)(2,1)S(1)}, u32[]{:S(2)}, u32[]{:S(2)}) collective-permute-start(bf16[16,8192]{1,0:T(8,128)(2,1)S(1)} %get-tuple-element.156), channel_id=1, source_target_pairs={{0,8},{1,9},{2,10},{3,11},{4,12},{5,13},{6,14},{7,15},{8,0},{9,1},... | collective-permute-start | bytes 786440 | tf_op jit(solution)/shard_map/ppermute | solution.py:340
  104.3 43.6 %collective-permute-start.25 = (bf16[16,8320]{1,0:T(8,128)(2,1)S(1)}, bf16[16,8320]{1,0:T(8,128)(2,1)S(1)}, u32[]{:S(2)}, u32[]{:S(2)}) collective-permute-start(bf16[16,8320]{1,0:T(8,128)(2,1)S(1)} %get-tuple-element.146), channel_id=1, source_target_pairs={{0,3},{1,2},{2,1},{3,0},{4,7},{5,6},{6,5},{7,4},{8,11},{9,10},{10,... | collective-permute-start | bytes 798728 | tf_op jit(solution)/shard_map/ppermute | solution.py:340
  125.0 23.5 %collective-permute-start.17 = (bf16[16,8320]{1,0:T(8,128)(2,1)S(1)}, bf16[16,8320]{1,0:T(8,128)(2,1)S(1)}, u32[]{:S(2)}, u32[]{:S(2)}) collective-permute-start(bf16[16,8320]{1,0:T(8,128)(2,1)S(1)} %get-tuple-element.129), channel_id=1, source_target_pairs={{0,4},{1,5},{2,6},{3,7},{4,0},{5,1},{6,2},{7,3},{8,12},{9,13},{10,... | collective-permute-start | bytes 798728 | tf_op jit(solution)/shard_map/ppermute | solution.py:340
  130.8 20.2 %collective-permute-start.22 = (bf16[16,8320]{1,0:T(8,128)(2,1)S(1)}, bf16[16,8320]{1,0:T(8,128)(2,1)S(1)}, u32[]{:S(2)}, u32[]{:S(2)}) collective-permute-start(bf16[16,8320]{1,0:T(8,128)(2,1)S(1)} %get-tuple-element.140), channel_id=1, source_target_pairs={{0,2},{1,3},{2,0},{3,1},{4,6},{5,7},{6,4},{7,5},{8,10},{9,11},{10,... | collective-permute-start | bytes 798728 | tf_op jit(solution)/shard_map/ppermute | solution.py:340
  137.7 14.0 %collective-permute-start.20 = (bf16[16,8320]{1,0:T(8,128)(2,1)S(1)}, bf16[16,8320]{1,0:T(8,128)(2,1)S(1)}, u32[]{:S(2)}, u32[]{:S(2)}) collective-permute-start(bf16[16,8320]{1,0:T(8,128)(2,1)S(1)} %get-tuple-element.135), channel_id=1, source_target_pairs={{0,5},{1,4},{2,7},{3,6},{4,1},{5,0},{6,3},{7,2},{8,13},{9,12},{10,... | collective-permute-start | bytes 798728 | tf_op jit(solution)/shard_map/ppermute | solution.py:340
  141.7 25.5 %collective-permute-start.43 = (bf16[16,8320]{1,0:T(8,128)(2,1)S(1)}, bf16[16,8320]{1,0:T(8,128)(2,1)S(1)}, u32[]{:S(2)}, u32[]{:S(2)}) collective-permute-start(bf16[16,8320]{1,0:T(8,128)(2,1)S(1)} %get-tuple-element.179), channel_id=1, source_target_pairs={{0,11},{1,10},{2,9},{3,8},{4,15},{5,14},{6,13},{7,12},{8,3},{9,2},... | collective-permute-start | bytes 798728 | tf_op jit(solution)/shard_map/ppermute | solution.py:340
  145.5 5.4 %copy-start = (bf16[1,64,8192]{2,1,0:T(8,128)(2,1)S(1)}, bf16[1,64,8192]{2,1,0:T(8,128)(2,1)}, u32[]{:S(2)}) copy-start(bf16[1,64,8192]{2,1,0:T(8,128)(2,1)} %param.10) | copy-start | bytes 3145732
  147.9 25.1 %collective-permute-start.42 = (bf16[16,8320]{1,0:T(8,128)(2,1)S(1)}, bf16[16,8320]{1,0:T(8,128)(2,1)S(1)}, u32[]{:S(2)}, u32[]{:S(2)}) collective-permute-start(bf16[16,8320]{1,0:T(8,128)(2,1)S(1)} %get-tuple-element.177), channel_id=1, source_target_pairs={{0,10},{1,11},{2,8},{3,9},{4,14},{5,15},{6,12},{7,13},{8,2},{9,3},... | collective-permute-start | bytes 798728 | tf_op jit(solution)/shard_map/ppermute | solution.py:340
  148.6 36.2 %collective-permute-start.41 = (bf16[16,8320]{1,0:T(8,128)(2,1)S(1)}, bf16[16,8320]{1,0:T(8,128)(2,1)S(1)}, u32[]{:S(2)}, u32[]{:S(2)}) collective-permute-start(bf16[16,8320]{1,0:T(8,128)(2,1)S(1)} %get-tuple-element.175), channel_id=1, source_target_pairs={{0,9},{1,8},{2,11},{3,10},{4,13},{5,12},{6,15},{7,14},{8,1},{9,0},... | collective-permute-start | bytes 798728 | tf_op jit(solution)/shard_map/ppermute | solution.py:340
  150.9 36.5 %collective-permute-start.26 = (bf16[16,8320]{1,0:T(8,128)(2,1)S(1)}, bf16[16,8320]{1,0:T(8,128)(2,1)S(1)}, u32[]{:S(2)}, u32[]{:S(2)}) collective-permute-start(bf16[16,8320]{1,0:T(8,128)(2,1)S(1)} %get-tuple-element.147), channel_id=1, source_target_pairs={{0,7},{1,6},{2,5},{3,4},{4,3},{5,2},{6,1},{7,0},{8,15},{9,14},{10,... | collective-permute-start | bytes 798728 | tf_op jit(solution)/shard_map/ppermute | solution.py:340
  151.7 36.7 %collective-permute-start.23 = (bf16[16,8320]{1,0:T(8,128)(2,1)S(1)}, bf16[16,8320]{1,0:T(8,128)(2,1)S(1)}, u32[]{:S(2)}, u32[]{:S(2)}) collective-permute-start(bf16[16,8320]{1,0:T(8,128)(2,1)S(1)} %get-tuple-element.141), channel_id=1, source_target_pairs={{0,6},{1,7},{2,4},{3,5},{4,2},{5,3},{6,0},{7,1},{8,14},{9,15},{10,... | collective-permute-start | bytes 798728 | tf_op jit(solution)/shard_map/ppermute | solution.py:340
  167.3 18.9 %collective-permute-start.18 = (bf16[16,8192]{1,0:T(8,128)(2,1)S(1)}, bf16[16,8192]{1,0:T(8,128)(2,1)S(1)}, u32[]{:S(2)}, u32[]{:S(2)}) collective-permute-start(bf16[16,8192]{1,0:T(8,128)(2,1)S(1)} %get-tuple-element.130), channel_id=1, source_target_pairs={{0,1},{1,0},{2,3},{3,2},{4,5},{5,4},{6,7},{7,6},{8,9},{9,8},{10,11... | collective-permute-start | bytes 786440 | tf_op jit(solution)/shard_map/ppermute | solution.py:340
  173.0 29.2 %collective-permute-start.31 = (bf16[16,8832]{1,0:T(8,128)(2,1)S(1)}, bf16[16,8832]{1,0:T(8,128)(2,1)S(1)}, u32[]{:S(2)}, u32[]{:S(2)}) collective-permute-start(bf16[16,8832]{1,0:T(8,128)(2,1)S(1)} %shard_map.89), channel_id=1, source_target_pairs={{0,8},{1,9},{2,10},{3,11},{4,12},{5,13},{6,14},{7,15},{8,0},{9,1},... | collective-permute-start | bytes 847880 | tf_op jit(solution)/shard_map/ppermute | solution.py:340
  184.7 27.7 %collective-permute-start.47 = (bf16[16,8320]{1,0:T(8,128)(2,1)S(1)}, bf16[16,8320]{1,0:T(8,128)(2,1)S(1)}, u32[]{:S(2)}, u32[]{:S(2)}) collective-permute-start(bf16[16,8320]{1,0:T(8,128)(2,1)S(1)} %get-tuple-element.187), channel_id=1, source_target_pairs={{0,15},{1,14},{2,13},{3,12},{4,11},{5,10},{6,9},{7,8},{8,7},{9,6},... | collective-permute-start | bytes 798728 | tf_op jit(solution)/shard_map/ppermute | solution.py:340
  186.1 34.8 %collective-permute-start.46 = (bf16[16,8320]{1,0:T(8,128)(2,1)S(1)}, bf16[16,8320]{1,0:T(8,128)(2,1)S(1)}, u32[]{:S(2)}, u32[]{:S(2)}) collective-permute-start(bf16[16,8320]{1,0:T(8,128)(2,1)S(1)} %get-tuple-element.185), channel_id=1, source_target_pairs={{0,14},{1,15},{2,12},{3,13},{4,10},{5,11},{6,8},{7,9},{8,6},{9,7},... | collective-permute-start | bytes 798728 | tf_op jit(solution)/shard_map/ppermute | solution.py:340
  187.4 8.3 %collective-permute-start.21 = (bf16[16,8192]{1,0:T(8,128)(2,1)S(1)}, bf16[16,8192]{1,0:T(8,128)(2,1)S(1)}, u32[]{:S(2)}, u32[]{:S(2)}) collective-permute-start(bf16[16,8192]{1,0:T(8,128)(2,1)S(1)} %get-tuple-element.136), channel_id=1, source_target_pairs={{0,2},{1,3},{2,0},{3,1},{4,6},{5,7},{6,4},{7,5},{8,10},{9,11},{10,... | collective-permute-start | bytes 786440 | tf_op jit(solution)/shard_map/ppermute | solution.py:340
  188.3 24.1 %collective-permute-start.28 = (bf16[16,8192]{1,0:T(8,128)(2,1)S(1)}, bf16[16,8192]{1,0:T(8,128)(2,1)S(1)}, u32[]{:S(2)}, u32[]{:S(2)}) collective-permute-start(bf16[16,8192]{1,0:T(8,128)(2,1)S(1)} %get-tuple-element.150), channel_id=1, source_target_pairs={{0,5},{1,4},{2,7},{3,6},{4,1},{5,0},{6,3},{7,2},{8,13},{9,12},{10,... | collective-permute-start | bytes 786440 | tf_op jit(solution)/shard_map/ppermute | solution.py:340
  195.8 35.8 %collective-permute-start.44 = (bf16[16,8320]{1,0:T(8,128)(2,1)S(1)}, bf16[16,8320]{1,0:T(8,128)(2,1)S(1)}, u32[]{:S(2)}, u32[]{:S(2)}) collective-permute-start(bf16[16,8320]{1,0:T(8,128)(2,1)S(1)} %get-tuple-element.181), channel_id=1, source_target_pairs={{0,12},{1,13},{2,14},{3,15},{4,8},{5,9},{6,10},{7,11},{8,4},{9,5},... | collective-permute-start | bytes 798728 | tf_op jit(solution)/shard_map/ppermute | solution.py:340
  202.1 23.2 %collective-permute-start.27 = (bf16[16,8192]{1,0:T(8,128)(2,1)S(1)}, bf16[16,8192]{1,0:T(8,128)(2,1)S(1)}, u32[]{:S(2)}, u32[]{:S(2)}) collective-permute-start(bf16[16,8192]{1,0:T(8,128)(2,1)S(1)} %get-tuple-element.148), channel_id=1, source_target_pairs={{0,4},{1,5},{2,6},{3,7},{4,0},{5,1},{6,2},{7,3},{8,12},{9,13},{10,... | collective-permute-start | bytes 786440 | tf_op jit(solution)/shard_map/ppermute | solution.py:340
  212.4 13.8 %collective-permute-start.24 = (bf16[16,8192]{1,0:T(8,128)(2,1)S(1)}, bf16[16,8192]{1,0:T(8,128)(2,1)S(1)}, u32[]{:S(2)}, u32[]{:S(2)}) collective-permute-start(bf16[16,8192]{1,0:T(8,128)(2,1)S(1)} %get-tuple-element.142), channel_id=1, source_target_pairs={{0,3},{1,2},{2,1},{3,0},{4,7},{5,6},{6,5},{7,4},{8,11},{9,10},{10,... | collective-permute-start | bytes 786440 | tf_op jit(solution)/shard_map/ppermute | solution.py:340
  212.4 18.9 %collective-permute-start.29 = (bf16[16,8192]{1,0:T(8,128)(2,1)S(1)}, bf16[16,8192]{1,0:T(8,128)(2,1)S(1)}, u32[]{:S(2)}, u32[]{:S(2)}) collective-permute-start(bf16[16,8192]{1,0:T(8,128)(2,1)S(1)} %get-tuple-element.152), channel_id=1, source_target_pairs={{0,6},{1,7},{2,4},{3,5},{4,2},{5,3},{6,0},{7,1},{8,14},{9,15},{10,... | collective-permute-start | bytes 786440 | tf_op jit(solution)/shard_map/ppermute | solution.py:340
  221.0 17.4 %collective-permute-start.45 = (bf16[16,8320]{1,0:T(8,128)(2,1)S(1)}, bf16[16,8320]{1,0:T(8,128)(2,1)S(1)}, u32[]{:S(2)}, u32[]{:S(2)}) collective-permute-start(bf16[16,8320]{1,0:T(8,128)(2,1)S(1)} %get-tuple-element.183), channel_id=1, source_target_pairs={{0,13},{1,12},{2,15},{3,14},{4,9},{5,8},{6,11},{7,10},{8,5},{9,4},... | collective-permute-start | bytes 798728 | tf_op jit(solution)/shard_map/ppermute | solution.py:340
  225.3 15.4 %collective-permute-start.35 = (bf16[16,8192]{1,0:T(8,128)(2,1)S(1)}, bf16[16,8192]{1,0:T(8,128)(2,1)S(1)}, u32[]{:S(2)}, u32[]{:S(2)}) collective-permute-start(bf16[16,8192]{1,0:T(8,128)(2,1)S(1)} %get-tuple-element.162), channel_id=1, source_target_pairs={{0,2},{1,3},{2,0},{3,1},{4,6},{5,7},{6,4},{7,5},{8,10},{9,11},{10,... | collective-permute-start | bytes 786440 | tf_op jit(solution)/shard_map/ppermute | solution.py:340
  226.2 14.6 %collective-permute-start.34 = (bf16[16,8192]{1,0:T(8,128)(2,1)S(1)}, bf16[16,8192]{1,0:T(8,128)(2,1)S(1)}, u32[]{:S(2)}, u32[]{:S(2)}) collective-permute-start(bf16[16,8192]{1,0:T(8,128)(2,1)S(1)} %get-tuple-element.160), channel_id=1, source_target_pairs={{0,1},{1,0},{2,3},{3,2},{4,5},{5,4},{6,7},{7,6},{8,9},{9,8},{10,11... | collective-permute-start | bytes 786440 | tf_op jit(solution)/shard_map/ppermute | solution.py:340
  231.3 10.6 %collective-permute-start.30 = (bf16[16,8192]{1,0:T(8,128)(2,1)S(1)}, bf16[16,8192]{1,0:T(8,128)(2,1)S(1)}, u32[]{:S(2)}, u32[]{:S(2)}) collective-permute-start(bf16[16,8192]{1,0:T(8,128)(2,1)S(1)} %get-tuple-element.154), channel_id=1, source_target_pairs={{0,7},{1,6},{2,5},{3,4},{4,3},{5,2},{6,1},{7,0},{8,15},{9,14},{10,... | collective-permute-start | bytes 786440 | tf_op jit(solution)/shard_map/ppermute | solution.py:340
  231.6 21.1 %collective-permute-start.36 = (bf16[16,8192]{1,0:T(8,128)(2,1)S(1)}, bf16[16,8192]{1,0:T(8,128)(2,1)S(1)}, u32[]{:S(2)}, u32[]{:S(2)}) collective-permute-start(bf16[16,8192]{1,0:T(8,128)(2,1)S(1)} %get-tuple-element.164), channel_id=1, source_target_pairs={{0,3},{1,2},{2,1},{3,0},{4,7},{5,6},{6,5},{7,4},{8,11},{9,10},{10,... | collective-permute-start | bytes 786440 | tf_op jit(solution)/shard_map/ppermute | solution.py:340
  240.7 36.7 %collective-permute-start.39 = (bf16[16,8192]{1,0:T(8,128)(2,1)S(1)}, bf16[16,8192]{1,0:T(8,128)(2,1)S(1)}, u32[]{:S(2)}, u32[]{:S(2)}) collective-permute-start(bf16[16,8192]{1,0:T(8,128)(2,1)S(1)} %get-tuple-element.170), channel_id=1, source_target_pairs={{0,6},{1,7},{2,4},{3,5},{4,2},{5,3},{6,0},{7,1},{8,14},{9,15},{10,... | collective-permute-start | bytes 786440 | tf_op jit(solution)/shard_map/ppermute | solution.py:340
  240.8 36.6 %collective-permute-start.38 = (bf16[16,8192]{1,0:T(8,128)(2,1)S(1)}, bf16[16,8192]{1,0:T(8,128)(2,1)S(1)}, u32[]{:S(2)}, u32[]{:S(2)}) collective-permute-start(bf16[16,8192]{1,0:T(8,128)(2,1)S(1)} %get-tuple-element.168), channel_id=1, source_target_pairs={{0,5},{1,4},{2,7},{3,6},{4,1},{5,0},{6,3},{7,2},{8,13},{9,12},{10,... | collective-permute-start | bytes 786440 | tf_op jit(solution)/shard_map/ppermute | solution.py:340
  241.9 35.5 %collective-permute-start.37 = (bf16[16,8192]{1,0:T(8,128)(2,1)S(1)}, bf16[16,8192]{1,0:T(8,128)(2,1)S(1)}, u32[]{:S(2)}, u32[]{:S(2)}) collective-permute-start(bf16[16,8192]{1,0:T(8,128)(2,1)S(1)} %get-tuple-element.166), channel_id=1, source_target_pairs={{0,4},{1,5},{2,6},{3,7},{4,0},{5,1},{6,2},{7,3},{8,12},{9,13},{10,... | collective-permute-start | bytes 786440 | tf_op jit(solution)/shard_map/ppermute | solution.py:340
  252.7 24.7 %collective-permute-start.40 = (bf16[16,8192]{1,0:T(8,128)(2,1)S(1)}, bf16[16,8192]{1,0:T(8,128)(2,1)S(1)}, u32[]{:S(2)}, u32[]{:S(2)}) collective-permute-start(bf16[16,8192]{1,0:T(8,128)(2,1)S(1)} %get-tuple-element.172), channel_id=1, source_target_pairs={{0,7},{1,6},{2,5},{3,4},{4,3},{5,2},{6,1},{7,0},{8,15},{9,14},{10,... | collective-permute-start | bytes 786440 | tf_op jit(solution)/shard_map/ppermute | solution.py:340
  258.3 1.2 collective-permute-start.48
  260.9 3.6 %collective-permute-start.49 = (f32[1,1]{1,0:T(1,128)}, f32[1,1]{1,0:T(1,128)}, u32[]{:S(2)}, u32[]{:S(2)}) collective-permute-start(f32[1,1]{1,0:T(1,128)} %add.15), channel_id=1, source_target_pairs={{0,2},{1,3},{2,0},{3,1},{4,6},{5,7},{6,4},{7,5},{8,10},{9,11},{10,... | collective-permute-start | bytes 20 | tf_op jit(solution)/shard_map/ppermute | solution.py:27
  265.1 3.6 %collective-permute-start.50 = (f32[1,1]{1,0:T(1,128)}, f32[1,1]{1,0:T(1,128)}, u32[]{:S(2)}, u32[]{:S(2)}) collective-permute-start(f32[1,1]{1,0:T(1,128)} %add.16), channel_id=1, source_target_pairs={{0,4},{1,5},{2,6},{3,7},{4,0},{5,1},{6,2},{7,3},{8,12},{9,13},{10,... | collective-permute-start | bytes 20 | tf_op jit(solution)/shard_map/ppermute | solution.py:27
  269.2 4.5 %collective-permute-start.51 = (f32[1,1]{1,0:T(1,128)}, f32[1,1]{1,0:T(1,128)}, u32[]{:S(2)}, u32[]{:S(2)}) collective-permute-start(f32[1,1]{1,0:T(1,128)} %add.17), channel_id=1, source_target_pairs={{0,8},{1,9},{2,10},{3,11},{4,12},{5,13},{6,14},{7,15},{8,0},{9,1},... | collective-permute-start | bytes 20 | tf_op jit(solution)/shard_map/ppermute | solution.py:27

commit v6 on v5

--- a/solution.py
+++ b/solution.py
@@ -12,6 +12,9 @@
 LANES = 128
 FAR_WINDOW = 4
 CHUNK = 8192
+WEIGHT_FIRST = 2
+RATE = 1
+WEIGHT_MID = 11
 MIRROR_ORDER = [1, 2, 3, 4, 5, 6, 7]
 NEAR_WINDOW = 4
 LAST = (((1,), (1,)), ((), ()))
@@ -362,7 +365,7 @@
             at = len(mirror_parts)
             mirror_parts.append(far.swap(down_weight[at * cap : (at + 1) * cap], half))
 
-    send_weight(parts // 2)
+    send_weight(WEIGHT_FIRST)
     sent_dy = place(list(range(count_blk)), cap, me, owner, tenant, cotangent)
     others = [s for s in range(count_blk) if s != half]
     sent_x = dict(zip(others, place(others, cap, me, owner, tenant, tokens, with_live=True)))
@@ -370,9 +373,13 @@
     near_queue = [(got_dy, sent_dy, s) for s in range(1, half)] + [(got_x, sent_x, s) for s in range(1, half)]
     for s in range(half, count_blk):
         got_dy[s] = far.swap(sent_dy[s], s)
-        for got, sent, partner in near_queue[:2]:
+        for got, sent, partner in near_queue[:RATE]:
             got[partner] = near.swap(sent[partner], partner)
-        del near_queue[:2]
+        del near_queue[:RATE]
+        if s == WEIGHT_MID:
+            send_weight(1)
+    for got, sent, partner in near_queue:
+        got[partner] = near.swap(sent[partner], partner)
     send_weight(parts - len(mirror_parts))
 
     blocks_dy = [got_dy[s] for s in range(count_blk)]

time: 282 us -> 279 us (0.989)
  no operation moved by 1% of the time
where the time goes in v6:
time: 279 us; the launch traced here: 277 us
  waiting for transfers between devices  153 us (55%)
  starting transfers between devices  98.1 us (35%)
  Pallas kernels  16.8 us (6%)
  local copies, waits for them, and re-layouts  4.43 us (2%)
  between operations  4.09 us (1%)
    ppermute x48, waiting for transfers between devices, swap(): result = lax.ppermute(value, 'blk', [(i, i ^ partner) for i in range(size)])  147 us
    ppermute x48, starting transfers between devices, swap(): result = lax.ppermute(value, 'blk', [(i, i ^ partner) for i in range(size)])  90.8 us
    ppermute x4, starting transfers between devices, total_over_blk(): lax.ppermute(value, 'blk', [(i, i ^ step) for i in range(size)])  7.21 us
    ppermute x4, waiting for transfers between devices, total_over_blk(): lax.ppermute(value, 'blk', [(i, i ^ step) for i in range(size)])  5.71 us
  transfers between devices with their start and end apart: 52, of which 27 were waited for; matrix products, arithmetic and copies ran while one was open for 1% of the time, Pallas kernels for 5%

profile of v6, /device:TPU:16, one launch (start us, length us, event | category | flops | bytes accessed | tf_op | source)
XLA Modules:
  0.0 276.9 jit_solution(2734217438146908125)
XLA Ops:
  0.7 2.1 slice_bitcast_fusion
  2.8 2.9 %collective-permute-start.11 = (bf16[16,8192]{1,0:T(8,128)(2,1)S(1)}, bf16[16,8192]{1,0:T(8,128)(2,1)S(1)}, u32[]{:S(2)}, u32[]{:S(2)}) collective-permute-start(bf16[16,8192]{1,0:T(8,128)(2,1)S(1)} %get-tuple-element.199), channel_id=1, source_target_pairs={{0,8},{1,9},{2,10},{3,11},{4,12},{5,13},{6,14},{7,15},{8,0},{9,1},... | collective-permute-start | bytes 786440 | tf_op jit(solution)/shard_map/ppermute | solution.py:343
  5.9 1.6 copy-done.2
  7.5 1.3 shard_map.85
  8.9 1.6 collective-permute-start.1
  10.6 16.0 %collective-permute-done.9 = bf16[16,8192]{1,0:T(8,128)(2,1)S(1)} collective-permute-done((bf16[16,8192]{1,0:T(8,128)(2,1)}, bf16[16,8192]{1,0:T(8,128)(2,1)S(1)}, u32[]{:S(2)}, u32[]{:S(2)}) %collective-permute-start.9) | collective-permute-done | bytes 262176 | tf_op jit(solution)/shard_map/ppermute | solution.py:343
  26.6 3.3 %collective-permute-start.7 = (bf16[16,8192]{1,0:T(8,128)(2,1)S(1)}, bf16[16,8192]{1,0:T(8,128)(2,1)S(1)}, u32[]{:S(2)}, u32[]{:S(2)}) collective-permute-start(bf16[16,8192]{1,0:T(8,128)(2,1)S(1)} %get-tuple-element.111), channel_id=1, source_target_pairs={{0,8},{1,9},{2,10},{3,11},{4,12},{5,13},{6,14},{7,15},{8,0},{9,1},... | collective-permute-start | bytes 786440 | tf_op jit(solution)/shard_map/ppermute | solution.py:343
  29.9 7.9 %collective-permute-done.11 = bf16[16,8192]{1,0:T(8,128)(2,1)S(1)} collective-permute-done((bf16[16,8192]{1,0:T(8,128)(2,1)S(1)}, bf16[16,8192]{1,0:T(8,128)(2,1)S(1)}, u32[]{:S(2)}, u32[]{:S(2)}) %collective-permute-start.11) | collective-permute-done | bytes 262176 | tf_op jit(solution)/shard_map/ppermute | solution.py:343
  37.8 4.9 %collective-permute-start.3 = (bf16[16,8192]{1,0:T(8,128)(2,1)S(1)}, bf16[16,8192]{1,0:T(8,128)(2,1)S(1)}, u32[]{:S(2)}, u32[]{:S(2)}) collective-permute-start(bf16[16,8192]{1,0:T(8,128)(2,1)S(1)} %get-tuple-element.104), channel_id=1, source_target_pairs={{0,4},{1,5},{2,6},{3,7},{4,0},{5,1},{6,2},{7,3},{8,12},{9,13},{10,... | collective-permute-start | bytes 786440 | tf_op jit(solution)/shard_map/ppermute | solution.py:343
  43.4 3.0 %collective-permute-start.10 = (bf16[16,8192]{1,0:T(8,128)(2,1)S(1)}, bf16[16,8192]{1,0:T(8,128)(2,1)S(1)}, u32[]{:S(2)}, u32[]{:S(2)}) collective-permute-start(bf16[16,8192]{1,0:T(8,128)(2,1)S(1)} %get-tuple-element.114), channel_id=1, source_target_pairs={{0,10},{1,11},{2,8},{3,9},{4,14},{5,15},{6,12},{7,13},{8,2},{9,3},... | collective-permute-start | bytes 786440 | tf_op jit(solution)/shard_map/ppermute | solution.py:343
  46.4 2.6 collective-permute-done.7.refs_8_.refs_27_
  49.0 13.2 %collective-permute-start.13 = (bf16[16,8192]{1,0:T(8,128)(2,1)S(1)}, bf16[16,8192]{1,0:T(8,128)(2,1)S(1)}, u32[]{:S(2)}, u32[]{:S(2)}) collective-permute-start(bf16[16,8192]{1,0:T(8,128)(2,1)S(1)} %get-tuple-element.118), channel_id=1, source_target_pairs={{0,12},{1,13},{2,14},{3,15},{4,8},{5,9},{6,10},{7,11},{8,4},{9,5},... | collective-permute-start | bytes 786440 | tf_op jit(solution)/shard_map/ppermute | solution.py:343
  62.2 4.3 %collective-permute-start.16 = (bf16[16,8192]{1,0:T(8,128)(2,1)S(1)}, bf16[16,8192]{1,0:T(8,128)(2,1)S(1)}, u32[]{:S(2)}, u32[]{:S(2)}) collective-permute-start(bf16[16,8192]{1,0:T(8,128)(2,1)S(1)} %get-tuple-element.124), channel_id=1, source_target_pairs={{0,8},{1,9},{2,10},{3,11},{4,12},{5,13},{6,14},{7,15},{8,0},{9,1},... | collective-permute-start | bytes 786440 | tf_op jit(solution)/shard_map/ppermute | solution.py:343
  66.5 10.4 %collective-permute-done.12.refs_11_.refs_30_ = bf16[16,8192]{1,0:T(8,128)(2,1)S(1)} collective-permute-done((bf16[16,8192]{1,0:T(8,128)(2,1)S(1)}, bf16[16,8192]{1,0:T(8,128)(2,1)S(1)}, u32[]{:S(2)}, u32[]{:S(2)}) %collective-permute-start.12) | collective-permute-done | bytes 262176 | tf_op jit(solution)/shard_map/ppermute | solution.py:343
  76.8 4.9 %collective-permute-start.5 = (bf16[16,8192]{1,0:T(8,128)(2,1)S(1)}, bf16[16,8192]{1,0:T(8,128)(2,1)S(1)}, u32[]{:S(2)}, u32[]{:S(2)}) collective-permute-start(bf16[16,8192]{1,0:T(8,128)(2,1)S(1)} %get-tuple-element.108), channel_id=1, source_target_pairs={{0,6},{1,7},{2,4},{3,5},{4,2},{5,3},{6,0},{7,1},{8,14},{9,15},{10,... | collective-permute-start | bytes 786440 | tf_op jit(solution)/shard_map/ppermute | solution.py:343
  81.7 1.1 collective-permute-done.10.refs_10_.refs_29_
  82.8 4.3 %collective-permute-start.6 = (bf16[16,8192]{1,0:T(8,128)(2,1)S(1)}, bf16[16,8192]{1,0:T(8,128)(2,1)S(1)}, u32[]{:S(2)}, u32[]{:S(2)}) collective-permute-start(bf16[16,8192]{1,0:T(8,128)(2,1)S(1)} %get-tuple-element.110), channel_id=1, source_target_pairs={{0,7},{1,6},{2,5},{3,4},{4,3},{5,2},{6,1},{7,0},{8,15},{9,14},{10,... | collective-permute-start | bytes 786440 | tf_op jit(solution)/shard_map/ppermute | solution.py:343
  87.1 1.3 shard_map.88
  88.3 2.5 collective-permute-done.13.refs_12_.refs_31_
  90.8 2.4 collective-permute-done.16
  93.2 3.4 %collective-permute-start.33 = (bf16[16,8192]{1,0:T(8,128)(2,1)S(1)}, bf16[16,8192]{1,0:T(8,128)(2,1)S(1)}, u32[]{:S(2)}, u32[]{:S(2)}) collective-permute-start(bf16[16,8192]{1,0:T(8,128)(2,1)S(1)} %get-tuple-element.157), channel_id=1, source_target_pairs={{0,8},{1,9},{2,10},{3,11},{4,12},{5,13},{6,14},{7,15},{8,0},{9,1},... | collective-permute-start | bytes 786440 | tf_op jit(solution)/shard_map/ppermute | solution.py:343
  96.7 3.6 %collective-permute-start.15 = (bf16[16,8192]{1,0:T(8,128)(2,1)S(1)}, bf16[16,8192]{1,0:T(8,128)(2,1)S(1)}, u32[]{:S(2)}, u32[]{:S(2)}) collective-permute-start(bf16[16,8192]{1,0:T(8,128)(2,1)S(1)} %get-tuple-element.122), channel_id=1, source_target_pairs={{0,14},{1,15},{2,12},{3,13},{4,10},{5,11},{6,8},{7,9},{8,6},{9,7},... | collective-permute-start | bytes 786440 | tf_op jit(solution)/shard_map/ppermute | solution.py:343
  101.1 2.0 collective-permute-start.17
  103.0 22.9 %collective-permute-done.33 = bf16[16,8192]{1,0:T(8,128)(2,1)S(1)} collective-permute-done((bf16[16,8192]{1,0:T(8,128)(2,1)S(1)}, bf16[16,8192]{1,0:T(8,128)(2,1)S(1)}, u32[]{:S(2)}, u32[]{:S(2)}) %collective-permute-start.33) | collective-permute-done | bytes 262176 | tf_op jit(solution)/shard_map/ppermute | solution.py:343
  126.4 5.1 %collective-permute-done.15.refs_14_.refs_33_ = bf16[16,8192]{1,0:T(8,128)(2,1)S(1)} collective-permute-done((bf16[16,8192]{1,0:T(8,128)(2,1)S(1)}, bf16[16,8192]{1,0:T(8,128)(2,1)S(1)}, u32[]{:S(2)}, u32[]{:S(2)}) %collective-permute-start.15) | collective-permute-done | bytes 262176 | tf_op jit(solution)/shard_map/ppermute | solution.py:343
  131.5 1.5 collective-permute-start.23
  133.1 4.1 %collective-permute-done.14.refs_13_.refs_32_ = bf16[16,8192]{1,0:T(8,128)(2,1)S(1)} collective-permute-done((bf16[16,8192]{1,0:T(8,128)(2,1)S(1)}, bf16[16,8192]{1,0:T(8,128)(2,1)S(1)}, u32[]{:S(2)}, u32[]{:S(2)}) %collective-permute-start.14) | collective-permute-done | bytes 262176 | tf_op jit(solution)/shard_map/ppermute | solution.py:343
  137.1 5.3 %collective-permute-done.17.refs_15_.refs_34_ = bf16[16,8192]{1,0:T(8,128)(2,1)S(1)} collective-permute-done((bf16[16,8192]{1,0:T(8,128)(2,1)S(1)}, bf16[16,8192]{1,0:T(8,128)(2,1)S(1)}, u32[]{:S(2)}, u32[]{:S(2)}) %collective-permute-start.17) | collective-permute-done | bytes 262176 | tf_op jit(solution)/shard_map/ppermute | solution.py:343
  142.4 2.4 shard_map.86
  144.8 3.5 %collective-permute-start.42 = (bf16[16,8320]{1,0:T(8,128)(2,1)S(1)}, bf16[16,8320]{1,0:T(8,128)(2,1)S(1)}, u32[]{:S(2)}, u32[]{:S(2)}) collective-permute-start(bf16[16,8320]{1,0:T(8,128)(2,1)S(1)} %get-tuple-element.177), channel_id=1, source_target_pairs={{0,10},{1,11},{2,8},{3,9},{4,14},{5,15},{6,12},{7,13},{8,2},{9,3},... | collective-permute-start | bytes 798728 | tf_op jit(solution)/shard_map/ppermute | solution.py:343
  148.4 3.0 %collective-permute-start.27 = (bf16[16,8320]{1,0:T(8,128)(2,1)S(1)}, bf16[16,8320]{1,0:T(8,128)(2,1)S(1)}, u32[]{:S(2)}, u32[]{:S(2)}) collective-permute-start(bf16[16,8320]{1,0:T(8,128)(2,1)S(1)} %get-tuple-element.148), channel_id=1, source_target_pairs={{0,7},{1,6},{2,5},{3,4},{4,3},{5,2},{6,1},{7,0},{8,15},{9,14},{10,... | collective-permute-start | bytes 798728 | tf_op jit(solution)/shard_map/ppermute | solution.py:343
  152.2 14.1 %collective-permute-done.43.refs_11_.refs_14_ = bf16[16,8320]{1,0:T(8,128)(2,1)S(1)} collective-permute-done((bf16[16,8320]{1,0:T(8,128)(2,1)S(1)}, bf16[16,8320]{1,0:T(8,128)(2,1)S(1)}, u32[]{:S(2)}, u32[]{:S(2)}) %collective-permute-start.43) | collective-permute-done | bytes 266272 | tf_op jit(solution)/shard_map/ppermute | solution.py:343
  166.7 5.2 %collective-permute-done.42.refs_10_.refs_13_ = bf16[16,8320]{1,0:T(8,128)(2,1)S(1)} collective-permute-done((bf16[16,8320]{1,0:T(8,128)(2,1)S(1)}, bf16[16,8320]{1,0:T(8,128)(2,1)S(1)}, u32[]{:S(2)}, u32[]{:S(2)}) %collective-permute-start.42) | collective-permute-done | bytes 266272 | tf_op jit(solution)/shard_map/ppermute | solution.py:343
  172.0 3.6 %collective-permute-start.32 = (bf16[16,8832]{1,0:T(8,128)(2,1)S(1)}, bf16[16,8832]{1,0:T(8,128)(2,1)S(1)}, u32[]{:S(2)}, u32[]{:S(2)}) collective-permute-start(bf16[16,8832]{1,0:T(8,128)(2,1)S(1)} %shard_map.89), channel_id=1, source_target_pairs={{0,8},{1,9},{2,10},{3,11},{4,12},{5,13},{6,14},{7,15},{8,0},{9,1},... | collective-permute-start | bytes 847880 | tf_op jit(solution)/shard_map/ppermute | solution.py:343
  175.6 8.1 %collective-permute-done.41.refs_9_.refs_12_ = bf16[16,8320]{1,0:T(8,128)(2,1)S(1)} collective-permute-done((bf16[16,8320]{1,0:T(8,128)(2,1)S(1)}, bf16[16,8320]{1,0:T(8,128)(2,1)S(1)}, u32[]{:S(2)}, u32[]{:S(2)}) %collective-permute-start.41) | collective-permute-done | bytes 266272 | tf_op jit(solution)/shard_map/ppermute | solution.py:343
  183.8 0.9 collective-permute-start.47
  185.3 0.8 collective-permute-start.22
  186.1 5.3 %collective-permute-start.29 = (bf16[16,8192]{1,0:T(8,128)(2,1)S(1)}, bf16[16,8192]{1,0:T(8,128)(2,1)S(1)}, u32[]{:S(2)}, u32[]{:S(2)}) collective-permute-start(bf16[16,8192]{1,0:T(8,128)(2,1)S(1)} %get-tuple-element.151), channel_id=1, source_target_pairs={{0,5},{1,4},{2,7},{3,6},{4,1},{5,0},{6,3},{7,2},{8,13},{9,12},{10,... | collective-permute-start | bytes 786440 | tf_op jit(solution)/shard_map/ppermute | solution.py:343
  191.3 2.8 %collective-permute-done.22.refs_6_ = bf16[16,8192]{1,0:T(8,128)(2,1)S(1)} collective-permute-done((bf16[16,8192]{1,0:T(8,128)(2,1)S(1)}, bf16[16,8192]{1,0:T(8,128)(2,1)S(1)}, u32[]{:S(2)}, u32[]{:S(2)}) %collective-permute-start.22) | collective-permute-done | bytes 262176 | tf_op jit(solution)/shard_map/ppermute | solution.py:343
  194.4 6.9 %collective-permute-done.32.refs_0_.refs_8_.refs_11_ = bf16[16,8832]{1,0:T(8,128)(2,1)S(1)} collective-permute-done((bf16[16,8832]{1,0:T(8,128)(2,1)S(1)}, bf16[16,8832]{1,0:T(8,128)(2,1)S(1)}, u32[]{:S(2)}, u32[]{:S(2)}) %collective-permute-start.32) | collective-permute-done | bytes 282656 | tf_op jit(solution)/shard_map/ppermute | solution.py:343
  201.3 9.0 %collective-permute-start.28 = (bf16[16,8192]{1,0:T(8,128)(2,1)S(1)}, bf16[16,8192]{1,0:T(8,128)(2,1)S(1)}, u32[]{:S(2)}, u32[]{:S(2)}) collective-permute-start(bf16[16,8192]{1,0:T(8,128)(2,1)S(1)} %get-tuple-element.149), channel_id=1, source_target_pairs={{0,4},{1,5},{2,6},{3,7},{4,0},{5,1},{6,2},{7,3},{8,12},{9,13},{10,... | collective-permute-start | bytes 786440 | tf_op jit(solution)/shard_map/ppermute | solution.py:343
  210.3 0.9 collective-permute-start.30
  211.2 7.3 %collective-permute-done.46.refs_14_.refs_17_ = bf16[16,8320]{1,0:T(8,128)(2,1)S(1)} collective-permute-done((bf16[16,8320]{1,0:T(8,128)(2,1)S(1)}, bf16[16,8320]{1,0:T(8,128)(2,1)S(1)}, u32[]{:S(2)}, u32[]{:S(2)}) %collective-permute-start.46) | collective-permute-done | bytes 266272 | tf_op jit(solution)/shard_map/ppermute | solution.py:343
  218.4 1.3 collective-permute-start.45
  220.5 2.7 collective-permute-done.28.refs_8_
  223.9 5.1 %collective-permute-done.30.refs_10_ = bf16[16,8192]{1,0:T(8,128)(2,1)S(1)} collective-permute-done((bf16[16,8192]{1,0:T(8,128)(2,1)S(1)}, bf16[16,8192]{1,0:T(8,128)(2,1)S(1)}, u32[]{:S(2)}, u32[]{:S(2)}) %collective-permute-start.30) | collective-permute-done | bytes 262176 | tf_op jit(solution)/shard_map/ppermute | solution.py:343
  229.0 1.1 collective-permute-start.31
  230.2 1.5 collective-permute-start.36
  231.6 4.2 %collective-permute-done.45.refs_13_.refs_16_ = bf16[16,8320]{1,0:T(8,128)(2,1)S(1)} collective-permute-done((bf16[16,8320]{1,0:T(8,128)(2,1)S(1)}, bf16[16,8320]{1,0:T(8,128)(2,1)S(1)}, u32[]{:S(2)}, u32[]{:S(2)}) %collective-permute-start.45) | collective-permute-done | bytes 266272 | tf_op jit(solution)/shard_map/ppermute | solution.py:343
  235.8 2.4 shard_map.92
  238.3 1.1 collective-permute-start.38
  239.3 2.0 collective-permute-start.37
  241.4 9.0 %collective-permute-done.36.refs_15_ = bf16[16,8192]{1,0:T(8,128)(2,1)S(1)} collective-permute-done((bf16[16,8192]{1,0:T(8,128)(2,1)S(1)}, bf16[16,8192]{1,0:T(8,128)(2,1)S(1)}, u32[]{:S(2)}, u32[]{:S(2)}) %collective-permute-start.36) | collective-permute-done | bytes 262176 | tf_op jit(solution)/shard_map/ppermute | solution.py:343
  250.4 1.6 collective-permute-start.40
  252.6 2.4 shard_map.93
  255.9 1.0 collective-permute-done.48
  258.1 2.7 collective-permute-start.49
  260.8 0.9 collective-permute-done.49
  262.3 2.2 collective-permute-start.50
  264.6 1.3 collective-permute-done.50
  266.5 1.9 collective-permute-start.51
  268.4 2.5 collective-permute-done.51
  271.7 3.0 %shard_map.94 = (bf16[64,8192]{1,0:T(8,128)(2,1)}, bf16[64,8192]{1,0:T(8,128)(2,1)}) custom-call(f32[1,1]{1,0:T(1,128)S(6)} %min.3.refs_0_, bf16[256,192]{1,0:T(8,128)(2,1)S(1)} %get-tuple-element.193.refs_1_, bf16[256,192]{1,0:T(8,128)(2,1)S(1)} %get-tuple-element.194.refs_2_, bf16[16,8320]{1,0:T(8,128)(2,1)S(1)} %get-tuple-element.173.refs_0_.refs_3_, ...), custom_call_target="tpu_custom_call" | custom-call | flops 1610612736 | bytes 10485760 | tf_op jit(solution)/shard_map/pallas_call | solution.py:315
  274.7 2.2 shard_map.91
  (69 shorter events, 7.8 us)
Async XLA Ops:
  0.6 5.1 %copy-start.5 = (s32[16]{0:T(128)S(1)}, s32[16]{0:T(128)}, u32[]{:S(2)}) copy-start(s32[16]{0:T(128)} %param.9) | copy-start | bytes 196
  0.6 5.1 %copy-start.4 = (s32[128,1]{0,1:T(1,128)S(1)}, s32[128,1]{0,1:T(1,128)}, u32[]{:S(2)}) copy-start(s32[128,1]{0,1:T(1,128)} %param.8) | copy-start | bytes 1540
  0.7 86.4 %copy-start.1 = (bf16[128,8192]{1,0:T(8,128)(2,1)S(1)}, bf16[128,8192]{1,0:T(8,128)(2,1)}, u32[]{:S(2)}) copy-start(bf16[128,8192]{1,0:T(8,128)(2,1)} %refs_4_.5) | copy-start | bytes 6291460
  2.8 23.8 %collective-permute-start.9 = (bf16[16,8192]{1,0:T(8,128)(2,1)}, bf16[16,8192]{1,0:T(8,128)(2,1)S(1)}, u32[]{:S(2)}, u32[]{:S(2)}) collective-permute-start(bf16[16,8192]{1,0:T(8,128)(2,1)} %get-tuple-element.200), channel_id=1, source_target_pairs={{0,8},{1,9},{2,10},{3,11},{4,12},{5,13},{6,14},{7,15},{8,0},{9,1},... | collective-permute-start | bytes 786440 | tf_op jit(solution)/shard_map/ppermute | solution.py:343
  2.8 35.0 %collective-permute-start.11 = (bf16[16,8192]{1,0:T(8,128)(2,1)S(1)}, bf16[16,8192]{1,0:T(8,128)(2,1)S(1)}, u32[]{:S(2)}, u32[]{:S(2)}) collective-permute-start(bf16[16,8192]{1,0:T(8,128)(2,1)S(1)} %get-tuple-element.199), channel_id=1, source_target_pairs={{0,8},{1,9},{2,10},{3,11},{4,12},{5,13},{6,14},{7,15},{8,0},{9,1},... | collective-permute-start | bytes 786440 | tf_op jit(solution)/shard_map/ppermute | solution.py:343
  5.9 1.6 copy-start.2
  7.5 134.9 %copy-start.3 = (bf16[1,64,8192]{2,1,0:T(8,128)(2,1)S(1)}, bf16[1,64,8192]{2,1,0:T(8,128)(2,1)}, u32[]{:S(2)}) copy-start(bf16[1,64,8192]{2,1,0:T(8,128)(2,1)} %param.11) | copy-start | bytes 3145732
  8.8 28.9 %collective-permute-start = (bf16[16,8192]{1,0:T(8,128)(2,1)S(1)}, bf16[16,8192]{1,0:T(8,128)(2,1)S(1)}, u32[]{:S(2)}, u32[]{:S(2)}) collective-permute-start(bf16[16,8192]{1,0:T(8,128)(2,1)S(1)} %get-tuple-element.101), channel_id=1, source_target_pairs={{0,1},{1,0},{2,3},{3,2},{4,5},{5,4},{6,7},{7,6},{8,9},{9,8},{10,11... | collective-permute-start | bytes 786440 | tf_op jit(solution)/shard_map/ppermute | solution.py:343
  8.9 33.7 %collective-permute-start.1 = (bf16[16,8192]{1,0:T(8,128)(2,1)S(1)}, bf16[16,8192]{1,0:T(8,128)(2,1)S(1)}, u32[]{:S(2)}, u32[]{:S(2)}) collective-permute-start(bf16[16,8192]{1,0:T(8,128)(2,1)S(1)} %get-tuple-element.102), channel_id=1, source_target_pairs={{0,2},{1,3},{2,0},{3,1},{4,6},{5,7},{6,4},{7,5},{8,10},{9,11},{10,... | collective-permute-start | bytes 786440 | tf_op jit(solution)/shard_map/ppermute | solution.py:343
  10.5 32.9 %collective-permute-start.8 = (bf16[16,8192]{1,0:T(8,128)(2,1)S(1)}, bf16[16,8192]{1,0:T(8,128)(2,1)S(1)}, u32[]{:S(2)}, u32[]{:S(2)}) collective-permute-start(bf16[16,8192]{1,0:T(8,128)(2,1)S(1)} %get-tuple-element.112), channel_id=1, source_target_pairs={{0,9},{1,8},{2,11},{3,10},{4,13},{5,12},{6,15},{7,14},{8,1},{9,0},... | collective-permute-start | bytes 786440 | tf_op jit(solution)/shard_map/ppermute | solution.py:343
  26.6 22.4 %collective-permute-start.7 = (bf16[16,8192]{1,0:T(8,128)(2,1)S(1)}, bf16[16,8192]{1,0:T(8,128)(2,1)S(1)}, u32[]{:S(2)}, u32[]{:S(2)}) collective-permute-start(bf16[16,8192]{1,0:T(8,128)(2,1)S(1)} %get-tuple-element.111), channel_id=1, source_target_pairs={{0,8},{1,9},{2,10},{3,11},{4,12},{5,13},{6,14},{7,15},{8,0},{9,1},... | collective-permute-start | bytes 786440 | tf_op jit(solution)/shard_map/ppermute | solution.py:343
  37.7 24.4 %collective-permute-start.2 = (bf16[16,8192]{1,0:T(8,128)(2,1)S(1)}, bf16[16,8192]{1,0:T(8,128)(2,1)S(1)}, u32[]{:S(2)}, u32[]{:S(2)}) collective-permute-start(bf16[16,8192]{1,0:T(8,128)(2,1)S(1)} %get-tuple-element.103), channel_id=1, source_target_pairs={{0,3},{1,2},{2,1},{3,0},{4,7},{5,6},{6,5},{7,4},{8,11},{9,10},{10,... | collective-permute-start | bytes 786440 | tf_op jit(solution)/shard_map/ppermute | solution.py:343
  37.8 28.7 %collective-permute-start.3 = (bf16[16,8192]{1,0:T(8,128)(2,1)S(1)}, bf16[16,8192]{1,0:T(8,128)(2,1)S(1)}, u32[]{:S(2)}, u32[]{:S(2)}) collective-permute-start(bf16[16,8192]{1,0:T(8,128)(2,1)S(1)} %get-tuple-element.104), channel_id=1, source_target_pairs={{0,4},{1,5},{2,6},{3,7},{4,0},{5,1},{6,2},{7,3},{8,12},{9,13},{10,... | collective-permute-start | bytes 786440 | tf_op jit(solution)/shard_map/ppermute | solution.py:343
  42.6 34.2 %collective-permute-start.12 = (bf16[16,8192]{1,0:T(8,128)(2,1)S(1)}, bf16[16,8192]{1,0:T(8,128)(2,1)S(1)}, u32[]{:S(2)}, u32[]{:S(2)}) collective-permute-start(bf16[16,8192]{1,0:T(8,128)(2,1)S(1)} %get-tuple-element.116), channel_id=1, source_target_pairs={{0,11},{1,10},{2,9},{3,8},{4,15},{5,14},{6,13},{7,12},{8,3},{9,2},... | collective-permute-start | bytes 786440 | tf_op jit(solution)/shard_map/ppermute | solution.py:343
  43.4 39.4 %collective-permute-start.10 = (bf16[16,8192]{1,0:T(8,128)(2,1)S(1)}, bf16[16,8192]{1,0:T(8,128)(2,1)S(1)}, u32[]{:S(2)}, u32[]{:S(2)}) collective-permute-start(bf16[16,8192]{1,0:T(8,128)(2,1)S(1)} %get-tuple-element.114), channel_id=1, source_target_pairs={{0,10},{1,11},{2,8},{3,9},{4,14},{5,15},{6,12},{7,13},{8,2},{9,3},... | collective-permute-start | bytes 786440 | tf_op jit(solution)/shard_map/ppermute | solution.py:343
  49.0 41.8 %collective-permute-start.13 = (bf16[16,8192]{1,0:T(8,128)(2,1)S(1)}, bf16[16,8192]{1,0:T(8,128)(2,1)S(1)}, u32[]{:S(2)}, u32[]{:S(2)}) collective-permute-start(bf16[16,8192]{1,0:T(8,128)(2,1)S(1)} %get-tuple-element.118), channel_id=1, source_target_pairs={{0,12},{1,13},{2,14},{3,15},{4,8},{5,9},{6,10},{7,11},{8,4},{9,5},... | collective-permute-start | bytes 786440 | tf_op jit(solution)/shard_map/ppermute | solution.py:343
  62.2 31.1 %collective-permute-start.16 = (bf16[16,8192]{1,0:T(8,128)(2,1)S(1)}, bf16[16,8192]{1,0:T(8,128)(2,1)S(1)}, u32[]{:S(2)}, u32[]{:S(2)}) collective-permute-start(bf16[16,8192]{1,0:T(8,128)(2,1)S(1)} %get-tuple-element.124), channel_id=1, source_target_pairs={{0,8},{1,9},{2,10},{3,11},{4,12},{5,13},{6,14},{7,15},{8,0},{9,1},... | collective-permute-start | bytes 786440 | tf_op jit(solution)/shard_map/ppermute | solution.py:343
  66.5 30.2 %collective-permute-start.4 = (bf16[16,8192]{1,0:T(8,128)(2,1)S(1)}, bf16[16,8192]{1,0:T(8,128)(2,1)S(1)}, u32[]{:S(2)}, u32[]{:S(2)}) collective-permute-start(bf16[16,8192]{1,0:T(8,128)(2,1)S(1)} %get-tuple-element.106), channel_id=1, source_target_pairs={{0,5},{1,4},{2,7},{3,6},{4,1},{5,0},{6,3},{7,2},{8,13},{9,12},{10,... | collective-permute-start | bytes 786440 | tf_op jit(solution)/shard_map/ppermute | solution.py:343
  76.8 23.5 %collective-permute-start.5 = (bf16[16,8192]{1,0:T(8,128)(2,1)S(1)}, bf16[16,8192]{1,0:T(8,128)(2,1)S(1)}, u32[]{:S(2)}, u32[]{:S(2)}) collective-permute-start(bf16[16,8192]{1,0:T(8,128)(2,1)S(1)} %get-tuple-element.108), channel_id=1, source_target_pairs={{0,6},{1,7},{2,4},{3,5},{4,2},{5,3},{6,0},{7,1},{8,14},{9,15},{10,... | collective-permute-start | bytes 786440 | tf_op jit(solution)/shard_map/ppermute | solution.py:343
  82.8 18.3 %collective-permute-start.6 = (bf16[16,8192]{1,0:T(8,128)(2,1)S(1)}, bf16[16,8192]{1,0:T(8,128)(2,1)S(1)}, u32[]{:S(2)}, u32[]{:S(2)}) collective-permute-start(bf16[16,8192]{1,0:T(8,128)(2,1)S(1)} %get-tuple-element.110), channel_id=1, source_target_pairs={{0,7},{1,6},{2,5},{3,4},{4,3},{5,2},{6,1},{7,0},{8,15},{9,14},{10,... | collective-permute-start | bytes 786440 | tf_op jit(solution)/shard_map/ppermute | solution.py:343
  90.8 12.2 %collective-permute-start.20 = (bf16[16,8320]{1,0:T(8,128)(2,1)S(1)}, bf16[16,8320]{1,0:T(8,128)(2,1)S(1)}, u32[]{:S(2)}, u32[]{:S(2)}) collective-permute-start(bf16[16,8320]{1,0:T(8,128)(2,1)S(1)} %get-tuple-element.135), channel_id=1, source_target_pairs={{0,1},{1,0},{2,3},{3,2},{4,5},{5,4},{6,7},{7,6},{8,9},{9,8},{10,11... | collective-permute-start | bytes 798728 | tf_op jit(solution)/shard_map/ppermute | solution.py:343
  93.2 32.7 %collective-permute-start.33 = (bf16[16,8192]{1,0:T(8,128)(2,1)S(1)}, bf16[16,8192]{1,0:T(8,128)(2,1)S(1)}, u32[]{:S(2)}, u32[]{:S(2)}) collective-permute-start(bf16[16,8192]{1,0:T(8,128)(2,1)S(1)} %get-tuple-element.157), channel_id=1, source_target_pairs={{0,8},{1,9},{2,10},{3,11},{4,12},{5,13},{6,14},{7,15},{8,0},{9,1},... | collective-permute-start | bytes 786440 | tf_op jit(solution)/shard_map/ppermute | solution.py:343
  96.7 34.8 %collective-permute-start.15 = (bf16[16,8192]{1,0:T(8,128)(2,1)S(1)}, bf16[16,8192]{1,0:T(8,128)(2,1)S(1)}, u32[]{:S(2)}, u32[]{:S(2)}) collective-permute-start(bf16[16,8192]{1,0:T(8,128)(2,1)S(1)} %get-tuple-element.122), channel_id=1, source_target_pairs={{0,14},{1,15},{2,12},{3,13},{4,10},{5,11},{6,8},{7,9},{8,6},{9,7},... | collective-permute-start | bytes 786440 | tf_op jit(solution)/shard_map/ppermute | solution.py:343
  100.3 36.8 %collective-permute-start.14 = (bf16[16,8192]{1,0:T(8,128)(2,1)S(1)}, bf16[16,8192]{1,0:T(8,128)(2,1)S(1)}, u32[]{:S(2)}, u32[]{:S(2)}) collective-permute-start(bf16[16,8192]{1,0:T(8,128)(2,1)S(1)} %get-tuple-element.120), channel_id=1, source_target_pairs={{0,13},{1,12},{2,15},{3,14},{4,9},{5,8},{6,11},{7,10},{8,5},{9,4},... | collective-permute-start | bytes 786440 | tf_op jit(solution)/shard_map/ppermute | solution.py:343
  101.1 41.3 %collective-permute-start.17 = (bf16[16,8192]{1,0:T(8,128)(2,1)S(1)}, bf16[16,8192]{1,0:T(8,128)(2,1)S(1)}, u32[]{:S(2)}, u32[]{:S(2)}) collective-permute-start(bf16[16,8192]{1,0:T(8,128)(2,1)S(1)} %get-tuple-element.125), channel_id=1, source_target_pairs={{0,15},{1,14},{2,13},{3,12},{4,11},{5,10},{6,9},{7,8},{8,7},{9,6},... | collective-permute-start | bytes 786440 | tf_op jit(solution)/shard_map/ppermute | solution.py:343
  103.0 41.8 %collective-permute-start.26 = (bf16[16,8320]{1,0:T(8,128)(2,1)S(1)}, bf16[16,8320]{1,0:T(8,128)(2,1)S(1)}, u32[]{:S(2)}, u32[]{:S(2)}) collective-permute-start(bf16[16,8320]{1,0:T(8,128)(2,1)S(1)} %get-tuple-element.147), channel_id=1, source_target_pairs={{0,3},{1,2},{2,1},{3,0},{4,7},{5,6},{6,5},{7,4},{8,11},{9,10},{10,... | collective-permute-start | bytes 798728 | tf_op jit(solution)/shard_map/ppermute | solution.py:343
  125.9 22.4 %collective-permute-start.18 = (bf16[16,8320]{1,0:T(8,128)(2,1)S(1)}, bf16[16,8320]{1,0:T(8,128)(2,1)S(1)}, u32[]{:S(2)}, u32[]{:S(2)}) collective-permute-start(bf16[16,8320]{1,0:T(8,128)(2,1)S(1)} %get-tuple-element.130), channel_id=1, source_target_pairs={{0,4},{1,5},{2,6},{3,7},{4,0},{5,1},{6,2},{7,3},{8,12},{9,13},{10,... | collective-permute-start | bytes 798728 | tf_op jit(solution)/shard_map/ppermute | solution.py:343
  131.5 16.9 %collective-permute-start.23 = (bf16[16,8320]{1,0:T(8,128)(2,1)S(1)}, bf16[16,8320]{1,0:T(8,128)(2,1)S(1)}, u32[]{:S(2)}, u32[]{:S(2)}) collective-permute-start(bf16[16,8320]{1,0:T(8,128)(2,1)S(1)} %get-tuple-element.141), channel_id=1, source_target_pairs={{0,2},{1,3},{2,0},{3,1},{4,6},{5,7},{6,4},{7,5},{8,10},{9,11},{10,... | collective-permute-start | bytes 798728 | tf_op jit(solution)/shard_map/ppermute | solution.py:343
  137.1 15.0 %collective-permute-start.21 = (bf16[16,8320]{1,0:T(8,128)(2,1)S(1)}, bf16[16,8320]{1,0:T(8,128)(2,1)S(1)}, u32[]{:S(2)}, u32[]{:S(2)}) collective-permute-start(bf16[16,8320]{1,0:T(8,128)(2,1)S(1)} %get-tuple-element.136), channel_id=1, source_target_pairs={{0,5},{1,4},{2,7},{3,6},{4,1},{5,0},{6,3},{7,2},{8,13},{9,12},{10,... | collective-permute-start | bytes 798728 | tf_op jit(solution)/shard_map/ppermute | solution.py:343
  142.4 23.9 %collective-permute-start.43 = (bf16[16,8320]{1,0:T(8,128)(2,1)S(1)}, bf16[16,8320]{1,0:T(8,128)(2,1)S(1)}, u32[]{:S(2)}, u32[]{:S(2)}) collective-permute-start(bf16[16,8320]{1,0:T(8,128)(2,1)S(1)} %get-tuple-element.179), channel_id=1, source_target_pairs={{0,11},{1,10},{2,9},{3,8},{4,15},{5,14},{6,13},{7,12},{8,3},{9,2},... | collective-permute-start | bytes 798728 | tf_op jit(solution)/shard_map/ppermute | solution.py:343
  142.4 9.0 %copy-start = (bf16[1,64,8192]{2,1,0:T(8,128)(2,1)S(1)}, bf16[1,64,8192]{2,1,0:T(8,128)(2,1)}, u32[]{:S(2)}) copy-start(bf16[1,64,8192]{2,1,0:T(8,128)(2,1)} %param.10) | copy-start | bytes 3145732
  144.8 27.2 %collective-permute-start.42 = (bf16[16,8320]{1,0:T(8,128)(2,1)S(1)}, bf16[16,8320]{1,0:T(8,128)(2,1)S(1)}, u32[]{:S(2)}, u32[]{:S(2)}) collective-permute-start(bf16[16,8320]{1,0:T(8,128)(2,1)S(1)} %get-tuple-element.177), channel_id=1, source_target_pairs={{0,10},{1,11},{2,8},{3,9},{4,14},{5,15},{6,12},{7,13},{8,2},{9,3},... | collective-permute-start | bytes 798728 | tf_op jit(solution)/shard_map/ppermute | solution.py:343
  148.3 35.4 %collective-permute-start.41 = (bf16[16,8320]{1,0:T(8,128)(2,1)S(1)}, bf16[16,8320]{1,0:T(8,128)(2,1)S(1)}, u32[]{:S(2)}, u32[]{:S(2)}) collective-permute-start(bf16[16,8320]{1,0:T(8,128)(2,1)S(1)} %get-tuple-element.175), channel_id=1, source_target_pairs={{0,9},{1,8},{2,11},{3,10},{4,13},{5,12},{6,15},{7,14},{8,1},{9,0},... | collective-permute-start | bytes 798728 | tf_op jit(solution)/shard_map/ppermute | solution.py:343
  148.4 36.8 %collective-permute-start.27 = (bf16[16,8320]{1,0:T(8,128)(2,1)S(1)}, bf16[16,8320]{1,0:T(8,128)(2,1)S(1)}, u32[]{:S(2)}, u32[]{:S(2)}) collective-permute-start(bf16[16,8320]{1,0:T(8,128)(2,1)S(1)} %get-tuple-element.148), channel_id=1, source_target_pairs={{0,7},{1,6},{2,5},{3,4},{4,3},{5,2},{6,1},{7,0},{8,15},{9,14},{10,... | collective-permute-start | bytes 798728 | tf_op jit(solution)/shard_map/ppermute | solution.py:343
  152.1 33.9 %collective-permute-start.24 = (bf16[16,8320]{1,0:T(8,128)(2,1)S(1)}, bf16[16,8320]{1,0:T(8,128)(2,1)S(1)}, u32[]{:S(2)}, u32[]{:S(2)}) collective-permute-start(bf16[16,8320]{1,0:T(8,128)(2,1)S(1)} %get-tuple-element.142), channel_id=1, source_target_pairs={{0,6},{1,7},{2,4},{3,5},{4,2},{5,3},{6,0},{7,1},{8,14},{9,15},{10,... | collective-permute-start | bytes 798728 | tf_op jit(solution)/shard_map/ppermute | solution.py:343
  166.3 18.4 %collective-permute-start.19 = (bf16[16,8192]{1,0:T(8,128)(2,1)S(1)}, bf16[16,8192]{1,0:T(8,128)(2,1)S(1)}, u32[]{:S(2)}, u32[]{:S(2)}) collective-permute-start(bf16[16,8192]{1,0:T(8,128)(2,1)S(1)} %get-tuple-element.131), channel_id=1, source_target_pairs={{0,1},{1,0},{2,3},{3,2},{4,5},{5,4},{6,7},{7,6},{8,9},{9,8},{10,11... | collective-permute-start | bytes 786440 | tf_op jit(solution)/shard_map/ppermute | solution.py:343
  172.0 29.3 %collective-permute-start.32 = (bf16[16,8832]{1,0:T(8,128)(2,1)S(1)}, bf16[16,8832]{1,0:T(8,128)(2,1)S(1)}, u32[]{:S(2)}, u32[]{:S(2)}) collective-permute-start(bf16[16,8832]{1,0:T(8,128)(2,1)S(1)} %shard_map.89), channel_id=1, source_target_pairs={{0,8},{1,9},{2,10},{3,11},{4,12},{5,13},{6,14},{7,15},{8,0},{9,1},... | collective-permute-start | bytes 847880 | tf_op jit(solution)/shard_map/ppermute | solution.py:343
  183.8 26.5 %collective-permute-start.47 = (bf16[16,8320]{1,0:T(8,128)(2,1)S(1)}, bf16[16,8320]{1,0:T(8,128)(2,1)S(1)}, u32[]{:S(2)}, u32[]{:S(2)}) collective-permute-start(bf16[16,8320]{1,0:T(8,128)(2,1)S(1)} %get-tuple-element.187), channel_id=1, source_target_pairs={{0,15},{1,14},{2,13},{3,12},{4,11},{5,10},{6,9},{7,8},{8,7},{9,6},... | collective-permute-start | bytes 798728 | tf_op jit(solution)/shard_map/ppermute | solution.py:343
  184.7 33.7 %collective-permute-start.46 = (bf16[16,8320]{1,0:T(8,128)(2,1)S(1)}, bf16[16,8320]{1,0:T(8,128)(2,1)S(1)}, u32[]{:S(2)}, u32[]{:S(2)}) collective-permute-start(bf16[16,8320]{1,0:T(8,128)(2,1)S(1)} %get-tuple-element.185), channel_id=1, source_target_pairs={{0,14},{1,15},{2,12},{3,13},{4,10},{5,11},{6,8},{7,9},{8,6},{9,7},... | collective-permute-start | bytes 798728 | tf_op jit(solution)/shard_map/ppermute | solution.py:343
  185.3 8.9 %collective-permute-start.22 = (bf16[16,8192]{1,0:T(8,128)(2,1)S(1)}, bf16[16,8192]{1,0:T(8,128)(2,1)S(1)}, u32[]{:S(2)}, u32[]{:S(2)}) collective-permute-start(bf16[16,8192]{1,0:T(8,128)(2,1)S(1)} %get-tuple-element.137), channel_id=1, source_target_pairs={{0,2},{1,3},{2,0},{3,1},{4,6},{5,7},{6,4},{7,5},{8,10},{9,11},{10,... | collective-permute-start | bytes 786440 | tf_op jit(solution)/shard_map/ppermute | solution.py:343
  186.1 24.2 %collective-permute-start.29 = (bf16[16,8192]{1,0:T(8,128)(2,1)S(1)}, bf16[16,8192]{1,0:T(8,128)(2,1)S(1)}, u32[]{:S(2)}, u32[]{:S(2)}) collective-permute-start(bf16[16,8192]{1,0:T(8,128)(2,1)S(1)} %get-tuple-element.151), channel_id=1, source_target_pairs={{0,5},{1,4},{2,7},{3,6},{4,1},{5,0},{6,3},{7,2},{8,13},{9,12},{10,... | collective-permute-start | bytes 786440 | tf_op jit(solution)/shard_map/ppermute | solution.py:343
  194.1 36.0 %collective-permute-start.44 = (bf16[16,8320]{1,0:T(8,128)(2,1)S(1)}, bf16[16,8320]{1,0:T(8,128)(2,1)S(1)}, u32[]{:S(2)}, u32[]{:S(2)}) collective-permute-start(bf16[16,8320]{1,0:T(8,128)(2,1)S(1)} %get-tuple-element.181), channel_id=1, source_target_pairs={{0,12},{1,13},{2,14},{3,15},{4,8},{5,9},{6,10},{7,11},{8,4},{9,5},... | collective-permute-start | bytes 798728 | tf_op jit(solution)/shard_map/ppermute | solution.py:343
  201.3 21.9 %collective-permute-start.28 = (bf16[16,8192]{1,0:T(8,128)(2,1)S(1)}, bf16[16,8192]{1,0:T(8,128)(2,1)S(1)}, u32[]{:S(2)}, u32[]{:S(2)}) collective-permute-start(bf16[16,8192]{1,0:T(8,128)(2,1)S(1)} %get-tuple-element.149), channel_id=1, source_target_pairs={{0,4},{1,5},{2,6},{3,7},{4,0},{5,1},{6,2},{7,3},{8,12},{9,13},{10,... | collective-permute-start | bytes 786440 | tf_op jit(solution)/shard_map/ppermute | solution.py:343
  210.3 13.7 %collective-permute-start.25 = (bf16[16,8192]{1,0:T(8,128)(2,1)S(1)}, bf16[16,8192]{1,0:T(8,128)(2,1)S(1)}, u32[]{:S(2)}, u32[]{:S(2)}) collective-permute-start(bf16[16,8192]{1,0:T(8,128)(2,1)S(1)} %get-tuple-element.143), channel_id=1, source_target_pairs={{0,3},{1,2},{2,1},{3,0},{4,7},{5,6},{6,5},{7,4},{8,11},{9,10},{10,... | collective-permute-start | bytes 786440 | tf_op jit(solution)/shard_map/ppermute | solution.py:343
  210.3 18.7 %collective-permute-start.30 = (bf16[16,8192]{1,0:T(8,128)(2,1)S(1)}, bf16[16,8192]{1,0:T(8,128)(2,1)S(1)}, u32[]{:S(2)}, u32[]{:S(2)}) collective-permute-start(bf16[16,8192]{1,0:T(8,128)(2,1)S(1)} %get-tuple-element.153), channel_id=1, source_target_pairs={{0,6},{1,7},{2,4},{3,5},{4,2},{5,3},{6,0},{7,1},{8,14},{9,15},{10,... | collective-permute-start | bytes 786440 | tf_op jit(solution)/shard_map/ppermute | solution.py:343
  218.4 17.4 %collective-permute-start.45 = (bf16[16,8320]{1,0:T(8,128)(2,1)S(1)}, bf16[16,8320]{1,0:T(8,128)(2,1)S(1)}, u32[]{:S(2)}, u32[]{:S(2)}) collective-permute-start(bf16[16,8320]{1,0:T(8,128)(2,1)S(1)} %get-tuple-element.183), channel_id=1, source_target_pairs={{0,13},{1,12},{2,15},{3,14},{4,9},{5,8},{6,11},{7,10},{8,5},{9,4},... | collective-permute-start | bytes 798728 | tf_op jit(solution)/shard_map/ppermute | solution.py:343
  223.2 15.0 %collective-permute-start.35 = (bf16[16,8192]{1,0:T(8,128)(2,1)S(1)}, bf16[16,8192]{1,0:T(8,128)(2,1)S(1)}, u32[]{:S(2)}, u32[]{:S(2)}) collective-permute-start(bf16[16,8192]{1,0:T(8,128)(2,1)S(1)} %get-tuple-element.162), channel_id=1, source_target_pairs={{0,2},{1,3},{2,0},{3,1},{4,6},{5,7},{6,4},{7,5},{8,10},{9,11},{10,... | collective-permute-start | bytes 786440 | tf_op jit(solution)/shard_map/ppermute | solution.py:343
  223.9 14.3 %collective-permute-start.34 = (bf16[16,8192]{1,0:T(8,128)(2,1)S(1)}, bf16[16,8192]{1,0:T(8,128)(2,1)S(1)}, u32[]{:S(2)}, u32[]{:S(2)}) collective-permute-start(bf16[16,8192]{1,0:T(8,128)(2,1)S(1)} %get-tuple-element.160), channel_id=1, source_target_pairs={{0,1},{1,0},{2,3},{3,2},{4,5},{5,4},{6,7},{7,6},{8,9},{9,8},{10,11... | collective-permute-start | bytes 786440 | tf_op jit(solution)/shard_map/ppermute | solution.py:343
  229.0 10.3 %collective-permute-start.31 = (bf16[16,8192]{1,0:T(8,128)(2,1)S(1)}, bf16[16,8192]{1,0:T(8,128)(2,1)S(1)}, u32[]{:S(2)}, u32[]{:S(2)}) collective-permute-start(bf16[16,8192]{1,0:T(8,128)(2,1)S(1)} %get-tuple-element.155), channel_id=1, source_target_pairs={{0,7},{1,6},{2,5},{3,4},{4,3},{5,2},{6,1},{7,0},{8,15},{9,14},{10,... | collective-permute-start | bytes 786440 | tf_op jit(solution)/shard_map/ppermute | solution.py:343
  230.2 20.2 %collective-permute-start.36 = (bf16[16,8192]{1,0:T(8,128)(2,1)S(1)}, bf16[16,8192]{1,0:T(8,128)(2,1)S(1)}, u32[]{:S(2)}, u32[]{:S(2)}) collective-permute-start(bf16[16,8192]{1,0:T(8,128)(2,1)S(1)} %get-tuple-element.164), channel_id=1, source_target_pairs={{0,3},{1,2},{2,1},{3,0},{4,7},{5,6},{6,5},{7,4},{8,11},{9,10},{10,... | collective-permute-start | bytes 786440 | tf_op jit(solution)/shard_map/ppermute | solution.py:343
  238.2 36.5 %collective-permute-start.39 = (bf16[16,8192]{1,0:T(8,128)(2,1)S(1)}, bf16[16,8192]{1,0:T(8,128)(2,1)S(1)}, u32[]{:S(2)}, u32[]{:S(2)}) collective-permute-start(bf16[16,8192]{1,0:T(8,128)(2,1)S(1)} %get-tuple-element.170), channel_id=1, source_target_pairs={{0,6},{1,7},{2,4},{3,5},{4,2},{5,3},{6,0},{7,1},{8,14},{9,15},{10,... | collective-permute-start | bytes 786440 | tf_op jit(solution)/shard_map/ppermute | solution.py:343
  238.3 36.4 %collective-permute-start.38 = (bf16[16,8192]{1,0:T(8,128)(2,1)S(1)}, bf16[16,8192]{1,0:T(8,128)(2,1)S(1)}, u32[]{:S(2)}, u32[]{:S(2)}) collective-permute-start(bf16[16,8192]{1,0:T(8,128)(2,1)S(1)} %get-tuple-element.168), channel_id=1, source_target_pairs={{0,5},{1,4},{2,7},{3,6},{4,1},{5,0},{6,3},{7,2},{8,13},{9,12},{10,... | collective-permute-start | bytes 786440 | tf_op jit(solution)/shard_map/ppermute | solution.py:343
  239.3 35.4 %collective-permute-start.37 = (bf16[16,8192]{1,0:T(8,128)(2,1)S(1)}, bf16[16,8192]{1,0:T(8,128)(2,1)S(1)}, u32[]{:S(2)}, u32[]{:S(2)}) collective-permute-start(bf16[16,8192]{1,0:T(8,128)(2,1)S(1)} %get-tuple-element.166), channel_id=1, source_target_pairs={{0,4},{1,5},{2,6},{3,7},{4,0},{5,1},{6,2},{7,3},{8,12},{9,13},{10,... | collective-permute-start | bytes 786440 | tf_op jit(solution)/shard_map/ppermute | solution.py:343
  250.4 24.3 %collective-permute-start.40 = (bf16[16,8192]{1,0:T(8,128)(2,1)S(1)}, bf16[16,8192]{1,0:T(8,128)(2,1)S(1)}, u32[]{:S(2)}, u32[]{:S(2)}) collective-permute-start(bf16[16,8192]{1,0:T(8,128)(2,1)S(1)} %get-tuple-element.172), channel_id=1, source_target_pairs={{0,7},{1,6},{2,5},{3,4},{4,3},{5,2},{6,1},{7,0},{8,15},{9,14},{10,... | collective-permute-start | bytes 786440 | tf_op jit(solution)/shard_map/ppermute | solution.py:343
  255.5 1.3 collective-permute-start.48
  258.1 3.6 %collective-permute-start.49 = (f32[1,1]{1,0:T(1,128)}, f32[1,1]{1,0:T(1,128)}, u32[]{:S(2)}, u32[]{:S(2)}) collective-permute-start(f32[1,1]{1,0:T(1,128)} %add.15), channel_id=1, source_target_pairs={{0,2},{1,3},{2,0},{3,1},{4,6},{5,7},{6,4},{7,5},{8,10},{9,11},{10,... | collective-permute-start | bytes 20 | tf_op jit(solution)/shard_map/ppermute | solution.py:30
  262.3 3.6 %collective-permute-start.50 = (f32[1,1]{1,0:T(1,128)}, f32[1,1]{1,0:T(1,128)}, u32[]{:S(2)}, u32[]{:S(2)}) collective-permute-start(f32[1,1]{1,0:T(1,128)} %add.16), channel_id=1, source_target_pairs={{0,4},{1,5},{2,6},{3,7},{4,0},{5,1},{6,2},{7,3},{8,12},{9,13},{10,... | collective-permute-start | bytes 20 | tf_op jit(solution)/shard_map/ppermute | solution.py:30
  266.5 4.5 %collective-permute-start.51 = (f32[1,1]{1,0:T(1,128)}, f32[1,1]{1,0:T(1,128)}, u32[]{:S(2)}, u32[]{:S(2)}) collective-permute-start(f32[1,1]{1,0:T(1,128)} %add.17), channel_id=1, source_target_pairs={{0,8},{1,9},{2,10},{3,11},{4,12},{5,13},{6,14},{7,15},{8,0},{9,1},... | collective-permute-start | bytes 20 | tf_op jit(solution)/shard_map/ppermute | solution.py:30

commit v7 on v6

--- a/solution.py
+++ b/solution.py
@@ -14,7 +14,7 @@
 CHUNK = 8192
 WEIGHT_FIRST = 2
 RATE = 1
-WEIGHT_MID = 11
+WEIGHT_MID = 10
 MIRROR_ORDER = [1, 2, 3, 4, 5, 6, 7]
 NEAR_WINDOW = 4
 LAST = (((1,), (1,)), ((), ()))

time: 279 us -> 281 us (level)
  starting transfers between devices: 98.1 us -> 102 us
    ppermute x48, starting transfers between devices: 90.8 us -> 94.2 us  [swap(): result = lax.ppermute(value, 'blk', [(i, i ^ partner) for i in range(size)])]
where the time goes in v7:
time: 281 us; the launch traced here: 278 us
  waiting for transfers between devices  151 us (54%)
  starting transfers between devices  102 us (36%)
  Pallas kernels  16.8 us (6%)
  local copies, waits for them, and re-layouts  4.43 us (2%)
  between operations  4.08 us (1%)
    ppermute x48, waiting for transfers between devices, swap(): result = lax.ppermute(value, 'blk', [(i, i ^ partner) for i in range(size)])  145 us
    ppermute x48, starting transfers between devices, swap(): result = lax.ppermute(value, 'blk', [(i, i ^ partner) for i in range(size)])  94.2 us
    ppermute x4, starting transfers between devices, total_over_blk(): lax.ppermute(value, 'blk', [(i, i ^ step) for i in range(size)])  7.32 us
  transfers between devices with their start and end apart: 52, of which 27 were waited for; matrix products, arithmetic and copies ran while one was open for 1% of the time, Pallas kernels for 5%

profile of v7, /device:TPU:16, one launch (start us, length us, event | category | flops | bytes accessed | tf_op | source)
XLA Modules:
  0.0 278.3 jit_solution(15872833698473976938)
XLA Ops:
  0.7 2.1 slice_bitcast_fusion
  2.8 2.9 %collective-permute-start.9 = (bf16[16,8192]{1,0:T(8,128)(2,1)S(1)}, bf16[16,8192]{1,0:T(8,128)(2,1)S(1)}, u32[]{:S(2)}, u32[]{:S(2)}) collective-permute-start(bf16[16,8192]{1,0:T(8,128)(2,1)S(1)} %get-tuple-element.200), channel_id=1, source_target_pairs={{0,8},{1,9},{2,10},{3,11},{4,12},{5,13},{6,14},{7,15},{8,0},{9,1},... | collective-permute-start | bytes 786440 | tf_op jit(solution)/shard_map/ppermute | solution.py:343
  5.9 1.6 copy-done.2
  7.5 1.3 shard_map.85
  8.9 1.6 collective-permute-start.1
  10.6 16.0 %collective-permute-done.14 = bf16[16,8192]{1,0:T(8,128)(2,1)S(1)} collective-permute-done((bf16[16,8192]{1,0:T(8,128)(2,1)}, bf16[16,8192]{1,0:T(8,128)(2,1)S(1)}, u32[]{:S(2)}, u32[]{:S(2)}) %collective-permute-start.14) | collective-permute-done | bytes 262176 | tf_op jit(solution)/shard_map/ppermute | solution.py:343
  26.6 3.3 %collective-permute-start.7 = (bf16[16,8192]{1,0:T(8,128)(2,1)S(1)}, bf16[16,8192]{1,0:T(8,128)(2,1)S(1)}, u32[]{:S(2)}, u32[]{:S(2)}) collective-permute-start(bf16[16,8192]{1,0:T(8,128)(2,1)S(1)} %get-tuple-element.111), channel_id=1, source_target_pairs={{0,8},{1,9},{2,10},{3,11},{4,12},{5,13},{6,14},{7,15},{8,0},{9,1},... | collective-permute-start | bytes 786440 | tf_op jit(solution)/shard_map/ppermute | solution.py:343
  29.9 7.9 %collective-permute-done.9 = bf16[16,8192]{1,0:T(8,128)(2,1)S(1)} collective-permute-done((bf16[16,8192]{1,0:T(8,128)(2,1)S(1)}, bf16[16,8192]{1,0:T(8,128)(2,1)S(1)}, u32[]{:S(2)}, u32[]{:S(2)}) %collective-permute-start.9) | collective-permute-done | bytes 262176 | tf_op jit(solution)/shard_map/ppermute | solution.py:343
  37.8 4.9 %collective-permute-start.3 = (bf16[16,8192]{1,0:T(8,128)(2,1)S(1)}, bf16[16,8192]{1,0:T(8,128)(2,1)S(1)}, u32[]{:S(2)}, u32[]{:S(2)}) collective-permute-start(bf16[16,8192]{1,0:T(8,128)(2,1)S(1)} %get-tuple-element.104), channel_id=1, source_target_pairs={{0,4},{1,5},{2,6},{3,7},{4,0},{5,1},{6,2},{7,3},{8,12},{9,13},{10,... | collective-permute-start | bytes 786440 | tf_op jit(solution)/shard_map/ppermute | solution.py:343
  43.4 2.4 collective-permute-start.10
  45.8 3.1 %collective-permute-done.7.refs_8_.refs_27_ = bf16[16,8192]{1,0:T(8,128)(2,1)S(1)} collective-permute-done((bf16[16,8192]{1,0:T(8,128)(2,1)S(1)}, bf16[16,8192]{1,0:T(8,128)(2,1)S(1)}, u32[]{:S(2)}, u32[]{:S(2)}) %collective-permute-start.7) | collective-permute-done | bytes 262176 | tf_op jit(solution)/shard_map/ppermute | solution.py:343
  49.0 13.2 %collective-permute-start.12 = (bf16[16,8192]{1,0:T(8,128)(2,1)S(1)}, bf16[16,8192]{1,0:T(8,128)(2,1)S(1)}, u32[]{:S(2)}, u32[]{:S(2)}) collective-permute-start(bf16[16,8192]{1,0:T(8,128)(2,1)S(1)} %get-tuple-element.118), channel_id=1, source_target_pairs={{0,12},{1,13},{2,14},{3,15},{4,8},{5,9},{6,10},{7,11},{8,4},{9,5},... | collective-permute-start | bytes 786440 | tf_op jit(solution)/shard_map/ppermute | solution.py:343
  62.2 4.5 %collective-permute-start.11 = (bf16[16,8192]{1,0:T(8,128)(2,1)S(1)}, bf16[16,8192]{1,0:T(8,128)(2,1)S(1)}, u32[]{:S(2)}, u32[]{:S(2)}) collective-permute-start(bf16[16,8192]{1,0:T(8,128)(2,1)S(1)} %get-tuple-element.116), channel_id=1, source_target_pairs={{0,11},{1,10},{2,9},{3,8},{4,15},{5,14},{6,13},{7,12},{8,3},{9,2},... | collective-permute-start | bytes 786440 | tf_op jit(solution)/shard_map/ppermute | solution.py:343
  66.7 10.2 %collective-permute-done.15 = bf16[16,8192]{1,0:T(8,128)(2,1)S(1)} collective-permute-done((bf16[16,8192]{1,0:T(8,128)(2,1)S(1)}, bf16[16,8192]{1,0:T(8,128)(2,1)S(1)}, u32[]{:S(2)}, u32[]{:S(2)}) %collective-permute-start.15) | collective-permute-done | bytes 262176 | tf_op jit(solution)/shard_map/ppermute | solution.py:343
  76.8 5.1 %collective-permute-start.5 = (bf16[16,8192]{1,0:T(8,128)(2,1)S(1)}, bf16[16,8192]{1,0:T(8,128)(2,1)S(1)}, u32[]{:S(2)}, u32[]{:S(2)}) collective-permute-start(bf16[16,8192]{1,0:T(8,128)(2,1)S(1)} %get-tuple-element.108), channel_id=1, source_target_pairs={{0,6},{1,7},{2,4},{3,5},{4,2},{5,3},{6,0},{7,1},{8,14},{9,15},{10,... | collective-permute-start | bytes 786440 | tf_op jit(solution)/shard_map/ppermute | solution.py:343
  81.9 0.9 collective-permute-done.10.refs_10_.refs_29_
  82.8 4.3 %collective-permute-start.6 = (bf16[16,8192]{1,0:T(8,128)(2,1)S(1)}, bf16[16,8192]{1,0:T(8,128)(2,1)S(1)}, u32[]{:S(2)}, u32[]{:S(2)}) collective-permute-start(bf16[16,8192]{1,0:T(8,128)(2,1)S(1)} %get-tuple-element.110), channel_id=1, source_target_pairs={{0,7},{1,6},{2,5},{3,4},{4,3},{5,2},{6,1},{7,0},{8,15},{9,14},{10,... | collective-permute-start | bytes 786440 | tf_op jit(solution)/shard_map/ppermute | solution.py:343
  87.1 1.3 shard_map.88
  88.3 2.5 collective-permute-done.12.refs_12_.refs_31_
  90.8 2.5 collective-permute-done.11.refs_11_.refs_30_
  93.3 3.3 %collective-permute-start.33 = (bf16[16,8192]{1,0:T(8,128)(2,1)S(1)}, bf16[16,8192]{1,0:T(8,128)(2,1)S(1)}, u32[]{:S(2)}, u32[]{:S(2)}) collective-permute-start(bf16[16,8192]{1,0:T(8,128)(2,1)S(1)} %get-tuple-element.157), channel_id=1, source_target_pairs={{0,8},{1,9},{2,10},{3,11},{4,12},{5,13},{6,14},{7,15},{8,0},{9,1},... | collective-permute-start | bytes 786440 | tf_op jit(solution)/shard_map/ppermute | solution.py:343
  96.5 3.6 %collective-permute-start.16 = (bf16[16,8192]{1,0:T(8,128)(2,1)S(1)}, bf16[16,8192]{1,0:T(8,128)(2,1)S(1)}, u32[]{:S(2)}, u32[]{:S(2)}) collective-permute-start(bf16[16,8192]{1,0:T(8,128)(2,1)S(1)} %get-tuple-element.123), channel_id=1, source_target_pairs={{0,14},{1,15},{2,12},{3,13},{4,10},{5,11},{6,8},{7,9},{8,6},{9,7},... | collective-permute-start | bytes 786440 | tf_op jit(solution)/shard_map/ppermute | solution.py:343
  100.2 0.8 collective-permute-done.6.refs_7_.refs_26_
  101.0 1.9 collective-permute-start.17
  102.9 22.9 %collective-permute-done.33 = bf16[16,8192]{1,0:T(8,128)(2,1)S(1)} collective-permute-done((bf16[16,8192]{1,0:T(8,128)(2,1)S(1)}, bf16[16,8192]{1,0:T(8,128)(2,1)S(1)}, u32[]{:S(2)}, u32[]{:S(2)}) %collective-permute-start.33) | collective-permute-done | bytes 262176 | tf_op jit(solution)/shard_map/ppermute | solution.py:343
  125.8 2.0 collective-permute-start.18
  127.7 4.3 %collective-permute-done.16.refs_14_.refs_33_ = bf16[16,8192]{1,0:T(8,128)(2,1)S(1)} collective-permute-done((bf16[16,8192]{1,0:T(8,128)(2,1)S(1)}, bf16[16,8192]{1,0:T(8,128)(2,1)S(1)}, u32[]{:S(2)}, u32[]{:S(2)}) %collective-permute-start.16) | collective-permute-done | bytes 262176 | tf_op jit(solution)/shard_map/ppermute | solution.py:343
  132.1 1.3 collective-permute-start.23
  133.3 4.0 %collective-permute-done.13.refs_13_.refs_32_ = bf16[16,8192]{1,0:T(8,128)(2,1)S(1)} collective-permute-done((bf16[16,8192]{1,0:T(8,128)(2,1)S(1)}, bf16[16,8192]{1,0:T(8,128)(2,1)S(1)}, u32[]{:S(2)}, u32[]{:S(2)}) %collective-permute-start.13) | collective-permute-done | bytes 262176 | tf_op jit(solution)/shard_map/ppermute | solution.py:343
  137.3 5.9 %collective-permute-done.17.refs_15_.refs_34_ = bf16[16,8192]{1,0:T(8,128)(2,1)S(1)} collective-permute-done((bf16[16,8192]{1,0:T(8,128)(2,1)S(1)}, bf16[16,8192]{1,0:T(8,128)(2,1)S(1)}, u32[]{:S(2)}, u32[]{:S(2)}) %collective-permute-start.17) | collective-permute-done | bytes 262176 | tf_op jit(solution)/shard_map/ppermute | solution.py:343
  143.2 2.4 shard_map.86
  145.6 3.5 %collective-permute-start.42 = (bf16[16,8320]{1,0:T(8,128)(2,1)S(1)}, bf16[16,8320]{1,0:T(8,128)(2,1)S(1)}, u32[]{:S(2)}, u32[]{:S(2)}) collective-permute-start(bf16[16,8320]{1,0:T(8,128)(2,1)S(1)} %get-tuple-element.177), channel_id=1, source_target_pairs={{0,10},{1,11},{2,8},{3,9},{4,14},{5,15},{6,12},{7,13},{8,2},{9,3},... | collective-permute-start | bytes 798728 | tf_op jit(solution)/shard_map/ppermute | solution.py:343
  149.2 4.0 %collective-permute-start.27 = (bf16[16,8320]{1,0:T(8,128)(2,1)S(1)}, bf16[16,8320]{1,0:T(8,128)(2,1)S(1)}, u32[]{:S(2)}, u32[]{:S(2)}) collective-permute-start(bf16[16,8320]{1,0:T(8,128)(2,1)S(1)} %get-tuple-element.148), channel_id=1, source_target_pairs={{0,7},{1,6},{2,5},{3,4},{4,3},{5,2},{6,1},{7,0},{8,15},{9,14},{10,... | collective-permute-start | bytes 798728 | tf_op jit(solution)/shard_map/ppermute | solution.py:343
  154.1 13.0 %collective-permute-done.43.refs_11_.refs_14_ = bf16[16,8320]{1,0:T(8,128)(2,1)S(1)} collective-permute-done((bf16[16,8320]{1,0:T(8,128)(2,1)S(1)}, bf16[16,8320]{1,0:T(8,128)(2,1)S(1)}, u32[]{:S(2)}, u32[]{:S(2)}) %collective-permute-start.43) | collective-permute-done | bytes 266272 | tf_op jit(solution)/shard_map/ppermute | solution.py:343
  167.6 5.2 %collective-permute-done.42.refs_10_.refs_13_ = bf16[16,8320]{1,0:T(8,128)(2,1)S(1)} collective-permute-done((bf16[16,8320]{1,0:T(8,128)(2,1)S(1)}, bf16[16,8320]{1,0:T(8,128)(2,1)S(1)}, u32[]{:S(2)}, u32[]{:S(2)}) %collective-permute-start.42) | collective-permute-done | bytes 266272 | tf_op jit(solution)/shard_map/ppermute | solution.py:343
  172.8 4.0 %collective-permute-start.32 = (bf16[16,8832]{1,0:T(8,128)(2,1)S(1)}, bf16[16,8832]{1,0:T(8,128)(2,1)S(1)}, u32[]{:S(2)}, u32[]{:S(2)}) collective-permute-start(bf16[16,8832]{1,0:T(8,128)(2,1)S(1)} %shard_map.89), channel_id=1, source_target_pairs={{0,8},{1,9},{2,10},{3,11},{4,12},{5,13},{6,14},{7,15},{8,0},{9,1},... | collective-permute-start | bytes 847880 | tf_op jit(solution)/shard_map/ppermute | solution.py:343
  176.9 7.7 %collective-permute-done.41.refs_9_.refs_12_ = bf16[16,8320]{1,0:T(8,128)(2,1)S(1)} collective-permute-done((bf16[16,8320]{1,0:T(8,128)(2,1)S(1)}, bf16[16,8320]{1,0:T(8,128)(2,1)S(1)}, u32[]{:S(2)}, u32[]{:S(2)}) %collective-permute-start.41) | collective-permute-done | bytes 266272 | tf_op jit(solution)/shard_map/ppermute | solution.py:343
  184.6 1.4 collective-permute-start.47
  186.0 1.5 collective-permute-start.46
  187.6 5.0 %collective-permute-start.29 = (bf16[16,8192]{1,0:T(8,128)(2,1)S(1)}, bf16[16,8192]{1,0:T(8,128)(2,1)S(1)}, u32[]{:S(2)}, u32[]{:S(2)}) collective-permute-start(bf16[16,8192]{1,0:T(8,128)(2,1)S(1)} %get-tuple-element.151), channel_id=1, source_target_pairs={{0,5},{1,4},{2,7},{3,6},{4,1},{5,0},{6,3},{7,2},{8,13},{9,12},{10,... | collective-permute-start | bytes 786440 | tf_op jit(solution)/shard_map/ppermute | solution.py:343
  192.6 3.2 %collective-permute-done.22.refs_6_ = bf16[16,8192]{1,0:T(8,128)(2,1)S(1)} collective-permute-done((bf16[16,8192]{1,0:T(8,128)(2,1)S(1)}, bf16[16,8192]{1,0:T(8,128)(2,1)S(1)}, u32[]{:S(2)}, u32[]{:S(2)}) %collective-permute-start.22) | collective-permute-done | bytes 262176 | tf_op jit(solution)/shard_map/ppermute | solution.py:343
  195.8 1.0 collective-permute-start.44
  196.8 5.2 %collective-permute-done.32.refs_0_.refs_8_.refs_11_ = bf16[16,8832]{1,0:T(8,128)(2,1)S(1)} collective-permute-done((bf16[16,8832]{1,0:T(8,128)(2,1)S(1)}, bf16[16,8832]{1,0:T(8,128)(2,1)S(1)}, u32[]{:S(2)}, u32[]{:S(2)}) %collective-permute-start.32) | collective-permute-done | bytes 282656 | tf_op jit(solution)/shard_map/ppermute | solution.py:343
  202.0 9.1 %collective-permute-start.28 = (bf16[16,8192]{1,0:T(8,128)(2,1)S(1)}, bf16[16,8192]{1,0:T(8,128)(2,1)S(1)}, u32[]{:S(2)}, u32[]{:S(2)}) collective-permute-start(bf16[16,8192]{1,0:T(8,128)(2,1)S(1)} %get-tuple-element.149), channel_id=1, source_target_pairs={{0,4},{1,5},{2,6},{3,7},{4,0},{5,1},{6,2},{7,3},{8,12},{9,13},{10,... | collective-permute-start | bytes 786440 | tf_op jit(solution)/shard_map/ppermute | solution.py:343
  212.0 10.5 %collective-permute-done.46.refs_14_.refs_17_ = bf16[16,8320]{1,0:T(8,128)(2,1)S(1)} collective-permute-done((bf16[16,8320]{1,0:T(8,128)(2,1)S(1)}, bf16[16,8320]{1,0:T(8,128)(2,1)S(1)}, u32[]{:S(2)}, u32[]{:S(2)}) %collective-permute-start.46) | collective-permute-done | bytes 266272 | tf_op jit(solution)/shard_map/ppermute | solution.py:343
  224.0 1.2 collective-permute-start.35
  225.3 5.1 %collective-permute-done.30.refs_10_ = bf16[16,8192]{1,0:T(8,128)(2,1)S(1)} collective-permute-done((bf16[16,8192]{1,0:T(8,128)(2,1)S(1)}, bf16[16,8192]{1,0:T(8,128)(2,1)S(1)}, u32[]{:S(2)}, u32[]{:S(2)}) %collective-permute-start.30) | collective-permute-done | bytes 262176 | tf_op jit(solution)/shard_map/ppermute | solution.py:343
  230.4 2.0 collective-permute-start.36
  232.3 5.1 %collective-permute-done.45.refs_13_.refs_16_ = bf16[16,8320]{1,0:T(8,128)(2,1)S(1)} collective-permute-done((bf16[16,8320]{1,0:T(8,128)(2,1)S(1)}, bf16[16,8320]{1,0:T(8,128)(2,1)S(1)}, u32[]{:S(2)}, u32[]{:S(2)}) %collective-permute-start.45) | collective-permute-done | bytes 266272 | tf_op jit(solution)/shard_map/ppermute | solution.py:343
  237.4 2.4 shard_map.92
  239.9 3.1 %collective-permute-start.38 = (bf16[16,8192]{1,0:T(8,128)(2,1)S(1)}, bf16[16,8192]{1,0:T(8,128)(2,1)S(1)}, u32[]{:S(2)}, u32[]{:S(2)}) collective-permute-start(bf16[16,8192]{1,0:T(8,128)(2,1)S(1)} %get-tuple-element.168), channel_id=1, source_target_pairs={{0,5},{1,4},{2,7},{3,6},{4,1},{5,0},{6,3},{7,2},{8,13},{9,12},{10,... | collective-permute-start | bytes 786440 | tf_op jit(solution)/shard_map/ppermute | solution.py:343
  243.0 1.0 collective-permute-start.37
  244.0 7.8 %collective-permute-done.36.refs_15_ = bf16[16,8192]{1,0:T(8,128)(2,1)S(1)} collective-permute-done((bf16[16,8192]{1,0:T(8,128)(2,1)S(1)}, bf16[16,8192]{1,0:T(8,128)(2,1)S(1)}, u32[]{:S(2)}, u32[]{:S(2)}) %collective-permute-start.36) | collective-permute-done | bytes 262176 | tf_op jit(solution)/shard_map/ppermute | solution.py:343
  251.7 1.7 collective-permute-start.40
  254.1 2.4 shard_map.93
  257.3 1.0 collective-permute-done.48
  259.5 2.4 collective-permute-start.49
  262.0 1.1 collective-permute-done.49
  263.7 1.7 collective-permute-start.50
  265.5 1.8 collective-permute-done.50
  267.9 2.9 %collective-permute-start.51 = (f32[1,1]{1,0:T(1,128)}, f32[1,1]{1,0:T(1,128)}, u32[]{:S(2)}, u32[]{:S(2)}) collective-permute-start(f32[1,1]{1,0:T(1,128)} %add.17), channel_id=1, source_target_pairs={{0,8},{1,9},{2,10},{3,11},{4,12},{5,13},{6,14},{7,15},{8,0},{9,1},... | collective-permute-start | bytes 20 | tf_op jit(solution)/shard_map/ppermute | solution.py:30
  270.8 1.6 collective-permute-done.51
  273.1 3.0 %shard_map.94 = (bf16[64,8192]{1,0:T(8,128)(2,1)}, bf16[64,8192]{1,0:T(8,128)(2,1)}) custom-call(f32[1,1]{1,0:T(1,128)S(6)} %min.3.refs_0_, bf16[256,192]{1,0:T(8,128)(2,1)S(1)} %get-tuple-element.193.refs_1_, bf16[256,192]{1,0:T(8,128)(2,1)S(1)} %get-tuple-element.194.refs_2_, bf16[16,8320]{1,0:T(8,128)(2,1)S(1)} %get-tuple-element.173.refs_0_.refs_3_, ...), custom_call_target="tpu_custom_call" | custom-call | flops 1610612736 | bytes 10485760 | tf_op jit(solution)/shard_map/pallas_call | solution.py:315
  276.1 2.2 shard_map.91
  (69 shorter events, 6.7 us)
Async XLA Ops:
  0.6 5.1 %copy-start.5 = (s32[16]{0:T(128)S(1)}, s32[16]{0:T(128)}, u32[]{:S(2)}) copy-start(s32[16]{0:T(128)} %param.9) | copy-start | bytes 196
  0.6 5.1 %copy-start.4 = (s32[128,1]{0,1:T(1,128)S(1)}, s32[128,1]{0,1:T(1,128)}, u32[]{:S(2)}) copy-start(s32[128,1]{0,1:T(1,128)} %param.8) | copy-start | bytes 1540
  0.7 86.4 %copy-start.1 = (bf16[128,8192]{1,0:T(8,128)(2,1)S(1)}, bf16[128,8192]{1,0:T(8,128)(2,1)}, u32[]{:S(2)}) copy-start(bf16[128,8192]{1,0:T(8,128)(2,1)} %refs_4_.5) | copy-start | bytes 6291460
  2.8 23.8 %collective-permute-start.14 = (bf16[16,8192]{1,0:T(8,128)(2,1)}, bf16[16,8192]{1,0:T(8,128)(2,1)S(1)}, u32[]{:S(2)}, u32[]{:S(2)}) collective-permute-start(bf16[16,8192]{1,0:T(8,128)(2,1)} %get-tuple-element.198), channel_id=1, source_target_pairs={{0,8},{1,9},{2,10},{3,11},{4,12},{5,13},{6,14},{7,15},{8,0},{9,1},... | collective-permute-start | bytes 786440 | tf_op jit(solution)/shard_map/ppermute | solution.py:343
  2.8 35.0 %collective-permute-start.9 = (bf16[16,8192]{1,0:T(8,128)(2,1)S(1)}, bf16[16,8192]{1,0:T(8,128)(2,1)S(1)}, u32[]{:S(2)}, u32[]{:S(2)}) collective-permute-start(bf16[16,8192]{1,0:T(8,128)(2,1)S(1)} %get-tuple-element.200), channel_id=1, source_target_pairs={{0,8},{1,9},{2,10},{3,11},{4,12},{5,13},{6,14},{7,15},{8,0},{9,1},... | collective-permute-start | bytes 786440 | tf_op jit(solution)/shard_map/ppermute | solution.py:343
  5.9 1.6 copy-start.2
  7.5 135.7 %copy-start.3 = (bf16[1,64,8192]{2,1,0:T(8,128)(2,1)S(1)}, bf16[1,64,8192]{2,1,0:T(8,128)(2,1)}, u32[]{:S(2)}) copy-start(bf16[1,64,8192]{2,1,0:T(8,128)(2,1)} %param.11) | copy-start | bytes 3145732
  8.8 28.9 %collective-permute-start = (bf16[16,8192]{1,0:T(8,128)(2,1)S(1)}, bf16[16,8192]{1,0:T(8,128)(2,1)S(1)}, u32[]{:S(2)}, u32[]{:S(2)}) collective-permute-start(bf16[16,8192]{1,0:T(8,128)(2,1)S(1)} %get-tuple-element.101), channel_id=1, source_target_pairs={{0,1},{1,0},{2,3},{3,2},{4,5},{5,4},{6,7},{7,6},{8,9},{9,8},{10,11... | collective-permute-start | bytes 786440 | tf_op jit(solution)/shard_map/ppermute | solution.py:343
  8.9 33.7 %collective-permute-start.1 = (bf16[16,8192]{1,0:T(8,128)(2,1)S(1)}, bf16[16,8192]{1,0:T(8,128)(2,1)S(1)}, u32[]{:S(2)}, u32[]{:S(2)}) collective-permute-start(bf16[16,8192]{1,0:T(8,128)(2,1)S(1)} %get-tuple-element.102), channel_id=1, source_target_pairs={{0,2},{1,3},{2,0},{3,1},{4,6},{5,7},{6,4},{7,5},{8,10},{9,11},{10,... | collective-permute-start | bytes 786440 | tf_op jit(solution)/shard_map/ppermute | solution.py:343
  10.5 32.9 %collective-permute-start.8 = (bf16[16,8192]{1,0:T(8,128)(2,1)S(1)}, bf16[16,8192]{1,0:T(8,128)(2,1)S(1)}, u32[]{:S(2)}, u32[]{:S(2)}) collective-permute-start(bf16[16,8192]{1,0:T(8,128)(2,1)S(1)} %get-tuple-element.112), channel_id=1, source_target_pairs={{0,9},{1,8},{2,11},{3,10},{4,13},{5,12},{6,15},{7,14},{8,1},{9,0},... | collective-permute-start | bytes 786440 | tf_op jit(solution)/shard_map/ppermute | solution.py:343
  26.6 22.4 %collective-permute-start.7 = (bf16[16,8192]{1,0:T(8,128)(2,1)S(1)}, bf16[16,8192]{1,0:T(8,128)(2,1)S(1)}, u32[]{:S(2)}, u32[]{:S(2)}) collective-permute-start(bf16[16,8192]{1,0:T(8,128)(2,1)S(1)} %get-tuple-element.111), channel_id=1, source_target_pairs={{0,8},{1,9},{2,10},{3,11},{4,12},{5,13},{6,14},{7,15},{8,0},{9,1},... | collective-permute-start | bytes 786440 | tf_op jit(solution)/shard_map/ppermute | solution.py:343
  37.7 24.4 %collective-permute-start.2 = (bf16[16,8192]{1,0:T(8,128)(2,1)S(1)}, bf16[16,8192]{1,0:T(8,128)(2,1)S(1)}, u32[]{:S(2)}, u32[]{:S(2)}) collective-permute-start(bf16[16,8192]{1,0:T(8,128)(2,1)S(1)} %get-tuple-element.103), channel_id=1, source_target_pairs={{0,3},{1,2},{2,1},{3,0},{4,7},{5,6},{6,5},{7,4},{8,11},{9,10},{10,... | collective-permute-start | bytes 786440 | tf_op jit(solution)/shard_map/ppermute | solution.py:343
  37.8 28.9 %collective-permute-start.3 = (bf16[16,8192]{1,0:T(8,128)(2,1)S(1)}, bf16[16,8192]{1,0:T(8,128)(2,1)S(1)}, u32[]{:S(2)}, u32[]{:S(2)}) collective-permute-start(bf16[16,8192]{1,0:T(8,128)(2,1)S(1)} %get-tuple-element.104), channel_id=1, source_target_pairs={{0,4},{1,5},{2,6},{3,7},{4,0},{5,1},{6,2},{7,3},{8,12},{9,13},{10,... | collective-permute-start | bytes 786440 | tf_op jit(solution)/shard_map/ppermute | solution.py:343
  42.6 34.2 %collective-permute-start.15 = (bf16[16,8192]{1,0:T(8,128)(2,1)S(1)}, bf16[16,8192]{1,0:T(8,128)(2,1)S(1)}, u32[]{:S(2)}, u32[]{:S(2)}) collective-permute-start(bf16[16,8192]{1,0:T(8,128)(2,1)S(1)} %get-tuple-element.122), channel_id=1, source_target_pairs={{0,8},{1,9},{2,10},{3,11},{4,12},{5,13},{6,14},{7,15},{8,0},{9,1},... | collective-permute-start | bytes 786440 | tf_op jit(solution)/shard_map/ppermute | solution.py:343
  43.4 39.4 %collective-permute-start.10 = (bf16[16,8192]{1,0:T(8,128)(2,1)S(1)}, bf16[16,8192]{1,0:T(8,128)(2,1)S(1)}, u32[]{:S(2)}, u32[]{:S(2)}) collective-permute-start(bf16[16,8192]{1,0:T(8,128)(2,1)S(1)} %get-tuple-element.114), channel_id=1, source_target_pairs={{0,10},{1,11},{2,8},{3,9},{4,14},{5,15},{6,12},{7,13},{8,2},{9,3},... | collective-permute-start | bytes 786440 | tf_op jit(solution)/shard_map/ppermute | solution.py:343
  49.0 41.8 %collective-permute-start.12 = (bf16[16,8192]{1,0:T(8,128)(2,1)S(1)}, bf16[16,8192]{1,0:T(8,128)(2,1)S(1)}, u32[]{:S(2)}, u32[]{:S(2)}) collective-permute-start(bf16[16,8192]{1,0:T(8,128)(2,1)S(1)} %get-tuple-element.118), channel_id=1, source_target_pairs={{0,12},{1,13},{2,14},{3,15},{4,8},{5,9},{6,10},{7,11},{8,4},{9,5},... | collective-permute-start | bytes 786440 | tf_op jit(solution)/shard_map/ppermute | solution.py:343
  62.2 31.1 %collective-permute-start.11 = (bf16[16,8192]{1,0:T(8,128)(2,1)S(1)}, bf16[16,8192]{1,0:T(8,128)(2,1)S(1)}, u32[]{:S(2)}, u32[]{:S(2)}) collective-permute-start(bf16[16,8192]{1,0:T(8,128)(2,1)S(1)} %get-tuple-element.116), channel_id=1, source_target_pairs={{0,11},{1,10},{2,9},{3,8},{4,15},{5,14},{6,13},{7,12},{8,3},{9,2},... | collective-permute-start | bytes 786440 | tf_op jit(solution)/shard_map/ppermute | solution.py:343
  66.7 29.9 %collective-permute-start.4 = (bf16[16,8192]{1,0:T(8,128)(2,1)S(1)}, bf16[16,8192]{1,0:T(8,128)(2,1)S(1)}, u32[]{:S(2)}, u32[]{:S(2)}) collective-permute-start(bf16[16,8192]{1,0:T(8,128)(2,1)S(1)} %get-tuple-element.106), channel_id=1, source_target_pairs={{0,5},{1,4},{2,7},{3,6},{4,1},{5,0},{6,3},{7,2},{8,13},{9,12},{10,... | collective-permute-start | bytes 786440 | tf_op jit(solution)/shard_map/ppermute | solution.py:343
  76.8 23.3 %collective-permute-start.5 = (bf16[16,8192]{1,0:T(8,128)(2,1)S(1)}, bf16[16,8192]{1,0:T(8,128)(2,1)S(1)}, u32[]{:S(2)}, u32[]{:S(2)}) collective-permute-start(bf16[16,8192]{1,0:T(8,128)(2,1)S(1)} %get-tuple-element.108), channel_id=1, source_target_pairs={{0,6},{1,7},{2,4},{3,5},{4,2},{5,3},{6,0},{7,1},{8,14},{9,15},{10,... | collective-permute-start | bytes 786440 | tf_op jit(solution)/shard_map/ppermute | solution.py:343
  82.8 18.2 %collective-permute-start.6 = (bf16[16,8192]{1,0:T(8,128)(2,1)S(1)}, bf16[16,8192]{1,0:T(8,128)(2,1)S(1)}, u32[]{:S(2)}, u32[]{:S(2)}) collective-permute-start(bf16[16,8192]{1,0:T(8,128)(2,1)S(1)} %get-tuple-element.110), channel_id=1, source_target_pairs={{0,7},{1,6},{2,5},{3,4},{4,3},{5,2},{6,1},{7,0},{8,15},{9,14},{10,... | collective-permute-start | bytes 786440 | tf_op jit(solution)/shard_map/ppermute | solution.py:343
  90.8 12.1 %collective-permute-start.20 = (bf16[16,8320]{1,0:T(8,128)(2,1)S(1)}, bf16[16,8320]{1,0:T(8,128)(2,1)S(1)}, u32[]{:S(2)}, u32[]{:S(2)}) collective-permute-start(bf16[16,8320]{1,0:T(8,128)(2,1)S(1)} %get-tuple-element.135), channel_id=1, source_target_pairs={{0,1},{1,0},{2,3},{3,2},{4,5},{5,4},{6,7},{7,6},{8,9},{9,8},{10,11... | collective-permute-start | bytes 798728 | tf_op jit(solution)/shard_map/ppermute | solution.py:343
  93.3 32.5 %collective-permute-start.33 = (bf16[16,8192]{1,0:T(8,128)(2,1)S(1)}, bf16[16,8192]{1,0:T(8,128)(2,1)S(1)}, u32[]{:S(2)}, u32[]{:S(2)}) collective-permute-start(bf16[16,8192]{1,0:T(8,128)(2,1)S(1)} %get-tuple-element.157), channel_id=1, source_target_pairs={{0,8},{1,9},{2,10},{3,11},{4,12},{5,13},{6,14},{7,15},{8,0},{9,1},... | collective-permute-start | bytes 786440 | tf_op jit(solution)/shard_map/ppermute | solution.py:343
  96.5 35.5 %collective-permute-start.16 = (bf16[16,8192]{1,0:T(8,128)(2,1)S(1)}, bf16[16,8192]{1,0:T(8,128)(2,1)S(1)}, u32[]{:S(2)}, u32[]{:S(2)}) collective-permute-start(bf16[16,8192]{1,0:T(8,128)(2,1)S(1)} %get-tuple-element.123), channel_id=1, source_target_pairs={{0,14},{1,15},{2,12},{3,13},{4,10},{5,11},{6,8},{7,9},{8,6},{9,7},... | collective-permute-start | bytes 786440 | tf_op jit(solution)/shard_map/ppermute | solution.py:343
  100.2 37.2 %collective-permute-start.13 = (bf16[16,8192]{1,0:T(8,128)(2,1)S(1)}, bf16[16,8192]{1,0:T(8,128)(2,1)S(1)}, u32[]{:S(2)}, u32[]{:S(2)}) collective-permute-start(bf16[16,8192]{1,0:T(8,128)(2,1)S(1)} %get-tuple-element.120), channel_id=1, source_target_pairs={{0,13},{1,12},{2,15},{3,14},{4,9},{5,8},{6,11},{7,10},{8,5},{9,4},... | collective-permute-start | bytes 786440 | tf_op jit(solution)/shard_map/ppermute | solution.py:343
  101.0 42.2 %collective-permute-start.17 = (bf16[16,8192]{1,0:T(8,128)(2,1)S(1)}, bf16[16,8192]{1,0:T(8,128)(2,1)S(1)}, u32[]{:S(2)}, u32[]{:S(2)}) collective-permute-start(bf16[16,8192]{1,0:T(8,128)(2,1)S(1)} %get-tuple-element.125), channel_id=1, source_target_pairs={{0,15},{1,14},{2,13},{3,12},{4,11},{5,10},{6,9},{7,8},{8,7},{9,6},... | collective-permute-start | bytes 786440 | tf_op jit(solution)/shard_map/ppermute | solution.py:343
  102.9 42.7 %collective-permute-start.26 = (bf16[16,8320]{1,0:T(8,128)(2,1)S(1)}, bf16[16,8320]{1,0:T(8,128)(2,1)S(1)}, u32[]{:S(2)}, u32[]{:S(2)}) collective-permute-start(bf16[16,8320]{1,0:T(8,128)(2,1)S(1)} %get-tuple-element.147), channel_id=1, source_target_pairs={{0,3},{1,2},{2,1},{3,0},{4,7},{5,6},{6,5},{7,4},{8,11},{9,10},{10,... | collective-permute-start | bytes 798728 | tf_op jit(solution)/shard_map/ppermute | solution.py:343
  125.8 23.4 %collective-permute-start.18 = (bf16[16,8320]{1,0:T(8,128)(2,1)S(1)}, bf16[16,8320]{1,0:T(8,128)(2,1)S(1)}, u32[]{:S(2)}, u32[]{:S(2)}) collective-permute-start(bf16[16,8320]{1,0:T(8,128)(2,1)S(1)} %get-tuple-element.130), channel_id=1, source_target_pairs={{0,4},{1,5},{2,6},{3,7},{4,0},{5,1},{6,2},{7,3},{8,12},{9,13},{10,... | collective-permute-start | bytes 798728 | tf_op jit(solution)/shard_map/ppermute | solution.py:343
  132.1 17.2 %collective-permute-start.23 = (bf16[16,8320]{1,0:T(8,128)(2,1)S(1)}, bf16[16,8320]{1,0:T(8,128)(2,1)S(1)}, u32[]{:S(2)}, u32[]{:S(2)}) collective-permute-start(bf16[16,8320]{1,0:T(8,128)(2,1)S(1)} %get-tuple-element.141), channel_id=1, source_target_pairs={{0,2},{1,3},{2,0},{3,1},{4,6},{5,7},{6,4},{7,5},{8,10},{9,11},{10,... | collective-permute-start | bytes 798728 | tf_op jit(solution)/shard_map/ppermute | solution.py:343
  137.3 16.6 %collective-permute-start.21 = (bf16[16,8320]{1,0:T(8,128)(2,1)S(1)}, bf16[16,8320]{1,0:T(8,128)(2,1)S(1)}, u32[]{:S(2)}, u32[]{:S(2)}) collective-permute-start(bf16[16,8320]{1,0:T(8,128)(2,1)S(1)} %get-tuple-element.136), channel_id=1, source_target_pairs={{0,5},{1,4},{2,7},{3,6},{4,1},{5,0},{6,3},{7,2},{8,13},{9,12},{10,... | collective-permute-start | bytes 798728 | tf_op jit(solution)/shard_map/ppermute | solution.py:343
  143.2 23.9 %collective-permute-start.43 = (bf16[16,8320]{1,0:T(8,128)(2,1)S(1)}, bf16[16,8320]{1,0:T(8,128)(2,1)S(1)}, u32[]{:S(2)}, u32[]{:S(2)}) collective-permute-start(bf16[16,8320]{1,0:T(8,128)(2,1)S(1)} %get-tuple-element.179), channel_id=1, source_target_pairs={{0,11},{1,10},{2,9},{3,8},{4,15},{5,14},{6,13},{7,12},{8,3},{9,2},... | collective-permute-start | bytes 798728 | tf_op jit(solution)/shard_map/ppermute | solution.py:343
  143.2 10.0 %copy-start = (bf16[1,64,8192]{2,1,0:T(8,128)(2,1)S(1)}, bf16[1,64,8192]{2,1,0:T(8,128)(2,1)}, u32[]{:S(2)}) copy-start(bf16[1,64,8192]{2,1,0:T(8,128)(2,1)} %param.10) | copy-start | bytes 3145732
  145.6 27.2 %collective-permute-start.42 = (bf16[16,8320]{1,0:T(8,128)(2,1)S(1)}, bf16[16,8320]{1,0:T(8,128)(2,1)S(1)}, u32[]{:S(2)}, u32[]{:S(2)}) collective-permute-start(bf16[16,8320]{1,0:T(8,128)(2,1)S(1)} %get-tuple-element.177), channel_id=1, source_target_pairs={{0,10},{1,11},{2,8},{3,9},{4,14},{5,15},{6,12},{7,13},{8,2},{9,3},... | collective-permute-start | bytes 798728 | tf_op jit(solution)/shard_map/ppermute | solution.py:343
  149.2 35.4 %collective-permute-start.41 = (bf16[16,8320]{1,0:T(8,128)(2,1)S(1)}, bf16[16,8320]{1,0:T(8,128)(2,1)S(1)}, u32[]{:S(2)}, u32[]{:S(2)}) collective-permute-start(bf16[16,8320]{1,0:T(8,128)(2,1)S(1)} %get-tuple-element.175), channel_id=1, source_target_pairs={{0,9},{1,8},{2,11},{3,10},{4,13},{5,12},{6,15},{7,14},{8,1},{9,0},... | collective-permute-start | bytes 798728 | tf_op jit(solution)/shard_map/ppermute | solution.py:343
  149.2 38.2 %collective-permute-start.27 = (bf16[16,8320]{1,0:T(8,128)(2,1)S(1)}, bf16[16,8320]{1,0:T(8,128)(2,1)S(1)}, u32[]{:S(2)}, u32[]{:S(2)}) collective-permute-start(bf16[16,8320]{1,0:T(8,128)(2,1)S(1)} %get-tuple-element.148), channel_id=1, source_target_pairs={{0,7},{1,6},{2,5},{3,4},{4,3},{5,2},{6,1},{7,0},{8,15},{9,14},{10,... | collective-permute-start | bytes 798728 | tf_op jit(solution)/shard_map/ppermute | solution.py:343
  153.9 33.7 %collective-permute-start.24 = (bf16[16,8320]{1,0:T(8,128)(2,1)S(1)}, bf16[16,8320]{1,0:T(8,128)(2,1)S(1)}, u32[]{:S(2)}, u32[]{:S(2)}) collective-permute-start(bf16[16,8320]{1,0:T(8,128)(2,1)S(1)} %get-tuple-element.142), channel_id=1, source_target_pairs={{0,6},{1,7},{2,4},{3,5},{4,2},{5,3},{6,0},{7,1},{8,14},{9,15},{10,... | collective-permute-start | bytes 798728 | tf_op jit(solution)/shard_map/ppermute | solution.py:343
  167.1 18.9 %collective-permute-start.19 = (bf16[16,8192]{1,0:T(8,128)(2,1)S(1)}, bf16[16,8192]{1,0:T(8,128)(2,1)S(1)}, u32[]{:S(2)}, u32[]{:S(2)}) collective-permute-start(bf16[16,8192]{1,0:T(8,128)(2,1)S(1)} %get-tuple-element.131), channel_id=1, source_target_pairs={{0,1},{1,0},{2,3},{3,2},{4,5},{5,4},{6,7},{7,6},{8,9},{9,8},{10,11... | collective-permute-start | bytes 786440 | tf_op jit(solution)/shard_map/ppermute | solution.py:343
  172.8 29.2 %collective-permute-start.32 = (bf16[16,8832]{1,0:T(8,128)(2,1)S(1)}, bf16[16,8832]{1,0:T(8,128)(2,1)S(1)}, u32[]{:S(2)}, u32[]{:S(2)}) collective-permute-start(bf16[16,8832]{1,0:T(8,128)(2,1)S(1)} %shard_map.89), channel_id=1, source_target_pairs={{0,8},{1,9},{2,10},{3,11},{4,12},{5,13},{6,14},{7,15},{8,0},{9,1},... | collective-permute-start | bytes 847880 | tf_op jit(solution)/shard_map/ppermute | solution.py:343
  184.6 26.8 %collective-permute-start.47 = (bf16[16,8320]{1,0:T(8,128)(2,1)S(1)}, bf16[16,8320]{1,0:T(8,128)(2,1)S(1)}, u32[]{:S(2)}, u32[]{:S(2)}) collective-permute-start(bf16[16,8320]{1,0:T(8,128)(2,1)S(1)} %get-tuple-element.187), channel_id=1, source_target_pairs={{0,15},{1,14},{2,13},{3,12},{4,11},{5,10},{6,9},{7,8},{8,7},{9,6},... | collective-permute-start | bytes 798728 | tf_op jit(solution)/shard_map/ppermute | solution.py:343
  186.0 36.5 %collective-permute-start.46 = (bf16[16,8320]{1,0:T(8,128)(2,1)S(1)}, bf16[16,8320]{1,0:T(8,128)(2,1)S(1)}, u32[]{:S(2)}, u32[]{:S(2)}) collective-permute-start(bf16[16,8320]{1,0:T(8,128)(2,1)S(1)} %get-tuple-element.185), channel_id=1, source_target_pairs={{0,14},{1,15},{2,12},{3,13},{4,10},{5,11},{6,8},{7,9},{8,6},{9,7},... | collective-permute-start | bytes 798728 | tf_op jit(solution)/shard_map/ppermute | solution.py:343
  187.4 8.4 %collective-permute-start.22 = (bf16[16,8192]{1,0:T(8,128)(2,1)S(1)}, bf16[16,8192]{1,0:T(8,128)(2,1)S(1)}, u32[]{:S(2)}, u32[]{:S(2)}) collective-permute-start(bf16[16,8192]{1,0:T(8,128)(2,1)S(1)} %get-tuple-element.137), channel_id=1, source_target_pairs={{0,2},{1,3},{2,0},{3,1},{4,6},{5,7},{6,4},{7,5},{8,10},{9,11},{10,... | collective-permute-start | bytes 786440 | tf_op jit(solution)/shard_map/ppermute | solution.py:343
  187.6 23.5 %collective-permute-start.29 = (bf16[16,8192]{1,0:T(8,128)(2,1)S(1)}, bf16[16,8192]{1,0:T(8,128)(2,1)S(1)}, u32[]{:S(2)}, u32[]{:S(2)}) collective-permute-start(bf16[16,8192]{1,0:T(8,128)(2,1)S(1)} %get-tuple-element.151), channel_id=1, source_target_pairs={{0,5},{1,4},{2,7},{3,6},{4,1},{5,0},{6,3},{7,2},{8,13},{9,12},{10,... | collective-permute-start | bytes 786440 | tf_op jit(solution)/shard_map/ppermute | solution.py:343
  195.8 34.5 %collective-permute-start.44 = (bf16[16,8320]{1,0:T(8,128)(2,1)S(1)}, bf16[16,8320]{1,0:T(8,128)(2,1)S(1)}, u32[]{:S(2)}, u32[]{:S(2)}) collective-permute-start(bf16[16,8320]{1,0:T(8,128)(2,1)S(1)} %get-tuple-element.181), channel_id=1, source_target_pairs={{0,12},{1,13},{2,14},{3,15},{4,8},{5,9},{6,10},{7,11},{8,4},{9,5},... | collective-permute-start | bytes 798728 | tf_op jit(solution)/shard_map/ppermute | solution.py:343
  202.0 22.1 %collective-permute-start.28 = (bf16[16,8192]{1,0:T(8,128)(2,1)S(1)}, bf16[16,8192]{1,0:T(8,128)(2,1)S(1)}, u32[]{:S(2)}, u32[]{:S(2)}) collective-permute-start(bf16[16,8192]{1,0:T(8,128)(2,1)S(1)} %get-tuple-element.149), channel_id=1, source_target_pairs={{0,4},{1,5},{2,6},{3,7},{4,0},{5,1},{6,2},{7,3},{8,12},{9,13},{10,... | collective-permute-start | bytes 786440 | tf_op jit(solution)/shard_map/ppermute | solution.py:343
  211.1 14.2 %collective-permute-start.25 = (bf16[16,8192]{1,0:T(8,128)(2,1)S(1)}, bf16[16,8192]{1,0:T(8,128)(2,1)S(1)}, u32[]{:S(2)}, u32[]{:S(2)}) collective-permute-start(bf16[16,8192]{1,0:T(8,128)(2,1)S(1)} %get-tuple-element.143), channel_id=1, source_target_pairs={{0,3},{1,2},{2,1},{3,0},{4,7},{5,6},{6,5},{7,4},{8,11},{9,10},{10,... | collective-permute-start | bytes 786440 | tf_op jit(solution)/shard_map/ppermute | solution.py:343
  211.4 19.0 %collective-permute-start.30 = (bf16[16,8192]{1,0:T(8,128)(2,1)S(1)}, bf16[16,8192]{1,0:T(8,128)(2,1)S(1)}, u32[]{:S(2)}, u32[]{:S(2)}) collective-permute-start(bf16[16,8192]{1,0:T(8,128)(2,1)S(1)} %get-tuple-element.153), channel_id=1, source_target_pairs={{0,6},{1,7},{2,4},{3,5},{4,2},{5,3},{6,0},{7,1},{8,14},{9,15},{10,... | collective-permute-start | bytes 786440 | tf_op jit(solution)/shard_map/ppermute | solution.py:343
  222.5 14.9 %collective-permute-start.45 = (bf16[16,8320]{1,0:T(8,128)(2,1)S(1)}, bf16[16,8320]{1,0:T(8,128)(2,1)S(1)}, u32[]{:S(2)}, u32[]{:S(2)}) collective-permute-start(bf16[16,8320]{1,0:T(8,128)(2,1)S(1)} %get-tuple-element.183), channel_id=1, source_target_pairs={{0,13},{1,12},{2,15},{3,14},{4,9},{5,8},{6,11},{7,10},{8,5},{9,4},... | collective-permute-start | bytes 798728 | tf_op jit(solution)/shard_map/ppermute | solution.py:343
  224.0 15.7 %collective-permute-start.35 = (bf16[16,8192]{1,0:T(8,128)(2,1)S(1)}, bf16[16,8192]{1,0:T(8,128)(2,1)S(1)}, u32[]{:S(2)}, u32[]{:S(2)}) collective-permute-start(bf16[16,8192]{1,0:T(8,128)(2,1)S(1)} %get-tuple-element.162), channel_id=1, source_target_pairs={{0,2},{1,3},{2,0},{3,1},{4,6},{5,7},{6,4},{7,5},{8,10},{9,11},{10,... | collective-permute-start | bytes 786440 | tf_op jit(solution)/shard_map/ppermute | solution.py:343
  225.3 14.6 %collective-permute-start.34 = (bf16[16,8192]{1,0:T(8,128)(2,1)S(1)}, bf16[16,8192]{1,0:T(8,128)(2,1)S(1)}, u32[]{:S(2)}, u32[]{:S(2)}) collective-permute-start(bf16[16,8192]{1,0:T(8,128)(2,1)S(1)} %get-tuple-element.160), channel_id=1, source_target_pairs={{0,1},{1,0},{2,3},{3,2},{4,5},{5,4},{6,7},{7,6},{8,9},{9,8},{10,11... | collective-permute-start | bytes 786440 | tf_op jit(solution)/shard_map/ppermute | solution.py:343
  230.4 12.6 %collective-permute-start.31 = (bf16[16,8192]{1,0:T(8,128)(2,1)S(1)}, bf16[16,8192]{1,0:T(8,128)(2,1)S(1)}, u32[]{:S(2)}, u32[]{:S(2)}) collective-permute-start(bf16[16,8192]{1,0:T(8,128)(2,1)S(1)} %get-tuple-element.155), channel_id=1, source_target_pairs={{0,7},{1,6},{2,5},{3,4},{4,3},{5,2},{6,1},{7,0},{8,15},{9,14},{10,... | collective-permute-start | bytes 786440 | tf_op jit(solution)/shard_map/ppermute | solution.py:343
  230.4 21.4 %collective-permute-start.36 = (bf16[16,8192]{1,0:T(8,128)(2,1)S(1)}, bf16[16,8192]{1,0:T(8,128)(2,1)S(1)}, u32[]{:S(2)}, u32[]{:S(2)}) collective-permute-start(bf16[16,8192]{1,0:T(8,128)(2,1)S(1)} %get-tuple-element.164), channel_id=1, source_target_pairs={{0,3},{1,2},{2,1},{3,0},{4,7},{5,6},{6,5},{7,4},{8,11},{9,10},{10,... | collective-permute-start | bytes 786440 | tf_op jit(solution)/shard_map/ppermute | solution.py:343
  239.8 36.3 %collective-permute-start.39 = (bf16[16,8192]{1,0:T(8,128)(2,1)S(1)}, bf16[16,8192]{1,0:T(8,128)(2,1)S(1)}, u32[]{:S(2)}, u32[]{:S(2)}) collective-permute-start(bf16[16,8192]{1,0:T(8,128)(2,1)S(1)} %get-tuple-element.170), channel_id=1, source_target_pairs={{0,6},{1,7},{2,4},{3,5},{4,2},{5,3},{6,0},{7,1},{8,14},{9,15},{10,... | collective-permute-start | bytes 786440 | tf_op jit(solution)/shard_map/ppermute | solution.py:343
  239.9 36.2 %collective-permute-start.38 = (bf16[16,8192]{1,0:T(8,128)(2,1)S(1)}, bf16[16,8192]{1,0:T(8,128)(2,1)S(1)}, u32[]{:S(2)}, u32[]{:S(2)}) collective-permute-start(bf16[16,8192]{1,0:T(8,128)(2,1)S(1)} %get-tuple-element.168), channel_id=1, source_target_pairs={{0,5},{1,4},{2,7},{3,6},{4,1},{5,0},{6,3},{7,2},{8,13},{9,12},{10,... | collective-permute-start | bytes 786440 | tf_op jit(solution)/shard_map/ppermute | solution.py:343
  243.0 33.1 %collective-permute-start.37 = (bf16[16,8192]{1,0:T(8,128)(2,1)S(1)}, bf16[16,8192]{1,0:T(8,128)(2,1)S(1)}, u32[]{:S(2)}, u32[]{:S(2)}) collective-permute-start(bf16[16,8192]{1,0:T(8,128)(2,1)S(1)} %get-tuple-element.166), channel_id=1, source_target_pairs={{0,4},{1,5},{2,6},{3,7},{4,0},{5,1},{6,2},{7,3},{8,12},{9,13},{10,... | collective-permute-start | bytes 786440 | tf_op jit(solution)/shard_map/ppermute | solution.py:343
  251.7 24.3 %collective-permute-start.40 = (bf16[16,8192]{1,0:T(8,128)(2,1)S(1)}, bf16[16,8192]{1,0:T(8,128)(2,1)S(1)}, u32[]{:S(2)}, u32[]{:S(2)}) collective-permute-start(bf16[16,8192]{1,0:T(8,128)(2,1)S(1)} %get-tuple-element.172), channel_id=1, source_target_pairs={{0,7},{1,6},{2,5},{3,4},{4,3},{5,2},{6,1},{7,0},{8,15},{9,14},{10,... | collective-permute-start | bytes 786440 | tf_op jit(solution)/shard_map/ppermute | solution.py:343
  257.0 1.2 collective-permute-start.48
  259.5 3.6 %collective-permute-start.49 = (f32[1,1]{1,0:T(1,128)}, f32[1,1]{1,0:T(1,128)}, u32[]{:S(2)}, u32[]{:S(2)}) collective-permute-start(f32[1,1]{1,0:T(1,128)} %add.15), channel_id=1, source_target_pairs={{0,2},{1,3},{2,0},{3,1},{4,6},{5,7},{6,4},{7,5},{8,10},{9,11},{10,... | collective-permute-start | bytes 20 | tf_op jit(solution)/shard_map/ppermute | solution.py:30
  263.7 3.6 %collective-permute-start.50 = (f32[1,1]{1,0:T(1,128)}, f32[1,1]{1,0:T(1,128)}, u32[]{:S(2)}, u32[]{:S(2)}) collective-permute-start(f32[1,1]{1,0:T(1,128)} %add.16), channel_id=1, source_target_pairs={{0,4},{1,5},{2,6},{3,7},{4,0},{5,1},{6,2},{7,3},{8,12},{9,13},{10,... | collective-permute-start | bytes 20 | tf_op jit(solution)/shard_map/ppermute | solution.py:30
  267.9 4.5 %collective-permute-start.51 = (f32[1,1]{1,0:T(1,128)}, f32[1,1]{1,0:T(1,128)}, u32[]{:S(2)}, u32[]{:S(2)}) collective-permute-start(f32[1,1]{1,0:T(1,128)} %add.17), channel_id=1, source_target_pairs={{0,8},{1,9},{2,10},{3,11},{4,12},{5,13},{6,14},{7,15},{8,0},{9,1},... | collective-permute-start | bytes 20 | tf_op jit(solution)/shard_map/ppermute | solution.py:30
